TPU v7x, 256 devices: a whole 4x4x8 slice. The times are simulated.
256 devices in a mesh: blk: 64 (over z, y, x_hi), rep: 4 (over x_lo, core).
Axes of the slice: x: 4 (x_hi: 2, x_lo: 2; x = x_hi * 2 + x_lo), y: 4, z: 8, core: 2. Of those that a mesh axis runs over, the one named last changes fastest.
Arguments:
- entities: float32 [131072, 256], P('blk'), may hold values from -3 to 3
- entity_acc: float32 [131072], P('blk'), may hold values from 0.001 to 1
- relations: float32 [2048, 256], replicated, may hold values from -6 to 6
- relation_acc: float32 [2048], replicated, may hold values from 0.1 to 10
- src_ids: int32 [64, 4096], P('blk', 'rep'), may hold values from 0 to 2047
- rel_ids: int32 [64, 4096], P('blk', 'rep'), may hold values from 0 to 2047
- dst_ids: int32 [64, 4096], P('blk', 'rep'), may hold values from 0 to 2047
- neg_ids: int32 [64, 16384], P('blk', 'rep'), may hold values from 0 to 2047
- counts: int32 [64, 4], P('blk', 'rep'), may hold values from 512 to 1024, as said below
Outputs:
- new_entities: float32 [131072, 256], P('blk')
- new_entity_acc: float32 [131072], P('blk')
- new_relations: float32 [2048, 256], replicated
- new_relation_acc: float32 [2048], replicated
Inputs may be any that keep to these rules, and one draw needn't show every extreme that they name: `counts`: every count lies between 512 and 1024; some bucket and replica row is full in every draw, at a place drawn from the seed.
All inputs are finite; a program needn't handle non-finite values.
Results may differ from a plain program's by a relative error of at most 0.0011.
Values may be sent and summed in bfloat16 or wider, within the bound.
No kernel may reach another device: no remote copies, remote signals or barrier semaphores. Data moves between devices by JAX's collectives and lax.ppermute only.
A program may use at most 64 MiB of HBM per device.

v0:
```python
import jax
import jax.numpy as jnp
from jax import lax
from jax.sharding import PartitionSpec as P

GROUP = 256
NEG = 1024


entity_rate = 0.1
relation_rate = 0.1


def passed_along(block, axis, distance):
    devices = range(lax.axis_size(axis))
    route = [((i - distance) % len(devices), i) for i in devices]
    return lax.ppermute(block, axis, route)


def complex_mul(left, right):
    half = left.shape[1] // 2
    left_real, left_imag = (left[:, :half], left[:, half:])
    right_real, right_imag = (right[:, :half], right[:, half:])
    return jnp.concatenate(
        [
            left_real * right_real - left_imag * right_imag,
            left_real * right_imag + left_imag * right_real,
        ],
        axis=1,
    )


def conj_mul(grad, other):
    half = grad.shape[1] // 2
    grad_real, grad_imag = (grad[:, :half], grad[:, half:])
    other_real, other_imag = (other[:, :half], other[:, half:])
    return jnp.concatenate(
        [
            grad_real * other_real + grad_imag * other_imag,
            -grad_real * other_imag + grad_imag * other_real,
        ],
        axis=1,
    )


def bucket_terms(
    src_rows, dst_rows, relations, src_index, rel_index, dst_index, neg_index, edge_count
):
    edges = src_index.shape[0]
    width = src_rows.shape[1]
    groups = edges // GROUP
    heads = jnp.take(src_rows, src_index, axis=0).astype(jnp.float32)
    tails = jnp.take(dst_rows, dst_index, axis=0).astype(jnp.float32)
    rel_rows = jnp.take(relations, rel_index, axis=0)
    product = complex_mul(heads, rel_rows)
    live_mask = (jnp.arange(edges, dtype=jnp.int32) < edge_count).astype(jnp.float32)
    positive = jnp.sum(product * tails, axis=1)
    pos_coef = -live_mask * jax.nn.sigmoid(-positive)
    product_low = product.astype(jnp.bfloat16).reshape(groups, GROUP, width)
    negatives = jnp.take(dst_rows, neg_index, axis=0).reshape(groups, NEG, width)
    neg_scores = jnp.einsum(
        "cid,cnd->cin", product_low, negatives, preferred_element_type=jnp.float32
    )
    neg_coef = (live_mask.reshape(groups, GROUP, 1) * jax.nn.sigmoid(neg_scores) / NEG).astype(
        jnp.bfloat16
    )
    neg_part = jnp.einsum("cin,cnd->cid", neg_coef, negatives, preferred_element_type=jnp.float32)
    grad_product = pos_coef[:, None] * tails + neg_part.reshape(edges, width)
    grad_neg = jnp.einsum("cin,cid->cnd", neg_coef, product_low, preferred_element_type=jnp.float32)
    rows = src_rows.shape[0]
    dst_grad = jnp.zeros((rows, width), jnp.float32).at[dst_index].add(pos_coef[:, None] * product)
    dst_grad = dst_grad.at[neg_index].add(grad_neg.reshape(groups * NEG, width))
    src_grad = (
        jnp.zeros((rows, width), jnp.float32).at[src_index].add(conj_mul(grad_product, rel_rows))
    )
    rel_grad = (
        jnp.zeros((relations.shape[0], width), jnp.float32)
        .at[rel_index]
        .add(conj_mul(grad_product, heads))
    )
    return (src_grad, dst_grad, rel_grad)


def adagrad_rows(rows, accum, grad, rate):
    new_accum = accum + jnp.mean(grad * grad, axis=1)
    return (rows - rate * grad / jnp.sqrt(new_accum)[:, None], new_accum)


def shards(
    entities, entity_acc, relations, relation_acc, src_ids, rel_ids, dst_ids, neg_ids, counts
):
    local_low = entities.astype(jnp.bfloat16)
    next_rows = passed_along(local_low, "blk", -1)
    src_grad, dst_grad, rel_grad = bucket_terms(
        local_low,
        next_rows,
        relations,
        src_ids[0],
        rel_ids[0],
        dst_ids[0],
        neg_ids[0],
        counts[0, 0],
    )
    returned = passed_along(dst_grad, "blk", 1)
    total = lax.psum(src_grad + returned, "rep")
    new_entities, new_entity_acc = adagrad_rows(entities, entity_acc, total, entity_rate)
    rel_total = lax.psum(rel_grad, ("blk", "rep"))
    new_relations, new_relation_acc = adagrad_rows(
        relations, relation_acc, rel_total, relation_rate
    )
    return (new_entities, new_entity_acc, new_relations, new_relation_acc)


def solution(mesh):
    in_specs = (
        P("blk", None),
        P("blk"),
        P(),
        P(),
        P("blk", "rep"),
        P("blk", "rep"),
        P("blk", "rep"),
        P("blk", "rep"),
        P("blk", "rep"),
    )
    out_specs = (P("blk", None), P("blk"), P(), P())
    return jax.shard_map(shards, mesh=mesh, in_specs=in_specs, out_specs=out_specs, check_vma=False)
```

profile of v0, /device:TPU:1, one launch (start us, length us, event | category | flops | bytes accessed | tf_op | source)
XLA Modules:
  0.0 460.0 jit_solution(4661275387359697798)
XLA Ops:
  7.2 2.7 convert_element_type.28
  9.9 11.3 %collective-permute-start = (bf16[2048,256]{1,0:T(8,128)(2,1)}, bf16[2048,256]{1,0:T(8,128)(2,1)S(1)}, u32[]{:S(2)}, u32[]{:S(2)}) collective-permute-start(bf16[2048,256]{1,0:T(8,128)(2,1)} %convert_element_type.28), channel_id=1, source_target_pairs={{4,0},{8,4},{12,8},{16,12},{20,16},{24,20},{28,24},{32,28},{36,32}... | collective-permute-start | bytes 3145736 | tf_op jit(solution)/shard_map/ppermute | solution.py:17
  21.3 6.1 %gather_fusion.2 = bf16[1024,256]{1,0:T(8,128)(2,1)} fusion(bf16[2048,256]{1,0:T(8,128)(2,1)} %convert_element_type.28, s32[1024]{0:T(1024)S(1)} %fusion.20), kind=kCustom, calls=%fused_computation.clone | custom fusion | bytes 1052672 | tf_op jit(solution)/shard_map/jit(_take)/gather | solution.py:52
  29.4 4.7 %gather_fusion = f32[1024,256]{1,0:T(8,128)} fusion(f32[2048,256]{1,0:T(8,128)S(1)} %copy-done, s32[1024]{0:T(1024)S(1)} %broadcast_clamp_fusion.1), kind=kCustom, calls=%fused_computation.2 | custom fusion | bytes 2101248 | tf_op jit(solution)/shard_map/jit(_take)/gather | solution.py:54
  34.1 1.3 select_convert_fusion
  37.0 6.3 %collective-permute-done = bf16[2048,256]{1,0:T(8,128)(2,1)S(1)} collective-permute-done((bf16[2048,256]{1,0:T(8,128)(2,1)}, bf16[2048,256]{1,0:T(8,128)(2,1)S(1)}, u32[]{:S(2)}, u32[]{:S(2)}) %collective-permute-start) | collective-permute-done | bytes 1048608 | tf_op jit(solution)/shard_map/ppermute | solution.py:17
  43.4 17.0 %gather_fusion.1 = bf16[4096,256]{1,0:T(8,128)(2,1)} fusion(bf16[2048,256]{1,0:T(8,128)(2,1)S(1)} %collective-permute-done, s32[4096]{0:T(1024)S(1)} %broadcast_clamp_fusion), kind=kCustom, calls=%fused_computation.3 | custom fusion | bytes 4210688 | tf_op jit(solution)/shard_map/jit(_take)/gather | solution.py:60
  60.4 3.2 multiply_convert_fusion
  64.9 2.9 fusion.18
  67.8 5.0 %gather_fusion.3 = bf16[1024,256]{1,0:T(8,128)(2,1)} fusion(bf16[2048,256]{1,0:T(8,128)(2,1)S(1)} %collective-permute-done, s32[1024]{0:T(1024)S(1)} %fusion.21), kind=kCustom, calls=%fused_computation.1.clone | custom fusion | bytes 1052672 | tf_op jit(solution)/shard_map/jit(_take)/gather | solution.py:53
  72.7 1.4 fusion.1
  74.2 7.6 %scatter_custom_fusion = f32[2048,256]{1,0:T(8,128)S(1)} fusion(s32[1024]{0:T(1024)S(1)} %bitcast.42, f32[]{:T(128)} %constant.26.clone.1, f32[1024,128]{1,0:T(8,128)} %get-tuple-element.18, f32[]{:T(128)} %constant.67, f32[1024,128]{1,0:T(8,128)} %get-tuple-element.10, f32[1024]{0:T(1024)S(1)} %divide_multiply_fusion), kind=kCustom, calls=%fused_computation.30 | custom fusion | flops 786432 | bytes 3149832 | tf_op jit(solution)/shard_map/scatter-add | solution.py:71
  81.7 23.6 %scatter_fusion = f32[2048,256]{1,0:T(8,128)S(1)} fusion(f32[2048,256]{1,0:T(8,128)S(1)} %scatter_custom_fusion, s32[4096]{0:T(1024)S(1)} %bitcast.34, f32[4096,256]{1,0:T(8,128)} %bitcast.26), kind=kCustom, calls=%fused_computation.5 | custom fusion | flops 1048576 | bytes 12599296 | tf_op jit(solution)/shard_map/scatter-add | solution.py:72
  105.6 3.0 fusion
  109.9 1.6 multiply_add_fusion.1
  111.5 8.1 %scatter_custom_fusion.3 = f32[2048,256]{1,0:T(8,128)} fusion(s32[1024]{0:T(1024)S(1)} %bitcast.41, f32[1024,128]{1,0:T(8,128)} %get-tuple-element.14, f32[]{:T(128)} %constant.67, f32[1024,128]{1,0:T(8,128)} %get-tuple-element.13, f32[]{:T(128)} %constant.26.clone.1), kind=kCustom, calls=%fused_computation.24 | custom fusion | flops 524288 | bytes 3145736 | tf_op jit(solution)/shard_map/scatter-add | solution.py:79
  119.7 40.5 %collective-permute-done.1 = f32[2048,256]{1,0:T(8,128)} collective-permute-done((f32[2048,256]{1,0:T(8,128)S(1)}, f32[2048,256]{1,0:T(8,128)}, u32[]{:S(2)}, u32[]{:S(2)}) %collective-permute-start.1) | collective-permute-done | bytes 2097184 | tf_op jit(solution)/shard_map/ppermute | solution.py:17
  160.2 9.0 %scatter_custom_fusion.2 = f32[2048,256]{1,0:T(8,128)} fusion(f32[2048,256]{1,0:T(8,128)} %collective-permute-done.1, s32[1024]{0:T(1024)S(1)} %bitcast.43, f32[1024,128]{1,0:T(8,128)S(1)} %copy-done.11, f32[]{:T(128)} %constant.67, f32[1024,128]{1,0:T(8,128)S(1)} %copy-done.12), kind=kCustom, calls=%fused_computation.20 | custom fusion | flops 524288 | bytes 3146240 | tf_op jit(solution)/shard_map/scatter-add | solution.py:74
  169.2 212.4 %all-reduce.5.cloned.1.call-done = f32[2048,256]{1,0:T(8,128)} async-done(((f32[2048,256]{1,0:T(8,128)}), f32[2048,256]{1,0:T(8,128)}) %all-reduce.5.cloned.1.call-update) | async-done | bytes 2097168 | tf_op jit(solution)/shard_map/psum | solution.py:107
  381.6 2.1 multiply_reduce_fusion
  384.3 1.8 divide_subtract_fusion
  386.0 61.3 %all-reduce.3.cloned.1.call-done = f32[2048,256]{1,0:T(8,128)} async-done(((f32[2048,256]{1,0:T(8,128)}), f32[2048,256]{1,0:T(8,128)}) %all-reduce.3.cloned.1.call-update) | async-done | bytes 2097168 | tf_op jit(solution)/shard_map/psum | solution.py:105
  447.3 1.9 multiply_reduce_fusion.1
  449.9 3.3 divide_subtract_fusion.1
  (67 shorter events, 7.1 us)
Async XLA Ops:
  7.2 14.1 %copy-start.16 = (s32[1,1024]{1,0:T(1,128)S(1)}, s32[1,1024]{1,0:T(1,128)}, u32[]{:S(2)}) copy-start(s32[1,1024]{1,0:T(1,128)} %param.15) | copy-start | bytes 12292
  7.2 14.1 %copy-start.15 = (s32[1,1024]{1,0:T(1,128)S(1)}, s32[1,1024]{1,0:T(1,128)}, u32[]{:S(2)}) copy-start(s32[1,1024]{1,0:T(1,128)} %param.17) | copy-start | bytes 12292
  7.2 374.4 %all-reduce.5.cloned.1.call-start = ((), (), s32[]{:S(2)}) async-start(), calls=%async_computation.1 | async-start | bytes 4194304 | tf_op jit(solution)/shard_map/psum | solution.py:107
  9.9 33.5 %collective-permute-start = (bf16[2048,256]{1,0:T(8,128)(2,1)}, bf16[2048,256]{1,0:T(8,128)(2,1)S(1)}, u32[]{:S(2)}, u32[]{:S(2)}) collective-permute-start(bf16[2048,256]{1,0:T(8,128)(2,1)} %convert_element_type.28), channel_id=1, source_target_pairs={{4,0},{8,4},{12,8},{16,12},{20,16},{24,20},{28,24},{32,28},{36,32}... | collective-permute-start | bytes 3145736 | tf_op jit(solution)/shard_map/ppermute | solution.py:17
  21.3 6.1 %copy-start.17 = (s32[1,1024]{1,0:T(1,128)S(1)}, s32[1,1024]{1,0:T(1,128)}, u32[]{:S(2)}) copy-start(s32[1,1024]{1,0:T(1,128)} %param.16) | copy-start | bytes 12292
  21.3 6.2 %copy-start.14 = (s32[1,4096]{1,0:T(1,128)S(1)}, s32[1,4096]{1,0:T(1,128)}, u32[]{:S(2)}) copy-start(s32[1,4096]{1,0:T(1,128)} %param.18) | copy-start | bytes 49156
  21.3 8.1 %copy-start = (f32[2048,256]{1,0:T(8,128)S(1)}, f32[2048,256]{1,0:T(8,128)}, u32[]{:S(2)}) copy-start(f32[2048,256]{1,0:T(8,128)} %param.13) | copy-start | bytes 6291460
  34.1 1.4 copy-start.9
  35.7 24.7 %copy-start.2 = (f32[1024,256]{1,0:T(8,128)}, f32[1024,256]{1,0:T(8,128)S(1)}, u32[]{:S(2)}) copy-start(f32[1024,256]{1,0:T(8,128)S(1)} %broadcast_select_fusion.3) | copy-start | bytes 3145732
  60.4 4.5 copy-start.13
  63.6 1.3 copy-start.10
  67.8 5.0 %copy-start.6 = (f32[1024,128]{1,0:T(8,128)S(1)}, f32[1024,128]{1,0:T(8,128)}, u32[]{:S(2)}) copy-start(f32[1024,128]{1,0:T(8,128)} %get-tuple-element.10) | copy-start | bytes 1572868
  67.8 5.0 %copy-start.7 = (f32[1024,128]{1,0:T(8,128)S(1)}, f32[1024,128]{1,0:T(8,128)}, u32[]{:S(2)}) copy-start(f32[1024,128]{1,0:T(8,128)} %get-tuple-element.18) | copy-start | bytes 1572868
  105.4 3.3 copy-start.8
  105.4 54.8 %collective-permute-start.1 = (f32[2048,256]{1,0:T(8,128)S(1)}, f32[2048,256]{1,0:T(8,128)}, u32[]{:S(2)}, u32[]{:S(2)}) collective-permute-start(f32[2048,256]{1,0:T(8,128)S(1)} %scatter_fusion), channel_id=1, source_target_pairs={{252,0},{0,4},{4,8},{8,12},{12,16},{16,20},{20,24},{24,28},{28,32}... | collective-permute-start | bytes 6291464 | tf_op jit(solution)/shard_map/ppermute | solution.py:17
  108.7 1.2 copy-start.3
  111.5 48.7 %copy-start.11 = (f32[1024,128]{1,0:T(8,128)S(1)}, f32[1024,128]{1,0:T(8,128)}, u32[]{:S(2)}) copy-start(f32[1024,128]{1,0:T(8,128)} %get-tuple-element.19) | copy-start | bytes 1572868
  111.5 48.7 %copy-start.12 = (f32[1024,128]{1,0:T(8,128)S(1)}, f32[1024,128]{1,0:T(8,128)}, u32[]{:S(2)}) copy-start(f32[1024,128]{1,0:T(8,128)} %get-tuple-element.20) | copy-start | bytes 1572868
  119.6 327.7 %all-reduce.3.cloned.1.call-start = ((), (), s32[]{:S(2)}) async-start(), calls=%async_computation | async-start | bytes 4194304 | tf_op jit(solution)/shard_map/psum | solution.py:105
  169.2 214.5 %copy-start.18 = (f32[2048]{0:T(1024)S(1)}, f32[2048]{0:T(1024)}, u32[]{:S(2)}) copy-start(f32[2048]{0:T(1024)} %param.14) | copy-start | bytes 24580
  169.2 215.1 %copy-start.1 = (f32[2048,256]{1,0:T(8,128)S(1)}, f32[2048,256]{1,0:T(8,128)}, u32[]{:S(2)}) copy-start(f32[2048,256]{1,0:T(8,128)} %param.13) | copy-start | bytes 6291460
  381.6 2.7 copy-start.5
  386.0 63.3 %copy-start.19 = (f32[2048]{0:T(1024)S(1)}, f32[2048]{0:T(1024)}, u32[]{:S(2)}) copy-start(f32[2048]{0:T(1024)} %param.12) | copy-start | bytes 24580
  386.0 63.9 %copy-start.4 = (f32[2048,256]{1,0:T(8,128)S(1)}, f32[2048,256]{1,0:T(8,128)}, u32[]{:S(2)}) copy-start(f32[2048,256]{1,0:T(8,128)} %param.11) | copy-start | bytes 6291460
Sparse Core Ops, SparseCore 0:
  119.7 261.7 all-reduce.4
  384.2 63.0 all-reduce.2
where the time goes:
time: 460 us
  waiting for transfers between devices  321 us (70%)
  other arithmetic  68.1 us (15%)
  local copies, waits for them, and re-layouts  35.6 us (8%)
  between operations  15 us (3%)
  starting transfers between devices  11.7 us (3%)
  matrix products  9.09 us (2%)
    psum x1, waiting for transfers between devices, shards(): rel_total = lax.psum(rel_grad, ('blk', 'rep'))  212 us
    psum x1, waiting for transfers between devices, shards(): total = lax.psum(src_grad + returned, 'rep')  61.3 us
    ppermute x2, waiting for transfers between devices, passed_along(): return lax.ppermute(block, axis, route)  46.8 us
    scatter-add x1, other arithmetic, bucket_terms(): dst_grad = dst_grad.at[neg_index].add(grad_neg.reshape(groups * NEG, width))  23.6 us
    gather x1, local copies, waits for them, and re-layouts, bucket_terms(): jnp.take(dst_rows, neg_index, axis=0).reshape(groups, NEG, width)  17 us
    ppermute x2, starting transfers between devices, passed_along(): return lax.ppermute(block, axis, route)  11.6 us
  transfers between devices with their start and end apart: 4, of which 4 were waited for; matrix products, arithmetic and copies ran while one was open for 9% of the time, Pallas kernels for 0%

commit v1 on v0

v1 whole, which is shorter than its diff:
```python
import functools

import jax
import jax.numpy as jnp
from jax import lax
from jax.experimental import pallas as pl
from jax.experimental.pallas import tpu as pltpu
from jax.sharding import PartitionSpec as P

F32 = jnp.float32
BF16 = jnp.bfloat16
D = 256
H = 128
ENT = 2048
EDGES = 1024
GROUP = 256
NEG = 1024
NREL = 2048
RATE = 0.1
AXES = ("blk", "rep")
VMEM_LIMIT = 48 * 1024 * 1024
CHUNK = 256


def vmem():
    return pl.BlockSpec(memory_space=pltpu.VMEM)


def smem():
    return pl.BlockSpec(memory_space=pltpu.SMEM)


def call(kernel, out_shape, n_smem, n_vmem, scratch=(), flops=0, bytes_accessed=0):
    return pl.pallas_call(
        kernel,
        out_shape=out_shape,
        in_specs=[smem()] * n_smem + [vmem()] * n_vmem,
        out_specs=jax.tree.map(lambda _: vmem(), out_shape),
        scratch_shapes=list(scratch),
        cost_estimate=pl.CostEstimate(
            flops=flops, bytes_accessed=bytes_accessed, transcendentals=0
        ),
        compiler_params=pltpu.CompilerParams(vmem_limit_bytes=VMEM_LIMIT),
    )


def columns(row):
    n = row.shape[1]
    parts = [
        jnp.transpose(jnp.broadcast_to(row[:, i : i + H], (H, H))) for i in range(0, n, H)
    ]
    return parts[0] if len(parts) == 1 else jnp.concatenate(parts, axis=0)


def one_hot_rows(col, n, base=0):
    e = col.shape[0]
    lane = lax.broadcasted_iota(jnp.int32, (e, H), 1)
    parts = [jnp.where(col == lane + (base + j), 1.0, 0.0).astype(BF16) for j in range(0, n, H)]
    return jnp.concatenate(parts, axis=1)


def one_hot_cols(row, n, base):
    e = row.shape[1]
    sub = lax.broadcasted_iota(jnp.int32, (n, e), 0) + base
    return jnp.where(jnp.broadcast_to(row, (n, e)) == sub, 1.0, 0.0).astype(BF16)


def dot(a, b):
    return jnp.dot(a, b, preferred_element_type=F32)


def dot_nt(a, b):
    return lax.dot_general(a, b, (((1,), (1,)), ((), ())), preferred_element_type=F32)


def gather_kernel(ids_ref, negs_ref, low_ref, rel_ref, head_ref, relrow_ref, prod_ref, cnt_ref, hi_ref, mid_ref, lo_ref):
    for r in range(0, NREL, 256):
        x = rel_ref[r : r + 256, :]
        for ref in (hi_ref, mid_ref, lo_ref):
            part = x.astype(BF16)
            ref[r : r + 256, :] = part
            x = x - part.astype(F32)

    def group(g, _):
        rows = pl.ds(pl.multiple_of(g * GROUP, GROUP), GROUP)
        src = columns(ids_ref[0:1, rows])
        heads = dot(one_hot_rows(src, ENT), low_ref[...])
        pick = one_hot_rows(columns(ids_ref[1:2, rows]), NREL)
        rel = dot(pick, hi_ref[...]) + dot(pick, mid_ref[...]) + dot(pick, lo_ref[...])
        hr, hi, rr, ri = heads[:, :H], heads[:, H:], rel[:, :H], rel[:, H:]
        head_ref[rows, :] = heads.astype(BF16)
        relrow_ref[rows, :] = rel
        prod_ref[rows, :H] = hr * rr - hi * ri
        prod_ref[rows, H:] = hr * ri + hi * rr
        negs = negs_ref[pl.ds(g, 1), :]
        high = one_hot_cols(lax.shift_right_logical(negs, 7), ENT // H, 0)
        low = one_hot_cols(lax.bitwise_and(negs, H - 1), H, 0)
        cnt_ref[g] = dot_nt(high, low) * (1.0 / NEG)
        return 0

    lax.fori_loop(0, EDGES // GROUP, group, 0)


def score_kernel(
    count_ref,
    ids_ref,
    near_ref,
    far_ref,
    head_ref,
    relrow_ref,
    prod_ref,
    cnt_ref,
    keep_ref,
    send_ref,
    cc_ref,
    plt_ref,
    pd_ref,
    gh_ref,
    gr_ref,
):
    half = ENT // 2
    count = count_ref[0, 0]

    def group(g, _):
        rows = pl.ds(pl.multiple_of(g * GROUP, GROUP), GROUP)
        dst = columns(ids_ref[2:3, rows])
        tails = dot(one_hot_rows(dst, half), near_ref[...]) + dot(
            one_hot_rows(dst, half, half), far_ref[...]
        )
        prod = prod_ref[rows, :]
        edge = lax.broadcasted_iota(jnp.int32, (GROUP, 1), 0) + g * GROUP
        live = jnp.where(edge < count, 1.0, 0.0).astype(F32)
        positive = jnp.sum(prod * tails, axis=1, keepdims=True)
        pos = -live * jax.nn.sigmoid(-positive)
        low = prod.astype(BF16)
        for j, table in ((0, near_ref), (1, far_ref)):
            scores = dot_nt(low, table[...])
            for i in range(half // H):
                w = cnt_ref[g, pl.ds(j * (half // H) + i, 1), :]
                part = scores[:, i * H : (i + 1) * H]
                cc_ref[rows, j * half + i * H : j * half + (i + 1) * H] = (
                    jax.nn.sigmoid(part) * w
                ).astype(BF16)
        neg = dot(cc_ref[rows, :half], near_ref[...]) + dot(cc_ref[rows, half:], far_ref[...])
        grad = pos * tails + live * neg
        rel = relrow_ref[rows, :]
        head = head_ref[rows, :].astype(F32)
        gr, gi = grad[:, :H], grad[:, H:]
        for out, other in ((gh_ref, rel), (gr_ref, head)):
            a, b = other[:, :H], other[:, H:]
            out[rows, :H] = (gr * a + gi * b).astype(BF16)
            out[rows, H:] = (gi * a - gr * b).astype(BF16)
        pd_ref[rows, :] = (pos * prod).astype(BF16)
        plt_ref[:, rows] = jnp.transpose(live * prod).astype(BF16)
        return 0

    lax.fori_loop(0, EDGES // GROUP, group, 0)

    def scatter(i, _):
        rows = pl.ds(pl.multiple_of(i * CHUNK, CHUNK), CHUNK)
        keep_ref[rows, :] = dot(one_hot_cols(ids_ref[3:4, :], CHUNK, i * CHUNK), gr_ref[...])
        send_ref[rows, :] = dot(
            one_hot_cols(ids_ref[3:4, :], CHUNK, half + i * CHUNK), gr_ref[...]
        ).astype(BF16)
        return 0

    lax.fori_loop(0, half // CHUNK, scatter, 0)


def scatter_kernel(
    place_ref,
    ids_ref,
    cc_ref,
    plt_ref,
    pd_ref,
    gh_ref,
    src_keep_ref,
    src_send_ref,
    dst_keep_ref,
    dst_send_ref,
):
    half = ENT // 2
    xl = place_ref[0]

    def scatter(i, _):
        rows = pl.ds(pl.multiple_of(i * CHUNK, CHUNK), CHUNK)
        to = lax.bitwise_xor(i, xl * (half // 2 // CHUNK))
        out = pl.ds(pl.multiple_of(to * CHUNK, CHUNK), CHUNK)
        for base, src_ref, dst_ref in (
            (0, src_keep_ref, dst_keep_ref),
            (half, src_send_ref, dst_send_ref),
        ):
            src = dot(one_hot_cols(ids_ref[4:5, :], CHUNK, base + i * CHUNK), gh_ref[...])
            src_ref[rows, :] = src.astype(src_ref.dtype)
            cols = pl.ds(pl.multiple_of(base + i * CHUNK, CHUNK), CHUNK)
            drawn = jnp.transpose(dot(plt_ref[...], cc_ref[:, cols]))
            dst = dot(one_hot_cols(ids_ref[2:3, :], CHUNK, base + i * CHUNK), pd_ref[...])
            dst_ref[out, :] = (drawn + dst).astype(dst_ref.dtype)
        return 0

    lax.fori_loop(0, half // CHUNK, scatter, 0)


def add_split_kernel(n_in, n_out, *refs):
    ins, outs = refs[:n_in], refs[n_in:]
    size = outs[0].shape[0]
    step = min(size, 64)
    for k, out in enumerate(outs):
        for r in range(0, size, step):
            total = ins[0][k * size + r : k * size + r + step, :].astype(F32)
            for ref in ins[1:]:
                total = total + ref[k * size + r : k * size + r + step, :].astype(F32)
            out[r : r + step, :] = total.astype(out.dtype)


def add_split(parts, n_out, own=BF16, sent=BF16):
    rows = parts[0].shape[0] // n_out
    shapes = [jax.ShapeDtypeStruct((rows, D), sent if k else own) for k in range(n_out)]
    return call(
        functools.partial(add_split_kernel, len(parts), n_out),
        shapes,
        0,
        len(parts),
        flops=len(parts) * n_out * rows * D,
        bytes_accessed=3 * len(parts) * n_out * rows * D,
    )(*parts)


def split3(x):
    hi = x.astype(BF16).astype(F32)
    mid = (x - hi).astype(BF16).astype(F32)
    return hi, mid, x - hi - mid


def sum_with_means_kernel(place_ref, *refs):
    parts, out_ref = refs[:-1], refs[-1]
    rows = parts[0].shape[0]
    step = min(rows, H)
    means = []
    for r in range(0, rows, step):
        terms = [ref[r : r + step, :].astype(F32) for ref in parts]
        if len(terms) == 8:
            z = place_ref[0]
            for bit in (1, 2, 4):
                flip = lax.bitwise_and(z, bit) != 0
                terms = [jnp.where(flip, terms[k ^ bit], terms[k]) for k in range(8)]
        total = terms[0]
        for term in terms[1:]:
            total = total + term
        out_ref[r : r + step, :] = total.astype(BF16)
        mean = jnp.sum(total * total, axis=1, keepdims=True) * (1.0 / D)
        mean = jnp.broadcast_to(mean, (step, H))
        if step < H:
            mean = jnp.concatenate([mean] * (H // step), axis=0)
        means.append(jnp.transpose(mean)[0:1, :])
    pad = jnp.zeros((8 - len(means), H), F32)
    hi, mid, lo = (jnp.concatenate([part, pad], axis=0) for part in split3(jnp.concatenate(means, axis=0)))
    top = jnp.concatenate([hi, mid], axis=1)
    bottom = jnp.concatenate([lo, jnp.zeros_like(lo)], axis=1)
    out_ref[rows : rows + 16, :] = jnp.concatenate([top, bottom], axis=0).astype(BF16)


def sum_with_means(parts, place=None):
    rows = parts[0].shape[0]
    place = jnp.zeros((1,), jnp.int32) if place is None else place.reshape(1)
    return call(
        sum_with_means_kernel,
        jax.ShapeDtypeStruct((rows + 16, D), BF16),
        1,
        len(parts),
        flops=len(parts) * rows * D,
        bytes_accessed=3 * len(parts) * rows * D,
    )(place, *parts)


def means_of(piece, start, row):
    tile = piece[pl.ds(pl.multiple_of(start, 16), 16), :].astype(F32)
    return tile[row : row + 1, :H] + tile[row : row + 1, H:] + tile[8 + row : 9 + row, :H]


def update_kernel(n_pieces, sub, place_ref, rows_ref, acc_ref, *refs):
    pieces, new_ref, new_acc_ref = refs[:n_pieces], refs[n_pieces], refs[n_pieces + 1]
    size = rows_ref.shape[0]
    i = pl.program_id(0)
    want = lax.bitwise_xor(i, place_ref[0])
    lane = lax.broadcasted_iota(jnp.int32, (1, H), 1)
    for k, piece in enumerate(pieces):

        @pl.when(want == k)
        def _(piece=piece):
            for r in range(0, size, H):
                if sub >= H:
                    g = piece[r : r + H, :].astype(F32)
                    mean = means_of(piece, size, r // H)
                else:
                    starts = [
                        lax.bitwise_xor(c // sub, place_ref[1]) * (sub + 16)
                        for c in range(r, r + H, sub)
                    ]
                    g = jnp.concatenate(
                        [
                            piece[pl.ds(pl.multiple_of(start, 16), sub), :].astype(F32)
                            for start in starts
                        ],
                        axis=0,
                    )
                    first, second = (means_of(piece, start + sub, 0) for start in starts)
                    mean = jnp.where(lane < sub, first, second)
                at = pl.ds(i * (size // H) + r // H, 1)
                acc = acc_ref[at, :] + mean
                new_acc_ref[at, :] = acc
                scale = jnp.transpose(jnp.broadcast_to(RATE / jnp.sqrt(acc), (H, H)))
                new_ref[r : r + H, :H] = rows_ref[r : r + H, :H] - g[:, :H] * scale
                new_ref[r : r + H, H:] = rows_ref[r : r + H, H:] - g[:, H:] * scale


def update(rows, acc, pieces, place, size, sub):
    n = rows.shape[0]
    whole = lambda i: (0, 0)
    new, new_acc = pl.pallas_call(
        functools.partial(update_kernel, len(pieces), sub),
        grid=(n // size,),
        out_shape=[
            jax.ShapeDtypeStruct((n, D), F32),
            jax.ShapeDtypeStruct((n // H, H), F32),
        ],
        in_specs=[
            smem(),
            pl.BlockSpec((size, D), lambda i: (i, 0)),
            pl.BlockSpec((n // H, H), whole),
        ]
        + [pl.BlockSpec(piece.shape, whole) for piece in pieces],
        out_specs=[
            pl.BlockSpec((size, D), lambda i: (i, 0)),
            pl.BlockSpec((n // H, H), whole),
        ],
        cost_estimate=pl.CostEstimate(flops=8 * n * D, bytes_accessed=10 * n * D, transcendentals=n),
        compiler_params=pltpu.CompilerParams(vmem_limit_bytes=VMEM_LIMIT),
    )(place, rows, acc.reshape(n // H, H), *pieces)
    return new, new_acc.reshape(n)


def swap(x, mask):
    return lax.ppermute(x, AXES, [(i, i ^ mask) for i in range(256)])


def shift(x, distance, mask):
    route = [(((i // 4 - distance) % 64) * 4 + ((i % 4) ^ mask), i) for i in range(256)]
    return lax.ppermute(x, AXES, route)


CORE, XL = 1, 2
X_MASKS = (2, 4, 6)
Y_MASKS = (8, 16, 24)
Z_MASKS = tuple(range(32, 256, 32))


def shards(
    entities, entity_acc, relations, relation_acc, src_ids, rel_ids, dst_ids, neg_ids, counts
):
    blk, rep = lax.axis_index("blk"), lax.axis_index("rep")
    core, xl = rep % 2, rep // 2
    x = (blk % 2) * 2 + xl
    y = (blk // 2) % 4

    low = entities.astype(BF16)
    half = lax.dynamic_slice_in_dim(entities, core * (ENT // 2), ENT // 2, 0).astype(BF16)
    near = shift(half, -1, XL)
    far = swap(near, CORE)

    ids = jnp.concatenate(
        [
            src_ids,
            rel_ids,
            dst_ids ^ (core * 1024),
            rel_ids ^ (core * 1024 + x * 256 + y * 64),
            src_ids ^ (core * 1024 + xl * 512),
            jnp.zeros((3, EDGES), jnp.int32),
        ],
        axis=0,
    )
    negs = (neg_ids ^ (core * 1024)).reshape(4, NEG)
    head, rel_rows, prod, cnt = call(
        gather_kernel,
        [
            jax.ShapeDtypeStruct((EDGES, D), BF16),
            jax.ShapeDtypeStruct((EDGES, D), F32),
            jax.ShapeDtypeStruct((EDGES, D), F32),
            jax.ShapeDtypeStruct((4, ENT // H, H), F32),
        ],
        0,
        4,
        [pltpu.VMEM((NREL, D), BF16)] * 3,
        flops=4 * 2 * EDGES * ENT * D,
        bytes_accessed=1 << 22,
    )(ids, negs, low, relations)

    kept = jax.ShapeDtypeStruct((ENT // 2, D), F32)
    sent = jax.ShapeDtypeStruct((ENT // 2, D), BF16)
    rel_keep, rel_send, cc, plt, pd, gh = call(
        score_kernel,
        [
            kept,
            sent,
            jax.ShapeDtypeStruct((EDGES, ENT), BF16),
            jax.ShapeDtypeStruct((D, EDGES), BF16),
            jax.ShapeDtypeStruct((EDGES, D), BF16),
            jax.ShapeDtypeStruct((EDGES, D), BF16),
        ],
        1,
        7,
        [pltpu.VMEM((EDGES, D), BF16)],
        flops=4 * 2 * EDGES * ENT * D,
        bytes_accessed=1 << 23,
    )(counts, ids, near, far, head, rel_rows, prod, cnt)
    src_keep, src_send, dst_keep, dst_send = call(
        scatter_kernel,
        [kept, sent, kept, sent],
        1,
        5,
        flops=3 * 2 * EDGES * ENT * D,
        bytes_accessed=1 << 23,
    )(xl.reshape(1), ids, cc, plt, pd, gh)

    rel_recv = swap(rel_send, CORE)
    parts = add_split([rel_keep, rel_recv], 4, own=F32)
    recv = [swap(part, mask) for part, mask in zip(parts[1:], X_MASKS)]
    src_recv = swap(src_send, CORE)
    dst_recv = swap(dst_send, CORE)
    src_own, src_away = add_split([src_keep, src_recv], 2, own=F32)
    dst_own, dst_away = add_split([dst_keep, dst_recv], 2)

    parts = add_split([parts[0], *recv], 4, own=F32)
    recv = [swap(part, mask) for part, mask in zip(parts[1:], Y_MASKS)]
    (mine,) = add_split([parts[0], *recv], 1)

    src_other = swap(src_away, XL)
    dst_first = shift(dst_own, 1, 0)
    dst_second = shift(dst_away, 1, XL)

    others = [swap(mine, mask) for mask in Z_MASKS]
    ent_own = sum_with_means([src_own, src_other, dst_first, dst_second])
    ent_xl = swap(ent_own, XL)
    ent_core = [swap(ent_own, CORE), swap(ent_xl, CORE)]
    place = jnp.stack([core * 2 + xl, jnp.zeros_like(core)])
    new_entities, new_entity_acc = update(
        entities, entity_acc, [ent_own, ent_xl, *ent_core], place, 512, 512
    )

    z = blk // 8
    total = sum_with_means([mine, *others], z)
    recv = [swap(total, mask) for mask in Y_MASKS]
    quarter = jnp.concatenate([total, *recv], axis=0)
    pieces = [quarter, *[swap(quarter, mask) for mask in X_MASKS]]
    pieces = pieces + [swap(piece, CORE) for piece in pieces]
    place = jnp.stack([core * 4 + x, y])
    new_relations, new_relation_acc = update(relations, relation_acc, pieces, place, 256, 64)
    return (new_entities, new_entity_acc, new_relations, new_relation_acc)


def solution(mesh):
    in_specs = (
        P("blk", None),
        P("blk"),
        P(),
        P(),
        P("blk", "rep"),
        P("blk", "rep"),
        P("blk", "rep"),
        P("blk", "rep"),
        P("blk", "rep"),
    )
    out_specs = (P("blk", None), P("blk"), P(), P())
    return jax.shard_map(shards, mesh=mesh, in_specs=in_specs, out_specs=out_specs, check_vma=False)
```

time: 460 us -> 141 us (0.31)
  waiting for transfers between devices: 321 us -> 41.7 us
  other arithmetic: 68.1 us -> 1.91 us
  starting transfers between devices: 11.7 us -> 58.5 us
  Pallas kernels: 0 us -> 32.2 us
  local copies, waits for them, and re-layouts: 35.6 us -> 4.88 us
  between operations: 15 us -> 1.61 us
  matrix products: 9.09 us -> 0 us
    psum x2 -> x0, waiting for transfers between devices: 274 us -> none  [the longest x1 212 us: shards(): rel_total = lax.psum(rel_grad, ('blk', 'rep'))]
    scatter-add x4 -> x0, other arithmetic: 48.3 us -> none  [the longest x1 23.6 us: bucket_terms(): dst_grad = dst_grad.at[neg_index].add(grad_neg.reshape(groups * NEG, width))]
    ppermute x2 -> x34, starting transfers between devices: 11.6 us -> 58.5 us  [the longest x31 46.3 us: swap(): return lax.ppermute(x, AXES, [(i, i ^ mask) for i in range(256)])]
    gather x4 -> x0, local copies, waits for them, and re-layouts: 32.8 us -> none  [the longest x1 17 us: bucket_terms(): jnp.take(dst_rows, neg_index, axis=0).reshape(groups, NEG, width)]
    pallas_call x0 -> x12, Pallas kernels: none -> 32.2 us  [the longest x1 11.1 us: shards(): call(score_kernel, [kept, sent, jax.ShapeDtypeStruct((EDGES, ENT), BF16),...]
    dot_general x3 -> x0, matrix products: 9.09 us -> none  [the longest x1 3.15 us: bucket_terms(): jnp.einsum('cid,cnd->cin', product_low, negatives, preferred_element_type...]
    reduce_sum x3 -> x0, other arithmetic: 5.43 us -> none  [the longest x2 4.02 us: adagrad_rows(): new_accum = accum + jnp.mean(grad * grad, axis=1)]
    ppermute x2 -> x34, waiting for transfers between devices: 46.8 us -> 41.7 us  [the longest x31 33.3 us: swap(): return lax.ppermute(x, AXES, [(i, i ^ mask) for i in range(256)])]
  transfers between devices with their start and end apart: 4 -> 34, of which waited for: 4 -> 16; matrix products, arithmetic and copies ran while one was open for 9% -> 1% of each run, Pallas kernels for 0% -> 13%
where the time goes in v1:
time: 141 us
  starting transfers between devices  58.5 us (41%)
  waiting for transfers between devices  41.7 us (30%)
  Pallas kernels  32.2 us (23%)
  local copies, waits for them, and re-layouts  4.88 us (3%)
  other arithmetic  1.91 us (1%)
  between operations  1.61 us (1%)
    ppermute x31, starting transfers between devices, swap(): return lax.ppermute(x, AXES, [(i, i ^ mask) for i in range(256)])  46.3 us
    ppermute x31, waiting for transfers between devices, swap(): return lax.ppermute(x, AXES, [(i, i ^ mask) for i in range(256)])  33.3 us
    ppermute x3, starting transfers between devices, shift(): return lax.ppermute(x, AXES, route)  12.3 us
    pallas_call x1, Pallas kernels, shards(): call(score_kernel, [kept, sent, jax.ShapeDtypeStruct((EDGES, ENT), BF16),...  11.1 us
    ppermute x3, waiting for transfers between devices, shift(): return lax.ppermute(x, AXES, route)  8.41 us
    pallas_call x2, Pallas kernels, update(): pl.pallas_call(functools.partial(update_kernel, len(pieces), sub), grid=(...  7.79 us
    pallas_call x1, Pallas kernels, shards(): call(scatter_kernel, [kept, sent, kept, sent], 1, 5, flops=3 * 2 * EDGES...  6.48 us
    pallas_call x1, Pallas kernels, shards(): call(gather_kernel, [jax.ShapeDtypeStruct((EDGES, D), BF16), jax.ShapeDty...  5.98 us
  transfers between devices with their start and end apart: 34, of which 16 were waited for; matrix products, arithmetic and copies ran while one was open for 1% of the time, Pallas kernels for 13%

profile of v1, /device:TPU:1, one launch (start us, length us, event | category | flops | bytes accessed | tf_op | source)
XLA Modules:
  0.0 140.9 jit_solution(11188170155032352413)
XLA Ops:
  0.7 2.2 %dynamic-slice_convert_fusion = bf16[1024,256]{1,0:T(8,128)(2,1)} fusion(f32[2048,256]{1,0:T(8,128)} %rows_ref.2, s32[]{:T(128)S(6)} %select_n.33), kind=kLoop, calls=%fused_computation | loop fusion | bytes 1048580 | tf_op jit(solution)/shard_map/convert_element_type | solution.py:367
  2.9 11.1 %collective-permute-start = (bf16[1024,256]{1,0:T(8,128)(2,1)}, bf16[1024,256]{1,0:T(8,128)(2,1)}, u32[]{:S(2)}, u32[]{:S(2)}) collective-permute-start(bf16[1024,256]{1,0:T(8,128)(2,1)} %dynamic-slice_convert_fusion), channel_id=1, source_target_pairs={{6,0},{7,1},{4,2},{5,3},{10,4},{11,5},{8,6},{9,7},{14,8},{15,9},{1... | collective-permute-start | bytes 1572872 | tf_op jit(solution)/shard_map/ppermute | solution.py:349
  16.5 8.4 %collective-permute-done.near_ref = bf16[1024,256]{1,0:T(8,128)(2,1)} collective-permute-done((bf16[1024,256]{1,0:T(8,128)(2,1)}, bf16[1024,256]{1,0:T(8,128)(2,1)}, u32[]{:S(2)}, u32[]{:S(2)}) %collective-permute-start) | collective-permute-done | bytes 524320 | tf_op jit(solution)/shard_map/ppermute | solution.py:349
  26.5 6.0 %shard_map.120 = (bf16[1024,256]{1,0:T(8,128)(2,1)S(1)}, f32[1024,256]{1,0:T(8,128)S(1)}, f32[1024,256]{1,0:T(8,128)S(1)}, f32[4,16,128]{2,1,0:T(8,128)S(1)}) custom-call(s32[8,1024]{1,0:T(8,128)S(1)} %concatenate.6.ids_ref, s32[4,1024]{1,0:T(4,128)S(1)} %reshape.31.negs_ref, bf16[2048,256]{1,0:T(8,128)(2,1)S(1)} %convert_element_type.7.low_ref, ...), custom_call_target="tpu_custom_call" | custom-call | flops 4294967296 | bytes 4194304 | tf_op jit(solution)/shard_map/pallas_call | solution.py:383
  33.5 11.1 %shard_map.121 = (f32[1024,256]{1,0:T(8,128)S(1)}, bf16[1024,256]{1,0:T(8,128)(2,1)S(1)}, bf16[1024,2048]{1,0:T(8,128)(2,1)}, bf16[256,1024]{1,0:T(8,128)(2,1)S(...) custom-call(s32[1,1]{1,0:T(1,128)S(6)} %copy.13.count_ref, s32[8,1024]{1,0:T(8,128)S(1)} %concatenate.6.ids_ref, ...), custom_call_target="tpu_custom_call" | custom-call | flops 4294967296 | bytes 8388608 | tf_op jit(solution)/shard_map/pallas_call | solution.py:400
  44.6 6.5 %shard_map.122 = (f32[1024,256]{1,0:T(8,128)S(1)}, bf16[1024,256]{1,0:T(8,128)(2,1)S(1)}, f32[1024,256]{1,0:T(8,128)S(1)}, bf16[1024,256]{1,0:T(8,128)(2,1)S(1)}) custom-call(s32[1]{0:T(128)} %bitcast.2.place_ref, s32[8,1024]{1,0:T(8,128)S(1)} %concatenate.6.ids_ref, bf16[1024,2048]{1,0:T(8,128)(2,1)} %get-tuple-element.38.cc_ref, ...), custom_call_target="tpu_custom_call" | custom-call | flops 3221225472 | bytes 8388608 | tf_op jit(solution)/shard_map/pallas_call | solution.py:416
  52.1 3.7 %collective-permute-start.13 = (bf16[256,256]{1,0:T(8,128)(2,1)S(1)}, bf16[256,256]{1,0:T(8,128)(2,1)S(1)}, u32[]{:S(2)}, u32[]{:S(2)}) collective-permute-start(bf16[256,256]{1,0:T(8,128)(2,1)S(1)} %get-tuple-element.57), channel_id=1, source_target_pairs={{0,6},{1,7},{2,4},{3,5},{4,2},{5,3},{6,0},{7,1},{8,14},{9,15},{10,... | collective-permute-start | bytes 393224 | tf_op jit(solution)/shard_map/ppermute | solution.py:344
  58.1 3.7 %collective-permute-done.13.refs_3_ = bf16[256,256]{1,0:T(8,128)(2,1)S(1)} collective-permute-done((bf16[256,256]{1,0:T(8,128)(2,1)S(1)}, bf16[256,256]{1,0:T(8,128)(2,1)S(1)}, u32[]{:S(2)}, u32[]{:S(2)}) %collective-permute-start.13) | collective-permute-done | bytes 131104 | tf_op jit(solution)/shard_map/ppermute | solution.py:344
  62.2 2.4 %collective-permute-start.15 = (bf16[64,256]{1,0:T(8,128)(2,1)S(1)}, bf16[64,256]{1,0:T(8,128)(2,1)S(1)}, u32[]{:S(2)}, u32[]{:S(2)}) collective-permute-start(bf16[64,256]{1,0:T(8,128)(2,1)S(1)} %get-tuple-element.60), channel_id=1, source_target_pairs={{0,16},{1,17},{2,18},{3,19},{4,20},{5,21},{6,22},{7,23},{8,24},{9,... | collective-permute-start | bytes 98312 | tf_op jit(solution)/shard_map/ppermute | solution.py:344
  64.6 8.0 %collective-permute-done.14.refs_1_ = bf16[64,256]{1,0:T(8,128)(2,1)S(1)} collective-permute-done((bf16[64,256]{1,0:T(8,128)(2,1)S(1)}, bf16[64,256]{1,0:T(8,128)(2,1)S(1)}, u32[]{:S(2)}, u32[]{:S(2)}) %collective-permute-start.14) | collective-permute-done | bytes 32800 | tf_op jit(solution)/shard_map/ppermute | solution.py:344
  72.6 2.9 %collective-permute-start.16 = (bf16[64,256]{1,0:T(8,128)(2,1)S(1)}, bf16[64,256]{1,0:T(8,128)(2,1)S(1)}, u32[]{:S(2)}, u32[]{:S(2)}) collective-permute-start(bf16[64,256]{1,0:T(8,128)(2,1)S(1)} %get-tuple-element.61), channel_id=1, source_target_pairs={{0,24},{1,25},{2,26},{3,27},{4,28},{5,29},{6,30},{7,31},{8,16},{9,... | collective-permute-start | bytes 98312 | tf_op jit(solution)/shard_map/ppermute | solution.py:344
  76.4 2.5 %collective-permute-done.16.refs_3_ = bf16[64,256]{1,0:T(8,128)(2,1)S(1)} collective-permute-done((bf16[64,256]{1,0:T(8,128)(2,1)S(1)}, bf16[64,256]{1,0:T(8,128)(2,1)S(1)}, u32[]{:S(2)}, u32[]{:S(2)}) %collective-permute-start.16) | collective-permute-done | bytes 32800 | tf_op jit(solution)/shard_map/ppermute | solution.py:344
  78.9 7.8 %collective-permute-start.23 = (bf16[64,256]{1,0:T(8,128)(2,1)S(1)}, bf16[64,256]{1,0:T(8,128)(2,1)S(1)}, u32[]{:S(2)}, u32[]{:S(2)}) collective-permute-start(bf16[64,256]{1,0:T(8,128)(2,1)S(1)} %shard_map.129.refs_0_), channel_id=1, source_target_pairs={{0,224},{1,225},{2,226},{3,227},{4,228},{5,229},{6,230},{7,231},{8... | collective-permute-start | bytes 98312 | tf_op jit(solution)/shard_map/ppermute | solution.py:344
  88.1 4.1 %collective-permute-start.21 = (bf16[64,256]{1,0:T(8,128)(2,1)S(1)}, bf16[64,256]{1,0:T(8,128)(2,1)S(1)}, u32[]{:S(2)}, u32[]{:S(2)}) collective-permute-start(bf16[64,256]{1,0:T(8,128)(2,1)S(1)} %shard_map.129.refs_0_), channel_id=1, source_target_pairs={{0,160},{1,161},{2,162},{3,163},{4,164},{5,165},{6,166},{7,167},{8... | collective-permute-start | bytes 98312 | tf_op jit(solution)/shard_map/ppermute | solution.py:344
  93.9 2.0 %collective-permute-start.19 = (bf16[64,256]{1,0:T(8,128)(2,1)S(1)}, bf16[64,256]{1,0:T(8,128)(2,1)S(1)}, u32[]{:S(2)}, u32[]{:S(2)}) collective-permute-start(bf16[64,256]{1,0:T(8,128)(2,1)S(1)} %shard_map.129.refs_0_), channel_id=1, source_target_pairs={{0,96},{1,97},{2,98},{3,99},{4,100},{5,101},{6,102},{7,103},{8,104... | collective-permute-start | bytes 98312 | tf_op jit(solution)/shard_map/ppermute | solution.py:344
  95.9 3.0 %collective-permute-done.20.refs_4_ = bf16[64,256]{1,0:T(8,128)(2,1)S(1)} collective-permute-done((bf16[64,256]{1,0:T(8,128)(2,1)S(1)}, bf16[64,256]{1,0:T(8,128)(2,1)S(1)}, u32[]{:S(2)}, u32[]{:S(2)}) %collective-permute-start.20) | collective-permute-done | bytes 32800 | tf_op jit(solution)/shard_map/ppermute | solution.py:344
  100.9 2.5 %collective-permute-done.18.refs_2_ = bf16[64,256]{1,0:T(8,128)(2,1)S(1)} collective-permute-done((bf16[64,256]{1,0:T(8,128)(2,1)S(1)}, bf16[64,256]{1,0:T(8,128)(2,1)S(1)}, u32[]{:S(2)}, u32[]{:S(2)}) %collective-permute-start.18) | collective-permute-done | bytes 32800 | tf_op jit(solution)/shard_map/ppermute | solution.py:344
  103.6 1.7 %collective-permute-start.26 = (bf16[80,256]{1,0:T(8,128)(2,1)S(1)}, bf16[80,256]{1,0:T(8,128)(2,1)S(1)}, u32[]{:S(2)}, u32[]{:S(2)}) collective-permute-start(bf16[80,256]{1,0:T(8,128)(2,1)S(1)} %shard_map.130), channel_id=1, source_target_pairs={{0,24},{1,25},{2,26},{3,27},{4,28},{5,29},{6,30},{7,31},{8,16},{9,... | collective-permute-start | bytes 122888 | tf_op jit(solution)/shard_map/ppermute | solution.py:344
  107.8 1.9 %collective-permute-done.25 = bf16[80,256]{1,0:T(8,128)(2,1)S(1)} collective-permute-done((bf16[80,256]{1,0:T(8,128)(2,1)S(1)}, bf16[80,256]{1,0:T(8,128)(2,1)S(1)}, u32[]{:S(2)}, u32[]{:S(2)}) %collective-permute-start.25) | collective-permute-done | bytes 40992 | tf_op jit(solution)/shard_map/ppermute | solution.py:344
  109.7 8.3 %collective-permute-start.30 = (bf16[320,256]{1,0:T(8,128)(2,1)S(1)}, bf16[320,256]{1,0:T(8,128)(2,1)S(1)}, u32[]{:S(2)}, u32[]{:S(2)}) collective-permute-start(bf16[320,256]{1,0:T(8,128)(2,1)S(1)} %pad_maximum_fusion.refs_0_), channel_id=1, source_target_pairs={{0,1},{1,0},{2,3},{3,2},{4,5},{5,4},{6,7},{7,6},{8,9},{9,8},{10,11... | collective-permute-start | bytes 491528 | tf_op jit(solution)/shard_map/ppermute | solution.py:344
  118.4 2.9 %collective-permute-start.27 = (bf16[320,256]{1,0:T(8,128)(2,1)S(1)}, bf16[320,256]{1,0:T(8,128)(2,1)}, u32[]{:S(2)}, u32[]{:S(2)}) collective-permute-start(bf16[320,256]{1,0:T(8,128)(2,1)S(1)} %pad_maximum_fusion.refs_0_), channel_id=1, source_target_pairs={{0,2},{1,3},{2,0},{3,1},{4,6},{5,7},{6,4},{7,5},{8,10},{9,11},{10,... | collective-permute-start | bytes 491528 | tf_op jit(solution)/shard_map/ppermute | solution.py:344
  122.3 6.5 %collective-permute-done.29.refs_3_ = bf16[320,256]{1,0:T(8,128)(2,1)} collective-permute-done((bf16[320,256]{1,0:T(8,128)(2,1)S(1)}, bf16[320,256]{1,0:T(8,128)(2,1)}, u32[]{:S(2)}, u32[]{:S(2)}) %collective-permute-start.29) | collective-permute-done | bytes 163872 | tf_op jit(solution)/shard_map/ppermute | solution.py:344
  133.1 5.0 %shard_map.131 = (f32[2048,256]{1,0:T(8,128)}, f32[16,128]{1,0:T(8,128)}) custom-call(s32[2]{0:T(128)S(1)} %pad_add_fusion.1.place_ref, f32[2048,256]{1,0:T(8,128)S(1)} %copy-done.2, f32[16,128]{1,0:T(8,128)S(1)} %bitcast.9, bf16[320,256]{1,0:T(8,128)(2,1)S(1)} %pad_maximum_fusion.refs_0_, bf16[320,256]{1,0:T(8,128)(2,1)} %collective-permute-done.27.refs_1_, ...), custom_call_target="tpu_custom_call" | custom-call | flops 4194304 | bytes 5242880 | tf_op jit(solution)/shard_map/pallas_call | solution.py:320
  138.2 2.7 %shard_map.126 = (f32[2048,256]{1,0:T(8,128)}, f32[16,128]{1,0:T(8,128)}) custom-call(s32[2]{0:T(128)S(1)} %pad_add_fusion.place_ref, f32[2048,256]{1,0:T(8,128)S(1)} %copy-done, f32[16,128]{1,0:T(8,128)S(1)} %bitcast.10, bf16[528,256]{1,0:T(8,128)(2,1)S(1)} %shard_map.125.refs_0_, bf16[528,256]{1,0:T(8,128)(2,1)S(1)} %collective-permute-done.7.refs_1_, ...), custom_call_target="tpu_custom_call" | custom-call | flops 4194304 | bytes 5242880 | tf_op jit(solution)/shard_map/pallas_call | solution.py:320
  (87 shorter events, 22.2 us)
Async XLA Ops:
  2.9 22.0 %collective-permute-start = (bf16[1024,256]{1,0:T(8,128)(2,1)}, bf16[1024,256]{1,0:T(8,128)(2,1)}, u32[]{:S(2)}, u32[]{:S(2)}) collective-permute-start(bf16[1024,256]{1,0:T(8,128)(2,1)} %dynamic-slice_convert_fusion), channel_id=1, source_target_pairs={{6,0},{7,1},{4,2},{5,3},{10,4},{11,5},{8,6},{9,7},{14,8},{15,9},{1... | collective-permute-start | bytes 1572872 | tf_op jit(solution)/shard_map/ppermute | solution.py:349
  24.9 8.6 %collective-permute-start.1 = (bf16[1024,256]{1,0:T(8,128)(2,1)}, bf16[1024,256]{1,0:T(8,128)(2,1)}, u32[]{:S(2)}, u32[]{:S(2)}) collective-permute-start(bf16[1024,256]{1,0:T(8,128)(2,1)} %collective-permute-done.near_ref), channel_id=1, source_target_pairs={{0,1},{1,0},{2,3},{3,2},{4,5},{5,4},{6,7},{7,6},{8,9},{9,8},{10,11... | collective-permute-start | bytes 1572872 | tf_op jit(solution)/shard_map/ppermute | solution.py:344
  44.6 7.2 %collective-permute-start.10 = (bf16[1024,256]{1,0:T(8,128)(2,1)S(1)}, bf16[1024,256]{1,0:T(8,128)(2,1)S(1)}, u32[]{:S(2)}, u32[]{:S(2)}) collective-permute-start(bf16[1024,256]{1,0:T(8,128)(2,1)S(1)} %get-tuple-element.53), channel_id=1, source_target_pairs={{0,1},{1,0},{2,3},{3,2},{4,5},{5,4},{6,7},{7,6},{8,9},{9,8},{10,11... | collective-permute-start | bytes 1572872 | tf_op jit(solution)/shard_map/ppermute | solution.py:344
  51.9 5.5 %collective-permute-start.11 = (bf16[256,256]{1,0:T(8,128)(2,1)S(1)}, bf16[256,256]{1,0:T(8,128)(2,1)S(1)}, u32[]{:S(2)}, u32[]{:S(2)}) collective-permute-start(bf16[256,256]{1,0:T(8,128)(2,1)S(1)} %get-tuple-element.55), channel_id=1, source_target_pairs={{0,2},{1,3},{2,0},{3,1},{4,6},{5,7},{6,4},{7,5},{8,10},{9,11},{10,... | collective-permute-start | bytes 393224 | tf_op jit(solution)/shard_map/ppermute | solution.py:344
  52.0 6.1 %collective-permute-start.12 = (bf16[256,256]{1,0:T(8,128)(2,1)S(1)}, bf16[256,256]{1,0:T(8,128)(2,1)S(1)}, u32[]{:S(2)}, u32[]{:S(2)}) collective-permute-start(bf16[256,256]{1,0:T(8,128)(2,1)S(1)} %get-tuple-element.56), channel_id=1, source_target_pairs={{0,4},{1,5},{2,6},{3,7},{4,0},{5,1},{6,2},{7,3},{8,12},{9,13},{10,... | collective-permute-start | bytes 393224 | tf_op jit(solution)/shard_map/ppermute | solution.py:344
  52.1 9.7 %collective-permute-start.13 = (bf16[256,256]{1,0:T(8,128)(2,1)S(1)}, bf16[256,256]{1,0:T(8,128)(2,1)S(1)}, u32[]{:S(2)}, u32[]{:S(2)}) collective-permute-start(bf16[256,256]{1,0:T(8,128)(2,1)S(1)} %get-tuple-element.57), channel_id=1, source_target_pairs={{0,6},{1,7},{2,4},{3,5},{4,2},{5,3},{6,0},{7,1},{8,14},{9,15},{10,... | collective-permute-start | bytes 393224 | tf_op jit(solution)/shard_map/ppermute | solution.py:344
  56.0 49.4 %collective-permute-start.3 = (bf16[512,256]{1,0:T(8,128)(2,1)S(1)}, bf16[512,256]{1,0:T(8,128)(2,1)S(1)}, u32[]{:S(2)}, u32[]{:S(2)}) collective-permute-start(bf16[512,256]{1,0:T(8,128)(2,1)S(1)} %get-tuple-element.45), channel_id=1, source_target_pairs={{0,2},{1,3},{2,0},{3,1},{4,6},{5,7},{6,4},{7,5},{8,10},{9,11},{10,... | collective-permute-start | bytes 786440 | tf_op jit(solution)/shard_map/ppermute | solution.py:344
  56.2 50.8 %collective-permute-start.5 = (bf16[512,256]{1,0:T(8,128)(2,1)S(1)}, bf16[512,256]{1,0:T(8,128)(2,1)S(1)}, u32[]{:S(2)}, u32[]{:S(2)}) collective-permute-start(bf16[512,256]{1,0:T(8,128)(2,1)S(1)} %get-tuple-element.48), channel_id=1, source_target_pairs={{252,0},{253,1},{254,2},{255,3},{0,4},{1,5},{2,6},{3,7},{4,8},{5,9... | collective-permute-start | bytes 786440 | tf_op jit(solution)/shard_map/ppermute | solution.py:349
  57.4 49.5 %collective-permute-start.6 = (bf16[512,256]{1,0:T(8,128)(2,1)S(1)}, bf16[512,256]{1,0:T(8,128)(2,1)S(1)}, u32[]{:S(2)}, u32[]{:S(2)}) collective-permute-start(bf16[512,256]{1,0:T(8,128)(2,1)S(1)} %get-tuple-element.49), channel_id=1, source_target_pairs={{254,0},{255,1},{252,2},{253,3},{2,4},{3,5},{0,6},{1,7},{6,8},{7,9... | collective-permute-start | bytes 786440 | tf_op jit(solution)/shard_map/ppermute | solution.py:349
  61.9 10.7 %collective-permute-start.14 = (bf16[64,256]{1,0:T(8,128)(2,1)S(1)}, bf16[64,256]{1,0:T(8,128)(2,1)S(1)}, u32[]{:S(2)}, u32[]{:S(2)}) collective-permute-start(bf16[64,256]{1,0:T(8,128)(2,1)S(1)} %get-tuple-element.59), channel_id=1, source_target_pairs={{0,8},{1,9},{2,10},{3,11},{4,12},{5,13},{6,14},{7,15},{8,0},{9,1},... | collective-permute-start | bytes 98312 | tf_op jit(solution)/shard_map/ppermute | solution.py:344
  62.2 14.2 %collective-permute-start.15 = (bf16[64,256]{1,0:T(8,128)(2,1)S(1)}, bf16[64,256]{1,0:T(8,128)(2,1)S(1)}, u32[]{:S(2)}, u32[]{:S(2)}) collective-permute-start(bf16[64,256]{1,0:T(8,128)(2,1)S(1)} %get-tuple-element.60), channel_id=1, source_target_pairs={{0,16},{1,17},{2,18},{3,19},{4,20},{5,21},{6,22},{7,23},{8,24},{9,... | collective-permute-start | bytes 98312 | tf_op jit(solution)/shard_map/ppermute | solution.py:344
  72.6 6.3 %collective-permute-start.16 = (bf16[64,256]{1,0:T(8,128)(2,1)S(1)}, bf16[64,256]{1,0:T(8,128)(2,1)S(1)}, u32[]{:S(2)}, u32[]{:S(2)}) collective-permute-start(bf16[64,256]{1,0:T(8,128)(2,1)S(1)} %get-tuple-element.61), channel_id=1, source_target_pairs={{0,24},{1,25},{2,26},{3,27},{4,28},{5,29},{6,30},{7,31},{8,16},{9,... | collective-permute-start | bytes 98312 | tf_op jit(solution)/shard_map/ppermute | solution.py:344
  78.9 9.1 %collective-permute-start.23 = (bf16[64,256]{1,0:T(8,128)(2,1)S(1)}, bf16[64,256]{1,0:T(8,128)(2,1)S(1)}, u32[]{:S(2)}, u32[]{:S(2)}) collective-permute-start(bf16[64,256]{1,0:T(8,128)(2,1)S(1)} %shard_map.129.refs_0_), channel_id=1, source_target_pairs={{0,224},{1,225},{2,226},{3,227},{4,228},{5,229},{6,230},{7,231},{8... | collective-permute-start | bytes 98312 | tf_op jit(solution)/shard_map/ppermute | solution.py:344
  86.8 5.4 %collective-permute-start.22 = (bf16[64,256]{1,0:T(8,128)(2,1)S(1)}, bf16[64,256]{1,0:T(8,128)(2,1)S(1)}, u32[]{:S(2)}, u32[]{:S(2)}) collective-permute-start(bf16[64,256]{1,0:T(8,128)(2,1)S(1)} %shard_map.129.refs_0_), channel_id=1, source_target_pairs={{0,192},{1,193},{2,194},{3,195},{4,196},{5,197},{6,198},{7,199},{8... | collective-permute-start | bytes 98312 | tf_op jit(solution)/shard_map/ppermute | solution.py:344
  88.1 5.8 %collective-permute-start.21 = (bf16[64,256]{1,0:T(8,128)(2,1)S(1)}, bf16[64,256]{1,0:T(8,128)(2,1)S(1)}, u32[]{:S(2)}, u32[]{:S(2)}) collective-permute-start(bf16[64,256]{1,0:T(8,128)(2,1)S(1)} %shard_map.129.refs_0_), channel_id=1, source_target_pairs={{0,160},{1,161},{2,162},{3,163},{4,164},{5,165},{6,166},{7,167},{8... | collective-permute-start | bytes 98312 | tf_op jit(solution)/shard_map/ppermute | solution.py:344
  92.2 6.7 %collective-permute-start.20 = (bf16[64,256]{1,0:T(8,128)(2,1)S(1)}, bf16[64,256]{1,0:T(8,128)(2,1)S(1)}, u32[]{:S(2)}, u32[]{:S(2)}) collective-permute-start(bf16[64,256]{1,0:T(8,128)(2,1)S(1)} %shard_map.129.refs_0_), channel_id=1, source_target_pairs={{0,128},{1,129},{2,130},{3,131},{4,132},{5,133},{6,134},{7,135},{8... | collective-permute-start | bytes 98312 | tf_op jit(solution)/shard_map/ppermute | solution.py:344
  93.9 6.0 %collective-permute-start.19 = (bf16[64,256]{1,0:T(8,128)(2,1)S(1)}, bf16[64,256]{1,0:T(8,128)(2,1)S(1)}, u32[]{:S(2)}, u32[]{:S(2)}) collective-permute-start(bf16[64,256]{1,0:T(8,128)(2,1)S(1)} %shard_map.129.refs_0_), channel_id=1, source_target_pairs={{0,96},{1,97},{2,98},{3,99},{4,100},{5,101},{6,102},{7,103},{8,104... | collective-permute-start | bytes 98312 | tf_op jit(solution)/shard_map/ppermute | solution.py:344
  107.2 15.0 %collective-permute-start.7 = (bf16[528,256]{1,0:T(8,128)(2,1)S(1)}, bf16[528,256]{1,0:T(8,128)(2,1)S(1)}, u32[]{:S(2)}, u32[]{:S(2)}) collective-permute-start(bf16[528,256]{1,0:T(8,128)(2,1)S(1)} %shard_map.125.refs_0_), channel_id=1, source_target_pairs={{0,2},{1,3},{2,0},{3,1},{4,6},{5,7},{6,4},{7,5},{8,10},{9,11},{10,... | collective-permute-start | bytes 811016 | tf_op jit(solution)/shard_map/ppermute | solution.py:344
  109.7 11.6 %collective-permute-start.30 = (bf16[320,256]{1,0:T(8,128)(2,1)S(1)}, bf16[320,256]{1,0:T(8,128)(2,1)S(1)}, u32[]{:S(2)}, u32[]{:S(2)}) collective-permute-start(bf16[320,256]{1,0:T(8,128)(2,1)S(1)} %pad_maximum_fusion.refs_0_), channel_id=1, source_target_pairs={{0,1},{1,0},{2,3},{3,2},{4,5},{5,4},{6,7},{7,6},{8,9},{9,8},{10,11... | collective-permute-start | bytes 491528 | tf_op jit(solution)/shard_map/ppermute | solution.py:344
  118.0 10.8 %collective-permute-start.29 = (bf16[320,256]{1,0:T(8,128)(2,1)S(1)}, bf16[320,256]{1,0:T(8,128)(2,1)}, u32[]{:S(2)}, u32[]{:S(2)}) collective-permute-start(bf16[320,256]{1,0:T(8,128)(2,1)S(1)} %pad_maximum_fusion.refs_0_), channel_id=1, source_target_pairs={{0,6},{1,7},{2,4},{3,5},{4,2},{5,3},{6,0},{7,1},{8,14},{9,15},{10,... | collective-permute-start | bytes 491528 | tf_op jit(solution)/shard_map/ppermute | solution.py:344
  118.0 11.5 %collective-permute-start.28 = (bf16[320,256]{1,0:T(8,128)(2,1)S(1)}, bf16[320,256]{1,0:T(8,128)(2,1)}, u32[]{:S(2)}, u32[]{:S(2)}) collective-permute-start(bf16[320,256]{1,0:T(8,128)(2,1)S(1)} %pad_maximum_fusion.refs_0_), channel_id=1, source_target_pairs={{0,4},{1,5},{2,6},{3,7},{4,0},{5,1},{6,2},{7,3},{8,12},{9,13},{10,... | collective-permute-start | bytes 491528 | tf_op jit(solution)/shard_map/ppermute | solution.py:344
  118.4 11.1 %collective-permute-start.27 = (bf16[320,256]{1,0:T(8,128)(2,1)S(1)}, bf16[320,256]{1,0:T(8,128)(2,1)}, u32[]{:S(2)}, u32[]{:S(2)}) collective-permute-start(bf16[320,256]{1,0:T(8,128)(2,1)S(1)} %pad_maximum_fusion.refs_0_), channel_id=1, source_target_pairs={{0,2},{1,3},{2,0},{3,1},{4,6},{5,7},{6,4},{7,5},{8,10},{9,11},{10,... | collective-permute-start | bytes 491528 | tf_op jit(solution)/shard_map/ppermute | solution.py:344
  121.3 16.8 %collective-permute-start.8 = (bf16[528,256]{1,0:T(8,128)(2,1)S(1)}, bf16[528,256]{1,0:T(8,128)(2,1)S(1)}, u32[]{:S(2)}, u32[]{:S(2)}) collective-permute-start(bf16[528,256]{1,0:T(8,128)(2,1)S(1)} %shard_map.125.refs_0_), channel_id=1, source_target_pairs={{0,1},{1,0},{2,3},{3,2},{4,5},{5,4},{6,7},{7,6},{8,9},{9,8},{10,11... | collective-permute-start | bytes 811016 | tf_op jit(solution)/shard_map/ppermute | solution.py:344
  122.2 15.9 %collective-permute-start.9 = (bf16[528,256]{1,0:T(8,128)(2,1)S(1)}, bf16[528,256]{1,0:T(8,128)(2,1)S(1)}, u32[]{:S(2)}, u32[]{:S(2)}) collective-permute-start(bf16[528,256]{1,0:T(8,128)(2,1)S(1)} %collective-permute-done.7.refs_1_), channel_id=1, source_target_pairs={{0,1},{1,0},{2,3},{3,2},{4,5},{5,4},{6,7},{7,6},{8,9},{9,8},{10,11... | collective-permute-start | bytes 811016 | tf_op jit(solution)/shard_map/ppermute | solution.py:344
  (20 other events, 274.8 us)

commit v2 on v1

--- a/solution.py
+++ b/solution.py
@@ -232,93 +232,66 @@
     return hi, mid, x - hi - mid
 
 
-def sum_with_means_kernel(place_ref, *refs):
+def sum_with_means_kernel(*refs):
     parts, out_ref = refs[:-1], refs[-1]
     rows = parts[0].shape[0]
-    step = min(rows, H)
     means = []
-    for r in range(0, rows, step):
-        terms = [ref[r : r + step, :].astype(F32) for ref in parts]
-        if len(terms) == 8:
-            z = place_ref[0]
-            for bit in (1, 2, 4):
-                flip = lax.bitwise_and(z, bit) != 0
-                terms = [jnp.where(flip, terms[k ^ bit], terms[k]) for k in range(8)]
-        total = terms[0]
-        for term in terms[1:]:
-            total = total + term
-        out_ref[r : r + step, :] = total.astype(BF16)
+    for r in range(0, rows, H):
+        total = parts[0][r : r + H, :].astype(F32)
+        for ref in parts[1:]:
+            total = total + ref[r : r + H, :].astype(F32)
+        out_ref[r : r + H, :] = total.astype(BF16)
         mean = jnp.sum(total * total, axis=1, keepdims=True) * (1.0 / D)
-        mean = jnp.broadcast_to(mean, (step, H))
-        if step < H:
-            mean = jnp.concatenate([mean] * (H // step), axis=0)
-        means.append(jnp.transpose(mean)[0:1, :])
-    pad = jnp.zeros((8 - len(means), H), F32)
-    hi, mid, lo = (jnp.concatenate([part, pad], axis=0) for part in split3(jnp.concatenate(means, axis=0)))
+        means.append(jnp.transpose(jnp.broadcast_to(mean, (H, H)))[0:1, :])
+    means.append(jnp.zeros((8 - len(means), H), F32))
+    hi, mid, lo = split3(jnp.concatenate(means, axis=0))
     top = jnp.concatenate([hi, mid], axis=1)
     bottom = jnp.concatenate([lo, jnp.zeros_like(lo)], axis=1)
     out_ref[rows : rows + 16, :] = jnp.concatenate([top, bottom], axis=0).astype(BF16)
 
 
-def sum_with_means(parts, place=None):
+def sum_with_means(parts):
     rows = parts[0].shape[0]
-    place = jnp.zeros((1,), jnp.int32) if place is None else place.reshape(1)
     return call(
         sum_with_means_kernel,
         jax.ShapeDtypeStruct((rows + 16, D), BF16),
-        1,
+        0,
         len(parts),
         flops=len(parts) * rows * D,
         bytes_accessed=3 * len(parts) * rows * D,
-    )(place, *parts)
+    )(*parts)
 
 
 def means_of(piece, start, row):
-    tile = piece[pl.ds(pl.multiple_of(start, 16), 16), :].astype(F32)
+    tile = piece[start : start + 16, :].astype(F32)
     return tile[row : row + 1, :H] + tile[row : row + 1, H:] + tile[8 + row : 9 + row, :H]
 
 
-def update_kernel(n_pieces, sub, place_ref, rows_ref, acc_ref, *refs):
+def update_kernel(n_pieces, place_ref, rows_ref, acc_ref, *refs):
     pieces, new_ref, new_acc_ref = refs[:n_pieces], refs[n_pieces], refs[n_pieces + 1]
     size = rows_ref.shape[0]
     i = pl.program_id(0)
     want = lax.bitwise_xor(i, place_ref[0])
-    lane = lax.broadcasted_iota(jnp.int32, (1, H), 1)
     for k, piece in enumerate(pieces):
 
         @pl.when(want == k)
         def _(piece=piece):
             for r in range(0, size, H):
-                if sub >= H:
-                    g = piece[r : r + H, :].astype(F32)
-                    mean = means_of(piece, size, r // H)
-                else:
-                    starts = [
-                        lax.bitwise_xor(c // sub, place_ref[1]) * (sub + 16)
-                        for c in range(r, r + H, sub)
-                    ]
-                    g = jnp.concatenate(
-                        [
-                            piece[pl.ds(pl.multiple_of(start, 16), sub), :].astype(F32)
-                            for start in starts
-                        ],
-                        axis=0,
-                    )
-                    first, second = (means_of(piece, start + sub, 0) for start in starts)
-                    mean = jnp.where(lane < sub, first, second)
+                g = piece[r : r + H, :].astype(F32)
                 at = pl.ds(i * (size // H) + r // H, 1)
-                acc = acc_ref[at, :] + mean
+                acc = acc_ref[at, :] + means_of(piece, size, r // H)
                 new_acc_ref[at, :] = acc
                 scale = jnp.transpose(jnp.broadcast_to(RATE / jnp.sqrt(acc), (H, H)))
                 new_ref[r : r + H, :H] = rows_ref[r : r + H, :H] - g[:, :H] * scale
                 new_ref[r : r + H, H:] = rows_ref[r : r + H, H:] - g[:, H:] * scale
 
 
-def update(rows, acc, pieces, place, size, sub):
+def update(rows, acc, pieces, place):
     n = rows.shape[0]
+    size = n // len(pieces)
     whole = lambda i: (0, 0)
     new, new_acc = pl.pallas_call(
-        functools.partial(update_kernel, len(pieces), sub),
+        functools.partial(update_kernel, len(pieces)),
         grid=(n // size,),
         out_shape=[
             jax.ShapeDtypeStruct((n, D), F32),
@@ -340,6 +313,29 @@
     return new, new_acc.reshape(n)
 
 
+def sum_rows_kernel(parts_ref, out_ref):
+    total = parts_ref[0].astype(F32)
+    for k in range(1, parts_ref.shape[0]):
+        total = total + parts_ref[k].astype(F32)
+    out_ref[...] = jnp.broadcast_to(total, out_ref.shape)
+
+
+def sum_rows(parts):
+    return call(
+        sum_rows_kernel,
+        jax.ShapeDtypeStruct(parts.shape, F32),
+        0,
+        1,
+        flops=parts.size,
+        bytes_accessed=6 * parts.size,
+    )(parts)
+
+
+def spread(parts):
+    groups = [[2 * k + hi for k in range(32)] for hi in range(2)]
+    return lax.all_to_all(parts, "blk", 0, 0, axis_index_groups=groups, tiled=True)
+
+
 def swap(x, mask):
     return lax.ppermute(x, AXES, [(i, i ^ mask) for i in range(256)])
 
@@ -351,8 +347,6 @@
 
 CORE, XL = 1, 2
 X_MASKS = (2, 4, 6)
-Y_MASKS = (8, 16, 24)
-Z_MASKS = tuple(range(32, 256, 32))
 
 
 def shards(
@@ -361,19 +355,17 @@
     blk, rep = lax.axis_index("blk"), lax.axis_index("rep")
     core, xl = rep % 2, rep // 2
     x = (blk % 2) * 2 + xl
-    y = (blk // 2) % 4
 
     low = entities.astype(BF16)
     half = lax.dynamic_slice_in_dim(entities, core * (ENT // 2), ENT // 2, 0).astype(BF16)
     near = shift(half, -1, XL)
-    far = swap(near, CORE)
 
     ids = jnp.concatenate(
         [
             src_ids,
             rel_ids,
             dst_ids ^ (core * 1024),
-            rel_ids ^ (core * 1024 + x * 256 + y * 64),
+            rel_ids ^ (core * 1024 + x * 256),
             src_ids ^ (core * 1024 + xl * 512),
             jnp.zeros((3, EDGES), jnp.int32),
         ],
@@ -395,6 +387,8 @@
         bytes_accessed=1 << 22,
     )(ids, negs, low, relations)
 
+    near, head = lax.optimization_barrier((near, head))
+    far = swap(near, CORE)
     kept = jax.ShapeDtypeStruct((ENT // 2, D), F32)
     sent = jax.ShapeDtypeStruct((ENT // 2, D), BF16)
     rel_keep, rel_send, cc, plt, pd, gh = call(
@@ -413,6 +407,11 @@
         flops=4 * 2 * EDGES * ENT * D,
         bytes_accessed=1 << 23,
     )(counts, ids, near, far, head, rel_rows, prod, cnt)
+    rel_recv = swap(rel_send, CORE)
+    parts = add_split([rel_keep, rel_recv], 4, own=F32)
+    parts, cc = lax.optimization_barrier((parts, cc))
+    recv = [swap(part, mask) for part, mask in zip(parts[1:], X_MASKS)]
+
     src_keep, src_send, dst_keep, dst_send = call(
         scatter_kernel,
         [kept, sent, kept, sent],
@@ -421,40 +420,38 @@
         flops=3 * 2 * EDGES * ENT * D,
         bytes_accessed=1 << 23,
     )(xl.reshape(1), ids, cc, plt, pd, gh)
-
-    rel_recv = swap(rel_send, CORE)
-    parts = add_split([rel_keep, rel_recv], 4, own=F32)
-    recv = [swap(part, mask) for part, mask in zip(parts[1:], X_MASKS)]
+    recv, src_send, dst_send = lax.optimization_barrier((recv, src_send, dst_send))
     src_recv = swap(src_send, CORE)
     dst_recv = swap(dst_send, CORE)
     src_own, src_away = add_split([src_keep, src_recv], 2, own=F32)
     dst_own, dst_away = add_split([dst_keep, dst_recv], 2)
-
-    parts = add_split([parts[0], *recv], 4, own=F32)
-    recv = [swap(part, mask) for part, mask in zip(parts[1:], Y_MASKS)]
     (mine,) = add_split([parts[0], *recv], 1)
-
+    mine, src_away, dst_own, dst_away = lax.optimization_barrier(
+        (mine, src_away, dst_own, dst_away)
+    )
     src_other = swap(src_away, XL)
     dst_first = shift(dst_own, 1, 0)
     dst_second = shift(dst_away, 1, XL)
 
-    others = [swap(mine, mask) for mask in Z_MASKS]
+    landed = spread(mine.reshape(32, 8, D))
     ent_own = sum_with_means([src_own, src_other, dst_first, dst_second])
+    summed = sum_rows(landed)
+    summed, ent_own = lax.optimization_barrier((summed, ent_own))
     ent_xl = swap(ent_own, XL)
+    total = spread(summed).reshape(256, D)
+    quarter = sum_with_means([total])
+    recv = [swap(quarter, mask) for mask in X_MASKS]
+
     ent_core = [swap(ent_own, CORE), swap(ent_xl, CORE)]
-    place = jnp.stack([core * 2 + xl, jnp.zeros_like(core)])
+    place = (core * 2 + xl).reshape(1)
     new_entities, new_entity_acc = update(
-        entities, entity_acc, [ent_own, ent_xl, *ent_core], place, 512, 512
+        entities, entity_acc, [ent_own, ent_xl, *ent_core], place
     )
 
-    z = blk // 8
-    total = sum_with_means([mine, *others], z)
-    recv = [swap(total, mask) for mask in Y_MASKS]
-    quarter = jnp.concatenate([total, *recv], axis=0)
-    pieces = [quarter, *[swap(quarter, mask) for mask in X_MASKS]]
+    pieces = [quarter, *recv]
     pieces = pieces + [swap(piece, CORE) for piece in pieces]
-    place = jnp.stack([core * 4 + x, y])
-    new_relations, new_relation_acc = update(relations, relation_acc, pieces, place, 256, 64)
+    place = (core * 4 + x).reshape(1)
+    new_relations, new_relation_acc = update(relations, relation_acc, pieces, place)
     return (new_entities, new_entity_acc, new_relations, new_relation_acc)
 
 

time: 141 us -> 115 us (0.82)
  waiting for transfers between devices: 41.7 us -> 14.4 us
  blocking collectives: 0 us -> 19.7 us
  starting transfers between devices: 58.5 us -> 40.9 us
  local copies, waits for them, and re-layouts: 4.88 us -> 3.3 us
    ppermute x31 -> x18, waiting for transfers between devices: 33.3 us -> 4.66 us  [swap(): return lax.ppermute(x, AXES, [(i, i ^ mask) for i in range(256)])]
    ppermute x31 -> x18, starting transfers between devices: 46.3 us -> 22.9 us  [swap(): return lax.ppermute(x, AXES, [(i, i ^ mask) for i in range(256)])]
    all_to_all x0 -> x1, blocking collectives: none -> 19.7 us  [spread(): lax.all_to_all(parts, 'blk', 0, 0, axis_index_groups=groups, tiled=True)]
    all_to_all x0 -> x1, waiting for transfers between devices: none -> 7.7 us  [spread(): lax.all_to_all(parts, 'blk', 0, 0, axis_index_groups=groups, tiled=True)]
    ppermute x3, waiting for transfers between devices: 8.41 us -> 2.01 us  [shift(): return lax.ppermute(x, AXES, route)]
    all_to_all x0 -> x1, starting transfers between devices: none -> 4.02 us  [spread(): lax.all_to_all(parts, 'blk', 0, 0, axis_index_groups=groups, tiled=True)]
    ppermute x3, starting transfers between devices: 12.3 us -> 14 us  [shift(): return lax.ppermute(x, AXES, route)]
    unnamed x20, local copies, waits for them, and re-layouts: 2.59 us -> 1 us
  transfers between devices with their start and end apart: 34 -> 22, of which waited for: 16 -> 6; matrix products, arithmetic and copies ran while one was open for 1% -> 2% of each run, Pallas kernels for 13% -> 15%
where the time goes in v2:
time: 115 us
  starting transfers between devices  40.9 us (36%)
  Pallas kernels  33.1 us (29%)
  blocking collectives  19.7 us (17%)
  waiting for transfers between devices  14.4 us (13%)
  local copies, waits for them, and re-layouts  3.3 us (3%)
  other arithmetic  1.75 us (2%)
  between operations  1.61 us (1%)
    ppermute x18, starting transfers between devices, swap(): return lax.ppermute(x, AXES, [(i, i ^ mask) for i in range(256)])  22.9 us
    all_to_all x1, blocking collectives, spread(): lax.all_to_all(parts, 'blk', 0, 0, axis_index_groups=groups, tiled=True)  19.7 us
    ppermute x3, starting transfers between devices, shift(): return lax.ppermute(x, AXES, route)  14 us
    pallas_call x1, Pallas kernels, shards(): call(score_kernel, [kept, sent, jax.ShapeDtypeStruct((EDGES, ENT), BF16),...  11 us
    pallas_call x2, Pallas kernels, update(): pl.pallas_call(functools.partial(update_kernel, len(pieces)), grid=(n //...  8.07 us
    all_to_all x1, waiting for transfers between devices, spread(): lax.all_to_all(parts, 'blk', 0, 0, axis_index_groups=groups, tiled=True)  7.7 us
    pallas_call x1, Pallas kernels, shards(): call(scatter_kernel, [kept, sent, kept, sent], 1, 5, flops=3 * 2 * EDGES...  6.47 us
    pallas_call x1, Pallas kernels, shards(): call(gather_kernel, [jax.ShapeDtypeStruct((EDGES, D), BF16), jax.ShapeDty...  5.98 us
  transfers between devices with their start and end apart: 22, of which 6 were waited for; matrix products, arithmetic and copies ran while one was open for 2% of the time, Pallas kernels for 15%

profile of v2, /device:TPU:1, one launch (start us, length us, event | category | flops | bytes accessed | tf_op | source)
XLA Modules:
  0.0 114.8 jit_solution(2972206577942244571)
XLA Ops:
  0.7 2.2 %dynamic-slice_convert_fusion = bf16[1024,256]{1,0:T(8,128)(2,1)} fusion(f32[2048,256]{1,0:T(8,128)} %rows_ref.2, s32[]{:T(128)S(6)} %select_n.21), kind=kLoop, calls=%fused_computation | loop fusion | bytes 1048580 | tf_op jit(solution)/shard_map/convert_element_type | solution.py:360
  2.9 11.1 %collective-permute-start = (bf16[1024,256]{1,0:T(8,128)(2,1)}, bf16[1024,256]{1,0:T(8,128)(2,1)}, u32[]{:S(2)}, u32[]{:S(2)}) collective-permute-start(bf16[1024,256]{1,0:T(8,128)(2,1)} %dynamic-slice_convert_fusion), channel_id=1, source_target_pairs={{6,0},{7,1},{4,2},{5,3},{10,4},{11,5},{8,6},{9,7},{14,8},{15,9},{1... | collective-permute-start | bytes 1572872 | tf_op jit(solution)/shard_map/ppermute | solution.py:345
  14.0 1.7 %convert_element_type.7.low_ref = bf16[2048,256]{1,0:T(8,128)(2,1)S(1)} convert(f32[2048,256]{1,0:T(8,128)} %rows_ref.2) | non-fusion elementwise | flops 524288 | bytes 3145728 | tf_op jit(solution)/shard_map/convert_element_type | solution.py:359
  15.9 6.0 %shard_map.120 = (bf16[1024,256]{1,0:T(8,128)(2,1)S(1)}, f32[1024,256]{1,0:T(8,128)S(1)}, f32[1024,256]{1,0:T(8,128)S(1)}, f32[4,16,128]{2,1,0:T(8,128)S(1)}) custom-call(s32[8,1024]{1,0:T(8,128)S(1)} %concatenate.3.ids_ref, s32[4,1024]{1,0:T(4,128)S(1)} %reshape.40.negs_ref, bf16[2048,256]{1,0:T(8,128)(2,1)S(1)} %convert_element_type.7.low_ref, ...), custom_call_target="tpu_custom_call" | custom-call | flops 4294967296 | bytes 4194304 | tf_op jit(solution)/shard_map/pallas_call | solution.py:375
  21.9 1.0 copy-done.5
  22.9 2.0 %collective-permute-done.near_ref = bf16[1024,256]{1,0:T(8,128)(2,1)} collective-permute-done((bf16[1024,256]{1,0:T(8,128)(2,1)}, bf16[1024,256]{1,0:T(8,128)(2,1)}, u32[]{:S(2)}, u32[]{:S(2)}) %collective-permute-start) | collective-permute-done | bytes 524320 | tf_op jit(solution)/shard_map/ppermute | solution.py:345
  24.9 1.5 %collective-permute-start.1 = (bf16[1024,256]{1,0:T(8,128)(2,1)}, bf16[1024,256]{1,0:T(8,128)(2,1)S(1)}, u32[]{:S(2)}, u32[]{:S(2)}) collective-permute-start(bf16[1024,256]{1,0:T(8,128)(2,1)} %collective-permute-done.near_ref), channel_id=1, source_target_pairs={{0,1},{1,0},{2,3},{3,2},{4,5},{5,4},{6,7},{7,6},{8,9},{9,8},{10,11... | collective-permute-start | bytes 1572872 | tf_op jit(solution)/shard_map/ppermute | solution.py:340
  27.1 1.1 collective-permute-done.1.far_ref
  28.2 11.0 %shard_map.121 = (f32[1024,256]{1,0:T(8,128)S(1)}, bf16[1024,256]{1,0:T(8,128)(2,1)S(1)}, bf16[1024,2048]{1,0:T(8,128)(2,1)}, bf16[256,1024]{1,0:T(8,128)(2,1)S(...) custom-call(s32[1,1]{1,0:T(1,128)S(6)} %copy.13.count_ref, s32[8,1024]{1,0:T(8,128)S(1)} %concatenate.3.ids_ref, ...), custom_call_target="tpu_custom_call" | custom-call | flops 4294967296 | bytes 8388608 | tf_op jit(solution)/shard_map/pallas_call | solution.py:394
  39.5 1.5 %collective-permute-done.2.refs_1_ = bf16[1024,256]{1,0:T(8,128)(2,1)S(1)} collective-permute-done((bf16[1024,256]{1,0:T(8,128)(2,1)S(1)}, bf16[1024,256]{1,0:T(8,128)(2,1)S(1)}, u32[]{:S(2)}, u32[]{:S(2)}) %collective-permute-start.2) | collective-permute-done | bytes 524320 | tf_op jit(solution)/shard_map/ppermute | solution.py:340
  41.4 3.7 %collective-permute-start.5 = (bf16[256,256]{1,0:T(8,128)(2,1)S(1)}, bf16[256,256]{1,0:T(8,128)(2,1)S(1)}, u32[]{:S(2)}, u32[]{:S(2)}) collective-permute-start(bf16[256,256]{1,0:T(8,128)(2,1)S(1)} %get-tuple-element.64), channel_id=1, source_target_pairs={{0,6},{1,7},{2,4},{3,5},{4,2},{5,3},{6,0},{7,1},{8,14},{9,15},{10,... | collective-permute-start | bytes 393224 | tf_op jit(solution)/shard_map/ppermute | solution.py:340
  45.1 6.5 %shard_map.123 = (f32[1024,256]{1,0:T(8,128)S(1)}, bf16[1024,256]{1,0:T(8,128)(2,1)S(1)}, f32[1024,256]{1,0:T(8,128)S(1)}, bf16[1024,256]{1,0:T(8,128)(2,1)S(1)}) custom-call(s32[1]{0:T(128)} %bitcast.2.place_ref, s32[8,1024]{1,0:T(8,128)S(1)} %concatenate.3.ids_ref, bf16[1024,2048]{1,0:T(8,128)(2,1)} %get-tuple-element.65.cc_ref, ...), custom_call_target="tpu_custom_call" | custom-call | flops 3221225472 | bytes 8388608 | tf_op jit(solution)/shard_map/pallas_call | solution.py:415
  51.6 1.3 %collective-permute-start.6 = (bf16[1024,256]{1,0:T(8,128)(2,1)S(1)}, bf16[1024,256]{1,0:T(8,128)(2,1)S(1)}, u32[]{:S(2)}, u32[]{:S(2)}) collective-permute-start(bf16[1024,256]{1,0:T(8,128)(2,1)S(1)} %get-tuple-element.75), channel_id=1, source_target_pairs={{0,1},{1,0},{2,3},{3,2},{4,5},{5,4},{6,7},{7,6},{8,9},{9,8},{10,11... | collective-permute-start | bytes 1572872 | tf_op jit(solution)/shard_map/ppermute | solution.py:340
  53.1 1.4 %collective-permute-done.6.refs_1_ = bf16[1024,256]{1,0:T(8,128)(2,1)S(1)} collective-permute-done((bf16[1024,256]{1,0:T(8,128)(2,1)S(1)}, bf16[1024,256]{1,0:T(8,128)(2,1)S(1)}, u32[]{:S(2)}, u32[]{:S(2)}) %collective-permute-start.6) | collective-permute-done | bytes 524320 | tf_op jit(solution)/shard_map/ppermute | solution.py:340
  55.4 3.0 %collective-permute-start.9 = (bf16[512,256]{1,0:T(8,128)(2,1)S(1)}, bf16[512,256]{1,0:T(8,128)(2,1)S(1)}, u32[]{:S(2)}, u32[]{:S(2)}) collective-permute-start(bf16[512,256]{1,0:T(8,128)(2,1)S(1)} %get-tuple-element.84), channel_id=1, source_target_pairs={{252,0},{253,1},{254,2},{255,3},{0,4},{1,5},{2,6},{3,7},{4,8},{5,9... | collective-permute-start | bytes 786440 | tf_op jit(solution)/shard_map/ppermute | solution.py:345
  58.4 19.7 %all_to_all.10.parts_ref = bf16[32,8,256]{2,1,0:T(8,128)(2,1)S(1)} all-to-all(bf16[32,8,256]{2,1,0:T(8,128)(2,1)S(1)} %bitcast.10), channel_id=1, replica_groups={{0,8,16,24,32,40,48,56,64,72,80,88,96,104,112,120,128,136,144,152,160,1..., dimensions={0} | all-to-all | bytes 262144 | tf_op jit(solution)/shard_map/all_to_all | solution.py:336
  79.2 4.0 %all-to-all-start.1 = ((f32[32,8,256]{2,1,0:T(8,128)}), f32[32,8,256]{2,1,0:T(8,128)S(1)}, u32[]{:S(2)}, u32[]{:S(2)}) async-start(f32[32,8,256]{2,1,0:T(8,128)} %shard_map.127), calls=%async_computation.1 | async-start | bytes 524288 | tf_op jit(solution)/shard_map/all_to_all | solution.py:336
  83.3 2.8 %collective-permute-start.12 = (bf16[528,256]{1,0:T(8,128)(2,1)S(1)}, bf16[528,256]{1,0:T(8,128)(2,1)S(1)}, u32[]{:S(2)}, u32[]{:S(2)}) collective-permute-start(bf16[528,256]{1,0:T(8,128)(2,1)S(1)} %shard_map.128.refs_0_), channel_id=1, source_target_pairs={{0,1},{1,0},{2,3},{3,2},{4,5},{5,4},{6,7},{7,6},{8,9},{9,8},{10,11... | collective-permute-start | bytes 811016 | tf_op jit(solution)/shard_map/ppermute | solution.py:340
  86.1 7.7 %all-to-all-done.1 = f32[32,8,256]{2,1,0:T(8,128)S(1)} async-done(((f32[32,8,256]{2,1,0:T(8,128)}), f32[32,8,256]{2,1,0:T(8,128)S(1)}, u32[]{:S(2)}, u32[]{:S(2)}) %all-to-all-start.1) | async-done | bytes 262176 | tf_op jit(solution)/shard_map/all_to_all | solution.py:336
  95.4 1.8 %collective-permute-start.14 = (bf16[272,256]{1,0:T(8,128)(2,1)S(1)}, bf16[272,256]{1,0:T(8,128)(2,1)}, u32[]{:S(2)}, u32[]{:S(2)}) collective-permute-start(bf16[272,256]{1,0:T(8,128)(2,1)S(1)} %shard_map.130.refs_0_), channel_id=1, source_target_pairs={{0,2},{1,3},{2,0},{3,1},{4,6},{5,7},{6,4},{7,5},{8,10},{9,11},{10,... | collective-permute-start | bytes 417800 | tf_op jit(solution)/shard_map/ppermute | solution.py:340
  97.3 4.7 %collective-permute-start.13 = (bf16[528,256]{1,0:T(8,128)(2,1)S(1)}, bf16[528,256]{1,0:T(8,128)(2,1)}, u32[]{:S(2)}, u32[]{:S(2)}) collective-permute-start(bf16[528,256]{1,0:T(8,128)(2,1)S(1)} %collective-permute-done.11.refs_1_), channel_id=1, source_target_pairs={{0,1},{1,0},{2,3},{3,2},{4,5},{5,4},{6,7},{7,6},{8,9},{9,8},{10,11... | collective-permute-start | bytes 811016 | tf_op jit(solution)/shard_map/ppermute | solution.py:340
  102.1 3.6 %collective-permute-start.20 = (bf16[272,256]{1,0:T(8,128)(2,1)S(1)}, bf16[272,256]{1,0:T(8,128)(2,1)}, u32[]{:S(2)}, u32[]{:S(2)}) collective-permute-start(bf16[272,256]{1,0:T(8,128)(2,1)S(1)} %collective-permute-done.16.refs_3_), channel_id=1, source_target_pairs={{0,1},{1,0},{2,3},{3,2},{4,5},{5,4},{6,7},{7,6},{8,9},{9,8},{10,11... | collective-permute-start | bytes 417800 | tf_op jit(solution)/shard_map/ppermute | solution.py:340
  106.6 3.2 %shard_map.129 = (f32[2048,256]{1,0:T(8,128)}, f32[16,128]{1,0:T(8,128)}) custom-call(s32[1]{0:T(128)} %bitcast.place_ref, f32[2048,256]{1,0:T(8,128)S(1)} %copy-done, f32[16,128]{1,0:T(8,128)S(1)} %bitcast.11, bf16[528,256]{1,0:T(8,128)(2,1)S(1)} %shard_map.128.refs_0_, bf16[528,256]{1,0:T(8,128)(2,1)S(1)} %collective-permute-done.11.refs_1_, ...), custom_call_target="tpu_custom_call" | custom-call | flops 4194304 | bytes 5242880 | tf_op jit(solution)/shard_map/pallas_call | solution.py:293
  109.9 4.8 %shard_map.131 = (f32[2048,256]{1,0:T(8,128)}, f32[16,128]{1,0:T(8,128)}) custom-call(s32[1]{0:T(128)} %bitcast.5.place_ref, f32[2048,256]{1,0:T(8,128)S(1)} %copy-done.2, f32[16,128]{1,0:T(8,128)S(1)} %bitcast.12, bf16[272,256]{1,0:T(8,128)(2,1)S(1)} %shard_map.130.refs_0_, bf16[272,256]{1,0:T(8,128)(2,1)} %collective-permute-done.14.refs_1_, ...), custom_call_target="tpu_custom_call" | custom-call | flops 4194304 | bytes 5242880 | tf_op jit(solution)/shard_map/pallas_call | solution.py:293
  (61 shorter events, 5.8 us)
Async XLA Ops:
  2.9 22.0 %collective-permute-start = (bf16[1024,256]{1,0:T(8,128)(2,1)}, bf16[1024,256]{1,0:T(8,128)(2,1)}, u32[]{:S(2)}, u32[]{:S(2)}) collective-permute-start(bf16[1024,256]{1,0:T(8,128)(2,1)} %dynamic-slice_convert_fusion), channel_id=1, source_target_pairs={{6,0},{7,1},{4,2},{5,3},{10,4},{11,5},{8,6},{9,7},{14,8},{15,9},{1... | collective-permute-start | bytes 1572872 | tf_op jit(solution)/shard_map/ppermute | solution.py:345
  24.9 3.3 %collective-permute-start.1 = (bf16[1024,256]{1,0:T(8,128)(2,1)}, bf16[1024,256]{1,0:T(8,128)(2,1)S(1)}, u32[]{:S(2)}, u32[]{:S(2)}) collective-permute-start(bf16[1024,256]{1,0:T(8,128)(2,1)} %collective-permute-done.near_ref), channel_id=1, source_target_pairs={{0,1},{1,0},{2,3},{3,2},{4,5},{5,4},{6,7},{7,6},{8,9},{9,8},{10,11... | collective-permute-start | bytes 1572872 | tf_op jit(solution)/shard_map/ppermute | solution.py:340
  39.2 1.9 %collective-permute-start.2 = (bf16[1024,256]{1,0:T(8,128)(2,1)S(1)}, bf16[1024,256]{1,0:T(8,128)(2,1)S(1)}, u32[]{:S(2)}, u32[]{:S(2)}) collective-permute-start(bf16[1024,256]{1,0:T(8,128)(2,1)S(1)} %get-tuple-element.55), channel_id=1, source_target_pairs={{0,1},{1,0},{2,3},{3,2},{4,5},{5,4},{6,7},{7,6},{8,9},{9,8},{10,11... | collective-permute-start | bytes 1572872 | tf_op jit(solution)/shard_map/ppermute | solution.py:340
  41.2 10.4 %collective-permute-start.3 = (bf16[256,256]{1,0:T(8,128)(2,1)S(1)}, bf16[256,256]{1,0:T(8,128)(2,1)S(1)}, u32[]{:S(2)}, u32[]{:S(2)}) collective-permute-start(bf16[256,256]{1,0:T(8,128)(2,1)S(1)} %get-tuple-element.62), channel_id=1, source_target_pairs={{0,2},{1,3},{2,0},{3,1},{4,6},{5,7},{6,4},{7,5},{8,10},{9,11},{10,... | collective-permute-start | bytes 393224 | tf_op jit(solution)/shard_map/ppermute | solution.py:340
  41.3 10.3 %collective-permute-start.4 = (bf16[256,256]{1,0:T(8,128)(2,1)S(1)}, bf16[256,256]{1,0:T(8,128)(2,1)S(1)}, u32[]{:S(2)}, u32[]{:S(2)}) collective-permute-start(bf16[256,256]{1,0:T(8,128)(2,1)S(1)} %get-tuple-element.63), channel_id=1, source_target_pairs={{0,4},{1,5},{2,6},{3,7},{4,0},{5,1},{6,2},{7,3},{8,12},{9,13},{10,... | collective-permute-start | bytes 393224 | tf_op jit(solution)/shard_map/ppermute | solution.py:340
  41.4 10.3 %collective-permute-start.5 = (bf16[256,256]{1,0:T(8,128)(2,1)S(1)}, bf16[256,256]{1,0:T(8,128)(2,1)S(1)}, u32[]{:S(2)}, u32[]{:S(2)}) collective-permute-start(bf16[256,256]{1,0:T(8,128)(2,1)S(1)} %get-tuple-element.64), channel_id=1, source_target_pairs={{0,6},{1,7},{2,4},{3,5},{4,2},{5,3},{6,0},{7,1},{8,14},{9,15},{10,... | collective-permute-start | bytes 393224 | tf_op jit(solution)/shard_map/ppermute | solution.py:340
  51.6 2.8 %collective-permute-start.6 = (bf16[1024,256]{1,0:T(8,128)(2,1)S(1)}, bf16[1024,256]{1,0:T(8,128)(2,1)S(1)}, u32[]{:S(2)}, u32[]{:S(2)}) collective-permute-start(bf16[1024,256]{1,0:T(8,128)(2,1)S(1)} %get-tuple-element.75), channel_id=1, source_target_pairs={{0,1},{1,0},{2,3},{3,2},{4,5},{5,4},{6,7},{7,6},{8,9},{9,8},{10,11... | collective-permute-start | bytes 1572872 | tf_op jit(solution)/shard_map/ppermute | solution.py:340
  52.9 2.3 %collective-permute-start.7 = (bf16[1024,256]{1,0:T(8,128)(2,1)S(1)}, bf16[1024,256]{1,0:T(8,128)(2,1)S(1)}, u32[]{:S(2)}, u32[]{:S(2)}) collective-permute-start(bf16[1024,256]{1,0:T(8,128)(2,1)S(1)} %get-tuple-element.78), channel_id=1, source_target_pairs={{0,1},{1,0},{2,3},{3,2},{4,5},{5,4},{6,7},{7,6},{8,9},{9,8},{10,11... | collective-permute-start | bytes 1572872 | tf_op jit(solution)/shard_map/ppermute | solution.py:340
  55.2 51.4 %copy-start = (f32[2048,256]{1,0:T(8,128)S(1)}, f32[2048,256]{1,0:T(8,128)}, u32[]{:S(2)}) copy-start(f32[2048,256]{1,0:T(8,128)} %rows_ref.2) | copy-start | bytes 6291460
  55.2 51.4 %copy-start.3 = (f32[2048]{0:T(1024)S(1)}, f32[2048]{0:T(1024)}, u32[]{:S(2)}) copy-start(f32[2048]{0:T(1024)} %param.10) | copy-start | bytes 24580
  55.3 23.6 %collective-permute-start.8 = (bf16[512,256]{1,0:T(8,128)(2,1)S(1)}, bf16[512,256]{1,0:T(8,128)(2,1)S(1)}, u32[]{:S(2)}, u32[]{:S(2)}) collective-permute-start(bf16[512,256]{1,0:T(8,128)(2,1)S(1)} %get-tuple-element.83), channel_id=1, source_target_pairs={{0,2},{1,3},{2,0},{3,1},{4,6},{5,7},{6,4},{7,5},{8,10},{9,11},{10,... | collective-permute-start | bytes 786440 | tf_op jit(solution)/shard_map/ppermute | solution.py:340
  55.4 23.5 %collective-permute-start.9 = (bf16[512,256]{1,0:T(8,128)(2,1)S(1)}, bf16[512,256]{1,0:T(8,128)(2,1)S(1)}, u32[]{:S(2)}, u32[]{:S(2)}) collective-permute-start(bf16[512,256]{1,0:T(8,128)(2,1)S(1)} %get-tuple-element.84), channel_id=1, source_target_pairs={{252,0},{253,1},{254,2},{255,3},{0,4},{1,5},{2,6},{3,7},{4,8},{5,9... | collective-permute-start | bytes 786440 | tf_op jit(solution)/shard_map/ppermute | solution.py:345
  58.4 20.5 %collective-permute-start.10 = (bf16[512,256]{1,0:T(8,128)(2,1)S(1)}, bf16[512,256]{1,0:T(8,128)(2,1)S(1)}, u32[]{:S(2)}, u32[]{:S(2)}) collective-permute-start(bf16[512,256]{1,0:T(8,128)(2,1)S(1)} %get-tuple-element.85), channel_id=1, source_target_pairs={{254,0},{255,1},{252,2},{253,3},{2,4},{3,5},{0,6},{1,7},{6,8},{7,9... | collective-permute-start | bytes 786440 | tf_op jit(solution)/shard_map/ppermute | solution.py:345
  79.2 14.6 %all-to-all-start.1 = ((f32[32,8,256]{2,1,0:T(8,128)}), f32[32,8,256]{2,1,0:T(8,128)S(1)}, u32[]{:S(2)}, u32[]{:S(2)}) async-start(f32[32,8,256]{2,1,0:T(8,128)} %shard_map.127), calls=%async_computation.1 | async-start | bytes 524288 | tf_op jit(solution)/shard_map/all_to_all | solution.py:336
  83.2 14.1 %collective-permute-start.11 = (bf16[528,256]{1,0:T(8,128)(2,1)S(1)}, bf16[528,256]{1,0:T(8,128)(2,1)S(1)}, u32[]{:S(2)}, u32[]{:S(2)}) collective-permute-start(bf16[528,256]{1,0:T(8,128)(2,1)S(1)} %shard_map.128.refs_0_), channel_id=1, source_target_pairs={{0,2},{1,3},{2,0},{3,1},{4,6},{5,7},{6,4},{7,5},{8,10},{9,11},{10,... | collective-permute-start | bytes 811016 | tf_op jit(solution)/shard_map/ppermute | solution.py:340
  83.3 18.7 %collective-permute-start.12 = (bf16[528,256]{1,0:T(8,128)(2,1)S(1)}, bf16[528,256]{1,0:T(8,128)(2,1)S(1)}, u32[]{:S(2)}, u32[]{:S(2)}) collective-permute-start(bf16[528,256]{1,0:T(8,128)(2,1)S(1)} %shard_map.128.refs_0_), channel_id=1, source_target_pairs={{0,1},{1,0},{2,3},{3,2},{4,5},{5,4},{6,7},{7,6},{8,9},{9,8},{10,11... | collective-permute-start | bytes 811016 | tf_op jit(solution)/shard_map/ppermute | solution.py:340
  93.9 8.2 %collective-permute-start.16 = (bf16[272,256]{1,0:T(8,128)(2,1)S(1)}, bf16[272,256]{1,0:T(8,128)(2,1)S(1)}, u32[]{:S(2)}, u32[]{:S(2)}) collective-permute-start(bf16[272,256]{1,0:T(8,128)(2,1)S(1)} %shard_map.130.refs_0_), channel_id=1, source_target_pairs={{0,6},{1,7},{2,4},{3,5},{4,2},{5,3},{6,0},{7,1},{8,14},{9,15},{10,... | collective-permute-start | bytes 417800 | tf_op jit(solution)/shard_map/ppermute | solution.py:340
  94.8 10.9 %collective-permute-start.15 = (bf16[272,256]{1,0:T(8,128)(2,1)S(1)}, bf16[272,256]{1,0:T(8,128)(2,1)S(1)}, u32[]{:S(2)}, u32[]{:S(2)}) collective-permute-start(bf16[272,256]{1,0:T(8,128)(2,1)S(1)} %shard_map.130.refs_0_), channel_id=1, source_target_pairs={{0,4},{1,5},{2,6},{3,7},{4,0},{5,1},{6,2},{7,3},{8,12},{9,13},{10,... | collective-permute-start | bytes 417800 | tf_op jit(solution)/shard_map/ppermute | solution.py:340
  95.4 10.3 %collective-permute-start.14 = (bf16[272,256]{1,0:T(8,128)(2,1)S(1)}, bf16[272,256]{1,0:T(8,128)(2,1)}, u32[]{:S(2)}, u32[]{:S(2)}) collective-permute-start(bf16[272,256]{1,0:T(8,128)(2,1)S(1)} %shard_map.130.refs_0_), channel_id=1, source_target_pairs={{0,2},{1,3},{2,0},{3,1},{4,6},{5,7},{6,4},{7,5},{8,10},{9,11},{10,... | collective-permute-start | bytes 417800 | tf_op jit(solution)/shard_map/ppermute | solution.py:340
  97.3 9.4 %collective-permute-start.13 = (bf16[528,256]{1,0:T(8,128)(2,1)S(1)}, bf16[528,256]{1,0:T(8,128)(2,1)}, u32[]{:S(2)}, u32[]{:S(2)}) collective-permute-start(bf16[528,256]{1,0:T(8,128)(2,1)S(1)} %collective-permute-done.11.refs_1_), channel_id=1, source_target_pairs={{0,1},{1,0},{2,3},{3,2},{4,5},{5,4},{6,7},{7,6},{8,9},{9,8},{10,11... | collective-permute-start | bytes 811016 | tf_op jit(solution)/shard_map/ppermute | solution.py:340
  102.0 7.9 %collective-permute-start.17 = (bf16[272,256]{1,0:T(8,128)(2,1)S(1)}, bf16[272,256]{1,0:T(8,128)(2,1)}, u32[]{:S(2)}, u32[]{:S(2)}) collective-permute-start(bf16[272,256]{1,0:T(8,128)(2,1)S(1)} %shard_map.130.refs_0_), channel_id=1, source_target_pairs={{0,1},{1,0},{2,3},{3,2},{4,5},{5,4},{6,7},{7,6},{8,9},{9,8},{10,11... | collective-permute-start | bytes 417800 | tf_op jit(solution)/shard_map/ppermute | solution.py:340
  102.1 7.8 %collective-permute-start.20 = (bf16[272,256]{1,0:T(8,128)(2,1)S(1)}, bf16[272,256]{1,0:T(8,128)(2,1)}, u32[]{:S(2)}, u32[]{:S(2)}) collective-permute-start(bf16[272,256]{1,0:T(8,128)(2,1)S(1)} %collective-permute-done.16.refs_3_), channel_id=1, source_target_pairs={{0,1},{1,0},{2,3},{3,2},{4,5},{5,4},{6,7},{7,6},{8,9},{9,8},{10,11... | collective-permute-start | bytes 417800 | tf_op jit(solution)/shard_map/ppermute | solution.py:340
  105.7 4.2 %collective-permute-start.19 = (bf16[272,256]{1,0:T(8,128)(2,1)S(1)}, bf16[272,256]{1,0:T(8,128)(2,1)}, u32[]{:S(2)}, u32[]{:S(2)}) collective-permute-start(bf16[272,256]{1,0:T(8,128)(2,1)S(1)} %collective-permute-done.15.refs_2_), channel_id=1, source_target_pairs={{0,1},{1,0},{2,3},{3,2},{4,5},{5,4},{6,7},{7,6},{8,9},{9,8},{10,11... | collective-permute-start | bytes 417800 | tf_op jit(solution)/shard_map/ppermute | solution.py:340
  105.7 4.2 %collective-permute-start.18 = (bf16[272,256]{1,0:T(8,128)(2,1)}, bf16[272,256]{1,0:T(8,128)(2,1)}, u32[]{:S(2)}, u32[]{:S(2)}) collective-permute-start(bf16[272,256]{1,0:T(8,128)(2,1)} %collective-permute-done.14.refs_1_), channel_id=1, source_target_pairs={{0,1},{1,0},{2,3},{3,2},{4,5},{5,4},{6,7},{7,6},{8,9},{9,8},{10,11... | collective-permute-start | bytes 417800 | tf_op jit(solution)/shard_map/ppermute | solution.py:340
  (8 other events, 110.7 us)

commit v3 on v2

--- a/solution.py
+++ b/solution.py
@@ -426,27 +426,25 @@
     src_own, src_away = add_split([src_keep, src_recv], 2, own=F32)
     dst_own, dst_away = add_split([dst_keep, dst_recv], 2)
     (mine,) = add_split([parts[0], *recv], 1)
-    mine, src_away, dst_own, dst_away = lax.optimization_barrier(
-        (mine, src_away, dst_own, dst_away)
-    )
     src_other = swap(src_away, XL)
     dst_first = shift(dst_own, 1, 0)
     dst_second = shift(dst_away, 1, XL)
 
     landed = spread(mine.reshape(32, 8, D))
+    landed, src_other, dst_first, dst_second = lax.optimization_barrier(
+        (landed, src_other, dst_first, dst_second)
+    )
+    summed = sum_rows(landed)
     ent_own = sum_with_means([src_own, src_other, dst_first, dst_second])
-    summed = sum_rows(landed)
-    summed, ent_own = lax.optimization_barrier((summed, ent_own))
     ent_xl = swap(ent_own, XL)
-    total = spread(summed).reshape(256, D)
-    quarter = sum_with_means([total])
-    recv = [swap(quarter, mask) for mask in X_MASKS]
-
     ent_core = [swap(ent_own, CORE), swap(ent_xl, CORE)]
     place = (core * 2 + xl).reshape(1)
     new_entities, new_entity_acc = update(
         entities, entity_acc, [ent_own, ent_xl, *ent_core], place
     )
+    total, new_entity_acc = lax.optimization_barrier((spread(summed), new_entity_acc))
+    quarter = sum_with_means([total.reshape(256, D)])
+    recv = [swap(quarter, mask) for mask in X_MASKS]
 
     pieces = [quarter, *recv]
     pieces = pieces + [swap(piece, CORE) for piece in pieces]

time: 115 us -> 113 us (0.983)
  waiting for transfers between devices: 14.4 us -> 11.7 us
  Pallas kernels: 33.1 us -> 30.7 us
  local copies, waits for them, and re-layouts: 3.3 us -> 4.89 us
  starting transfers between devices: 40.9 us -> 42.3 us
    all_to_all x1, waiting for transfers between devices: 7.7 us -> 2.9 us  [spread(): lax.all_to_all(parts, 'blk', 0, 0, axis_index_groups=groups, tiled=True)]
    pallas_call x2, Pallas kernels: 8.07 us -> 5.69 us  [update(): pl.pallas_call(functools.partial(update_kernel, len(pieces)), grid=(n //...]
    ppermute x18, waiting for transfers between devices: 4.66 us -> 6.79 us  [swap(): return lax.ppermute(x, AXES, [(i, i ^ mask) for i in range(256)])]
    ppermute x18, starting transfers between devices: 22.9 us -> 24.8 us  [swap(): return lax.ppermute(x, AXES, [(i, i ^ mask) for i in range(256)])]
    unnamed x20, local copies, waits for them, and re-layouts: 1 us -> 2.6 us
  transfers between devices with their start and end apart: 22 -> 22, of which waited for: 6 -> 9; matrix products, arithmetic and copies ran while one was open for 2% -> 2% of each run, Pallas kernels for 15% -> 14%
where the time goes in v3:
time: 113 us
  starting transfers between devices  42.3 us (37%)
  Pallas kernels  30.7 us (27%)
  blocking collectives  19.7 us (17%)
  waiting for transfers between devices  11.7 us (10%)
  local copies, waits for them, and re-layouts  4.89 us (4%)
  other arithmetic  1.75 us (2%)
  between operations  1.6 us (1%)
    ppermute x18, starting transfers between devices, swap(): return lax.ppermute(x, AXES, [(i, i ^ mask) for i in range(256)])  24.8 us
    all_to_all x1, blocking collectives, spread(): lax.all_to_all(parts, 'blk', 0, 0, axis_index_groups=groups, tiled=True)  19.7 us
    ppermute x3, starting transfers between devices, shift(): return lax.ppermute(x, AXES, route)  13.6 us
    pallas_call x1, Pallas kernels, shards(): call(score_kernel, [kept, sent, jax.ShapeDtypeStruct((EDGES, ENT), BF16),...  11 us
    ppermute x18, waiting for transfers between devices, swap(): return lax.ppermute(x, AXES, [(i, i ^ mask) for i in range(256)])  6.79 us
    pallas_call x1, Pallas kernels, shards(): call(scatter_kernel, [kept, sent, kept, sent], 1, 5, flops=3 * 2 * EDGES...  6.47 us
    pallas_call x1, Pallas kernels, shards(): call(gather_kernel, [jax.ShapeDtypeStruct((EDGES, D), BF16), jax.ShapeDty...  5.98 us
    pallas_call x2, Pallas kernels, update(): pl.pallas_call(functools.partial(update_kernel, len(pieces)), grid=(n //...  5.69 us
  transfers between devices with their start and end apart: 22, of which 9 were waited for; matrix products, arithmetic and copies ran while one was open for 2% of the time, Pallas kernels for 14%

profile of v3, /device:TPU:1, one launch (start us, length us, event | category | flops | bytes accessed | tf_op | source)
XLA Modules:
  0.0 112.7 jit_solution(2400184519157132936)
XLA Ops:
  0.7 2.2 %dynamic-slice_convert_fusion = bf16[1024,256]{1,0:T(8,128)(2,1)} fusion(f32[2048,256]{1,0:T(8,128)} %rows_ref.2, s32[]{:T(128)S(6)} %select_n.21), kind=kLoop, calls=%fused_computation | loop fusion | bytes 1048580 | tf_op jit(solution)/shard_map/convert_element_type | solution.py:360
  2.9 11.1 %collective-permute-start = (bf16[1024,256]{1,0:T(8,128)(2,1)}, bf16[1024,256]{1,0:T(8,128)(2,1)}, u32[]{:S(2)}, u32[]{:S(2)}) collective-permute-start(bf16[1024,256]{1,0:T(8,128)(2,1)} %dynamic-slice_convert_fusion), channel_id=1, source_target_pairs={{6,0},{7,1},{4,2},{5,3},{10,4},{11,5},{8,6},{9,7},{14,8},{15,9},{1... | collective-permute-start | bytes 1572872 | tf_op jit(solution)/shard_map/ppermute | solution.py:345
  14.0 1.7 %convert_element_type.7.low_ref = bf16[2048,256]{1,0:T(8,128)(2,1)S(1)} convert(f32[2048,256]{1,0:T(8,128)} %rows_ref.2) | non-fusion elementwise | flops 524288 | bytes 3145728 | tf_op jit(solution)/shard_map/convert_element_type | solution.py:359
  15.9 6.0 %shard_map.120 = (bf16[1024,256]{1,0:T(8,128)(2,1)S(1)}, f32[1024,256]{1,0:T(8,128)S(1)}, f32[1024,256]{1,0:T(8,128)S(1)}, f32[4,16,128]{2,1,0:T(8,128)S(1)}) custom-call(s32[8,1024]{1,0:T(8,128)S(1)} %concatenate.3.ids_ref, s32[4,1024]{1,0:T(4,128)S(1)} %reshape.41.negs_ref, bf16[2048,256]{1,0:T(8,128)(2,1)S(1)} %convert_element_type.7.low_ref, ...), custom_call_target="tpu_custom_call" | custom-call | flops 4294967296 | bytes 4194304 | tf_op jit(solution)/shard_map/pallas_call | solution.py:375
  22.9 2.0 %collective-permute-done.near_ref = bf16[1024,256]{1,0:T(8,128)(2,1)} collective-permute-done((bf16[1024,256]{1,0:T(8,128)(2,1)}, bf16[1024,256]{1,0:T(8,128)(2,1)}, u32[]{:S(2)}, u32[]{:S(2)}) %collective-permute-start) | collective-permute-done | bytes 524320 | tf_op jit(solution)/shard_map/ppermute | solution.py:345
  24.9 1.5 %collective-permute-start.1 = (bf16[1024,256]{1,0:T(8,128)(2,1)}, bf16[1024,256]{1,0:T(8,128)(2,1)S(1)}, u32[]{:S(2)}, u32[]{:S(2)}) collective-permute-start(bf16[1024,256]{1,0:T(8,128)(2,1)} %collective-permute-done.near_ref), channel_id=1, source_target_pairs={{0,1},{1,0},{2,3},{3,2},{4,5},{5,4},{6,7},{7,6},{8,9},{9,8},{10,11... | collective-permute-start | bytes 1572872 | tf_op jit(solution)/shard_map/ppermute | solution.py:340
  28.2 11.0 %shard_map.121 = (f32[1024,256]{1,0:T(8,128)S(1)}, bf16[1024,256]{1,0:T(8,128)(2,1)S(1)}, bf16[1024,2048]{1,0:T(8,128)(2,1)}, bf16[256,1024]{1,0:T(8,128)(2,1)S(...) custom-call(s32[1,1]{1,0:T(1,128)S(6)} %copy.13.count_ref, s32[8,1024]{1,0:T(8,128)S(1)} %concatenate.3.ids_ref, ...), custom_call_target="tpu_custom_call" | custom-call | flops 4294967296 | bytes 8388608 | tf_op jit(solution)/shard_map/pallas_call | solution.py:394
  39.5 1.5 %collective-permute-done.2.refs_1_ = bf16[1024,256]{1,0:T(8,128)(2,1)S(1)} collective-permute-done((bf16[1024,256]{1,0:T(8,128)(2,1)S(1)}, bf16[1024,256]{1,0:T(8,128)(2,1)S(1)}, u32[]{:S(2)}, u32[]{:S(2)}) %collective-permute-start.2) | collective-permute-done | bytes 524320 | tf_op jit(solution)/shard_map/ppermute | solution.py:340
  41.4 3.7 %collective-permute-start.5 = (bf16[256,256]{1,0:T(8,128)(2,1)S(1)}, bf16[256,256]{1,0:T(8,128)(2,1)S(1)}, u32[]{:S(2)}, u32[]{:S(2)}) collective-permute-start(bf16[256,256]{1,0:T(8,128)(2,1)S(1)} %get-tuple-element.68), channel_id=1, source_target_pairs={{0,6},{1,7},{2,4},{3,5},{4,2},{5,3},{6,0},{7,1},{8,14},{9,15},{10,... | collective-permute-start | bytes 393224 | tf_op jit(solution)/shard_map/ppermute | solution.py:340
  45.1 6.5 %shard_map.123 = (f32[1024,256]{1,0:T(8,128)S(1)}, bf16[1024,256]{1,0:T(8,128)(2,1)S(1)}, f32[1024,256]{1,0:T(8,128)S(1)}, bf16[1024,256]{1,0:T(8,128)(2,1)S(1)}) custom-call(s32[1]{0:T(128)} %bitcast.2.place_ref, s32[8,1024]{1,0:T(8,128)S(1)} %concatenate.3.ids_ref, bf16[1024,2048]{1,0:T(8,128)(2,1)} %get-tuple-element.61.cc_ref, ...), custom_call_target="tpu_custom_call" | custom-call | flops 3221225472 | bytes 8388608 | tf_op jit(solution)/shard_map/pallas_call | solution.py:415
  55.4 2.5 %collective-permute-start.9 = (bf16[512,256]{1,0:T(8,128)(2,1)S(1)}, bf16[512,256]{1,0:T(8,128)(2,1)S(1)}, u32[]{:S(2)}, u32[]{:S(2)}) collective-permute-start(bf16[512,256]{1,0:T(8,128)(2,1)S(1)} %get-tuple-element.80), channel_id=1, source_target_pairs={{252,0},{253,1},{254,2},{255,3},{0,4},{1,5},{2,6},{3,7},{4,8},{5,9... | collective-permute-start | bytes 786440 | tf_op jit(solution)/shard_map/ppermute | solution.py:345
  57.9 19.7 %all_to_all.10.parts_ref = bf16[32,8,256]{2,1,0:T(8,128)(2,1)S(1)} all-to-all(bf16[32,8,256]{2,1,0:T(8,128)(2,1)S(1)} %bitcast.10), channel_id=1, replica_groups={{0,8,16,24,32,40,48,56,64,72,80,88,96,104,112,120,128,136,144,152,160,1..., dimensions={0} | all-to-all | bytes 262144 | tf_op jit(solution)/shard_map/all_to_all | solution.py:336
  78.8 4.0 %all-to-all-start.1 = ((f32[32,8,256]{2,1,0:T(8,128)}), f32[32,8,256]{2,1,0:T(8,128)S(1)}, u32[]{:S(2)}, u32[]{:S(2)}) async-start(f32[32,8,256]{2,1,0:T(8,128)} %shard_map.129), calls=%async_computation.1 | async-start | bytes 524288 | tf_op jit(solution)/shard_map/all_to_all | solution.py:336
  82.8 2.8 %collective-permute-start.12 = (bf16[528,256]{1,0:T(8,128)(2,1)S(1)}, bf16[528,256]{1,0:T(8,128)(2,1)S(1)}, u32[]{:S(2)}, u32[]{:S(2)}) collective-permute-start(bf16[528,256]{1,0:T(8,128)(2,1)S(1)} %shard_map.127.refs_0_), channel_id=1, source_target_pairs={{0,1},{1,0},{2,3},{3,2},{4,5},{5,4},{6,7},{7,6},{8,9},{9,8},{10,11... | collective-permute-start | bytes 811016 | tf_op jit(solution)/shard_map/ppermute | solution.py:340
  85.6 1.6 %collective-permute-start.13 = (bf16[528,256]{1,0:T(8,128)(2,1)S(1)}, bf16[528,256]{1,0:T(8,128)(2,1)S(1)}, u32[]{:S(2)}, u32[]{:S(2)}) collective-permute-start(bf16[528,256]{1,0:T(8,128)(2,1)S(1)} %collective-permute-done.11.refs_1_), channel_id=1, source_target_pairs={{0,1},{1,0},{2,3},{3,2},{4,5},{5,4},{6,7},{7,6},{8,9},{9,8},{10,11... | collective-permute-start | bytes 811016 | tf_op jit(solution)/shard_map/ppermute | solution.py:340
  88.4 2.1 %shard_map.128 = (f32[2048,256]{1,0:T(8,128)}, f32[16,128]{1,0:T(8,128)}) custom-call(s32[1]{0:T(128)} %bitcast.place_ref, f32[2048,256]{1,0:T(8,128)S(1)} %copy-done, f32[16,128]{1,0:T(8,128)S(1)} %bitcast.11, bf16[528,256]{1,0:T(8,128)(2,1)S(1)} %shard_map.127.refs_0_, bf16[528,256]{1,0:T(8,128)(2,1)S(1)} %collective-permute-done.11.refs_1_, ...), custom_call_target="tpu_custom_call" | custom-call | flops 4194304 | bytes 5242880 | tf_op jit(solution)/shard_map/pallas_call | solution.py:293
  90.5 2.9 %all-to-all-done.1 = f32[32,8,256]{2,1,0:T(8,128)S(1)} async-done(((f32[32,8,256]{2,1,0:T(8,128)}), f32[32,8,256]{2,1,0:T(8,128)S(1)}, u32[]{:S(2)}, u32[]{:S(2)}) %all-to-all-start.1) | async-done | bytes 262176 | tf_op jit(solution)/shard_map/all_to_all | solution.py:336
  93.5 1.8 %collective-permute-start.16 = (bf16[272,256]{1,0:T(8,128)(2,1)S(1)}, bf16[272,256]{1,0:T(8,128)(2,1)S(1)}, u32[]{:S(2)}, u32[]{:S(2)}) collective-permute-start(bf16[272,256]{1,0:T(8,128)(2,1)S(1)} %shard_map.130.refs_0_), channel_id=1, source_target_pairs={{0,6},{1,7},{2,4},{3,5},{4,2},{5,3},{6,0},{7,1},{8,14},{9,15},{10,... | collective-permute-start | bytes 417800 | tf_op jit(solution)/shard_map/ppermute | solution.py:340
  95.4 1.5 %collective-permute-start.15 = (bf16[272,256]{1,0:T(8,128)(2,1)S(1)}, bf16[272,256]{1,0:T(8,128)(2,1)S(1)}, u32[]{:S(2)}, u32[]{:S(2)}) collective-permute-start(bf16[272,256]{1,0:T(8,128)(2,1)S(1)} %shard_map.130.refs_0_), channel_id=1, source_target_pairs={{0,4},{1,5},{2,6},{3,7},{4,0},{5,1},{6,2},{7,3},{8,12},{9,13},{10,... | collective-permute-start | bytes 417800 | tf_op jit(solution)/shard_map/ppermute | solution.py:340
  96.9 4.7 %collective-permute-start.17 = (bf16[272,256]{1,0:T(8,128)(2,1)S(1)}, bf16[272,256]{1,0:T(8,128)(2,1)S(1)}, u32[]{:S(2)}, u32[]{:S(2)}) collective-permute-start(bf16[272,256]{1,0:T(8,128)(2,1)S(1)} %shard_map.130.refs_0_), channel_id=1, source_target_pairs={{0,1},{1,0},{2,3},{3,2},{4,5},{5,4},{6,7},{7,6},{8,9},{9,8},{10,11... | collective-permute-start | bytes 417800 | tf_op jit(solution)/shard_map/ppermute | solution.py:340
  101.6 2.2 %collective-permute-start.20 = (bf16[272,256]{1,0:T(8,128)(2,1)S(1)}, bf16[272,256]{1,0:T(8,128)(2,1)S(1)}, u32[]{:S(2)}, u32[]{:S(2)}) collective-permute-start(bf16[272,256]{1,0:T(8,128)(2,1)S(1)} %collective-permute-done.16.refs_3_), channel_id=1, source_target_pairs={{0,1},{1,0},{2,3},{3,2},{4,5},{5,4},{6,7},{7,6},{8,9},{9,8},{10,11... | collective-permute-start | bytes 417800 | tf_op jit(solution)/shard_map/ppermute | solution.py:340
  103.8 2.2 %collective-permute-start.19 = (bf16[272,256]{1,0:T(8,128)(2,1)S(1)}, bf16[272,256]{1,0:T(8,128)(2,1)S(1)}, u32[]{:S(2)}, u32[]{:S(2)}) collective-permute-start(bf16[272,256]{1,0:T(8,128)(2,1)S(1)} %collective-permute-done.15.refs_2_), channel_id=1, source_target_pairs={{0,1},{1,0},{2,3},{3,2},{4,5},{5,4},{6,7},{7,6},{8,9},{9,8},{10,11... | collective-permute-start | bytes 417800 | tf_op jit(solution)/shard_map/ppermute | solution.py:340
  107.5 1.6 %copy-done.2 = f32[2048,256]{1,0:T(8,128)S(1)} copy-done((f32[2048,256]{1,0:T(8,128)S(1)}, f32[2048,256]{1,0:T(8,128)}, u32[]{:S(2)}) %copy-start.2) | copy-done | bytes 2097176
  109.1 3.6 %shard_map.131 = (f32[2048,256]{1,0:T(8,128)}, f32[16,128]{1,0:T(8,128)}) custom-call(s32[1]{0:T(128)} %bitcast.5.place_ref, f32[2048,256]{1,0:T(8,128)S(1)} %copy-done.2, f32[16,128]{1,0:T(8,128)S(1)} %bitcast.12, bf16[272,256]{1,0:T(8,128)(2,1)S(1)} %shard_map.130.refs_0_, bf16[272,256]{1,0:T(8,128)(2,1)S(1)} %collective-permute-done.14.refs_1_, ...), custom_call_target="tpu_custom_call" | custom-call | flops 4194304 | bytes 5242880 | tf_op jit(solution)/shard_map/pallas_call | solution.py:293
  (61 shorter events, 10.6 us)
Async XLA Ops:
  2.9 22.0 %collective-permute-start = (bf16[1024,256]{1,0:T(8,128)(2,1)}, bf16[1024,256]{1,0:T(8,128)(2,1)}, u32[]{:S(2)}, u32[]{:S(2)}) collective-permute-start(bf16[1024,256]{1,0:T(8,128)(2,1)} %dynamic-slice_convert_fusion), channel_id=1, source_target_pairs={{6,0},{7,1},{4,2},{5,3},{10,4},{11,5},{8,6},{9,7},{14,8},{15,9},{1... | collective-permute-start | bytes 1572872 | tf_op jit(solution)/shard_map/ppermute | solution.py:345
  24.9 3.3 %collective-permute-start.1 = (bf16[1024,256]{1,0:T(8,128)(2,1)}, bf16[1024,256]{1,0:T(8,128)(2,1)S(1)}, u32[]{:S(2)}, u32[]{:S(2)}) collective-permute-start(bf16[1024,256]{1,0:T(8,128)(2,1)} %collective-permute-done.near_ref), channel_id=1, source_target_pairs={{0,1},{1,0},{2,3},{3,2},{4,5},{5,4},{6,7},{7,6},{8,9},{9,8},{10,11... | collective-permute-start | bytes 1572872 | tf_op jit(solution)/shard_map/ppermute | solution.py:340
  39.2 1.9 %collective-permute-start.2 = (bf16[1024,256]{1,0:T(8,128)(2,1)S(1)}, bf16[1024,256]{1,0:T(8,128)(2,1)S(1)}, u32[]{:S(2)}, u32[]{:S(2)}) collective-permute-start(bf16[1024,256]{1,0:T(8,128)(2,1)S(1)} %get-tuple-element.55), channel_id=1, source_target_pairs={{0,1},{1,0},{2,3},{3,2},{4,5},{5,4},{6,7},{7,6},{8,9},{9,8},{10,11... | collective-permute-start | bytes 1572872 | tf_op jit(solution)/shard_map/ppermute | solution.py:340
  41.2 10.4 %collective-permute-start.3 = (bf16[256,256]{1,0:T(8,128)(2,1)S(1)}, bf16[256,256]{1,0:T(8,128)(2,1)S(1)}, u32[]{:S(2)}, u32[]{:S(2)}) collective-permute-start(bf16[256,256]{1,0:T(8,128)(2,1)S(1)} %get-tuple-element.66), channel_id=1, source_target_pairs={{0,2},{1,3},{2,0},{3,1},{4,6},{5,7},{6,4},{7,5},{8,10},{9,11},{10,... | collective-permute-start | bytes 393224 | tf_op jit(solution)/shard_map/ppermute | solution.py:340
  41.3 10.3 %collective-permute-start.4 = (bf16[256,256]{1,0:T(8,128)(2,1)S(1)}, bf16[256,256]{1,0:T(8,128)(2,1)S(1)}, u32[]{:S(2)}, u32[]{:S(2)}) collective-permute-start(bf16[256,256]{1,0:T(8,128)(2,1)S(1)} %get-tuple-element.67), channel_id=1, source_target_pairs={{0,4},{1,5},{2,6},{3,7},{4,0},{5,1},{6,2},{7,3},{8,12},{9,13},{10,... | collective-permute-start | bytes 393224 | tf_op jit(solution)/shard_map/ppermute | solution.py:340
  41.4 10.3 %collective-permute-start.5 = (bf16[256,256]{1,0:T(8,128)(2,1)S(1)}, bf16[256,256]{1,0:T(8,128)(2,1)S(1)}, u32[]{:S(2)}, u32[]{:S(2)}) collective-permute-start(bf16[256,256]{1,0:T(8,128)(2,1)S(1)} %get-tuple-element.68), channel_id=1, source_target_pairs={{0,6},{1,7},{2,4},{3,5},{4,2},{5,3},{6,0},{7,1},{8,14},{9,15},{10,... | collective-permute-start | bytes 393224 | tf_op jit(solution)/shard_map/ppermute | solution.py:340
  51.6 2.8 %collective-permute-start.6 = (bf16[1024,256]{1,0:T(8,128)(2,1)S(1)}, bf16[1024,256]{1,0:T(8,128)(2,1)S(1)}, u32[]{:S(2)}, u32[]{:S(2)}) collective-permute-start(bf16[1024,256]{1,0:T(8,128)(2,1)S(1)} %get-tuple-element.71), channel_id=1, source_target_pairs={{0,1},{1,0},{2,3},{3,2},{4,5},{5,4},{6,7},{7,6},{8,9},{9,8},{10,11... | collective-permute-start | bytes 1572872 | tf_op jit(solution)/shard_map/ppermute | solution.py:340
  52.9 2.3 %collective-permute-start.8 = (bf16[1024,256]{1,0:T(8,128)(2,1)S(1)}, bf16[1024,256]{1,0:T(8,128)(2,1)S(1)}, u32[]{:S(2)}, u32[]{:S(2)}) collective-permute-start(bf16[1024,256]{1,0:T(8,128)(2,1)S(1)} %get-tuple-element.79), channel_id=1, source_target_pairs={{0,1},{1,0},{2,3},{3,2},{4,5},{5,4},{6,7},{7,6},{8,9},{9,8},{10,11... | collective-permute-start | bytes 1572872 | tf_op jit(solution)/shard_map/ppermute | solution.py:340
  54.6 23.1 %collective-permute-start.7 = (bf16[512,256]{1,0:T(8,128)(2,1)S(1)}, bf16[512,256]{1,0:T(8,128)(2,1)S(1)}, u32[]{:S(2)}, u32[]{:S(2)}) collective-permute-start(bf16[512,256]{1,0:T(8,128)(2,1)S(1)} %get-tuple-element.77), channel_id=1, source_target_pairs={{0,2},{1,3},{2,0},{3,1},{4,6},{5,7},{6,4},{7,5},{8,10},{9,11},{10,... | collective-permute-start | bytes 786440 | tf_op jit(solution)/shard_map/ppermute | solution.py:340
  55.3 33.0 %copy-start = (f32[2048,256]{1,0:T(8,128)S(1)}, f32[2048,256]{1,0:T(8,128)}, u32[]{:S(2)}) copy-start(f32[2048,256]{1,0:T(8,128)} %rows_ref.2) | copy-start | bytes 6291460
  55.3 33.0 %copy-start.3 = (f32[2048]{0:T(1024)S(1)}, f32[2048]{0:T(1024)}, u32[]{:S(2)}) copy-start(f32[2048]{0:T(1024)} %param.10) | copy-start | bytes 24580
  55.4 22.3 %collective-permute-start.9 = (bf16[512,256]{1,0:T(8,128)(2,1)S(1)}, bf16[512,256]{1,0:T(8,128)(2,1)S(1)}, u32[]{:S(2)}, u32[]{:S(2)}) collective-permute-start(bf16[512,256]{1,0:T(8,128)(2,1)S(1)} %get-tuple-element.80), channel_id=1, source_target_pairs={{252,0},{253,1},{254,2},{255,3},{0,4},{1,5},{2,6},{3,7},{4,8},{5,9... | collective-permute-start | bytes 786440 | tf_op jit(solution)/shard_map/ppermute | solution.py:345
  57.9 19.8 %collective-permute-start.10 = (bf16[512,256]{1,0:T(8,128)(2,1)S(1)}, bf16[512,256]{1,0:T(8,128)(2,1)S(1)}, u32[]{:S(2)}, u32[]{:S(2)}) collective-permute-start(bf16[512,256]{1,0:T(8,128)(2,1)S(1)} %get-tuple-element.81), channel_id=1, source_target_pairs={{254,0},{255,1},{252,2},{253,3},{2,4},{3,5},{0,6},{1,7},{6,8},{7,9... | collective-permute-start | bytes 786440 | tf_op jit(solution)/shard_map/ppermute | solution.py:345
  78.0 7.6 %collective-permute-start.11 = (bf16[528,256]{1,0:T(8,128)(2,1)S(1)}, bf16[528,256]{1,0:T(8,128)(2,1)S(1)}, u32[]{:S(2)}, u32[]{:S(2)}) collective-permute-start(bf16[528,256]{1,0:T(8,128)(2,1)S(1)} %shard_map.127.refs_0_), channel_id=1, source_target_pairs={{0,2},{1,3},{2,0},{3,1},{4,6},{5,7},{6,4},{7,5},{8,10},{9,11},{10,... | collective-permute-start | bytes 811016 | tf_op jit(solution)/shard_map/ppermute | solution.py:340
  78.8 14.6 %all-to-all-start.1 = ((f32[32,8,256]{2,1,0:T(8,128)}), f32[32,8,256]{2,1,0:T(8,128)S(1)}, u32[]{:S(2)}, u32[]{:S(2)}) async-start(f32[32,8,256]{2,1,0:T(8,128)} %shard_map.129), calls=%async_computation.1 | async-start | bytes 524288 | tf_op jit(solution)/shard_map/all_to_all | solution.py:336
  82.8 4.4 %collective-permute-start.12 = (bf16[528,256]{1,0:T(8,128)(2,1)S(1)}, bf16[528,256]{1,0:T(8,128)(2,1)S(1)}, u32[]{:S(2)}, u32[]{:S(2)}) collective-permute-start(bf16[528,256]{1,0:T(8,128)(2,1)S(1)} %shard_map.127.refs_0_), channel_id=1, source_target_pairs={{0,1},{1,0},{2,3},{3,2},{4,5},{5,4},{6,7},{7,6},{8,9},{9,8},{10,11... | collective-permute-start | bytes 811016 | tf_op jit(solution)/shard_map/ppermute | solution.py:340
  85.6 2.8 %collective-permute-start.13 = (bf16[528,256]{1,0:T(8,128)(2,1)S(1)}, bf16[528,256]{1,0:T(8,128)(2,1)S(1)}, u32[]{:S(2)}, u32[]{:S(2)}) collective-permute-start(bf16[528,256]{1,0:T(8,128)(2,1)S(1)} %collective-permute-done.11.refs_1_), channel_id=1, source_target_pairs={{0,1},{1,0},{2,3},{3,2},{4,5},{5,4},{6,7},{7,6},{8,9},{9,8},{10,11... | collective-permute-start | bytes 811016 | tf_op jit(solution)/shard_map/ppermute | solution.py:340
  93.5 8.1 %collective-permute-start.16 = (bf16[272,256]{1,0:T(8,128)(2,1)S(1)}, bf16[272,256]{1,0:T(8,128)(2,1)S(1)}, u32[]{:S(2)}, u32[]{:S(2)}) collective-permute-start(bf16[272,256]{1,0:T(8,128)(2,1)S(1)} %shard_map.130.refs_0_), channel_id=1, source_target_pairs={{0,6},{1,7},{2,4},{3,5},{4,2},{5,3},{6,0},{7,1},{8,14},{9,15},{10,... | collective-permute-start | bytes 417800 | tf_op jit(solution)/shard_map/ppermute | solution.py:340
  95.4 8.4 %collective-permute-start.15 = (bf16[272,256]{1,0:T(8,128)(2,1)S(1)}, bf16[272,256]{1,0:T(8,128)(2,1)S(1)}, u32[]{:S(2)}, u32[]{:S(2)}) collective-permute-start(bf16[272,256]{1,0:T(8,128)(2,1)S(1)} %shard_map.130.refs_0_), channel_id=1, source_target_pairs={{0,4},{1,5},{2,6},{3,7},{4,0},{5,1},{6,2},{7,3},{8,12},{9,13},{10,... | collective-permute-start | bytes 417800 | tf_op jit(solution)/shard_map/ppermute | solution.py:340
  96.9 9.1 %collective-permute-start.14 = (bf16[272,256]{1,0:T(8,128)(2,1)S(1)}, bf16[272,256]{1,0:T(8,128)(2,1)S(1)}, u32[]{:S(2)}, u32[]{:S(2)}) collective-permute-start(bf16[272,256]{1,0:T(8,128)(2,1)S(1)} %shard_map.130.refs_0_), channel_id=1, source_target_pairs={{0,2},{1,3},{2,0},{3,1},{4,6},{5,7},{6,4},{7,5},{8,10},{9,11},{10,... | collective-permute-start | bytes 417800 | tf_op jit(solution)/shard_map/ppermute | solution.py:340
  96.9 9.7 %collective-permute-start.17 = (bf16[272,256]{1,0:T(8,128)(2,1)S(1)}, bf16[272,256]{1,0:T(8,128)(2,1)S(1)}, u32[]{:S(2)}, u32[]{:S(2)}) collective-permute-start(bf16[272,256]{1,0:T(8,128)(2,1)S(1)} %shard_map.130.refs_0_), channel_id=1, source_target_pairs={{0,1},{1,0},{2,3},{3,2},{4,5},{5,4},{6,7},{7,6},{8,9},{9,8},{10,11... | collective-permute-start | bytes 417800 | tf_op jit(solution)/shard_map/ppermute | solution.py:340
  101.6 4.9 %collective-permute-start.20 = (bf16[272,256]{1,0:T(8,128)(2,1)S(1)}, bf16[272,256]{1,0:T(8,128)(2,1)S(1)}, u32[]{:S(2)}, u32[]{:S(2)}) collective-permute-start(bf16[272,256]{1,0:T(8,128)(2,1)S(1)} %collective-permute-done.16.refs_3_), channel_id=1, source_target_pairs={{0,1},{1,0},{2,3},{3,2},{4,5},{5,4},{6,7},{7,6},{8,9},{9,8},{10,11... | collective-permute-start | bytes 417800 | tf_op jit(solution)/shard_map/ppermute | solution.py:340
  103.8 3.2 %collective-permute-start.19 = (bf16[272,256]{1,0:T(8,128)(2,1)S(1)}, bf16[272,256]{1,0:T(8,128)(2,1)S(1)}, u32[]{:S(2)}, u32[]{:S(2)}) collective-permute-start(bf16[272,256]{1,0:T(8,128)(2,1)S(1)} %collective-permute-done.15.refs_2_), channel_id=1, source_target_pairs={{0,1},{1,0},{2,3},{3,2},{4,5},{5,4},{6,7},{7,6},{8,9},{9,8},{10,11... | collective-permute-start | bytes 417800 | tf_op jit(solution)/shard_map/ppermute | solution.py:340
  106.0 1.5 %collective-permute-start.18 = (bf16[272,256]{1,0:T(8,128)(2,1)S(1)}, bf16[272,256]{1,0:T(8,128)(2,1)S(1)}, u32[]{:S(2)}, u32[]{:S(2)}) collective-permute-start(bf16[272,256]{1,0:T(8,128)(2,1)S(1)} %collective-permute-done.14.refs_1_), channel_id=1, source_target_pairs={{0,1},{1,0},{2,3},{3,2},{4,5},{5,4},{6,7},{7,6},{8,9},{9,8},{10,11... | collective-permute-start | bytes 417800 | tf_op jit(solution)/shard_map/ppermute | solution.py:340
  (8 other events, 107.0 us)

commit v4 on v3

--- a/solution.py
+++ b/solution.py
@@ -20,6 +20,7 @@
 AXES = ("blk", "rep")
 VMEM_LIMIT = 48 * 1024 * 1024
 CHUNK = 256
+UNROLL = 4
 
 
 def vmem():
@@ -98,7 +99,38 @@
         cnt_ref[g] = dot_nt(high, low) * (1.0 / NEG)
         return 0
 
-    lax.fori_loop(0, EDGES // GROUP, group, 0)
+    lax.fori_loop(0, EDGES // GROUP, group, 0, unroll=UNROLL)
+
+
+def against(part, ids_ref, near_ref, far_ref, prod_ref, cnt_ref, cc_ref, rows, g):
+    size = near_ref.shape[0]
+    dst = columns(ids_ref[2:3, rows])
+    low = prod_ref[rows, :].astype(BF16)
+    tails = neg = None
+    for j, table in ((0, near_ref), (1, far_ref)):
+        base = j * (ENT // 2) + part * size
+        tail = dot(one_hot_rows(dst, size, base), table[...])
+        scores = dot_nt(low, table[...])
+        for i in range(size // H):
+            w = cnt_ref[g, base // H + i : base // H + i + 1, :]
+            cc_ref[rows, j * size + i * H : j * size + (i + 1) * H] = (
+                jax.nn.sigmoid(scores[:, i * H : (i + 1) * H]) * w
+            ).astype(BF16)
+        drawn = dot(cc_ref[rows, j * size : (j + 1) * size], table[...])
+        tails = tail if tails is None else tails + tail
+        neg = drawn if neg is None else neg + drawn
+    return tails, neg
+
+
+def first_score_kernel(ids_ref, near_ref, far_ref, prod_ref, cnt_ref, cc_ref, tails_ref, neg_ref):
+    def group(g, _):
+        rows = pl.ds(pl.multiple_of(g * GROUP, GROUP), GROUP)
+        tails, neg = against(0, ids_ref, near_ref, far_ref, prod_ref, cnt_ref, cc_ref, rows, g)
+        tails_ref[rows, :] = tails
+        neg_ref[rows, :] = neg
+        return 0
+
+    lax.fori_loop(0, EDGES // GROUP, group, 0, unroll=UNROLL)
 
 
 def score_kernel(
@@ -110,6 +142,8 @@
     relrow_ref,
     prod_ref,
     cnt_ref,
+    tails_ref,
+    neg_ref,
     keep_ref,
     send_ref,
     cc_ref,
@@ -123,25 +157,14 @@
 
     def group(g, _):
         rows = pl.ds(pl.multiple_of(g * GROUP, GROUP), GROUP)
-        dst = columns(ids_ref[2:3, rows])
-        tails = dot(one_hot_rows(dst, half), near_ref[...]) + dot(
-            one_hot_rows(dst, half, half), far_ref[...]
-        )
+        tails, neg = against(1, ids_ref, near_ref, far_ref, prod_ref, cnt_ref, cc_ref, rows, g)
+        tails = tails + tails_ref[rows, :]
+        neg = neg + neg_ref[rows, :]
         prod = prod_ref[rows, :]
         edge = lax.broadcasted_iota(jnp.int32, (GROUP, 1), 0) + g * GROUP
         live = jnp.where(edge < count, 1.0, 0.0).astype(F32)
         positive = jnp.sum(prod * tails, axis=1, keepdims=True)
         pos = -live * jax.nn.sigmoid(-positive)
-        low = prod.astype(BF16)
-        for j, table in ((0, near_ref), (1, far_ref)):
-            scores = dot_nt(low, table[...])
-            for i in range(half // H):
-                w = cnt_ref[g, pl.ds(j * (half // H) + i, 1), :]
-                part = scores[:, i * H : (i + 1) * H]
-                cc_ref[rows, j * half + i * H : j * half + (i + 1) * H] = (
-                    jax.nn.sigmoid(part) * w
-                ).astype(BF16)
-        neg = dot(cc_ref[rows, :half], near_ref[...]) + dot(cc_ref[rows, half:], far_ref[...])
         grad = pos * tails + live * neg
         rel = relrow_ref[rows, :]
         head = head_ref[rows, :].astype(F32)
@@ -154,7 +177,7 @@
         plt_ref[:, rows] = jnp.transpose(live * prod).astype(BF16)
         return 0
 
-    lax.fori_loop(0, EDGES // GROUP, group, 0)
+    lax.fori_loop(0, EDGES // GROUP, group, 0, unroll=UNROLL)
 
     def scatter(i, _):
         rows = pl.ds(pl.multiple_of(i * CHUNK, CHUNK), CHUNK)
@@ -164,13 +187,14 @@
         ).astype(BF16)
         return 0
 
-    lax.fori_loop(0, half // CHUNK, scatter, 0)
+    lax.fori_loop(0, half // CHUNK, scatter, 0, unroll=UNROLL)
 
 
 def scatter_kernel(
     place_ref,
     ids_ref,
-    cc_ref,
+    first_ref,
+    second_ref,
     plt_ref,
     pd_ref,
     gh_ref,
@@ -180,25 +204,28 @@
     dst_send_ref,
 ):
     half = ENT // 2
+    quarter = half // 2
     xl = place_ref[0]
 
-    def scatter(i, _):
-        rows = pl.ds(pl.multiple_of(i * CHUNK, CHUNK), CHUNK)
-        to = lax.bitwise_xor(i, xl * (half // 2 // CHUNK))
-        out = pl.ds(pl.multiple_of(to * CHUNK, CHUNK), CHUNK)
-        for base, src_ref, dst_ref in (
+    def scatter(i, part, cc_ref):
+        at = part * quarter + i * CHUNK
+        rows = pl.ds(pl.multiple_of(at, CHUNK), CHUNK)
+        to = lax.bitwise_xor(part, xl) * quarter + i * CHUNK
+        out = pl.ds(pl.multiple_of(to, CHUNK), CHUNK)
+        for j, src_ref, dst_ref in (
             (0, src_keep_ref, dst_keep_ref),
-            (half, src_send_ref, dst_send_ref),
+            (1, src_send_ref, dst_send_ref),
         ):
-            src = dot(one_hot_cols(ids_ref[4:5, :], CHUNK, base + i * CHUNK), gh_ref[...])
+            src = dot(one_hot_cols(ids_ref[4:5, :], CHUNK, j * half + at), gh_ref[...])
             src_ref[rows, :] = src.astype(src_ref.dtype)
-            cols = pl.ds(pl.multiple_of(base + i * CHUNK, CHUNK), CHUNK)
+            cols = pl.ds(pl.multiple_of(j * quarter + i * CHUNK, CHUNK), CHUNK)
             drawn = jnp.transpose(dot(plt_ref[...], cc_ref[:, cols]))
-            dst = dot(one_hot_cols(ids_ref[2:3, :], CHUNK, base + i * CHUNK), pd_ref[...])
+            dst = dot(one_hot_cols(ids_ref[2:3, :], CHUNK, j * half + at), pd_ref[...])
             dst_ref[out, :] = (drawn + dst).astype(dst_ref.dtype)
-        return 0
-
-    lax.fori_loop(0, half // CHUNK, scatter, 0)
+
+    for part, ref in ((0, first_ref), (1, second_ref)):
+        for i in range(quarter // CHUNK):
+            scatter(i, part, ref)
 
 
 def add_split_kernel(n_in, n_out, *refs):
@@ -357,8 +384,11 @@
     x = (blk % 2) * 2 + xl
 
     low = entities.astype(BF16)
-    half = lax.dynamic_slice_in_dim(entities, core * (ENT // 2), ENT // 2, 0).astype(BF16)
-    near = shift(half, -1, XL)
+    halves = [
+        lax.dynamic_slice_in_dim(entities, core * 1024 + part * 512, 512, 0).astype(BF16)
+        for part in range(2)
+    ]
+    near = [shift(part, -1, XL) for part in halves]
 
     ids = jnp.concatenate(
         [
@@ -372,6 +402,7 @@
         axis=0,
     )
     negs = (neg_ids ^ (core * 1024)).reshape(4, NEG)
+    near_first, ids = lax.optimization_barrier((near[0], ids))
     head, rel_rows, prod, cnt = call(
         gather_kernel,
         [
@@ -383,30 +414,31 @@
         0,
         4,
         [pltpu.VMEM((NREL, D), BF16)] * 3,
-        flops=4 * 2 * EDGES * ENT * D,
-        bytes_accessed=1 << 22,
     )(ids, negs, low, relations)
 
-    near, head = lax.optimization_barrier((near, head))
-    far = swap(near, CORE)
     kept = jax.ShapeDtypeStruct((ENT // 2, D), F32)
     sent = jax.ShapeDtypeStruct((ENT // 2, D), BF16)
+    slots = jax.ShapeDtypeStruct((EDGES, D), F32)
+    slots_low = jax.ShapeDtypeStruct((EDGES, D), BF16)
+    weights = jax.ShapeDtypeStruct((EDGES, ENT // 2), BF16)
+    far_first = swap(near_first, CORE)
+    cc_first, tails, neg = call(
+        first_score_kernel,
+        [weights, slots, slots],
+        0,
+        5,
+    )(ids, near_first, far_first, prod, cnt)
+    near_second, tails = lax.optimization_barrier((near[1], tails))
+    far_second = swap(near_second, CORE)
     rel_keep, rel_send, cc, plt, pd, gh = call(
         score_kernel,
-        [
-            kept,
-            sent,
-            jax.ShapeDtypeStruct((EDGES, ENT), BF16),
-            jax.ShapeDtypeStruct((D, EDGES), BF16),
-            jax.ShapeDtypeStruct((EDGES, D), BF16),
-            jax.ShapeDtypeStruct((EDGES, D), BF16),
-        ],
+        [kept, sent, weights, jax.ShapeDtypeStruct((D, EDGES), BF16), slots_low, slots_low],
         1,
-        7,
+        9,
         [pltpu.VMEM((EDGES, D), BF16)],
-        flops=4 * 2 * EDGES * ENT * D,
+        flops=5 * EDGES * ENT * D,
         bytes_accessed=1 << 23,
-    )(counts, ids, near, far, head, rel_rows, prod, cnt)
+    )(counts, ids, near_second, far_second, head, rel_rows, prod, cnt, tails, neg)
     rel_recv = swap(rel_send, CORE)
     parts = add_split([rel_keep, rel_recv], 4, own=F32)
     parts, cc = lax.optimization_barrier((parts, cc))
@@ -416,10 +448,10 @@
         scatter_kernel,
         [kept, sent, kept, sent],
         1,
-        5,
+        6,
         flops=3 * 2 * EDGES * ENT * D,
         bytes_accessed=1 << 23,
-    )(xl.reshape(1), ids, cc, plt, pd, gh)
+    )(xl.reshape(1), ids, cc_first, cc, plt, pd, gh)
     recv, src_send, dst_send = lax.optimization_barrier((recv, src_send, dst_send))
     src_recv = swap(src_send, CORE)
     dst_recv = swap(dst_send, CORE)

time: 113 us -> 121 us (1.071)
  starting transfers between devices: 42.3 us -> 50.2 us
  blocking collectives: 19.7 us -> 15.9 us
  local copies, waits for them, and re-layouts: 4.89 us -> 7.78 us
  Pallas kernels: 30.7 us -> 28 us
  waiting for transfers between devices: 11.7 us -> 14.2 us
  other arithmetic: 1.75 us -> 3.14 us
    ppermute x3 -> x4, starting transfers between devices: 13.6 us -> 22.1 us  [shift(): return lax.ppermute(x, AXES, route)]
    all_to_all x1, blocking collectives: 19.7 us -> 15.9 us  [spread(): lax.all_to_all(parts, 'blk', 0, 0, axis_index_groups=groups, tiled=True)]
    unnamed x20, local copies, waits for them, and re-layouts: 2.6 us -> 4.91 us
    pallas_call x2 -> x3, Pallas kernels: 17.5 us -> 15.9 us  [the longest x1 6.79 us: shards(): call(score_kernel, [kept, sent, weights, jax.ShapeDtypeStruct((D, EDGES),...]
    ppermute x3 -> x4, waiting for transfers between devices: 2.01 us -> 3.04 us  [shift(): return lax.ppermute(x, AXES, route)]
    ppermute x18 -> x19, starting transfers between devices: 24.8 us -> 24.1 us  [swap(): return lax.ppermute(x, AXES, [(i, i ^ mask) for i in range(256)])]
    ppermute x18 -> x19, waiting for transfers between devices: 6.79 us -> 7.16 us  [swap(): return lax.ppermute(x, AXES, [(i, i ^ mask) for i in range(256)])]
  transfers between devices with their start and end apart: 22 -> 24, of which waited for: 9 -> 12; matrix products, arithmetic and copies ran while one was open for 2% -> 3% of each run, Pallas kernels for 14% -> 14%
where the time goes in v4:
time: 121 us
  starting transfers between devices  50.2 us (41%)
  Pallas kernels  28 us (23%)
  blocking collectives  15.9 us (13%)
  waiting for transfers between devices  14.2 us (12%)
  local copies, waits for them, and re-layouts  7.78 us (6%)
  other arithmetic  3.14 us (3%)
  between operations  1.51 us (1%)
    ppermute x19, starting transfers between devices, swap(): return lax.ppermute(x, AXES, [(i, i ^ mask) for i in range(256)])  24.1 us
    ppermute x4, starting transfers between devices, shift(): return lax.ppermute(x, AXES, route)  22.1 us
    all_to_all x1, blocking collectives, spread(): lax.all_to_all(parts, 'blk', 0, 0, axis_index_groups=groups, tiled=True)  15.9 us
    ppermute x19, waiting for transfers between devices, swap(): return lax.ppermute(x, AXES, [(i, i ^ mask) for i in range(256)])  7.16 us
    pallas_call x1, Pallas kernels, shards(): call(score_kernel, [kept, sent, weights, jax.ShapeDtypeStruct((D, EDGES),...  6.79 us
    pallas_call x1, Pallas kernels, shards(): call(scatter_kernel, [kept, sent, kept, sent], 1, 6, flops=3 * 2 * EDGES...  5.71 us
    pallas_call x2, Pallas kernels, update(): pl.pallas_call(functools.partial(update_kernel, len(pieces)), grid=(n //...  5.69 us
    unnamed x20, local copies, waits for them, and re-layouts  4.91 us
  transfers between devices with their start and end apart: 24, of which 12 were waited for; matrix products, arithmetic and copies ran while one was open for 3% of the time, Pallas kernels for 14%

profile of v4, /device:TPU:1, one launch (start us, length us, event | category | flops | bytes accessed | tf_op | source)
XLA Modules:
  0.0 120.8 jit_solution(9658737772708036147)
XLA Ops:
  0.7 2.1 %dynamic-slice_convert_fusion = (bf16[512,256]{1,0:T(8,128)(2,1)}, bf16[512,256]{1,0:T(8,128)(2,1)S(1)}) fusion(f32[2048,256]{1,0:T(8,128)} %rows_ref.2, s32[]{:T(128)S(6)} %select_n.25, s32[]{:T(128)S(6)} %select_n.23), kind=kLoop, calls=%fused_computation | loop fusion | bytes 1048584 | tf_op jit(solution)/shard_map/convert_element_type | solution.py:388
  2.8 11.1 %collective-permute-start = (bf16[512,256]{1,0:T(8,128)(2,1)S(1)}, bf16[512,256]{1,0:T(8,128)(2,1)S(1)}, u32[]{:S(2)}, u32[]{:S(2)}) collective-permute-start(bf16[512,256]{1,0:T(8,128)(2,1)S(1)} %get-tuple-element.103), channel_id=1, source_target_pairs={{6,0},{7,1},{4,2},{5,3},{10,4},{11,5},{8,6},{9,7},{14,8},{15,9},{1... | collective-permute-start | bytes 786440 | tf_op jit(solution)/shard_map/ppermute | solution.py:372
  16.0 2.8 %collective-permute-done.near_ref = bf16[512,256]{1,0:T(8,128)(2,1)S(1)} collective-permute-done((bf16[512,256]{1,0:T(8,128)(2,1)S(1)}, bf16[512,256]{1,0:T(8,128)(2,1)S(1)}, u32[]{:S(2)}, u32[]{:S(2)}) %collective-permute-start) | collective-permute-done | bytes 262176 | tf_op jit(solution)/shard_map/ppermute | solution.py:372
  18.8 1.5 %collective-permute-start.1 = (bf16[512,256]{1,0:T(8,128)(2,1)S(1)}, bf16[512,256]{1,0:T(8,128)(2,1)}, u32[]{:S(2)}, u32[]{:S(2)}) collective-permute-start(bf16[512,256]{1,0:T(8,128)(2,1)S(1)} %collective-permute-done.near_ref), channel_id=1, source_target_pairs={{0,1},{1,0},{2,3},{3,2},{4,5},{5,4},{6,7},{7,6},{8,9},{9,8},{10,11... | collective-permute-start | bytes 786440 | tf_op jit(solution)/shard_map/ppermute | solution.py:367
  20.4 7.6 %collective-permute-start.2 = (bf16[512,256]{1,0:T(8,128)(2,1)}, bf16[512,256]{1,0:T(8,128)(2,1)}, u32[]{:S(2)}, u32[]{:S(2)}) collective-permute-start(bf16[512,256]{1,0:T(8,128)(2,1)} %get-tuple-element.102), channel_id=1, source_target_pairs={{6,0},{7,1},{4,2},{5,3},{10,4},{11,5},{8,6},{9,7},{14,8},{15,9},{1... | collective-permute-start | bytes 786440 | tf_op jit(solution)/shard_map/ppermute | solution.py:372
  28.0 1.7 %convert_element_type.10.low_ref = bf16[2048,256]{1,0:T(8,128)(2,1)S(1)} convert(f32[2048,256]{1,0:T(8,128)} %rows_ref.2) | non-fusion elementwise | flops 524288 | bytes 3145728 | tf_op jit(solution)/shard_map/convert_element_type | solution.py:386
  29.8 4.9 %shard_map.120 = (bf16[1024,256]{1,0:T(8,128)(2,1)S(1)}, f32[1024,256]{1,0:T(8,128)S(1)}, f32[1024,256]{1,0:T(8,128)S(1)}, f32[4,16,128]{2,1,0:T(8,128)S(1)}) custom-call(s32[8,1024]{1,0:T(8,128)S(1)} %concatenate.3.ids_ref, s32[4,1024]{1,0:T(4,128)S(1)} %reshape.41.negs_ref, bf16[2048,256]{1,0:T(8,128)(2,1)S(1)} %convert_element_type.10.low_ref, ...), custom_call_target="tpu_custom_call" | custom-call | tf_op jit(solution)/shard_map/pallas_call | solution.py:406
  34.7 3.4 %shard_map.121 = (bf16[1024,1024]{1,0:T(8,128)(2,1)S(1)}, f32[1024,256]{1,0:T(8,128)S(1)}, f32[1024,256]{1,0:T(8,128)S(1)}) custom-call(s32[8,1024]{1,0:T(8,128)S(1)} %concatenate.3.ids_ref, bf16[512,256]{1,0:T(8,128)(2,1)S(1)} %collective-permute-done.near_ref, bf16[512,256]{1,0:T(8,128)(2,1)} %collective-permute-done.1.far_ref, ...), custom_call_target="tpu_custom_call" | custom-call | tf_op jit(solution)/shard_map/pallas_call | solution.py:425
  43.2 6.8 %shard_map.122 = (f32[1024,256]{1,0:T(8,128)S(1)}, bf16[1024,256]{1,0:T(8,128)(2,1)S(1)}, bf16[1024,1024]{1,0:T(8,128)(2,1)}, bf16[256,1024]{1,0:T(8,128)(2,1)S(...) custom-call(s32[1,1]{1,0:T(1,128)S(6)} %copy.13.count_ref, s32[8,1024]{1,0:T(8,128)S(1)} %concatenate.3.ids_ref, ...), custom_call_target="tpu_custom_call" | custom-call | flops 2684354560 | bytes 8388608 | tf_op jit(solution)/shard_map/pallas_call | solution.py:433
  50.2 1.6 %collective-permute-done.4.refs_1_ = bf16[1024,256]{1,0:T(8,128)(2,1)S(1)} collective-permute-done((bf16[1024,256]{1,0:T(8,128)(2,1)S(1)}, bf16[1024,256]{1,0:T(8,128)(2,1)S(1)}, u32[]{:S(2)}, u32[]{:S(2)}) %collective-permute-start.4) | collective-permute-done | bytes 524320 | tf_op jit(solution)/shard_map/ppermute | solution.py:367
  52.2 3.7 %collective-permute-start.7 = (bf16[256,256]{1,0:T(8,128)(2,1)S(1)}, bf16[256,256]{1,0:T(8,128)(2,1)S(1)}, u32[]{:S(2)}, u32[]{:S(2)}) collective-permute-start(bf16[256,256]{1,0:T(8,128)(2,1)S(1)} %get-tuple-element.78), channel_id=1, source_target_pairs={{0,6},{1,7},{2,4},{3,5},{4,2},{5,3},{6,0},{7,1},{8,14},{9,15},{10,... | collective-permute-start | bytes 393224 | tf_op jit(solution)/shard_map/ppermute | solution.py:367
  55.9 5.7 %shard_map.124 = (f32[1024,256]{1,0:T(8,128)S(1)}, bf16[1024,256]{1,0:T(8,128)(2,1)S(1)}, f32[1024,256]{1,0:T(8,128)S(1)}, bf16[1024,256]{1,0:T(8,128)(2,1)S(1)}) custom-call(s32[1]{0:T(128)} %bitcast.2.place_ref, s32[8,1024]{1,0:T(8,128)S(1)} %concatenate.3.ids_ref, bf16[1024,1024]{1,0:T(8,128)(2,1)} %copy-done.6, ...), custom_call_target="tpu_custom_call" | custom-call | flops 3221225472 | bytes 8388608 | tf_op jit(solution)/shard_map/pallas_call | solution.py:447
  65.3 3.4 %collective-permute-start.11 = (bf16[512,256]{1,0:T(8,128)(2,1)S(1)}, bf16[512,256]{1,0:T(8,128)(2,1)S(1)}, u32[]{:S(2)}, u32[]{:S(2)}) collective-permute-start(bf16[512,256]{1,0:T(8,128)(2,1)S(1)} %get-tuple-element.90), channel_id=1, source_target_pairs={{252,0},{253,1},{254,2},{255,3},{0,4},{1,5},{2,6},{3,7},{4,8},{5,9... | collective-permute-start | bytes 786440 | tf_op jit(solution)/shard_map/ppermute | solution.py:372
  68.8 15.9 %all_to_all.10.parts_ref = bf16[32,8,256]{2,1,0:T(8,128)(2,1)S(1)} all-to-all(bf16[32,8,256]{2,1,0:T(8,128)(2,1)S(1)} %bitcast.10), channel_id=1, replica_groups={{0,8,16,24,32,40,48,56,64,72,80,88,96,104,112,120,128,136,144,152,160,1..., dimensions={0} | all-to-all | bytes 262144 | tf_op jit(solution)/shard_map/all_to_all | solution.py:363
  87.4 4.0 %all-to-all-start.1 = ((f32[32,8,256]{2,1,0:T(8,128)}), f32[32,8,256]{2,1,0:T(8,128)S(1)}, u32[]{:S(2)}, u32[]{:S(2)}) async-start(f32[32,8,256]{2,1,0:T(8,128)} %shard_map.130), calls=%async_computation.1 | async-start | bytes 524288 | tf_op jit(solution)/shard_map/all_to_all | solution.py:363
  91.4 2.2 %collective-permute-start.14 = (bf16[528,256]{1,0:T(8,128)(2,1)S(1)}, bf16[528,256]{1,0:T(8,128)(2,1)S(1)}, u32[]{:S(2)}, u32[]{:S(2)}) collective-permute-start(bf16[528,256]{1,0:T(8,128)(2,1)S(1)} %shard_map.128.refs_0_), channel_id=1, source_target_pairs={{0,1},{1,0},{2,3},{3,2},{4,5},{5,4},{6,7},{7,6},{8,9},{9,8},{10,11... | collective-permute-start | bytes 811016 | tf_op jit(solution)/shard_map/ppermute | solution.py:367
  95.9 2.1 %shard_map.129 = (f32[2048,256]{1,0:T(8,128)}, f32[16,128]{1,0:T(8,128)}) custom-call(s32[1]{0:T(128)} %bitcast.place_ref, f32[2048,256]{1,0:T(8,128)S(1)} %copy-done, f32[16,128]{1,0:T(8,128)S(1)} %bitcast.11, bf16[528,256]{1,0:T(8,128)(2,1)S(1)} %shard_map.128.refs_0_, bf16[528,256]{1,0:T(8,128)(2,1)S(1)} %collective-permute-done.13.refs_1_, ...), custom_call_target="tpu_custom_call" | custom-call | flops 4194304 | bytes 5242880 | tf_op jit(solution)/shard_map/pallas_call | solution.py:320
  98.0 4.0 %all-to-all-done.1 = f32[32,8,256]{2,1,0:T(8,128)S(1)} async-done(((f32[32,8,256]{2,1,0:T(8,128)}), f32[32,8,256]{2,1,0:T(8,128)S(1)}, u32[]{:S(2)}, u32[]{:S(2)}) %all-to-all-start.1) | async-done | bytes 262176 | tf_op jit(solution)/shard_map/all_to_all | solution.py:363
  102.1 1.6 %collective-permute-start.18 = (bf16[272,256]{1,0:T(8,128)(2,1)S(1)}, bf16[272,256]{1,0:T(8,128)(2,1)S(1)}, u32[]{:S(2)}, u32[]{:S(2)}) collective-permute-start(bf16[272,256]{1,0:T(8,128)(2,1)S(1)} %shard_map.131.refs_0_), channel_id=1, source_target_pairs={{0,6},{1,7},{2,4},{3,5},{4,2},{5,3},{6,0},{7,1},{8,14},{9,15},{10,... | collective-permute-start | bytes 417800 | tf_op jit(solution)/shard_map/ppermute | solution.py:367
  105.4 4.4 %collective-permute-start.19 = (bf16[272,256]{1,0:T(8,128)(2,1)S(1)}, bf16[272,256]{1,0:T(8,128)(2,1)S(1)}, u32[]{:S(2)}, u32[]{:S(2)}) collective-permute-start(bf16[272,256]{1,0:T(8,128)(2,1)S(1)} %shard_map.131.refs_0_), channel_id=1, source_target_pairs={{0,1},{1,0},{2,3},{3,2},{4,5},{5,4},{6,7},{7,6},{8,9},{9,8},{10,11... | collective-permute-start | bytes 417800 | tf_op jit(solution)/shard_map/ppermute | solution.py:367
  109.8 2.2 %collective-permute-start.22 = (bf16[272,256]{1,0:T(8,128)(2,1)S(1)}, bf16[272,256]{1,0:T(8,128)(2,1)S(1)}, u32[]{:S(2)}, u32[]{:S(2)}) collective-permute-start(bf16[272,256]{1,0:T(8,128)(2,1)S(1)} %collective-permute-done.18.refs_3_), channel_id=1, source_target_pairs={{0,1},{1,0},{2,3},{3,2},{4,5},{5,4},{6,7},{7,6},{8,9},{9,8},{10,11... | collective-permute-start | bytes 417800 | tf_op jit(solution)/shard_map/ppermute | solution.py:367
  112.0 2.3 %collective-permute-start.21 = (bf16[272,256]{1,0:T(8,128)(2,1)S(1)}, bf16[272,256]{1,0:T(8,128)(2,1)S(1)}, u32[]{:S(2)}, u32[]{:S(2)}) collective-permute-start(bf16[272,256]{1,0:T(8,128)(2,1)S(1)} %collective-permute-done.17.refs_2_), channel_id=1, source_target_pairs={{0,1},{1,0},{2,3},{3,2},{4,5},{5,4},{6,7},{7,6},{8,9},{9,8},{10,11... | collective-permute-start | bytes 417800 | tf_op jit(solution)/shard_map/ppermute | solution.py:367
  115.6 1.6 %copy-done.2 = f32[2048,256]{1,0:T(8,128)S(1)} copy-done((f32[2048,256]{1,0:T(8,128)S(1)}, f32[2048,256]{1,0:T(8,128)}, u32[]{:S(2)}) %copy-start.2) | copy-done | bytes 2097176
  117.2 3.6 %shard_map.132 = (f32[2048,256]{1,0:T(8,128)}, f32[16,128]{1,0:T(8,128)}) custom-call(s32[1]{0:T(128)} %bitcast.5.place_ref, f32[2048,256]{1,0:T(8,128)S(1)} %copy-done.2, f32[16,128]{1,0:T(8,128)S(1)} %bitcast.12, bf16[272,256]{1,0:T(8,128)(2,1)S(1)} %shard_map.131.refs_0_, bf16[272,256]{1,0:T(8,128)(2,1)S(1)} %collective-permute-done.16.refs_1_, ...), custom_call_target="tpu_custom_call" | custom-call | flops 4194304 | bytes 5242880 | tf_op jit(solution)/shard_map/pallas_call | solution.py:320
  (66 shorter events, 19.0 us)
Async XLA Ops:
  2.8 16.0 %collective-permute-start = (bf16[512,256]{1,0:T(8,128)(2,1)S(1)}, bf16[512,256]{1,0:T(8,128)(2,1)S(1)}, u32[]{:S(2)}, u32[]{:S(2)}) collective-permute-start(bf16[512,256]{1,0:T(8,128)(2,1)S(1)} %get-tuple-element.103), channel_id=1, source_target_pairs={{6,0},{7,1},{4,2},{5,3},{10,4},{11,5},{8,6},{9,7},{14,8},{15,9},{1... | collective-permute-start | bytes 786440 | tf_op jit(solution)/shard_map/ppermute | solution.py:372
  18.8 15.9 %collective-permute-start.1 = (bf16[512,256]{1,0:T(8,128)(2,1)S(1)}, bf16[512,256]{1,0:T(8,128)(2,1)}, u32[]{:S(2)}, u32[]{:S(2)}) collective-permute-start(bf16[512,256]{1,0:T(8,128)(2,1)S(1)} %collective-permute-done.near_ref), channel_id=1, source_target_pairs={{0,1},{1,0},{2,3},{3,2},{4,5},{5,4},{6,7},{7,6},{8,9},{9,8},{10,11... | collective-permute-start | bytes 786440 | tf_op jit(solution)/shard_map/ppermute | solution.py:367
  20.4 21.1 %collective-permute-start.2 = (bf16[512,256]{1,0:T(8,128)(2,1)}, bf16[512,256]{1,0:T(8,128)(2,1)}, u32[]{:S(2)}, u32[]{:S(2)}) collective-permute-start(bf16[512,256]{1,0:T(8,128)(2,1)} %get-tuple-element.102), channel_id=1, source_target_pairs={{6,0},{7,1},{4,2},{5,3},{10,4},{11,5},{8,6},{9,7},{14,8},{15,9},{1... | collective-permute-start | bytes 786440 | tf_op jit(solution)/shard_map/ppermute | solution.py:372
  41.4 1.7 %collective-permute-start.3 = (bf16[512,256]{1,0:T(8,128)(2,1)}, bf16[512,256]{1,0:T(8,128)(2,1)S(1)}, u32[]{:S(2)}, u32[]{:S(2)}) collective-permute-start(bf16[512,256]{1,0:T(8,128)(2,1)} %collective-permute-done.2.near_ref), channel_id=1, source_target_pairs={{0,1},{1,0},{2,3},{3,2},{4,5},{5,4},{6,7},{7,6},{8,9},{9,8},{10,11... | collective-permute-start | bytes 786440 | tf_op jit(solution)/shard_map/ppermute | solution.py:367
  50.0 1.9 %collective-permute-start.4 = (bf16[1024,256]{1,0:T(8,128)(2,1)S(1)}, bf16[1024,256]{1,0:T(8,128)(2,1)S(1)}, u32[]{:S(2)}, u32[]{:S(2)}) collective-permute-start(bf16[1024,256]{1,0:T(8,128)(2,1)S(1)} %get-tuple-element.65), channel_id=1, source_target_pairs={{0,1},{1,0},{2,3},{3,2},{4,5},{5,4},{6,7},{7,6},{8,9},{9,8},{10,11... | collective-permute-start | bytes 1572872 | tf_op jit(solution)/shard_map/ppermute | solution.py:367
  52.0 9.7 %collective-permute-start.5 = (bf16[256,256]{1,0:T(8,128)(2,1)S(1)}, bf16[256,256]{1,0:T(8,128)(2,1)S(1)}, u32[]{:S(2)}, u32[]{:S(2)}) collective-permute-start(bf16[256,256]{1,0:T(8,128)(2,1)S(1)} %get-tuple-element.76), channel_id=1, source_target_pairs={{0,2},{1,3},{2,0},{3,1},{4,6},{5,7},{6,4},{7,5},{8,10},{9,11},{10,... | collective-permute-start | bytes 393224 | tf_op jit(solution)/shard_map/ppermute | solution.py:367
  52.1 9.6 %collective-permute-start.6 = (bf16[256,256]{1,0:T(8,128)(2,1)S(1)}, bf16[256,256]{1,0:T(8,128)(2,1)S(1)}, u32[]{:S(2)}, u32[]{:S(2)}) collective-permute-start(bf16[256,256]{1,0:T(8,128)(2,1)S(1)} %get-tuple-element.77), channel_id=1, source_target_pairs={{0,4},{1,5},{2,6},{3,7},{4,0},{5,1},{6,2},{7,3},{8,12},{9,13},{10,... | collective-permute-start | bytes 393224 | tf_op jit(solution)/shard_map/ppermute | solution.py:367
  52.2 9.7 %collective-permute-start.7 = (bf16[256,256]{1,0:T(8,128)(2,1)S(1)}, bf16[256,256]{1,0:T(8,128)(2,1)S(1)}, u32[]{:S(2)}, u32[]{:S(2)}) collective-permute-start(bf16[256,256]{1,0:T(8,128)(2,1)S(1)} %get-tuple-element.78), channel_id=1, source_target_pairs={{0,6},{1,7},{2,4},{3,5},{4,2},{5,3},{6,0},{7,1},{8,14},{9,15},{10,... | collective-permute-start | bytes 393224 | tf_op jit(solution)/shard_map/ppermute | solution.py:367
  61.9 2.5 %collective-permute-start.8 = (bf16[1024,256]{1,0:T(8,128)(2,1)S(1)}, bf16[1024,256]{1,0:T(8,128)(2,1)S(1)}, u32[]{:S(2)}, u32[]{:S(2)}) collective-permute-start(bf16[1024,256]{1,0:T(8,128)(2,1)S(1)} %get-tuple-element.81), channel_id=1, source_target_pairs={{0,1},{1,0},{2,3},{3,2},{4,5},{5,4},{6,7},{7,6},{8,9},{9,8},{10,11... | collective-permute-start | bytes 1572872 | tf_op jit(solution)/shard_map/ppermute | solution.py:367
  62.9 2.3 %collective-permute-start.10 = (bf16[1024,256]{1,0:T(8,128)(2,1)S(1)}, bf16[1024,256]{1,0:T(8,128)(2,1)S(1)}, u32[]{:S(2)}, u32[]{:S(2)}) collective-permute-start(bf16[1024,256]{1,0:T(8,128)(2,1)S(1)} %get-tuple-element.89), channel_id=1, source_target_pairs={{0,1},{1,0},{2,3},{3,2},{4,5},{5,4},{6,7},{7,6},{8,9},{9,8},{10,11... | collective-permute-start | bytes 1572872 | tf_op jit(solution)/shard_map/ppermute | solution.py:367
  64.5 20.2 %collective-permute-start.9 = (bf16[512,256]{1,0:T(8,128)(2,1)S(1)}, bf16[512,256]{1,0:T(8,128)(2,1)S(1)}, u32[]{:S(2)}, u32[]{:S(2)}) collective-permute-start(bf16[512,256]{1,0:T(8,128)(2,1)S(1)} %get-tuple-element.87), channel_id=1, source_target_pairs={{0,2},{1,3},{2,0},{3,1},{4,6},{5,7},{6,4},{7,5},{8,10},{9,11},{10,... | collective-permute-start | bytes 786440 | tf_op jit(solution)/shard_map/ppermute | solution.py:367
  65.3 19.4 %collective-permute-start.11 = (bf16[512,256]{1,0:T(8,128)(2,1)S(1)}, bf16[512,256]{1,0:T(8,128)(2,1)S(1)}, u32[]{:S(2)}, u32[]{:S(2)}) collective-permute-start(bf16[512,256]{1,0:T(8,128)(2,1)S(1)} %get-tuple-element.90), channel_id=1, source_target_pairs={{252,0},{253,1},{254,2},{255,3},{0,4},{1,5},{2,6},{3,7},{4,8},{5,9... | collective-permute-start | bytes 786440 | tf_op jit(solution)/shard_map/ppermute | solution.py:372
  68.7 16.2 %collective-permute-start.12 = (bf16[512,256]{1,0:T(8,128)(2,1)S(1)}, bf16[512,256]{1,0:T(8,128)(2,1)S(1)}, u32[]{:S(2)}, u32[]{:S(2)}) collective-permute-start(bf16[512,256]{1,0:T(8,128)(2,1)S(1)} %get-tuple-element.91), channel_id=1, source_target_pairs={{254,0},{255,1},{252,2},{253,3},{2,4},{3,5},{0,6},{1,7},{6,8},{7,9... | collective-permute-start | bytes 786440 | tf_op jit(solution)/shard_map/ppermute | solution.py:372
  85.2 8.4 %collective-permute-start.13 = (bf16[528,256]{1,0:T(8,128)(2,1)S(1)}, bf16[528,256]{1,0:T(8,128)(2,1)S(1)}, u32[]{:S(2)}, u32[]{:S(2)}) collective-permute-start(bf16[528,256]{1,0:T(8,128)(2,1)S(1)} %shard_map.128.refs_0_), channel_id=1, source_target_pairs={{0,2},{1,3},{2,0},{3,1},{4,6},{5,7},{6,4},{7,5},{8,10},{9,11},{10,... | collective-permute-start | bytes 811016 | tf_op jit(solution)/shard_map/ppermute | solution.py:367
  87.4 14.6 %all-to-all-start.1 = ((f32[32,8,256]{2,1,0:T(8,128)}), f32[32,8,256]{2,1,0:T(8,128)S(1)}, u32[]{:S(2)}, u32[]{:S(2)}) async-start(f32[32,8,256]{2,1,0:T(8,128)} %shard_map.130), calls=%async_computation.1 | async-start | bytes 524288 | tf_op jit(solution)/shard_map/all_to_all | solution.py:363
  91.4 3.4 %collective-permute-start.14 = (bf16[528,256]{1,0:T(8,128)(2,1)S(1)}, bf16[528,256]{1,0:T(8,128)(2,1)S(1)}, u32[]{:S(2)}, u32[]{:S(2)}) collective-permute-start(bf16[528,256]{1,0:T(8,128)(2,1)S(1)} %shard_map.128.refs_0_), channel_id=1, source_target_pairs={{0,1},{1,0},{2,3},{3,2},{4,5},{5,4},{6,7},{7,6},{8,9},{9,8},{10,11... | collective-permute-start | bytes 811016 | tf_op jit(solution)/shard_map/ppermute | solution.py:367
  93.6 2.3 %collective-permute-start.15 = (bf16[528,256]{1,0:T(8,128)(2,1)S(1)}, bf16[528,256]{1,0:T(8,128)(2,1)S(1)}, u32[]{:S(2)}, u32[]{:S(2)}) collective-permute-start(bf16[528,256]{1,0:T(8,128)(2,1)S(1)} %collective-permute-done.13.refs_1_), channel_id=1, source_target_pairs={{0,1},{1,0},{2,3},{3,2},{4,5},{5,4},{6,7},{7,6},{8,9},{9,8},{10,11... | collective-permute-start | bytes 811016 | tf_op jit(solution)/shard_map/ppermute | solution.py:367
  102.1 7.7 %collective-permute-start.18 = (bf16[272,256]{1,0:T(8,128)(2,1)S(1)}, bf16[272,256]{1,0:T(8,128)(2,1)S(1)}, u32[]{:S(2)}, u32[]{:S(2)}) collective-permute-start(bf16[272,256]{1,0:T(8,128)(2,1)S(1)} %shard_map.131.refs_0_), channel_id=1, source_target_pairs={{0,6},{1,7},{2,4},{3,5},{4,2},{5,3},{6,0},{7,1},{8,14},{9,15},{10,... | collective-permute-start | bytes 417800 | tf_op jit(solution)/shard_map/ppermute | solution.py:367
  103.7 8.3 %collective-permute-start.17 = (bf16[272,256]{1,0:T(8,128)(2,1)S(1)}, bf16[272,256]{1,0:T(8,128)(2,1)S(1)}, u32[]{:S(2)}, u32[]{:S(2)}) collective-permute-start(bf16[272,256]{1,0:T(8,128)(2,1)S(1)} %shard_map.131.refs_0_), channel_id=1, source_target_pairs={{0,4},{1,5},{2,6},{3,7},{4,0},{5,1},{6,2},{7,3},{8,12},{9,13},{10,... | collective-permute-start | bytes 417800 | tf_op jit(solution)/shard_map/ppermute | solution.py:367
  104.1 10.2 %collective-permute-start.16 = (bf16[272,256]{1,0:T(8,128)(2,1)S(1)}, bf16[272,256]{1,0:T(8,128)(2,1)S(1)}, u32[]{:S(2)}, u32[]{:S(2)}) collective-permute-start(bf16[272,256]{1,0:T(8,128)(2,1)S(1)} %shard_map.131.refs_0_), channel_id=1, source_target_pairs={{0,2},{1,3},{2,0},{3,1},{4,6},{5,7},{6,4},{7,5},{8,10},{9,11},{10,... | collective-permute-start | bytes 417800 | tf_op jit(solution)/shard_map/ppermute | solution.py:367
  105.4 8.9 %collective-permute-start.19 = (bf16[272,256]{1,0:T(8,128)(2,1)S(1)}, bf16[272,256]{1,0:T(8,128)(2,1)S(1)}, u32[]{:S(2)}, u32[]{:S(2)}) collective-permute-start(bf16[272,256]{1,0:T(8,128)(2,1)S(1)} %shard_map.131.refs_0_), channel_id=1, source_target_pairs={{0,1},{1,0},{2,3},{3,2},{4,5},{5,4},{6,7},{7,6},{8,9},{9,8},{10,11... | collective-permute-start | bytes 417800 | tf_op jit(solution)/shard_map/ppermute | solution.py:367
  109.8 4.5 %collective-permute-start.22 = (bf16[272,256]{1,0:T(8,128)(2,1)S(1)}, bf16[272,256]{1,0:T(8,128)(2,1)S(1)}, u32[]{:S(2)}, u32[]{:S(2)}) collective-permute-start(bf16[272,256]{1,0:T(8,128)(2,1)S(1)} %collective-permute-done.18.refs_3_), channel_id=1, source_target_pairs={{0,1},{1,0},{2,3},{3,2},{4,5},{5,4},{6,7},{7,6},{8,9},{9,8},{10,11... | collective-permute-start | bytes 417800 | tf_op jit(solution)/shard_map/ppermute | solution.py:367
  112.0 3.3 %collective-permute-start.21 = (bf16[272,256]{1,0:T(8,128)(2,1)S(1)}, bf16[272,256]{1,0:T(8,128)(2,1)S(1)}, u32[]{:S(2)}, u32[]{:S(2)}) collective-permute-start(bf16[272,256]{1,0:T(8,128)(2,1)S(1)} %collective-permute-done.17.refs_2_), channel_id=1, source_target_pairs={{0,1},{1,0},{2,3},{3,2},{4,5},{5,4},{6,7},{7,6},{8,9},{9,8},{10,11... | collective-permute-start | bytes 417800 | tf_op jit(solution)/shard_map/ppermute | solution.py:367
  114.3 1.4 %collective-permute-start.20 = (bf16[272,256]{1,0:T(8,128)(2,1)S(1)}, bf16[272,256]{1,0:T(8,128)(2,1)S(1)}, u32[]{:S(2)}, u32[]{:S(2)}) collective-permute-start(bf16[272,256]{1,0:T(8,128)(2,1)S(1)} %collective-permute-done.16.refs_1_), channel_id=1, source_target_pairs={{0,1},{1,0},{2,3},{3,2},{4,5},{5,4},{6,7},{7,6},{8,9},{9,8},{10,11... | collective-permute-start | bytes 417800 | tf_op jit(solution)/shard_map/ppermute | solution.py:367
  (10 other events, 161.0 us)

commit v5 on v4

--- a/solution.py
+++ b/solution.py
@@ -191,7 +191,6 @@
 
 
 def scatter_kernel(
-    place_ref,
     ids_ref,
     first_ref,
     second_ref,
@@ -205,23 +204,20 @@
 ):
     half = ENT // 2
     quarter = half // 2
-    xl = place_ref[0]
 
     def scatter(i, part, cc_ref):
         at = part * quarter + i * CHUNK
-        rows = pl.ds(pl.multiple_of(at, CHUNK), CHUNK)
-        to = lax.bitwise_xor(part, xl) * quarter + i * CHUNK
-        out = pl.ds(pl.multiple_of(to, CHUNK), CHUNK)
+        rows = pl.ds(at, CHUNK)
         for j, src_ref, dst_ref in (
             (0, src_keep_ref, dst_keep_ref),
             (1, src_send_ref, dst_send_ref),
         ):
             src = dot(one_hot_cols(ids_ref[4:5, :], CHUNK, j * half + at), gh_ref[...])
             src_ref[rows, :] = src.astype(src_ref.dtype)
-            cols = pl.ds(pl.multiple_of(j * quarter + i * CHUNK, CHUNK), CHUNK)
+            cols = pl.ds(j * quarter + i * CHUNK, CHUNK)
             drawn = jnp.transpose(dot(plt_ref[...], cc_ref[:, cols]))
             dst = dot(one_hot_cols(ids_ref[2:3, :], CHUNK, j * half + at), pd_ref[...])
-            dst_ref[out, :] = (drawn + dst).astype(dst_ref.dtype)
+            dst_ref[rows, :] = (drawn + dst).astype(dst_ref.dtype)
 
     for part, ref in ((0, first_ref), (1, second_ref)):
         for i in range(quarter // CHUNK):
@@ -294,46 +290,40 @@
     return tile[row : row + 1, :H] + tile[row : row + 1, H:] + tile[8 + row : 9 + row, :H]
 
 
-def update_kernel(n_pieces, place_ref, rows_ref, acc_ref, *refs):
-    pieces, new_ref, new_acc_ref = refs[:n_pieces], refs[n_pieces], refs[n_pieces + 1]
-    size = rows_ref.shape[0]
-    i = pl.program_id(0)
-    want = lax.bitwise_xor(i, place_ref[0])
+def update_kernel(n, place_ref, rows_ref, acc_ref, *refs):
+    pieces, (new_ref, new_acc_ref, buf_ref, sem_ref) = refs[:n], refs[n:]
+    size = rows_ref.shape[0] // n
+    copies = []
     for k, piece in enumerate(pieces):
-
-        @pl.when(want == k)
-        def _(piece=piece):
-            for r in range(0, size, H):
-                g = piece[r : r + H, :].astype(F32)
-                at = pl.ds(i * (size // H) + r // H, 1)
-                acc = acc_ref[at, :] + means_of(piece, size, r // H)
-                new_acc_ref[at, :] = acc
-                scale = jnp.transpose(jnp.broadcast_to(RATE / jnp.sqrt(acc), (H, H)))
-                new_ref[r : r + H, :H] = rows_ref[r : r + H, :H] - g[:, :H] * scale
-                new_ref[r : r + H, H:] = rows_ref[r : r + H, H:] - g[:, H:] * scale
+        i = lax.bitwise_xor(k, place_ref[0])
+        for r in range(0, size, H):
+            g = piece[r : r + H, :].astype(F32)
+            at = pl.ds(i * (size // H) + r // H, 1)
+            acc = acc_ref[at, :] + means_of(piece, size, r // H)
+            new_acc_ref[at, :] = acc
+            scale = jnp.transpose(jnp.broadcast_to(RATE / jnp.sqrt(acc), (H, H)))
+            rows = pl.ds(pl.multiple_of(i * size + r, H), H)
+            buf_ref[rows, :H] = rows_ref[rows, :H] - g[:, :H] * scale
+            buf_ref[rows, H:] = rows_ref[rows, H:] - g[:, H:] * scale
+        rows = pl.ds(pl.multiple_of(i * size, size), size)
+        copy = pltpu.make_async_copy(buf_ref.at[rows, :], new_ref.at[rows, :], sem_ref.at[k])
+        copy.start()
+        copies.append(copy)
+    for copy in copies:
+        copy.wait()
 
 
 def update(rows, acc, pieces, place):
     n = rows.shape[0]
-    size = n // len(pieces)
-    whole = lambda i: (0, 0)
     new, new_acc = pl.pallas_call(
         functools.partial(update_kernel, len(pieces)),
-        grid=(n // size,),
         out_shape=[
             jax.ShapeDtypeStruct((n, D), F32),
             jax.ShapeDtypeStruct((n // H, H), F32),
         ],
-        in_specs=[
-            smem(),
-            pl.BlockSpec((size, D), lambda i: (i, 0)),
-            pl.BlockSpec((n // H, H), whole),
-        ]
-        + [pl.BlockSpec(piece.shape, whole) for piece in pieces],
-        out_specs=[
-            pl.BlockSpec((size, D), lambda i: (i, 0)),
-            pl.BlockSpec((n // H, H), whole),
-        ],
+        in_specs=[smem()] + [vmem()] * (2 + len(pieces)),
+        out_specs=[pl.BlockSpec(memory_space=pl.ANY), vmem()],
+        scratch_shapes=[pltpu.VMEM((n, D), F32), pltpu.SemaphoreType.DMA((len(pieces),))],
         cost_estimate=pl.CostEstimate(flops=8 * n * D, bytes_accessed=10 * n * D, transcendentals=n),
         compiler_params=pltpu.CompilerParams(vmem_limit_bytes=VMEM_LIMIT),
     )(place, rows, acc.reshape(n // H, H), *pieces)
@@ -384,25 +374,21 @@
     x = (blk % 2) * 2 + xl
 
     low = entities.astype(BF16)
-    halves = [
-        lax.dynamic_slice_in_dim(entities, core * 1024 + part * 512, 512, 0).astype(BF16)
-        for part in range(2)
-    ]
-    near = [shift(part, -1, XL) for part in halves]
+    quarter = lax.dynamic_slice_in_dim(entities, core * 1024 + (1 - xl) * 512, 512, 0)
+    near_first = shift(quarter.astype(BF16), -1, XL)
 
     ids = jnp.concatenate(
         [
             src_ids,
             rel_ids,
-            dst_ids ^ (core * 1024),
+            dst_ids ^ (core * 1024 + xl * 512),
             rel_ids ^ (core * 1024 + x * 256),
             src_ids ^ (core * 1024 + xl * 512),
             jnp.zeros((3, EDGES), jnp.int32),
         ],
         axis=0,
     )
-    negs = (neg_ids ^ (core * 1024)).reshape(4, NEG)
-    near_first, ids = lax.optimization_barrier((near[0], ids))
+    negs = (neg_ids ^ (core * 1024 + xl * 512)).reshape(4, NEG)
     head, rel_rows, prod, cnt = call(
         gather_kernel,
         [
@@ -414,6 +400,8 @@
         0,
         4,
         [pltpu.VMEM((NREL, D), BF16)] * 3,
+        flops=4 * 2 * EDGES * ENT * D,
+        bytes_accessed=1 << 22,
     )(ids, negs, low, relations)
 
     kept = jax.ShapeDtypeStruct((ENT // 2, D), F32)
@@ -421,14 +409,18 @@
     slots = jax.ShapeDtypeStruct((EDGES, D), F32)
     slots_low = jax.ShapeDtypeStruct((EDGES, D), BF16)
     weights = jax.ShapeDtypeStruct((EDGES, ENT // 2), BF16)
+    near_first, head = lax.optimization_barrier((near_first, head))
+    near_second = swap(near_first, XL)
     far_first = swap(near_first, CORE)
     cc_first, tails, neg = call(
         first_score_kernel,
         [weights, slots, slots],
         0,
         5,
+        flops=3 * EDGES * ENT * D,
+        bytes_accessed=1 << 22,
     )(ids, near_first, far_first, prod, cnt)
-    near_second, tails = lax.optimization_barrier((near[1], tails))
+    near_second, tails = lax.optimization_barrier((near_second, tails))
     far_second = swap(near_second, CORE)
     rel_keep, rel_send, cc, plt, pd, gh = call(
         score_kernel,
@@ -447,11 +439,11 @@
     src_keep, src_send, dst_keep, dst_send = call(
         scatter_kernel,
         [kept, sent, kept, sent],
-        1,
+        0,
         6,
         flops=3 * 2 * EDGES * ENT * D,
         bytes_accessed=1 << 23,
-    )(xl.reshape(1), ids, cc_first, cc, plt, pd, gh)
+    )(ids, cc_first, cc, plt, pd, gh)
     recv, src_send, dst_send = lax.optimization_barrier((recv, src_send, dst_send))
     src_recv = swap(src_send, CORE)
     dst_recv = swap(dst_send, CORE)
@@ -463,9 +455,6 @@
     dst_second = shift(dst_away, 1, XL)
 
     landed = spread(mine.reshape(32, 8, D))
-    landed, src_other, dst_first, dst_second = lax.optimization_barrier(
-        (landed, src_other, dst_first, dst_second)
-    )
     summed = sum_rows(landed)
     ent_own = sum_with_means([src_own, src_other, dst_first, dst_second])
     ent_xl = swap(ent_own, XL)
@@ -474,12 +463,13 @@
     new_entities, new_entity_acc = update(
         entities, entity_acc, [ent_own, ent_xl, *ent_core], place
     )
-    total, new_entity_acc = lax.optimization_barrier((spread(summed), new_entity_acc))
+    total = spread(summed)
     quarter = sum_with_means([total.reshape(256, D)])
     recv = [swap(quarter, mask) for mask in X_MASKS]
 
     pieces = [quarter, *recv]
     pieces = pieces + [swap(piece, CORE) for piece in pieces]
+    pieces, new_entity_acc = lax.optimization_barrier((pieces, new_entity_acc))
     place = (core * 4 + x).reshape(1)
     new_relations, new_relation_acc = update(relations, relation_acc, pieces, place)
     return (new_entities, new_entity_acc, new_relations, new_relation_acc)

time: 121 us -> 111 us (0.917); the launches traced: 121 us -> 109 us
  blocking collectives: 15.9 us -> 0 us
  starting transfers between devices: 50.2 us -> 53.6 us
  waiting for transfers between devices: 14.2 us -> 11 us
  local copies, waits for them, and re-layouts: 7.78 us -> 10.6 us
  Pallas kernels: 28 us -> 30.5 us
  other arithmetic: 3.14 us -> 1.75 us
    all_to_all x1 -> x0, blocking collectives: 15.9 us -> none  [spread(): lax.all_to_all(parts, 'blk', 0, 0, axis_index_groups=groups, tiled=True)]
    all_to_all x1 -> x2, starting transfers between devices: 4 us -> 16.1 us  [spread(): lax.all_to_all(parts, 'blk', 0, 0, axis_index_groups=groups, tiled=True)]
    ppermute x4 -> x3, starting transfers between devices: 22.1 us -> 15.9 us  [shift(): return lax.ppermute(x, AXES, route)]
    unnamed x20 -> x38, local copies, waits for them, and re-layouts: 4.91 us -> 8.62 us
    all_to_all x1 -> x2, waiting for transfers between devices: 3.95 us -> 0.26 us  [spread(): lax.all_to_all(parts, 'blk', 0, 0, axis_index_groups=groups, tiled=True)]
    ppermute x19 -> x20, starting transfers between devices: 24.1 us -> 21.6 us  [swap(): return lax.ppermute(x, AXES, [(i, i ^ mask) for i in range(256)])]
    pallas_call x4, Pallas kernels: 0.37 us -> 2.43 us  [add_split(): call(functools.partial(add_split_kernel, len(parts), n_out), shapes, 0, l...]
    ppermute x4 -> x3, waiting for transfers between devices: 3.04 us -> 4.72 us  [shift(): return lax.ppermute(x, AXES, route)]
  transfers between devices with their start and end apart: 24 -> 25, of which waited for: 12 -> 7; matrix products, arithmetic and copies ran while one was open for 3% -> 2% of each run, Pallas kernels for 14% -> 19%
where the time goes in v5:
time: 111 us; the launch traced here: 109 us
  starting transfers between devices  53.6 us (48%)
  Pallas kernels  30.5 us (27%)
  waiting for transfers between devices  11 us (10%)
  local copies, waits for them, and re-layouts  10.6 us (10%)
  between operations  1.86 us (2%)
  other arithmetic  1.75 us (2%)
    ppermute x20, starting transfers between devices, swap(): return lax.ppermute(x, AXES, [(i, i ^ mask) for i in range(256)])  21.6 us
    all_to_all x2, starting transfers between devices, spread(): lax.all_to_all(parts, 'blk', 0, 0, axis_index_groups=groups, tiled=True)  16.1 us
    ppermute x3, starting transfers between devices, shift(): return lax.ppermute(x, AXES, route)  15.9 us
    unnamed x38, local copies, waits for them, and re-layouts  8.62 us
    pallas_call x1, Pallas kernels, shards(): call(score_kernel, [kept, sent, weights, jax.ShapeDtypeStruct((D, EDGES),...  6.73 us
    pallas_call x2, Pallas kernels, update(): pl.pallas_call(functools.partial(update_kernel, len(pieces)), out_shape=[...  6.51 us
    pallas_call x1, Pallas kernels, shards(): call(scatter_kernel, [kept, sent, kept, sent], 0, 6, flops=3 * 2 * EDGES...  6.5 us
    ppermute x20, waiting for transfers between devices, swap(): return lax.ppermute(x, AXES, [(i, i ^ mask) for i in range(256)])  6.01 us
  transfers between devices with their start and end apart: 25, of which 7 were waited for; matrix products, arithmetic and copies ran while one was open for 2% of the time, Pallas kernels for 19%

profile of v5, /device:TPU:1, one launch (start us, length us, event | category | flops | bytes accessed | tf_op | source)
XLA Modules:
  0.0 109.3 jit_solution(6714177556744641026)
XLA Ops:
  0.7 1.9 %dynamic-slice_convert_fusion = bf16[512,256]{1,0:T(8,128)(2,1)} fusion(f32[2048,256]{1,0:T(8,128)} %rows_ref.2, s32[]{:T(128)S(6)} %select_n.21), kind=kLoop, calls=%fused_computation | loop fusion | bytes 524292 | tf_op jit(solution)/shard_map/convert_element_type | solution.py:378
  2.6 11.1 %collective-permute-start = (bf16[512,256]{1,0:T(8,128)(2,1)}, bf16[512,256]{1,0:T(8,128)(2,1)S(1)}, u32[]{:S(2)}, u32[]{:S(2)}) collective-permute-start(bf16[512,256]{1,0:T(8,128)(2,1)} %dynamic-slice_convert_fusion), channel_id=1, source_target_pairs={{6,0},{7,1},{4,2},{5,3},{10,4},{11,5},{8,6},{9,7},{14,8},{15,9},{1... | collective-permute-start | bytes 786440 | tf_op jit(solution)/shard_map/ppermute | solution.py:362
  13.7 1.7 %convert_element_type.7.low_ref = bf16[2048,256]{1,0:T(8,128)(2,1)S(1)} convert(f32[2048,256]{1,0:T(8,128)} %rows_ref.2) | non-fusion elementwise | flops 524288 | bytes 3145728 | tf_op jit(solution)/shard_map/convert_element_type | solution.py:376
  15.6 4.9 %shard_map.120 = (bf16[1024,256]{1,0:T(8,128)(2,1)S(1)}, f32[1024,256]{1,0:T(8,128)S(1)}, f32[1024,256]{1,0:T(8,128)S(1)}, f32[4,16,128]{2,1,0:T(8,128)S(1)}) custom-call(s32[8,1024]{1,0:T(8,128)S(1)} %concatenate.3.ids_ref, s32[4,1024]{1,0:T(4,128)S(1)} %reshape.37.negs_ref, bf16[2048,256]{1,0:T(8,128)(2,1)S(1)} %convert_element_type.7.low_ref, ...), custom_call_target="tpu_custom_call" | custom-call | flops 4294967296 | bytes 4194304 | tf_op jit(solution)/shard_map/pallas_call | solution.py:392
  22.7 2.2 %shard_map.121 = (bf16[1024,1024]{1,0:T(8,128)(2,1)S(1)}, f32[1024,256]{1,0:T(8,128)S(1)}, f32[1024,256]{1,0:T(8,128)S(1)}) custom-call(s32[8,1024]{1,0:T(8,128)S(1)} %concatenate.3.ids_ref, bf16[512,256]{1,0:T(8,128)(2,1)S(1)} %collective-permute-done.near_ref, bf16[512,256]{1,0:T(8,128)(2,1)S(1)} %collective-permute-done.1.far_ref, ...), custom_call_target="tpu_custom_call" | custom-call | flops 1610612736 | bytes 4194304 | tf_op jit(solution)/shard_map/pallas_call | solution.py:415
  25.0 1.3 %copy-done.11 = bf16[1024,1024]{1,0:T(8,128)(2,1)} copy-done((bf16[1024,1024]{1,0:T(8,128)(2,1)}, bf16[1024,1024]{1,0:T(8,128)(2,1)S(1)}, u32[]{:S(2)}) %copy-start.11) | copy-done | bytes 2097176
  31.5 6.7 %shard_map.122 = (f32[1024,256]{1,0:T(8,128)S(1)}, bf16[1024,256]{1,0:T(8,128)(2,1)S(1)}, bf16[1024,1024]{1,0:T(8,128)(2,1)}, bf16[256,1024]{1,0:T(8,128)(2,1)S(...) custom-call(s32[1,1]{1,0:T(1,128)S(6)} %copy.13.count_ref, s32[8,1024]{1,0:T(8,128)S(1)} %concatenate.3.ids_ref, ...), custom_call_target="tpu_custom_call" | custom-call | flops 2684354560 | bytes 8388608 | tf_op jit(solution)/shard_map/pallas_call | solution.py:425
  38.6 1.5 %collective-permute-done.4.refs_1_ = bf16[1024,256]{1,0:T(8,128)(2,1)S(1)} collective-permute-done((bf16[1024,256]{1,0:T(8,128)(2,1)S(1)}, bf16[1024,256]{1,0:T(8,128)(2,1)S(1)}, u32[]{:S(2)}, u32[]{:S(2)}) %collective-permute-start.4) | collective-permute-done | bytes 524320 | tf_op jit(solution)/shard_map/ppermute | solution.py:357
  40.4 3.7 %collective-permute-start.7 = (bf16[256,256]{1,0:T(8,128)(2,1)S(1)}, bf16[256,256]{1,0:T(8,128)(2,1)S(1)}, u32[]{:S(2)}, u32[]{:S(2)}) collective-permute-start(bf16[256,256]{1,0:T(8,128)(2,1)S(1)} %get-tuple-element.81), channel_id=1, source_target_pairs={{0,6},{1,7},{2,4},{3,5},{4,2},{5,3},{6,0},{7,1},{8,14},{9,15},{10,... | collective-permute-start | bytes 393224 | tf_op jit(solution)/shard_map/ppermute | solution.py:357
  44.2 6.5 %shard_map.124 = (f32[1024,256]{1,0:T(8,128)S(1)}, bf16[1024,256]{1,0:T(8,128)(2,1)}, f32[1024,256]{1,0:T(8,128)S(1)}, bf16[1024,256]{1,0:T(8,128)(2,1)}) custom-call(s32[8,1024]{1,0:T(8,128)S(1)} %concatenate.3.ids_ref, bf16[1024,1024]{1,0:T(8,128)(2,1)} %copy-done.11, bf16[1024,1024]{1,0:T(8,128)(2,1)} %get-tuple-element.74.second_ref, ...), custom_call_target="tpu_custom_call" | custom-call | flops 3221225472 | bytes 8388608 | tf_op jit(solution)/shard_map/pallas_call | solution.py:439
  50.7 1.3 %collective-permute-start.8 = (bf16[1024,256]{1,0:T(8,128)(2,1)}, bf16[1024,256]{1,0:T(8,128)(2,1)S(1)}, u32[]{:S(2)}, u32[]{:S(2)}) collective-permute-start(bf16[1024,256]{1,0:T(8,128)(2,1)} %get-tuple-element.84), channel_id=1, source_target_pairs={{0,1},{1,0},{2,3},{3,2},{4,5},{5,4},{6,7},{7,6},{8,9},{9,8},{10,11... | collective-permute-start | bytes 1572872 | tf_op jit(solution)/shard_map/ppermute | solution.py:357
  52.8 7.5 %all-to-all-start = ((bf16[32,8,256]{2,1,0:T(8,128)(2,1)}), bf16[32,8,256]{2,1,0:T(8,128)(2,1)S(1)}, u32[]{:S(2)}, u32[]{:S(2)}) async-start(bf16[32,8,256]{2,1,0:T(8,128)(2,1)} %bitcast.2), calls=%async_computation | async-start | bytes 262144 | tf_op jit(solution)/shard_map/all_to_all | solution.py:353
  64.6 2.2 %collective-permute-start.11 = (bf16[512,256]{1,0:T(8,128)(2,1)}, bf16[512,256]{1,0:T(8,128)(2,1)S(1)}, u32[]{:S(2)}, u32[]{:S(2)}) collective-permute-start(bf16[512,256]{1,0:T(8,128)(2,1)} %get-tuple-element.89), channel_id=1, source_target_pairs={{252,0},{253,1},{254,2},{255,3},{0,4},{1,5},{2,6},{3,7},{4,8},{5,9... | collective-permute-start | bytes 786440 | tf_op jit(solution)/shard_map/ppermute | solution.py:362
  66.8 2.6 %collective-permute-start.12 = (bf16[512,256]{1,0:T(8,128)(2,1)}, bf16[512,256]{1,0:T(8,128)(2,1)S(1)}, u32[]{:S(2)}, u32[]{:S(2)}) collective-permute-start(bf16[512,256]{1,0:T(8,128)(2,1)} %get-tuple-element.90), channel_id=1, source_target_pairs={{254,0},{255,1},{252,2},{253,3},{2,4},{3,5},{0,6},{1,7},{6,8},{7,9... | collective-permute-start | bytes 786440 | tf_op jit(solution)/shard_map/ppermute | solution.py:362
  70.4 8.6 %all-to-all-start.1 = ((f32[32,8,256]{2,1,0:T(8,128)}), f32[32,8,256]{2,1,0:T(8,128)S(1)}, u32[]{:S(2)}, u32[]{:S(2)}) async-start(f32[32,8,256]{2,1,0:T(8,128)} %shard_map.130), calls=%async_computation.1 | async-start | bytes 524288 | tf_op jit(solution)/shard_map/all_to_all | solution.py:353
  79.1 4.7 %collective-permute-done.12.refs_3_ = bf16[512,256]{1,0:T(8,128)(2,1)S(1)} collective-permute-done((bf16[512,256]{1,0:T(8,128)(2,1)}, bf16[512,256]{1,0:T(8,128)(2,1)S(1)}, u32[]{:S(2)}, u32[]{:S(2)}) %collective-permute-start.12) | collective-permute-done | bytes 262176 | tf_op jit(solution)/shard_map/ppermute | solution.py:362
  87.9 3.4 %collective-permute-start.14 = (bf16[528,256]{1,0:T(8,128)(2,1)S(1)}, bf16[528,256]{1,0:T(8,128)(2,1)S(1)}, u32[]{:S(2)}, u32[]{:S(2)}) collective-permute-start(bf16[528,256]{1,0:T(8,128)(2,1)S(1)} %shard_map.127.refs_0_), channel_id=1, source_target_pairs={{0,1},{1,0},{2,3},{3,2},{4,5},{5,4},{6,7},{7,6},{8,9},{9,8},{10,11... | collective-permute-start | bytes 811016 | tf_op jit(solution)/shard_map/ppermute | solution.py:357
  91.5 1.6 %collective-permute-start.17 = (bf16[272,256]{1,0:T(8,128)(2,1)S(1)}, bf16[272,256]{1,0:T(8,128)(2,1)S(1)}, u32[]{:S(2)}, u32[]{:S(2)}) collective-permute-start(bf16[272,256]{1,0:T(8,128)(2,1)S(1)} %shard_map.131.refs_0_), channel_id=1, source_target_pairs={{0,4},{1,5},{2,6},{3,7},{4,0},{5,1},{6,2},{7,3},{8,12},{9,13},{10,... | collective-permute-start | bytes 417800 | tf_op jit(solution)/shard_map/ppermute | solution.py:357
  93.1 1.6 %collective-permute-start.16 = (bf16[272,256]{1,0:T(8,128)(2,1)S(1)}, bf16[272,256]{1,0:T(8,128)(2,1)}, u32[]{:S(2)}, u32[]{:S(2)}) collective-permute-start(bf16[272,256]{1,0:T(8,128)(2,1)S(1)} %shard_map.131.refs_0_), channel_id=1, source_target_pairs={{0,2},{1,3},{2,0},{3,1},{4,6},{5,7},{6,4},{7,5},{8,10},{9,11},{10,... | collective-permute-start | bytes 417800 | tf_op jit(solution)/shard_map/ppermute | solution.py:357
  94.8 2.8 %collective-permute-start.15 = (bf16[528,256]{1,0:T(8,128)(2,1)S(1)}, bf16[528,256]{1,0:T(8,128)(2,1)}, u32[]{:S(2)}, u32[]{:S(2)}) collective-permute-start(bf16[528,256]{1,0:T(8,128)(2,1)S(1)} %collective-permute-done.13.refs_1_), channel_id=1, source_target_pairs={{0,1},{1,0},{2,3},{3,2},{4,5},{5,4},{6,7},{7,6},{8,9},{9,8},{10,11... | collective-permute-start | bytes 811016 | tf_op jit(solution)/shard_map/ppermute | solution.py:357
  97.5 1.6 %collective-permute-done.18.refs_3_ = bf16[272,256]{1,0:T(8,128)(2,1)S(1)} collective-permute-done((bf16[272,256]{1,0:T(8,128)(2,1)S(1)}, bf16[272,256]{1,0:T(8,128)(2,1)S(1)}, u32[]{:S(2)}, u32[]{:S(2)}) %collective-permute-start.18) | collective-permute-done | bytes 139296 | tf_op jit(solution)/shard_map/ppermute | solution.py:357
  99.1 2.7 %collective-permute-start.19 = (bf16[272,256]{1,0:T(8,128)(2,1)S(1)}, bf16[272,256]{1,0:T(8,128)(2,1)}, u32[]{:S(2)}, u32[]{:S(2)}) collective-permute-start(bf16[272,256]{1,0:T(8,128)(2,1)S(1)} %shard_map.131.refs_0_), channel_id=1, source_target_pairs={{0,1},{1,0},{2,3},{3,2},{4,5},{5,4},{6,7},{7,6},{8,9},{9,8},{10,11... | collective-permute-start | bytes 417800 | tf_op jit(solution)/shard_map/ppermute | solution.py:357
  102.6 3.2 %shard_map.128 = (f32[2048,256]{1,0:T(8,128)}, f32[16,128]{1,0:T(8,128)}) custom-call(s32[1]{0:T(128)} %bitcast.place_ref, f32[2048,256]{1,0:T(8,128)S(1)} %copy-done, f32[16,128]{1,0:T(8,128)S(1)} %bitcast.9, bf16[528,256]{1,0:T(8,128)(2,1)S(1)} %shard_map.127.refs_0_, bf16[528,256]{1,0:T(8,128)(2,1)S(1)} %collective-permute-done.13.refs_1_, ...), custom_call_target="tpu_custom_call" | custom-call | flops 4194304 | bytes 5242880 | tf_op jit(solution)/shard_map/pallas_call | solution.py:318
  105.9 3.3 %shard_map.132 = (f32[2048,256]{1,0:T(8,128)}, f32[16,128]{1,0:T(8,128)}) custom-call(s32[1]{0:T(128)} %bitcast.5.place_ref, f32[2048,256]{1,0:T(8,128)S(1)} %copy-done.2, f32[16,128]{1,0:T(8,128)S(1)} %bitcast.10, bf16[272,256]{1,0:T(8,128)(2,1)S(1)} %shard_map.131.refs_0_, bf16[272,256]{1,0:T(8,128)(2,1)} %collective-permute-done.16.refs_1_, ...), custom_call_target="tpu_custom_call" | custom-call | flops 4194304 | bytes 5242880 | tf_op jit(solution)/shard_map/pallas_call | solution.py:318
  (85 shorter events, 18.7 us)
Async XLA Ops:
  2.6 17.9 %collective-permute-start = (bf16[512,256]{1,0:T(8,128)(2,1)}, bf16[512,256]{1,0:T(8,128)(2,1)S(1)}, u32[]{:S(2)}, u32[]{:S(2)}) collective-permute-start(bf16[512,256]{1,0:T(8,128)(2,1)} %dynamic-slice_convert_fusion), channel_id=1, source_target_pairs={{6,0},{7,1},{4,2},{5,3},{10,4},{11,5},{8,6},{9,7},{14,8},{15,9},{1... | collective-permute-start | bytes 786440 | tf_op jit(solution)/shard_map/ppermute | solution.py:362
  20.5 2.2 %collective-permute-start.1 = (bf16[512,256]{1,0:T(8,128)(2,1)S(1)}, bf16[512,256]{1,0:T(8,128)(2,1)S(1)}, u32[]{:S(2)}, u32[]{:S(2)}) collective-permute-start(bf16[512,256]{1,0:T(8,128)(2,1)S(1)} %collective-permute-done.near_ref), channel_id=1, source_target_pairs={{0,1},{1,0},{2,3},{3,2},{4,5},{5,4},{6,7},{7,6},{8,9},{9,8},{10,11... | collective-permute-start | bytes 786440 | tf_op jit(solution)/shard_map/ppermute | solution.py:357
  21.6 7.9 %collective-permute-start.2 = (bf16[512,256]{1,0:T(8,128)(2,1)S(1)}, bf16[512,256]{1,0:T(8,128)(2,1)S(1)}, u32[]{:S(2)}, u32[]{:S(2)}) collective-permute-start(bf16[512,256]{1,0:T(8,128)(2,1)S(1)} %collective-permute-done.near_ref), channel_id=1, source_target_pairs={{0,2},{1,3},{2,0},{3,1},{4,6},{5,7},{6,4},{7,5},{8,10},{9,11},{10,... | collective-permute-start | bytes 786440 | tf_op jit(solution)/shard_map/ppermute | solution.py:357
  29.5 2.0 %collective-permute-start.3 = (bf16[512,256]{1,0:T(8,128)(2,1)S(1)}, bf16[512,256]{1,0:T(8,128)(2,1)S(1)}, u32[]{:S(2)}, u32[]{:S(2)}) collective-permute-start(bf16[512,256]{1,0:T(8,128)(2,1)S(1)} %collective-permute-done.2.near_ref), channel_id=1, source_target_pairs={{0,1},{1,0},{2,3},{3,2},{4,5},{5,4},{6,7},{7,6},{8,9},{9,8},{10,11... | collective-permute-start | bytes 786440 | tf_op jit(solution)/shard_map/ppermute | solution.py:357
  40.2 10.5 %collective-permute-start.5 = (bf16[256,256]{1,0:T(8,128)(2,1)S(1)}, bf16[256,256]{1,0:T(8,128)(2,1)S(1)}, u32[]{:S(2)}, u32[]{:S(2)}) collective-permute-start(bf16[256,256]{1,0:T(8,128)(2,1)S(1)} %get-tuple-element.79), channel_id=1, source_target_pairs={{0,2},{1,3},{2,0},{3,1},{4,6},{5,7},{6,4},{7,5},{8,10},{9,11},{10,... | collective-permute-start | bytes 393224 | tf_op jit(solution)/shard_map/ppermute | solution.py:357
  40.3 10.4 %collective-permute-start.6 = (bf16[256,256]{1,0:T(8,128)(2,1)S(1)}, bf16[256,256]{1,0:T(8,128)(2,1)S(1)}, u32[]{:S(2)}, u32[]{:S(2)}) collective-permute-start(bf16[256,256]{1,0:T(8,128)(2,1)S(1)} %get-tuple-element.80), channel_id=1, source_target_pairs={{0,4},{1,5},{2,6},{3,7},{4,0},{5,1},{6,2},{7,3},{8,12},{9,13},{10,... | collective-permute-start | bytes 393224 | tf_op jit(solution)/shard_map/ppermute | solution.py:357
  40.4 10.3 %collective-permute-start.7 = (bf16[256,256]{1,0:T(8,128)(2,1)S(1)}, bf16[256,256]{1,0:T(8,128)(2,1)S(1)}, u32[]{:S(2)}, u32[]{:S(2)}) collective-permute-start(bf16[256,256]{1,0:T(8,128)(2,1)S(1)} %get-tuple-element.81), channel_id=1, source_target_pairs={{0,6},{1,7},{2,4},{3,5},{4,2},{5,3},{6,0},{7,1},{8,14},{9,15},{10,... | collective-permute-start | bytes 393224 | tf_op jit(solution)/shard_map/ppermute | solution.py:357
  50.7 9.6 %collective-permute-start.8 = (bf16[1024,256]{1,0:T(8,128)(2,1)}, bf16[1024,256]{1,0:T(8,128)(2,1)S(1)}, u32[]{:S(2)}, u32[]{:S(2)}) collective-permute-start(bf16[1024,256]{1,0:T(8,128)(2,1)} %get-tuple-element.84), channel_id=1, source_target_pairs={{0,1},{1,0},{2,3},{3,2},{4,5},{5,4},{6,7},{7,6},{8,9},{9,8},{10,11... | collective-permute-start | bytes 1572872 | tf_op jit(solution)/shard_map/ppermute | solution.py:357
  52.0 9.9 %collective-permute-start.10 = (bf16[1024,256]{1,0:T(8,128)(2,1)}, bf16[1024,256]{1,0:T(8,128)(2,1)S(1)}, u32[]{:S(2)}, u32[]{:S(2)}) collective-permute-start(bf16[1024,256]{1,0:T(8,128)(2,1)} %get-tuple-element.88), channel_id=1, source_target_pairs={{0,1},{1,0},{2,3},{3,2},{4,5},{5,4},{6,7},{7,6},{8,9},{9,8},{10,11... | collective-permute-start | bytes 1572872 | tf_op jit(solution)/shard_map/ppermute | solution.py:357
  52.8 16.9 %all-to-all-start = ((bf16[32,8,256]{2,1,0:T(8,128)(2,1)}), bf16[32,8,256]{2,1,0:T(8,128)(2,1)S(1)}, u32[]{:S(2)}, u32[]{:S(2)}) async-start(bf16[32,8,256]{2,1,0:T(8,128)(2,1)} %bitcast.2), calls=%async_computation | async-start | bytes 262144 | tf_op jit(solution)/shard_map/all_to_all | solution.py:353
  61.9 17.1 %collective-permute-start.9 = (bf16[512,256]{1,0:T(8,128)(2,1)}, bf16[512,256]{1,0:T(8,128)(2,1)S(1)}, u32[]{:S(2)}, u32[]{:S(2)}) collective-permute-start(bf16[512,256]{1,0:T(8,128)(2,1)} %get-tuple-element.86), channel_id=1, source_target_pairs={{0,2},{1,3},{2,0},{3,1},{4,6},{5,7},{6,4},{7,5},{8,10},{9,11},{10,... | collective-permute-start | bytes 786440 | tf_op jit(solution)/shard_map/ppermute | solution.py:357
  64.6 14.4 %collective-permute-start.11 = (bf16[512,256]{1,0:T(8,128)(2,1)}, bf16[512,256]{1,0:T(8,128)(2,1)S(1)}, u32[]{:S(2)}, u32[]{:S(2)}) collective-permute-start(bf16[512,256]{1,0:T(8,128)(2,1)} %get-tuple-element.89), channel_id=1, source_target_pairs={{252,0},{253,1},{254,2},{255,3},{0,4},{1,5},{2,6},{3,7},{4,8},{5,9... | collective-permute-start | bytes 786440 | tf_op jit(solution)/shard_map/ppermute | solution.py:362
  66.8 17.0 %collective-permute-start.12 = (bf16[512,256]{1,0:T(8,128)(2,1)}, bf16[512,256]{1,0:T(8,128)(2,1)S(1)}, u32[]{:S(2)}, u32[]{:S(2)}) collective-permute-start(bf16[512,256]{1,0:T(8,128)(2,1)} %get-tuple-element.90), channel_id=1, source_target_pairs={{254,0},{255,1},{252,2},{253,3},{2,4},{3,5},{0,6},{1,7},{6,8},{7,9... | collective-permute-start | bytes 786440 | tf_op jit(solution)/shard_map/ppermute | solution.py:362
  70.4 20.9 %all-to-all-start.1 = ((f32[32,8,256]{2,1,0:T(8,128)}), f32[32,8,256]{2,1,0:T(8,128)S(1)}, u32[]{:S(2)}, u32[]{:S(2)}) async-start(f32[32,8,256]{2,1,0:T(8,128)} %shard_map.130), calls=%async_computation.1 | async-start | bytes 524288 | tf_op jit(solution)/shard_map/all_to_all | solution.py:353
  86.8 8.0 %collective-permute-start.13 = (bf16[528,256]{1,0:T(8,128)(2,1)S(1)}, bf16[528,256]{1,0:T(8,128)(2,1)S(1)}, u32[]{:S(2)}, u32[]{:S(2)}) collective-permute-start(bf16[528,256]{1,0:T(8,128)(2,1)S(1)} %shard_map.127.refs_0_), channel_id=1, source_target_pairs={{0,2},{1,3},{2,0},{3,1},{4,6},{5,7},{6,4},{7,5},{8,10},{9,11},{10,... | collective-permute-start | bytes 811016 | tf_op jit(solution)/shard_map/ppermute | solution.py:357
  87.9 14.6 %collective-permute-start.14 = (bf16[528,256]{1,0:T(8,128)(2,1)S(1)}, bf16[528,256]{1,0:T(8,128)(2,1)S(1)}, u32[]{:S(2)}, u32[]{:S(2)}) collective-permute-start(bf16[528,256]{1,0:T(8,128)(2,1)S(1)} %shard_map.127.refs_0_), channel_id=1, source_target_pairs={{0,1},{1,0},{2,3},{3,2},{4,5},{5,4},{6,7},{7,6},{8,9},{9,8},{10,11... | collective-permute-start | bytes 811016 | tf_op jit(solution)/shard_map/ppermute | solution.py:357
  91.4 7.7 %collective-permute-start.18 = (bf16[272,256]{1,0:T(8,128)(2,1)S(1)}, bf16[272,256]{1,0:T(8,128)(2,1)S(1)}, u32[]{:S(2)}, u32[]{:S(2)}) collective-permute-start(bf16[272,256]{1,0:T(8,128)(2,1)S(1)} %shard_map.131.refs_0_), channel_id=1, source_target_pairs={{0,6},{1,7},{2,4},{3,5},{4,2},{5,3},{6,0},{7,1},{8,14},{9,15},{10,... | collective-permute-start | bytes 417800 | tf_op jit(solution)/shard_map/ppermute | solution.py:357
  91.5 10.3 %collective-permute-start.17 = (bf16[272,256]{1,0:T(8,128)(2,1)S(1)}, bf16[272,256]{1,0:T(8,128)(2,1)S(1)}, u32[]{:S(2)}, u32[]{:S(2)}) collective-permute-start(bf16[272,256]{1,0:T(8,128)(2,1)S(1)} %shard_map.131.refs_0_), channel_id=1, source_target_pairs={{0,4},{1,5},{2,6},{3,7},{4,0},{5,1},{6,2},{7,3},{8,12},{9,13},{10,... | collective-permute-start | bytes 417800 | tf_op jit(solution)/shard_map/ppermute | solution.py:357
  93.1 8.7 %collective-permute-start.16 = (bf16[272,256]{1,0:T(8,128)(2,1)S(1)}, bf16[272,256]{1,0:T(8,128)(2,1)}, u32[]{:S(2)}, u32[]{:S(2)}) collective-permute-start(bf16[272,256]{1,0:T(8,128)(2,1)S(1)} %shard_map.131.refs_0_), channel_id=1, source_target_pairs={{0,2},{1,3},{2,0},{3,1},{4,6},{5,7},{6,4},{7,5},{8,10},{9,11},{10,... | collective-permute-start | bytes 417800 | tf_op jit(solution)/shard_map/ppermute | solution.py:357
  94.8 7.8 %collective-permute-start.15 = (bf16[528,256]{1,0:T(8,128)(2,1)S(1)}, bf16[528,256]{1,0:T(8,128)(2,1)}, u32[]{:S(2)}, u32[]{:S(2)}) collective-permute-start(bf16[528,256]{1,0:T(8,128)(2,1)S(1)} %collective-permute-done.13.refs_1_), channel_id=1, source_target_pairs={{0,1},{1,0},{2,3},{3,2},{4,5},{5,4},{6,7},{7,6},{8,9},{9,8},{10,11... | collective-permute-start | bytes 811016 | tf_op jit(solution)/shard_map/ppermute | solution.py:357
  99.1 6.7 %collective-permute-start.19 = (bf16[272,256]{1,0:T(8,128)(2,1)S(1)}, bf16[272,256]{1,0:T(8,128)(2,1)}, u32[]{:S(2)}, u32[]{:S(2)}) collective-permute-start(bf16[272,256]{1,0:T(8,128)(2,1)S(1)} %shard_map.131.refs_0_), channel_id=1, source_target_pairs={{0,1},{1,0},{2,3},{3,2},{4,5},{5,4},{6,7},{7,6},{8,9},{9,8},{10,11... | collective-permute-start | bytes 417800 | tf_op jit(solution)/shard_map/ppermute | solution.py:357
  101.8 4.0 %collective-permute-start.22 = (bf16[272,256]{1,0:T(8,128)(2,1)S(1)}, bf16[272,256]{1,0:T(8,128)(2,1)}, u32[]{:S(2)}, u32[]{:S(2)}) collective-permute-start(bf16[272,256]{1,0:T(8,128)(2,1)S(1)} %collective-permute-done.18.refs_3_), channel_id=1, source_target_pairs={{0,1},{1,0},{2,3},{3,2},{4,5},{5,4},{6,7},{7,6},{8,9},{9,8},{10,11... | collective-permute-start | bytes 417800 | tf_op jit(solution)/shard_map/ppermute | solution.py:357
  101.8 4.0 %collective-permute-start.21 = (bf16[272,256]{1,0:T(8,128)(2,1)S(1)}, bf16[272,256]{1,0:T(8,128)(2,1)}, u32[]{:S(2)}, u32[]{:S(2)}) collective-permute-start(bf16[272,256]{1,0:T(8,128)(2,1)S(1)} %collective-permute-done.17.refs_2_), channel_id=1, source_target_pairs={{0,1},{1,0},{2,3},{3,2},{4,5},{5,4},{6,7},{7,6},{8,9},{9,8},{10,11... | collective-permute-start | bytes 417800 | tf_op jit(solution)/shard_map/ppermute | solution.py:357
  102.5 3.3 %collective-permute-start.20 = (bf16[272,256]{1,0:T(8,128)(2,1)}, bf16[272,256]{1,0:T(8,128)(2,1)}, u32[]{:S(2)}, u32[]{:S(2)}) collective-permute-start(bf16[272,256]{1,0:T(8,128)(2,1)} %collective-permute-done.16.refs_1_), channel_id=1, source_target_pairs={{0,1},{1,0},{2,3},{3,2},{4,5},{5,4},{6,7},{7,6},{8,9},{9,8},{10,11... | collective-permute-start | bytes 417800 | tf_op jit(solution)/shard_map/ppermute | solution.py:357
  (20 other events, 189.2 us)

commit v6 on v5

--- a/solution.py
+++ b/solution.py
@@ -144,15 +144,19 @@
     cnt_ref,
     tails_ref,
     neg_ref,
-    keep_ref,
-    send_ref,
+    first_ref,
+    src_keep_ref,
+    src_send_ref,
+    dst_keep_ref,
+    dst_send_ref,
+    gr_ref,
     cc_ref,
     plt_ref,
     pd_ref,
     gh_ref,
-    gr_ref,
 ):
     half = ENT // 2
+    quarter = half // 2
     count = count_ref[0, 0]
 
     def group(g, _):
@@ -179,49 +183,30 @@
 
     lax.fori_loop(0, EDGES // GROUP, group, 0, unroll=UNROLL)
 
-    def scatter(i, _):
-        rows = pl.ds(pl.multiple_of(i * CHUNK, CHUNK), CHUNK)
+    for part, ref in ((0, first_ref), (1, cc_ref)):
+        for i in range(quarter // CHUNK):
+            at = part * quarter + i * CHUNK
+            rows = slice(at, at + CHUNK)
+            for j, src_ref, dst_ref in (
+                (0, src_keep_ref, dst_keep_ref),
+                (1, src_send_ref, dst_send_ref),
+            ):
+                src = dot(one_hot_cols(ids_ref[4:5, :], CHUNK, j * half + at), gh_ref[...])
+                src_ref[rows, :] = src.astype(src_ref.dtype)
+                cols = slice(j * quarter + i * CHUNK, j * quarter + (i + 1) * CHUNK)
+                drawn = jnp.transpose(dot(plt_ref[...], ref[:, cols]))
+                dst = dot(one_hot_cols(ids_ref[2:3, :], CHUNK, j * half + at), pd_ref[...])
+                dst_ref[rows, :] = (drawn + dst).astype(dst_ref.dtype)
+
+
+def relation_kernel(ids_ref, gr_ref, keep_ref, send_ref):
+    half = NREL // 2
+    for i in range(half // CHUNK):
+        rows = slice(i * CHUNK, (i + 1) * CHUNK)
         keep_ref[rows, :] = dot(one_hot_cols(ids_ref[3:4, :], CHUNK, i * CHUNK), gr_ref[...])
         send_ref[rows, :] = dot(
             one_hot_cols(ids_ref[3:4, :], CHUNK, half + i * CHUNK), gr_ref[...]
         ).astype(BF16)
-        return 0
-
-    lax.fori_loop(0, half // CHUNK, scatter, 0, unroll=UNROLL)
-
-
-def scatter_kernel(
-    ids_ref,
-    first_ref,
-    second_ref,
-    plt_ref,
-    pd_ref,
-    gh_ref,
-    src_keep_ref,
-    src_send_ref,
-    dst_keep_ref,
-    dst_send_ref,
-):
-    half = ENT // 2
-    quarter = half // 2
-
-    def scatter(i, part, cc_ref):
-        at = part * quarter + i * CHUNK
-        rows = pl.ds(at, CHUNK)
-        for j, src_ref, dst_ref in (
-            (0, src_keep_ref, dst_keep_ref),
-            (1, src_send_ref, dst_send_ref),
-        ):
-            src = dot(one_hot_cols(ids_ref[4:5, :], CHUNK, j * half + at), gh_ref[...])
-            src_ref[rows, :] = src.astype(src_ref.dtype)
-            cols = pl.ds(j * quarter + i * CHUNK, CHUNK)
-            drawn = jnp.transpose(dot(plt_ref[...], cc_ref[:, cols]))
-            dst = dot(one_hot_cols(ids_ref[2:3, :], CHUNK, j * half + at), pd_ref[...])
-            dst_ref[rows, :] = (drawn + dst).astype(dst_ref.dtype)
-
-    for part, ref in ((0, first_ref), (1, second_ref)):
-        for i in range(quarter // CHUNK):
-            scatter(i, part, ref)
 
 
 def add_split_kernel(n_in, n_out, *refs):
@@ -422,54 +407,60 @@
     )(ids, near_first, far_first, prod, cnt)
     near_second, tails = lax.optimization_barrier((near_second, tails))
     far_second = swap(near_second, CORE)
-    rel_keep, rel_send, cc, plt, pd, gh = call(
+    src_keep, src_send, dst_keep, dst_send, gr = call(
         score_kernel,
-        [kept, sent, weights, jax.ShapeDtypeStruct((D, EDGES), BF16), slots_low, slots_low],
+        [kept, sent, kept, sent, slots_low],
         1,
-        9,
-        [pltpu.VMEM((EDGES, D), BF16)],
-        flops=5 * EDGES * ENT * D,
+        10,
+        [
+            pltpu.VMEM((EDGES, ENT // 2), BF16),
+            pltpu.VMEM((D, EDGES), BF16),
+            pltpu.VMEM((EDGES, D), BF16),
+            pltpu.VMEM((EDGES, D), BF16),
+        ],
+        flops=9 * EDGES * ENT * D,
         bytes_accessed=1 << 23,
-    )(counts, ids, near_second, far_second, head, rel_rows, prod, cnt, tails, neg)
-    rel_recv = swap(rel_send, CORE)
-    parts = add_split([rel_keep, rel_recv], 4, own=F32)
-    parts, cc = lax.optimization_barrier((parts, cc))
-    recv = [swap(part, mask) for part, mask in zip(parts[1:], X_MASKS)]
-
-    src_keep, src_send, dst_keep, dst_send = call(
-        scatter_kernel,
-        [kept, sent, kept, sent],
-        0,
-        6,
-        flops=3 * 2 * EDGES * ENT * D,
-        bytes_accessed=1 << 23,
-    )(ids, cc_first, cc, plt, pd, gh)
-    recv, src_send, dst_send = lax.optimization_barrier((recv, src_send, dst_send))
+    )(counts, ids, near_second, far_second, head, rel_rows, prod, cnt, tails, neg, cc_first)
     src_recv = swap(src_send, CORE)
     dst_recv = swap(dst_send, CORE)
+    rel_keep, rel_send = call(
+        relation_kernel,
+        [kept, sent],
+        0,
+        2,
+        flops=2 * EDGES * NREL * D,
+        bytes_accessed=1 << 21,
+    )(ids, gr)
+
+    rel_recv = swap(rel_send, CORE)
     src_own, src_away = add_split([src_keep, src_recv], 2, own=F32)
     dst_own, dst_away = add_split([dst_keep, dst_recv], 2)
-    (mine,) = add_split([parts[0], *recv], 1)
+    parts = add_split([rel_keep, rel_recv], 4, own=F32)
+    parts, src_away, dst_own, dst_away = lax.optimization_barrier(
+        (parts, src_away, dst_own, dst_away)
+    )
+    recv = [swap(part, mask) for part, mask in zip(parts[1:], X_MASKS)]
     src_other = swap(src_away, XL)
     dst_first = shift(dst_own, 1, 0)
     dst_second = shift(dst_away, 1, XL)
+    (mine,) = add_split([parts[0], *recv], 1)
 
     landed = spread(mine.reshape(32, 8, D))
+    ent_own = sum_with_means([src_own, src_other, dst_first, dst_second])
+    landed, ent_own = lax.optimization_barrier((landed, ent_own))
     summed = sum_rows(landed)
-    ent_own = sum_with_means([src_own, src_other, dst_first, dst_second])
     ent_xl = swap(ent_own, XL)
     ent_core = [swap(ent_own, CORE), swap(ent_xl, CORE)]
     place = (core * 2 + xl).reshape(1)
     new_entities, new_entity_acc = update(
         entities, entity_acc, [ent_own, ent_xl, *ent_core], place
     )
-    total = spread(summed)
+    total, new_entity_acc = lax.optimization_barrier((spread(summed), new_entity_acc))
     quarter = sum_with_means([total.reshape(256, D)])
     recv = [swap(quarter, mask) for mask in X_MASKS]
 
     pieces = [quarter, *recv]
     pieces = pieces + [swap(piece, CORE) for piece in pieces]
-    pieces, new_entity_acc = lax.optimization_barrier((pieces, new_entity_acc))
     place = (core * 4 + x).reshape(1)
     new_relations, new_relation_acc = update(relations, relation_acc, pieces, place)
     return (new_entities, new_entity_acc, new_relations, new_relation_acc)

time: 111 us -> 117 us (1.054); the launches traced: 109 us -> 117 us
  waiting for transfers between devices: 11 us -> 20.1 us
  starting transfers between devices: 53.6 us -> 59.8 us
  Pallas kernels: 30.5 us -> 26.6 us
  local copies, waits for them, and re-layouts: 10.6 us -> 6.94 us
    all_to_all x2, waiting for transfers between devices: 0.26 us -> 10.2 us  [spread(): lax.all_to_all(parts, 'blk', 0, 0, axis_index_groups=groups, tiled=True)]
    all_to_all x2, starting transfers between devices: 16.1 us -> 23.9 us  [spread(): lax.all_to_all(parts, 'blk', 0, 0, axis_index_groups=groups, tiled=True)]
    ppermute x3, waiting for transfers between devices: 4.72 us -> 0.01 us  [shift(): return lax.ppermute(x, AXES, route)]
    ppermute x20, waiting for transfers between devices: 6.01 us -> 9.91 us  [swap(): return lax.ppermute(x, AXES, [(i, i ^ mask) for i in range(256)])]
    unnamed x38 -> x26, local copies, waits for them, and re-layouts: 8.62 us -> 4.95 us
    ppermute x3, starting transfers between devices: 15.9 us -> 12.2 us  [shift(): return lax.ppermute(x, AXES, route)]
    pallas_call x2, Pallas kernels: 13.2 us -> 9.69 us  [the longest x1 8.45 us: shards(): call(score_kernel, [kept, sent, kept, sent, slots_low], 1, 10, [pltpu.VME...]
    ppermute x20, starting transfers between devices: 21.6 us -> 23.6 us  [swap(): return lax.ppermute(x, AXES, [(i, i ^ mask) for i in range(256)])]
  transfers between devices with their start and end apart: 25 -> 25, of which waited for: 7 -> 10; matrix products, arithmetic and copies ran while one was open for 2% -> 2% of each run, Pallas kernels for 19% -> 13%
where the time goes in v6:
time: 117 us
  starting transfers between devices  59.8 us (51%)
  Pallas kernels  26.6 us (23%)
  waiting for transfers between devices  20.1 us (17%)
  local copies, waits for them, and re-layouts  6.94 us (6%)
  between operations  1.81 us (2%)
  other arithmetic  1.75 us (1%)
    all_to_all x2, starting transfers between devices, spread(): lax.all_to_all(parts, 'blk', 0, 0, axis_index_groups=groups, tiled=True)  23.9 us
    ppermute x20, starting transfers between devices, swap(): return lax.ppermute(x, AXES, [(i, i ^ mask) for i in range(256)])  23.6 us
    ppermute x3, starting transfers between devices, shift(): return lax.ppermute(x, AXES, route)  12.2 us
    all_to_all x2, waiting for transfers between devices, spread(): lax.all_to_all(parts, 'blk', 0, 0, axis_index_groups=groups, tiled=True)  10.2 us
    ppermute x20, waiting for transfers between devices, swap(): return lax.ppermute(x, AXES, [(i, i ^ mask) for i in range(256)])  9.91 us
    pallas_call x1, Pallas kernels, shards(): call(score_kernel, [kept, sent, kept, sent, slots_low], 1, 10, [pltpu.VME...  8.45 us
    pallas_call x2, Pallas kernels, update(): pl.pallas_call(functools.partial(update_kernel, len(pieces)), out_shape=[...  5.18 us
    unnamed x26, local copies, waits for them, and re-layouts  4.95 us
  transfers between devices with their start and end apart: 25, of which 10 were waited for; matrix products, arithmetic and copies ran while one was open for 2% of the time, Pallas kernels for 13%

profile of v6, /device:TPU:1, one launch (start us, length us, event | category | flops | bytes accessed | tf_op | source)
XLA Modules:
  0.0 117.0 jit_solution(6595648163656990084)
XLA Ops:
  0.7 1.9 %dynamic-slice_convert_fusion = bf16[512,256]{1,0:T(8,128)(2,1)} fusion(f32[2048,256]{1,0:T(8,128)} %rows_ref.2, s32[]{:T(128)S(6)} %select_n.21), kind=kLoop, calls=%fused_computation | loop fusion | bytes 524292 | tf_op jit(solution)/shard_map/convert_element_type | solution.py:363
  2.6 11.1 %collective-permute-start = (bf16[512,256]{1,0:T(8,128)(2,1)}, bf16[512,256]{1,0:T(8,128)(2,1)S(1)}, u32[]{:S(2)}, u32[]{:S(2)}) collective-permute-start(bf16[512,256]{1,0:T(8,128)(2,1)} %dynamic-slice_convert_fusion), channel_id=1, source_target_pairs={{6,0},{7,1},{4,2},{5,3},{10,4},{11,5},{8,6},{9,7},{14,8},{15,9},{1... | collective-permute-start | bytes 786440 | tf_op jit(solution)/shard_map/ppermute | solution.py:347
  13.7 1.7 %convert_element_type.7.low_ref = bf16[2048,256]{1,0:T(8,128)(2,1)S(1)} convert(f32[2048,256]{1,0:T(8,128)} %rows_ref.2) | non-fusion elementwise | flops 524288 | bytes 3145728 | tf_op jit(solution)/shard_map/convert_element_type | solution.py:361
  15.6 4.9 %shard_map.120 = (bf16[1024,256]{1,0:T(8,128)(2,1)S(1)}, f32[1024,256]{1,0:T(8,128)S(1)}, f32[1024,256]{1,0:T(8,128)S(1)}, f32[4,16,128]{2,1,0:T(8,128)S(1)}) custom-call(s32[8,1024]{1,0:T(8,128)S(1)} %concatenate.3.ids_ref, s32[4,1024]{1,0:T(4,128)S(1)} %reshape.37.negs_ref, bf16[2048,256]{1,0:T(8,128)(2,1)S(1)} %convert_element_type.7.low_ref, ...), custom_call_target="tpu_custom_call" | custom-call | flops 4294967296 | bytes 4194304 | tf_op jit(solution)/shard_map/pallas_call | solution.py:377
  22.7 2.2 %shard_map.121 = (bf16[1024,1024]{1,0:T(8,128)(2,1)S(1)}, f32[1024,256]{1,0:T(8,128)S(1)}, f32[1024,256]{1,0:T(8,128)S(1)}) custom-call(s32[8,1024]{1,0:T(8,128)S(1)} %concatenate.3.ids_ref, bf16[512,256]{1,0:T(8,128)(2,1)S(1)} %collective-permute-done.near_ref, bf16[512,256]{1,0:T(8,128)(2,1)S(1)} %collective-permute-done.2.far_ref, ...), custom_call_target="tpu_custom_call" | custom-call | flops 1610612736 | bytes 4194304 | tf_op jit(solution)/shard_map/pallas_call | solution.py:400
  25.0 1.3 %copy-done.5 = bf16[1024,1024]{1,0:T(8,128)(2,1)} copy-done((bf16[1024,1024]{1,0:T(8,128)(2,1)}, bf16[1024,1024]{1,0:T(8,128)(2,1)S(1)}, u32[]{:S(2)}) %copy-start.5) | copy-done | bytes 2097176
  31.5 8.4 %shard_map.122 = (f32[1024,256]{1,0:T(8,128)S(1)}, bf16[1024,256]{1,0:T(8,128)(2,1)S(1)}, f32[1024,256]{1,0:T(8,128)S(1)}, bf16[1024,256]{1,0:T(8,128)(2,1)S(1)}, bf16[1024,256]{1,0:T(8,128)(2,1)S(1)}) custom-call(s32[1,1]{1,0:T(1,128)S(6)} %copy.13.count_ref, s32[8,1024]{1,0:T(8,128)S(1)} %concatenate.3.ids_ref, ...), custom_call_target="tpu_custom_call" | custom-call | flops 4831838208 | bytes 8388608 | tf_op jit(solution)/shard_map/pallas_call | solution.py:410
  40.5 1.2 %shard_map.123 = (f32[1024,256]{1,0:T(8,128)S(1)}, bf16[1024,256]{1,0:T(8,128)(2,1)S(1)}) custom-call(s32[8,1024]{1,0:T(8,128)S(1)} %concatenate.3.ids_ref, bf16[1024,256]{1,0:T(8,128)(2,1)S(1)} %get-tuple-element.56.gr_ref), custom_call_target="tpu_custom_call" | custom-call | flops 1073741824 | bytes 2097152 | tf_op jit(solution)/shard_map/pallas_call | solution.py:426
  44.2 3.7 %collective-permute-start.9 = (bf16[256,256]{1,0:T(8,128)(2,1)S(1)}, bf16[256,256]{1,0:T(8,128)(2,1)S(1)}, u32[]{:S(2)}, u32[]{:S(2)}) collective-permute-start(bf16[256,256]{1,0:T(8,128)(2,1)S(1)} %get-tuple-element.73), channel_id=1, source_target_pairs={{0,6},{1,7},{2,4},{3,5},{4,2},{5,3},{6,0},{7,1},{8,14},{9,15},{10,... | collective-permute-start | bytes 393224 | tf_op jit(solution)/shard_map/ppermute | solution.py:342
  50.4 3.6 %collective-permute-done.9.refs_3_ = bf16[256,256]{1,0:T(8,128)(2,1)S(1)} collective-permute-done((bf16[256,256]{1,0:T(8,128)(2,1)S(1)}, bf16[256,256]{1,0:T(8,128)(2,1)S(1)}, u32[]{:S(2)}, u32[]{:S(2)}) %collective-permute-start.9) | collective-permute-done | bytes 131104 | tf_op jit(solution)/shard_map/ppermute | solution.py:342
  54.7 19.9 %all-to-all-start = ((bf16[32,8,256]{2,1,0:T(8,128)(2,1)}), bf16[32,8,256]{2,1,0:T(8,128)(2,1)S(1)}, u32[]{:S(2)}, u32[]{:S(2)}) async-start(bf16[32,8,256]{2,1,0:T(8,128)(2,1)} %bitcast.2), calls=%async_computation | async-start | bytes 262144 | tf_op jit(solution)/shard_map/all_to_all | solution.py:338
  74.6 1.2 %shard_map.128.refs_0_ = bf16[528,256]{1,0:T(8,128)(2,1)S(1)} custom-call(f32[512,256]{1,0:T(8,128)S(1)} %get-tuple-element.74.refs_0_, bf16[512,256]{1,0:T(8,128)(2,1)S(1)} %collective-permute-done.10.refs_1_, bf16[512,256]{1,0:T(8,128)(2,1)S(1)} %collective-permute-done.11.refs_2_, bf16[512,256]{1,0:T(8,128)(2,1)} %collective-permute-done.12.refs_3_), custom_call_target="tpu_custom_call" | custom-call | flops 524288 | bytes 1572864 | tf_op jit(solution)/shard_map/pallas_call | solution.py:263
  75.8 8.1 %all-to-all-done.parts_ref = bf16[32,8,256]{2,1,0:T(8,128)(2,1)S(1)} async-done(((bf16[32,8,256]{2,1,0:T(8,128)(2,1)}), bf16[32,8,256]{2,1,0:T(8,128)(2,1)S(1)}, u32[]{:S(2)}, u32[]{:S(2)}) %all-to-all-start) | async-done | bytes 131104 | tf_op jit(solution)/shard_map/all_to_all | solution.py:338
  84.7 4.0 %all-to-all-start.1 = ((f32[32,8,256]{2,1,0:T(8,128)}), f32[32,8,256]{2,1,0:T(8,128)S(1)}, u32[]{:S(2)}, u32[]{:S(2)}) async-start(f32[32,8,256]{2,1,0:T(8,128)} %shard_map.130), calls=%async_computation.1 | async-start | bytes 524288 | tf_op jit(solution)/shard_map/all_to_all | solution.py:338
  88.7 2.4 %collective-permute-start.14 = (bf16[528,256]{1,0:T(8,128)(2,1)S(1)}, bf16[528,256]{1,0:T(8,128)(2,1)S(1)}, u32[]{:S(2)}, u32[]{:S(2)}) collective-permute-start(bf16[528,256]{1,0:T(8,128)(2,1)S(1)} %shard_map.128.refs_0_), channel_id=1, source_target_pairs={{0,1},{1,0},{2,3},{3,2},{4,5},{5,4},{6,7},{7,6},{8,9},{9,8},{10,11... | collective-permute-start | bytes 811016 | tf_op jit(solution)/shard_map/ppermute | solution.py:342
  91.1 1.7 %collective-permute-start.15 = (bf16[528,256]{1,0:T(8,128)(2,1)S(1)}, bf16[528,256]{1,0:T(8,128)(2,1)}, u32[]{:S(2)}, u32[]{:S(2)}) collective-permute-start(bf16[528,256]{1,0:T(8,128)(2,1)S(1)} %collective-permute-done.13.refs_1_), channel_id=1, source_target_pairs={{0,1},{1,0},{2,3},{3,2},{4,5},{5,4},{6,7},{7,6},{8,9},{9,8},{10,11... | collective-permute-start | bytes 811016 | tf_op jit(solution)/shard_map/ppermute | solution.py:342
  92.9 1.3 %collective-permute-done.15.refs_3_ = bf16[528,256]{1,0:T(8,128)(2,1)} collective-permute-done((bf16[528,256]{1,0:T(8,128)(2,1)S(1)}, bf16[528,256]{1,0:T(8,128)(2,1)}, u32[]{:S(2)}, u32[]{:S(2)}) %collective-permute-start.15) | collective-permute-done | bytes 270368 | tf_op jit(solution)/shard_map/ppermute | solution.py:342
  94.2 3.1 %shard_map.129 = (f32[2048,256]{1,0:T(8,128)}, f32[16,128]{1,0:T(8,128)}) custom-call(s32[1]{0:T(128)} %bitcast.place_ref, f32[2048,256]{1,0:T(8,128)S(1)} %copy-done, f32[16,128]{1,0:T(8,128)S(1)} %bitcast.9, bf16[528,256]{1,0:T(8,128)(2,1)S(1)} %shard_map.128.refs_0_, bf16[528,256]{1,0:T(8,128)(2,1)S(1)} %collective-permute-done.13.refs_1_, ...), custom_call_target="tpu_custom_call" | custom-call | flops 4194304 | bytes 5242880 | tf_op jit(solution)/shard_map/pallas_call | solution.py:303
  97.2 2.1 %all-to-all-done.1 = f32[32,8,256]{2,1,0:T(8,128)S(1)} async-done(((f32[32,8,256]{2,1,0:T(8,128)}), f32[32,8,256]{2,1,0:T(8,128)S(1)}, u32[]{:S(2)}, u32[]{:S(2)}) %all-to-all-start.1) | async-done | bytes 262176 | tf_op jit(solution)/shard_map/all_to_all | solution.py:338
  99.5 3.2 %collective-permute-start.17 = (bf16[272,256]{1,0:T(8,128)(2,1)S(1)}, bf16[272,256]{1,0:T(8,128)(2,1)S(1)}, u32[]{:S(2)}, u32[]{:S(2)}) collective-permute-start(bf16[272,256]{1,0:T(8,128)(2,1)S(1)} %shard_map.131.refs_0_), channel_id=1, source_target_pairs={{0,4},{1,5},{2,6},{3,7},{4,0},{5,1},{6,2},{7,3},{8,12},{9,13},{10,... | collective-permute-start | bytes 417800 | tf_op jit(solution)/shard_map/ppermute | solution.py:342
  102.8 4.4 %collective-permute-start.19 = (bf16[272,256]{1,0:T(8,128)(2,1)S(1)}, bf16[272,256]{1,0:T(8,128)(2,1)S(1)}, u32[]{:S(2)}, u32[]{:S(2)}) collective-permute-start(bf16[272,256]{1,0:T(8,128)(2,1)S(1)} %shard_map.131.refs_0_), channel_id=1, source_target_pairs={{0,1},{1,0},{2,3},{3,2},{4,5},{5,4},{6,7},{7,6},{8,9},{9,8},{10,11... | collective-permute-start | bytes 417800 | tf_op jit(solution)/shard_map/ppermute | solution.py:342
  107.2 3.7 %collective-permute-start.22 = (bf16[272,256]{1,0:T(8,128)(2,1)S(1)}, bf16[272,256]{1,0:T(8,128)(2,1)S(1)}, u32[]{:S(2)}, u32[]{:S(2)}) collective-permute-start(bf16[272,256]{1,0:T(8,128)(2,1)S(1)} %collective-permute-done.18.refs_3_), channel_id=1, source_target_pairs={{0,1},{1,0},{2,3},{3,2},{4,5},{5,4},{6,7},{7,6},{8,9},{9,8},{10,11... | collective-permute-start | bytes 417800 | tf_op jit(solution)/shard_map/ppermute | solution.py:342
  113.1 1.6 %copy-done.2 = f32[2048,256]{1,0:T(8,128)S(1)} copy-done((f32[2048,256]{1,0:T(8,128)S(1)}, f32[2048,256]{1,0:T(8,128)}, u32[]{:S(2)}) %copy-start.2) | copy-done | bytes 2097176
  114.7 2.1 %shard_map.132 = (f32[2048,256]{1,0:T(8,128)}, f32[16,128]{1,0:T(8,128)}) custom-call(s32[1]{0:T(128)} %bitcast.4.place_ref, f32[2048,256]{1,0:T(8,128)S(1)} %copy-done.2, f32[16,128]{1,0:T(8,128)S(1)} %bitcast.10, bf16[272,256]{1,0:T(8,128)(2,1)S(1)} %shard_map.131.refs_0_, bf16[272,256]{1,0:T(8,128)(2,1)S(1)} %collective-permute-done.16.refs_1_, ...), custom_call_target="tpu_custom_call" | custom-call | flops 4194304 | bytes 5242880 | tf_op jit(solution)/shard_map/pallas_call | solution.py:303
  (73 shorter events, 16.2 us)
Async XLA Ops:
  2.6 17.9 %collective-permute-start = (bf16[512,256]{1,0:T(8,128)(2,1)}, bf16[512,256]{1,0:T(8,128)(2,1)S(1)}, u32[]{:S(2)}, u32[]{:S(2)}) collective-permute-start(bf16[512,256]{1,0:T(8,128)(2,1)} %dynamic-slice_convert_fusion), channel_id=1, source_target_pairs={{6,0},{7,1},{4,2},{5,3},{10,4},{11,5},{8,6},{9,7},{14,8},{15,9},{1... | collective-permute-start | bytes 786440 | tf_op jit(solution)/shard_map/ppermute | solution.py:347
  20.5 2.2 %collective-permute-start.2 = (bf16[512,256]{1,0:T(8,128)(2,1)S(1)}, bf16[512,256]{1,0:T(8,128)(2,1)S(1)}, u32[]{:S(2)}, u32[]{:S(2)}) collective-permute-start(bf16[512,256]{1,0:T(8,128)(2,1)S(1)} %collective-permute-done.near_ref), channel_id=1, source_target_pairs={{0,1},{1,0},{2,3},{3,2},{4,5},{5,4},{6,7},{7,6},{8,9},{9,8},{10,11... | collective-permute-start | bytes 786440 | tf_op jit(solution)/shard_map/ppermute | solution.py:342
  21.6 7.9 %collective-permute-start.1 = (bf16[512,256]{1,0:T(8,128)(2,1)S(1)}, bf16[512,256]{1,0:T(8,128)(2,1)S(1)}, u32[]{:S(2)}, u32[]{:S(2)}) collective-permute-start(bf16[512,256]{1,0:T(8,128)(2,1)S(1)} %collective-permute-done.near_ref), channel_id=1, source_target_pairs={{0,2},{1,3},{2,0},{3,1},{4,6},{5,7},{6,4},{7,5},{8,10},{9,11},{10,... | collective-permute-start | bytes 786440 | tf_op jit(solution)/shard_map/ppermute | solution.py:342
  29.5 2.0 %collective-permute-start.3 = (bf16[512,256]{1,0:T(8,128)(2,1)S(1)}, bf16[512,256]{1,0:T(8,128)(2,1)S(1)}, u32[]{:S(2)}, u32[]{:S(2)}) collective-permute-start(bf16[512,256]{1,0:T(8,128)(2,1)S(1)} %collective-permute-done.1.near_ref), channel_id=1, source_target_pairs={{0,1},{1,0},{2,3},{3,2},{4,5},{5,4},{6,7},{7,6},{8,9},{9,8},{10,11... | collective-permute-start | bytes 786440 | tf_op jit(solution)/shard_map/ppermute | solution.py:342
  39.9 2.3 %collective-permute-start.5 = (bf16[1024,256]{1,0:T(8,128)(2,1)S(1)}, bf16[1024,256]{1,0:T(8,128)(2,1)S(1)}, u32[]{:S(2)}, u32[]{:S(2)}) collective-permute-start(bf16[1024,256]{1,0:T(8,128)(2,1)S(1)} %get-tuple-element.64), channel_id=1, source_target_pairs={{0,1},{1,0},{2,3},{3,2},{4,5},{5,4},{6,7},{7,6},{8,9},{9,8},{10,11... | collective-permute-start | bytes 1572872 | tf_op jit(solution)/shard_map/ppermute | solution.py:342
  40.4 2.6 %collective-permute-start.6 = (bf16[1024,256]{1,0:T(8,128)(2,1)S(1)}, bf16[1024,256]{1,0:T(8,128)(2,1)S(1)}, u32[]{:S(2)}, u32[]{:S(2)}) collective-permute-start(bf16[1024,256]{1,0:T(8,128)(2,1)S(1)} %get-tuple-element.67), channel_id=1, source_target_pairs={{0,1},{1,0},{2,3},{3,2},{4,5},{5,4},{6,7},{7,6},{8,9},{9,8},{10,11... | collective-permute-start | bytes 1572872 | tf_op jit(solution)/shard_map/ppermute | solution.py:342
  41.8 2.1 %collective-permute-start.4 = (bf16[1024,256]{1,0:T(8,128)(2,1)S(1)}, bf16[1024,256]{1,0:T(8,128)(2,1)S(1)}, u32[]{:S(2)}, u32[]{:S(2)}) collective-permute-start(bf16[1024,256]{1,0:T(8,128)(2,1)S(1)} %get-tuple-element.58), channel_id=1, source_target_pairs={{0,1},{1,0},{2,3},{3,2},{4,5},{5,4},{6,7},{7,6},{8,9},{9,8},{10,11... | collective-permute-start | bytes 1572872 | tf_op jit(solution)/shard_map/ppermute | solution.py:342
  44.0 5.1 %collective-permute-start.7 = (bf16[256,256]{1,0:T(8,128)(2,1)S(1)}, bf16[256,256]{1,0:T(8,128)(2,1)S(1)}, u32[]{:S(2)}, u32[]{:S(2)}) collective-permute-start(bf16[256,256]{1,0:T(8,128)(2,1)S(1)} %get-tuple-element.71), channel_id=1, source_target_pairs={{0,2},{1,3},{2,0},{3,1},{4,6},{5,7},{6,4},{7,5},{8,10},{9,11},{10,... | collective-permute-start | bytes 393224 | tf_op jit(solution)/shard_map/ppermute | solution.py:342
  44.1 6.2 %collective-permute-start.8 = (bf16[256,256]{1,0:T(8,128)(2,1)S(1)}, bf16[256,256]{1,0:T(8,128)(2,1)S(1)}, u32[]{:S(2)}, u32[]{:S(2)}) collective-permute-start(bf16[256,256]{1,0:T(8,128)(2,1)S(1)} %get-tuple-element.72), channel_id=1, source_target_pairs={{0,4},{1,5},{2,6},{3,7},{4,0},{5,1},{6,2},{7,3},{8,12},{9,13},{10,... | collective-permute-start | bytes 393224 | tf_op jit(solution)/shard_map/ppermute | solution.py:342
  44.2 9.7 %collective-permute-start.9 = (bf16[256,256]{1,0:T(8,128)(2,1)S(1)}, bf16[256,256]{1,0:T(8,128)(2,1)S(1)}, u32[]{:S(2)}, u32[]{:S(2)}) collective-permute-start(bf16[256,256]{1,0:T(8,128)(2,1)S(1)} %get-tuple-element.73), channel_id=1, source_target_pairs={{0,6},{1,7},{2,4},{3,5},{4,2},{5,3},{6,0},{7,1},{8,14},{9,15},{10,... | collective-permute-start | bytes 393224 | tf_op jit(solution)/shard_map/ppermute | solution.py:342
  48.0 26.6 %collective-permute-start.10 = (bf16[512,256]{1,0:T(8,128)(2,1)}, bf16[512,256]{1,0:T(8,128)(2,1)S(1)}, u32[]{:S(2)}, u32[]{:S(2)}) collective-permute-start(bf16[512,256]{1,0:T(8,128)(2,1)} %get-tuple-element.75), channel_id=1, source_target_pairs={{0,2},{1,3},{2,0},{3,1},{4,6},{5,7},{6,4},{7,5},{8,10},{9,11},{10,... | collective-permute-start | bytes 786440 | tf_op jit(solution)/shard_map/ppermute | solution.py:342
  48.0 26.6 %collective-permute-start.11 = (bf16[512,256]{1,0:T(8,128)(2,1)}, bf16[512,256]{1,0:T(8,128)(2,1)S(1)}, u32[]{:S(2)}, u32[]{:S(2)}) collective-permute-start(bf16[512,256]{1,0:T(8,128)(2,1)} %get-tuple-element.76), channel_id=1, source_target_pairs={{252,0},{253,1},{254,2},{255,3},{0,4},{1,5},{2,6},{3,7},{4,8},{5,9... | collective-permute-start | bytes 786440 | tf_op jit(solution)/shard_map/ppermute | solution.py:347
  49.2 25.5 %collective-permute-start.12 = (bf16[512,256]{1,0:T(8,128)(2,1)}, bf16[512,256]{1,0:T(8,128)(2,1)}, u32[]{:S(2)}, u32[]{:S(2)}) collective-permute-start(bf16[512,256]{1,0:T(8,128)(2,1)} %get-tuple-element.77), channel_id=1, source_target_pairs={{254,0},{255,1},{252,2},{253,3},{2,4},{3,5},{0,6},{1,7},{6,8},{7,9... | collective-permute-start | bytes 786440 | tf_op jit(solution)/shard_map/ppermute | solution.py:347
  54.7 29.3 %all-to-all-start = ((bf16[32,8,256]{2,1,0:T(8,128)(2,1)}), bf16[32,8,256]{2,1,0:T(8,128)(2,1)S(1)}, u32[]{:S(2)}, u32[]{:S(2)}) async-start(bf16[32,8,256]{2,1,0:T(8,128)(2,1)} %bitcast.2), calls=%async_computation | async-start | bytes 262144 | tf_op jit(solution)/shard_map/all_to_all | solution.py:338
  84.0 7.2 %collective-permute-start.13 = (bf16[528,256]{1,0:T(8,128)(2,1)S(1)}, bf16[528,256]{1,0:T(8,128)(2,1)S(1)}, u32[]{:S(2)}, u32[]{:S(2)}) collective-permute-start(bf16[528,256]{1,0:T(8,128)(2,1)S(1)} %shard_map.128.refs_0_), channel_id=1, source_target_pairs={{0,2},{1,3},{2,0},{3,1},{4,6},{5,7},{6,4},{7,5},{8,10},{9,11},{10,... | collective-permute-start | bytes 811016 | tf_op jit(solution)/shard_map/ppermute | solution.py:342
  84.7 14.6 %all-to-all-start.1 = ((f32[32,8,256]{2,1,0:T(8,128)}), f32[32,8,256]{2,1,0:T(8,128)S(1)}, u32[]{:S(2)}, u32[]{:S(2)}) async-start(f32[32,8,256]{2,1,0:T(8,128)} %shard_map.130), calls=%async_computation.1 | async-start | bytes 524288 | tf_op jit(solution)/shard_map/all_to_all | solution.py:338
  88.7 4.1 %collective-permute-start.14 = (bf16[528,256]{1,0:T(8,128)(2,1)S(1)}, bf16[528,256]{1,0:T(8,128)(2,1)S(1)}, u32[]{:S(2)}, u32[]{:S(2)}) collective-permute-start(bf16[528,256]{1,0:T(8,128)(2,1)S(1)} %shard_map.128.refs_0_), channel_id=1, source_target_pairs={{0,1},{1,0},{2,3},{3,2},{4,5},{5,4},{6,7},{7,6},{8,9},{9,8},{10,11... | collective-permute-start | bytes 811016 | tf_op jit(solution)/shard_map/ppermute | solution.py:342
  91.1 3.0 %collective-permute-start.15 = (bf16[528,256]{1,0:T(8,128)(2,1)S(1)}, bf16[528,256]{1,0:T(8,128)(2,1)}, u32[]{:S(2)}, u32[]{:S(2)}) collective-permute-start(bf16[528,256]{1,0:T(8,128)(2,1)S(1)} %collective-permute-done.13.refs_1_), channel_id=1, source_target_pairs={{0,1},{1,0},{2,3},{3,2},{4,5},{5,4},{6,7},{7,6},{8,9},{9,8},{10,11... | collective-permute-start | bytes 811016 | tf_op jit(solution)/shard_map/ppermute | solution.py:342
  99.4 7.8 %collective-permute-start.18 = (bf16[272,256]{1,0:T(8,128)(2,1)S(1)}, bf16[272,256]{1,0:T(8,128)(2,1)S(1)}, u32[]{:S(2)}, u32[]{:S(2)}) collective-permute-start(bf16[272,256]{1,0:T(8,128)(2,1)S(1)} %shard_map.131.refs_0_), channel_id=1, source_target_pairs={{0,6},{1,7},{2,4},{3,5},{4,2},{5,3},{6,0},{7,1},{8,14},{9,15},{10,... | collective-permute-start | bytes 417800 | tf_op jit(solution)/shard_map/ppermute | solution.py:342
  99.5 11.3 %collective-permute-start.17 = (bf16[272,256]{1,0:T(8,128)(2,1)S(1)}, bf16[272,256]{1,0:T(8,128)(2,1)S(1)}, u32[]{:S(2)}, u32[]{:S(2)}) collective-permute-start(bf16[272,256]{1,0:T(8,128)(2,1)S(1)} %shard_map.131.refs_0_), channel_id=1, source_target_pairs={{0,4},{1,5},{2,6},{3,7},{4,0},{5,1},{6,2},{7,3},{8,12},{9,13},{10,... | collective-permute-start | bytes 417800 | tf_op jit(solution)/shard_map/ppermute | solution.py:342
  102.8 8.1 %collective-permute-start.16 = (bf16[272,256]{1,0:T(8,128)(2,1)S(1)}, bf16[272,256]{1,0:T(8,128)(2,1)S(1)}, u32[]{:S(2)}, u32[]{:S(2)}) collective-permute-start(bf16[272,256]{1,0:T(8,128)(2,1)S(1)} %shard_map.131.refs_0_), channel_id=1, source_target_pairs={{0,2},{1,3},{2,0},{3,1},{4,6},{5,7},{6,4},{7,5},{8,10},{9,11},{10,... | collective-permute-start | bytes 417800 | tf_op jit(solution)/shard_map/ppermute | solution.py:342
  102.8 9.3 %collective-permute-start.19 = (bf16[272,256]{1,0:T(8,128)(2,1)S(1)}, bf16[272,256]{1,0:T(8,128)(2,1)S(1)}, u32[]{:S(2)}, u32[]{:S(2)}) collective-permute-start(bf16[272,256]{1,0:T(8,128)(2,1)S(1)} %shard_map.131.refs_0_), channel_id=1, source_target_pairs={{0,1},{1,0},{2,3},{3,2},{4,5},{5,4},{6,7},{7,6},{8,9},{9,8},{10,11... | collective-permute-start | bytes 417800 | tf_op jit(solution)/shard_map/ppermute | solution.py:342
  107.2 4.9 %collective-permute-start.22 = (bf16[272,256]{1,0:T(8,128)(2,1)S(1)}, bf16[272,256]{1,0:T(8,128)(2,1)S(1)}, u32[]{:S(2)}, u32[]{:S(2)}) collective-permute-start(bf16[272,256]{1,0:T(8,128)(2,1)S(1)} %collective-permute-done.18.refs_3_), channel_id=1, source_target_pairs={{0,1},{1,0},{2,3},{3,2},{4,5},{5,4},{6,7},{7,6},{8,9},{9,8},{10,11... | collective-permute-start | bytes 417800 | tf_op jit(solution)/shard_map/ppermute | solution.py:342
  110.9 2.2 %collective-permute-start.20 = (bf16[272,256]{1,0:T(8,128)(2,1)S(1)}, bf16[272,256]{1,0:T(8,128)(2,1)S(1)}, u32[]{:S(2)}, u32[]{:S(2)}) collective-permute-start(bf16[272,256]{1,0:T(8,128)(2,1)S(1)} %collective-permute-done.16.refs_1_), channel_id=1, source_target_pairs={{0,1},{1,0},{2,3},{3,2},{4,5},{5,4},{6,7},{7,6},{8,9},{9,8},{10,11... | collective-permute-start | bytes 417800 | tf_op jit(solution)/shard_map/ppermute | solution.py:342
  (14 other events, 213.6 us)

commit v7 on v6

--- a/solution.py
+++ b/solution.py
@@ -434,33 +434,36 @@
 
     rel_recv = swap(rel_send, CORE)
     src_own, src_away = add_split([src_keep, src_recv], 2, own=F32)
-    dst_own, dst_away = add_split([dst_keep, dst_recv], 2)
+    dst_away, dst_own = add_split([dst_keep, dst_recv], 2)
     parts = add_split([rel_keep, rel_recv], 4, own=F32)
     parts, src_away, dst_own, dst_away = lax.optimization_barrier(
         (parts, src_away, dst_own, dst_away)
     )
     recv = [swap(part, mask) for part, mask in zip(parts[1:], X_MASKS)]
+    dst_other = swap(dst_away, XL)
     src_other = swap(src_away, XL)
-    dst_first = shift(dst_own, 1, 0)
-    dst_second = shift(dst_away, 1, XL)
+    recv, dst_other = lax.optimization_barrier((recv, dst_other))
     (mine,) = add_split([parts[0], *recv], 1)
 
     landed = spread(mine.reshape(32, 8, D))
-    ent_own = sum_with_means([src_own, src_other, dst_first, dst_second])
+    (dst_sum,) = add_split([dst_own, dst_other], 1)
+    dst_total = shift(dst_sum, 1, XL)
+    ent_own = sum_with_means([src_own, src_other, dst_total])
     landed, ent_own = lax.optimization_barrier((landed, ent_own))
     summed = sum_rows(landed)
+    total = spread(summed)
     ent_xl = swap(ent_own, XL)
     ent_core = [swap(ent_own, CORE), swap(ent_xl, CORE)]
     place = (core * 2 + xl).reshape(1)
     new_entities, new_entity_acc = update(
         entities, entity_acc, [ent_own, ent_xl, *ent_core], place
     )
-    total, new_entity_acc = lax.optimization_barrier((spread(summed), new_entity_acc))
     quarter = sum_with_means([total.reshape(256, D)])
     recv = [swap(quarter, mask) for mask in X_MASKS]
 
     pieces = [quarter, *recv]
     pieces = pieces + [swap(piece, CORE) for piece in pieces]
+    pieces, new_entity_acc = lax.optimization_barrier((pieces, new_entity_acc))
     place = (core * 4 + x).reshape(1)
     new_relations, new_relation_acc = update(relations, relation_acc, pieces, place)
     return (new_entities, new_entity_acc, new_relations, new_relation_acc)

time: 117 us -> 114 us (0.974)
  starting transfers between devices: 59.8 us -> 51.7 us
  waiting for transfers between devices: 20.1 us -> 26.6 us
  local copies, waits for them, and re-layouts: 6.94 us -> 5.35 us
    all_to_all x2, starting transfers between devices: 23.9 us -> 10.1 us  [spread(): lax.all_to_all(parts, 'blk', 0, 0, axis_index_groups=groups, tiled=True)]
    all_to_all x2, waiting for transfers between devices: 10.2 us -> 16.1 us  [spread(): lax.all_to_all(parts, 'blk', 0, 0, axis_index_groups=groups, tiled=True)]
    ppermute x3 -> x2, starting transfers between devices: 12.2 us -> 15.6 us  [shift(): return lax.ppermute(x, AXES, route)]
    ppermute x20 -> x21, starting transfers between devices: 23.6 us -> 26 us  [swap(): return lax.ppermute(x, AXES, [(i, i ^ mask) for i in range(256)])]
    unnamed x26, local copies, waits for them, and re-layouts: 4.95 us -> 3.36 us
    pallas_call x2, Pallas kernels: 5.18 us -> 6.51 us  [update(): pl.pallas_call(functools.partial(update_kernel, len(pieces)), out_shape=[...]
    ppermute x20 -> x21, waiting for transfers between devices: 9.91 us -> 10.4 us  [swap(): return lax.ppermute(x, AXES, [(i, i ^ mask) for i in range(256)])]
    pallas_call x4 -> x5, Pallas kernels: 2.44 us -> 2.43 us  [add_split(): call(functools.partial(add_split_kernel, len(parts), n_out), shapes, 0, l...]
  transfers between devices with their start and end apart: 25 -> 25, of which waited for: 10 -> 9; matrix products, arithmetic and copies ran while one was open for 2% -> 2% of each run, Pallas kernels for 13% -> 13%
where the time goes in v7:
time: 114 us
  starting transfers between devices  51.7 us (45%)
  Pallas kernels  26.9 us (24%)
  waiting for transfers between devices  26.6 us (23%)
  local copies, waits for them, and re-layouts  5.35 us (5%)
  between operations  1.85 us (2%)
  other arithmetic  1.75 us (2%)
    ppermute x21, starting transfers between devices, swap(): return lax.ppermute(x, AXES, [(i, i ^ mask) for i in range(256)])  26 us
    all_to_all x2, waiting for transfers between devices, spread(): lax.all_to_all(parts, 'blk', 0, 0, axis_index_groups=groups, tiled=True)  16.1 us
    ppermute x2, starting transfers between devices, shift(): return lax.ppermute(x, AXES, route)  15.6 us
    ppermute x21, waiting for transfers between devices, swap(): return lax.ppermute(x, AXES, [(i, i ^ mask) for i in range(256)])  10.4 us
    all_to_all x2, starting transfers between devices, spread(): lax.all_to_all(parts, 'blk', 0, 0, axis_index_groups=groups, tiled=True)  10.1 us
    pallas_call x1, Pallas kernels, shards(): call(score_kernel, [kept, sent, kept, sent, slots_low], 1, 10, [pltpu.VME...  8.45 us
    pallas_call x2, Pallas kernels, update(): pl.pallas_call(functools.partial(update_kernel, len(pieces)), out_shape=[...  6.51 us
    pallas_call x1, Pallas kernels, shards(): call(gather_kernel, [jax.ShapeDtypeStruct((EDGES, D), BF16), jax.ShapeDty...  4.91 us
  transfers between devices with their start and end apart: 25, of which 9 were waited for; matrix products, arithmetic and copies ran while one was open for 2% of the time, Pallas kernels for 13%

profile of v7, /device:TPU:1, one launch (start us, length us, event | category | flops | bytes accessed | tf_op | source)
XLA Modules:
  0.0 114.1 jit_solution(12059878271918333354)
XLA Ops:
  0.7 1.9 %dynamic-slice_convert_fusion = bf16[512,256]{1,0:T(8,128)(2,1)} fusion(f32[2048,256]{1,0:T(8,128)} %rows_ref.2, s32[]{:T(128)S(6)} %select_n.21), kind=kLoop, calls=%fused_computation | loop fusion | bytes 524292 | tf_op jit(solution)/shard_map/convert_element_type | solution.py:363
  2.6 11.1 %collective-permute-start = (bf16[512,256]{1,0:T(8,128)(2,1)}, bf16[512,256]{1,0:T(8,128)(2,1)S(1)}, u32[]{:S(2)}, u32[]{:S(2)}) collective-permute-start(bf16[512,256]{1,0:T(8,128)(2,1)} %dynamic-slice_convert_fusion), channel_id=1, source_target_pairs={{6,0},{7,1},{4,2},{5,3},{10,4},{11,5},{8,6},{9,7},{14,8},{15,9},{1... | collective-permute-start | bytes 786440 | tf_op jit(solution)/shard_map/ppermute | solution.py:347
  13.7 1.7 %convert_element_type.7.low_ref = bf16[2048,256]{1,0:T(8,128)(2,1)S(1)} convert(f32[2048,256]{1,0:T(8,128)} %rows_ref.2) | non-fusion elementwise | flops 524288 | bytes 3145728 | tf_op jit(solution)/shard_map/convert_element_type | solution.py:361
  15.6 4.9 %shard_map.120 = (bf16[1024,256]{1,0:T(8,128)(2,1)S(1)}, f32[1024,256]{1,0:T(8,128)S(1)}, f32[1024,256]{1,0:T(8,128)S(1)}, f32[4,16,128]{2,1,0:T(8,128)S(1)}) custom-call(s32[8,1024]{1,0:T(8,128)S(1)} %concatenate.3.ids_ref, s32[4,1024]{1,0:T(4,128)S(1)} %reshape.37.negs_ref, bf16[2048,256]{1,0:T(8,128)(2,1)S(1)} %convert_element_type.7.low_ref, ...), custom_call_target="tpu_custom_call" | custom-call | flops 4294967296 | bytes 4194304 | tf_op jit(solution)/shard_map/pallas_call | solution.py:377
  21.6 1.2 %collective-permute-done.2.far_ref = bf16[512,256]{1,0:T(8,128)(2,1)S(1)} collective-permute-done((bf16[512,256]{1,0:T(8,128)(2,1)S(1)}, bf16[512,256]{1,0:T(8,128)(2,1)S(1)}, u32[]{:S(2)}, u32[]{:S(2)}) %collective-permute-start.2) | collective-permute-done | bytes 262176 | tf_op jit(solution)/shard_map/ppermute | solution.py:342
  22.7 2.2 %shard_map.121 = (bf16[1024,1024]{1,0:T(8,128)(2,1)S(1)}, f32[1024,256]{1,0:T(8,128)S(1)}, f32[1024,256]{1,0:T(8,128)S(1)}) custom-call(s32[8,1024]{1,0:T(8,128)S(1)} %concatenate.3.ids_ref, bf16[512,256]{1,0:T(8,128)(2,1)S(1)} %collective-permute-done.near_ref, bf16[512,256]{1,0:T(8,128)(2,1)S(1)} %collective-permute-done.2.far_ref, ...), custom_call_target="tpu_custom_call" | custom-call | flops 1610612736 | bytes 4194304 | tf_op jit(solution)/shard_map/pallas_call | solution.py:400
  25.0 1.3 %copy-done.5 = bf16[1024,1024]{1,0:T(8,128)(2,1)} copy-done((bf16[1024,1024]{1,0:T(8,128)(2,1)}, bf16[1024,1024]{1,0:T(8,128)(2,1)S(1)}, u32[]{:S(2)}) %copy-start.5) | copy-done | bytes 2097176
  31.5 8.4 %shard_map.122 = (f32[1024,256]{1,0:T(8,128)S(1)}, bf16[1024,256]{1,0:T(8,128)(2,1)S(1)}, f32[1024,256]{1,0:T(8,128)S(1)}, bf16[1024,256]{1,0:T(8,128)(2,1)S(1)}, bf16[1024,256]{1,0:T(8,128)(2,1)S(1)}) custom-call(s32[1,1]{1,0:T(1,128)S(6)} %copy.13.count_ref, s32[8,1024]{1,0:T(8,128)S(1)} %concatenate.3.ids_ref, ...), custom_call_target="tpu_custom_call" | custom-call | flops 4831838208 | bytes 8388608 | tf_op jit(solution)/shard_map/pallas_call | solution.py:410
  40.5 1.2 %shard_map.123 = (f32[1024,256]{1,0:T(8,128)S(1)}, bf16[1024,256]{1,0:T(8,128)(2,1)S(1)}) custom-call(s32[8,1024]{1,0:T(8,128)S(1)} %concatenate.3.ids_ref, bf16[1024,256]{1,0:T(8,128)(2,1)S(1)} %get-tuple-element.67.gr_ref), custom_call_target="tpu_custom_call" | custom-call | flops 1073741824 | bytes 2097152 | tf_op jit(solution)/shard_map/pallas_call | solution.py:426
  44.0 1.5 %collective-permute-start.7 = (bf16[256,256]{1,0:T(8,128)(2,1)S(1)}, bf16[256,256]{1,0:T(8,128)(2,1)S(1)}, u32[]{:S(2)}, u32[]{:S(2)}) collective-permute-start(bf16[256,256]{1,0:T(8,128)(2,1)S(1)} %get-tuple-element.82), channel_id=1, source_target_pairs={{0,2},{1,3},{2,0},{3,1},{4,6},{5,7},{6,4},{7,5},{8,10},{9,11},{10,... | collective-permute-start | bytes 393224 | tf_op jit(solution)/shard_map/ppermute | solution.py:342
  45.5 2.5 %collective-permute-start.9 = (bf16[256,256]{1,0:T(8,128)(2,1)S(1)}, bf16[256,256]{1,0:T(8,128)(2,1)S(1)}, u32[]{:S(2)}, u32[]{:S(2)}) collective-permute-start(bf16[256,256]{1,0:T(8,128)(2,1)S(1)} %get-tuple-element.84), channel_id=1, source_target_pairs={{0,6},{1,7},{2,4},{3,5},{4,2},{5,3},{6,0},{7,1},{8,14},{9,15},{10,... | collective-permute-start | bytes 393224 | tf_op jit(solution)/shard_map/ppermute | solution.py:342
  48.1 6.2 %collective-permute-done.7.refs_1_ = bf16[256,256]{1,0:T(8,128)(2,1)S(1)} collective-permute-done((bf16[256,256]{1,0:T(8,128)(2,1)S(1)}, bf16[256,256]{1,0:T(8,128)(2,1)S(1)}, u32[]{:S(2)}, u32[]{:S(2)}) %collective-permute-start.7) | collective-permute-done | bytes 131104 | tf_op jit(solution)/shard_map/ppermute | solution.py:342
  55.7 4.6 %collective-permute-start.12 = (bf16[512,256]{1,0:T(8,128)(2,1)}, bf16[512,256]{1,0:T(8,128)(2,1)S(1)}, u32[]{:S(2)}, u32[]{:S(2)}) collective-permute-start(bf16[512,256]{1,0:T(8,128)(2,1)} %shard_map.128), channel_id=1, source_target_pairs={{254,0},{255,1},{252,2},{253,3},{2,4},{3,5},{0,6},{1,7},{6,8},{7,9... | collective-permute-start | bytes 786440 | tf_op jit(solution)/shard_map/ppermute | solution.py:347
  61.0 6.1 %all-to-all-start = ((bf16[32,8,256]{2,1,0:T(8,128)(2,1)}), bf16[32,8,256]{2,1,0:T(8,128)(2,1)S(1)}, u32[]{:S(2)}, u32[]{:S(2)}) async-start(bf16[32,8,256]{2,1,0:T(8,128)(2,1)} %bitcast.2), calls=%async_computation | async-start | bytes 262144 | tf_op jit(solution)/shard_map/all_to_all | solution.py:338
  67.5 9.1 %all-to-all-done.parts_ref = bf16[32,8,256]{2,1,0:T(8,128)(2,1)S(1)} async-done(((bf16[32,8,256]{2,1,0:T(8,128)(2,1)}), bf16[32,8,256]{2,1,0:T(8,128)(2,1)S(1)}, u32[]{:S(2)}, u32[]{:S(2)}) %all-to-all-start) | async-done | bytes 131104 | tf_op jit(solution)/shard_map/all_to_all | solution.py:338
  77.3 4.0 %all-to-all-start.1 = ((f32[32,8,256]{2,1,0:T(8,128)}), f32[32,8,256]{2,1,0:T(8,128)S(1)}, u32[]{:S(2)}, u32[]{:S(2)}) async-start(f32[32,8,256]{2,1,0:T(8,128)} %shard_map.131), calls=%async_computation.1 | async-start | bytes 524288 | tf_op jit(solution)/shard_map/all_to_all | solution.py:338
  81.4 3.5 %collective-permute-start.14 = (bf16[528,256]{1,0:T(8,128)(2,1)S(1)}, bf16[528,256]{1,0:T(8,128)(2,1)S(1)}, u32[]{:S(2)}, u32[]{:S(2)}) collective-permute-start(bf16[528,256]{1,0:T(8,128)(2,1)S(1)} %shard_map.129.refs_0_), channel_id=1, source_target_pairs={{0,1},{1,0},{2,3},{3,2},{4,5},{5,4},{6,7},{7,6},{8,9},{9,8},{10,11... | collective-permute-start | bytes 811016 | tf_op jit(solution)/shard_map/ppermute | solution.py:342
  84.9 7.0 %all-to-all-done.1 = f32[32,8,256]{2,1,0:T(8,128)S(1)} async-done(((f32[32,8,256]{2,1,0:T(8,128)}), f32[32,8,256]{2,1,0:T(8,128)S(1)}, u32[]{:S(2)}, u32[]{:S(2)}) %all-to-all-start.1) | async-done | bytes 262176 | tf_op jit(solution)/shard_map/all_to_all | solution.py:338
  92.0 3.5 %collective-permute-start.18 = (bf16[272,256]{1,0:T(8,128)(2,1)S(1)}, bf16[272,256]{1,0:T(8,128)(2,1)S(1)}, u32[]{:S(2)}, u32[]{:S(2)}) collective-permute-start(bf16[272,256]{1,0:T(8,128)(2,1)S(1)} %shard_map.132.refs_0_), channel_id=1, source_target_pairs={{0,6},{1,7},{2,4},{3,5},{4,2},{5,3},{6,0},{7,1},{8,14},{9,15},{10,... | collective-permute-start | bytes 417800 | tf_op jit(solution)/shard_map/ppermute | solution.py:342
  96.3 5.5 %collective-permute-start.15 = (bf16[528,256]{1,0:T(8,128)(2,1)S(1)}, bf16[528,256]{1,0:T(8,128)(2,1)}, u32[]{:S(2)}, u32[]{:S(2)}) collective-permute-start(bf16[528,256]{1,0:T(8,128)(2,1)S(1)} %collective-permute-done.13.refs_1_), channel_id=1, source_target_pairs={{0,1},{1,0},{2,3},{3,2},{4,5},{5,4},{6,7},{7,6},{8,9},{9,8},{10,11... | collective-permute-start | bytes 811016 | tf_op jit(solution)/shard_map/ppermute | solution.py:342
  101.8 3.0 %collective-permute-start.22 = (bf16[272,256]{1,0:T(8,128)(2,1)S(1)}, bf16[272,256]{1,0:T(8,128)(2,1)}, u32[]{:S(2)}, u32[]{:S(2)}) collective-permute-start(bf16[272,256]{1,0:T(8,128)(2,1)S(1)} %collective-permute-done.18.refs_3_), channel_id=1, source_target_pairs={{0,1},{1,0},{2,3},{3,2},{4,5},{5,4},{6,7},{7,6},{8,9},{9,8},{10,11... | collective-permute-start | bytes 417800 | tf_op jit(solution)/shard_map/ppermute | solution.py:342
  104.9 2.5 %collective-permute-start.21 = (bf16[272,256]{1,0:T(8,128)(2,1)S(1)}, bf16[272,256]{1,0:T(8,128)(2,1)}, u32[]{:S(2)}, u32[]{:S(2)}) collective-permute-start(bf16[272,256]{1,0:T(8,128)(2,1)S(1)} %collective-permute-done.17.refs_2_), channel_id=1, source_target_pairs={{0,1},{1,0},{2,3},{3,2},{4,5},{5,4},{6,7},{7,6},{8,9},{9,8},{10,11... | collective-permute-start | bytes 417800 | tf_op jit(solution)/shard_map/ppermute | solution.py:342
  107.4 3.2 %shard_map.130 = (f32[2048,256]{1,0:T(8,128)}, f32[16,128]{1,0:T(8,128)}) custom-call(s32[1]{0:T(128)} %bitcast.place_ref, f32[2048,256]{1,0:T(8,128)S(1)} %copy-done, f32[16,128]{1,0:T(8,128)S(1)} %bitcast.9, bf16[528,256]{1,0:T(8,128)(2,1)S(1)} %shard_map.129.refs_0_, bf16[528,256]{1,0:T(8,128)(2,1)S(1)} %collective-permute-done.13.refs_1_, ...), custom_call_target="tpu_custom_call" | custom-call | flops 4194304 | bytes 5242880 | tf_op jit(solution)/shard_map/pallas_call | solution.py:303
  110.6 3.3 %shard_map.133 = (f32[2048,256]{1,0:T(8,128)}, f32[16,128]{1,0:T(8,128)}) custom-call(s32[1]{0:T(128)} %bitcast.5.place_ref, f32[2048,256]{1,0:T(8,128)S(1)} %copy-done.2, f32[16,128]{1,0:T(8,128)S(1)} %bitcast.10, bf16[272,256]{1,0:T(8,128)(2,1)S(1)} %shard_map.132.refs_0_, bf16[272,256]{1,0:T(8,128)(2,1)} %collective-permute-done.16.refs_1_, ...), custom_call_target="tpu_custom_call" | custom-call | flops 4194304 | bytes 5242880 | tf_op jit(solution)/shard_map/pallas_call | solution.py:303
  (74 shorter events, 12.9 us)
Async XLA Ops:
  2.6 17.9 %collective-permute-start = (bf16[512,256]{1,0:T(8,128)(2,1)}, bf16[512,256]{1,0:T(8,128)(2,1)S(1)}, u32[]{:S(2)}, u32[]{:S(2)}) collective-permute-start(bf16[512,256]{1,0:T(8,128)(2,1)} %dynamic-slice_convert_fusion), channel_id=1, source_target_pairs={{6,0},{7,1},{4,2},{5,3},{10,4},{11,5},{8,6},{9,7},{14,8},{15,9},{1... | collective-permute-start | bytes 786440 | tf_op jit(solution)/shard_map/ppermute | solution.py:347
  20.5 2.2 %collective-permute-start.2 = (bf16[512,256]{1,0:T(8,128)(2,1)S(1)}, bf16[512,256]{1,0:T(8,128)(2,1)S(1)}, u32[]{:S(2)}, u32[]{:S(2)}) collective-permute-start(bf16[512,256]{1,0:T(8,128)(2,1)S(1)} %collective-permute-done.near_ref), channel_id=1, source_target_pairs={{0,1},{1,0},{2,3},{3,2},{4,5},{5,4},{6,7},{7,6},{8,9},{9,8},{10,11... | collective-permute-start | bytes 786440 | tf_op jit(solution)/shard_map/ppermute | solution.py:342
  21.6 7.9 %collective-permute-start.1 = (bf16[512,256]{1,0:T(8,128)(2,1)S(1)}, bf16[512,256]{1,0:T(8,128)(2,1)S(1)}, u32[]{:S(2)}, u32[]{:S(2)}) collective-permute-start(bf16[512,256]{1,0:T(8,128)(2,1)S(1)} %collective-permute-done.near_ref), channel_id=1, source_target_pairs={{0,2},{1,3},{2,0},{3,1},{4,6},{5,7},{6,4},{7,5},{8,10},{9,11},{10,... | collective-permute-start | bytes 786440 | tf_op jit(solution)/shard_map/ppermute | solution.py:342
  29.5 2.0 %collective-permute-start.3 = (bf16[512,256]{1,0:T(8,128)(2,1)S(1)}, bf16[512,256]{1,0:T(8,128)(2,1)S(1)}, u32[]{:S(2)}, u32[]{:S(2)}) collective-permute-start(bf16[512,256]{1,0:T(8,128)(2,1)S(1)} %collective-permute-done.1.near_ref), channel_id=1, source_target_pairs={{0,1},{1,0},{2,3},{3,2},{4,5},{5,4},{6,7},{7,6},{8,9},{9,8},{10,11... | collective-permute-start | bytes 786440 | tf_op jit(solution)/shard_map/ppermute | solution.py:342
  39.9 2.3 %collective-permute-start.5 = (bf16[1024,256]{1,0:T(8,128)(2,1)S(1)}, bf16[1024,256]{1,0:T(8,128)(2,1)S(1)}, u32[]{:S(2)}, u32[]{:S(2)}) collective-permute-start(bf16[1024,256]{1,0:T(8,128)(2,1)S(1)} %get-tuple-element.75), channel_id=1, source_target_pairs={{0,1},{1,0},{2,3},{3,2},{4,5},{5,4},{6,7},{7,6},{8,9},{9,8},{10,11... | collective-permute-start | bytes 1572872 | tf_op jit(solution)/shard_map/ppermute | solution.py:342
  40.4 2.6 %collective-permute-start.6 = (bf16[1024,256]{1,0:T(8,128)(2,1)S(1)}, bf16[1024,256]{1,0:T(8,128)(2,1)S(1)}, u32[]{:S(2)}, u32[]{:S(2)}) collective-permute-start(bf16[1024,256]{1,0:T(8,128)(2,1)S(1)} %get-tuple-element.78), channel_id=1, source_target_pairs={{0,1},{1,0},{2,3},{3,2},{4,5},{5,4},{6,7},{7,6},{8,9},{9,8},{10,11... | collective-permute-start | bytes 1572872 | tf_op jit(solution)/shard_map/ppermute | solution.py:342
  43.9 11.1 %collective-permute-start.10 = (bf16[512,256]{1,0:T(8,128)(2,1)S(1)}, bf16[512,256]{1,0:T(8,128)(2,1)S(1)}, u32[]{:S(2)}, u32[]{:S(2)}) collective-permute-start(bf16[512,256]{1,0:T(8,128)(2,1)S(1)} %get-tuple-element.85), channel_id=1, source_target_pairs={{0,2},{1,3},{2,0},{3,1},{4,6},{5,7},{6,4},{7,5},{8,10},{9,11},{10,... | collective-permute-start | bytes 786440 | tf_op jit(solution)/shard_map/ppermute | solution.py:342
  44.0 10.3 %collective-permute-start.7 = (bf16[256,256]{1,0:T(8,128)(2,1)S(1)}, bf16[256,256]{1,0:T(8,128)(2,1)S(1)}, u32[]{:S(2)}, u32[]{:S(2)}) collective-permute-start(bf16[256,256]{1,0:T(8,128)(2,1)S(1)} %get-tuple-element.82), channel_id=1, source_target_pairs={{0,2},{1,3},{2,0},{3,1},{4,6},{5,7},{6,4},{7,5},{8,10},{9,11},{10,... | collective-permute-start | bytes 393224 | tf_op jit(solution)/shard_map/ppermute | solution.py:342
  45.5 9.5 %collective-permute-start.8 = (bf16[256,256]{1,0:T(8,128)(2,1)S(1)}, bf16[256,256]{1,0:T(8,128)(2,1)S(1)}, u32[]{:S(2)}, u32[]{:S(2)}) collective-permute-start(bf16[256,256]{1,0:T(8,128)(2,1)S(1)} %get-tuple-element.83), channel_id=1, source_target_pairs={{0,4},{1,5},{2,6},{3,7},{4,0},{5,1},{6,2},{7,3},{8,12},{9,13},{10,... | collective-permute-start | bytes 393224 | tf_op jit(solution)/shard_map/ppermute | solution.py:342
  45.5 9.5 %collective-permute-start.9 = (bf16[256,256]{1,0:T(8,128)(2,1)S(1)}, bf16[256,256]{1,0:T(8,128)(2,1)S(1)}, u32[]{:S(2)}, u32[]{:S(2)}) collective-permute-start(bf16[256,256]{1,0:T(8,128)(2,1)S(1)} %get-tuple-element.84), channel_id=1, source_target_pairs={{0,6},{1,7},{2,4},{3,5},{4,2},{5,3},{6,0},{7,1},{8,14},{9,15},{10,... | collective-permute-start | bytes 393224 | tf_op jit(solution)/shard_map/ppermute | solution.py:342
  48.0 19.1 %collective-permute-start.11 = (bf16[512,256]{1,0:T(8,128)(2,1)}, bf16[512,256]{1,0:T(8,128)(2,1)S(1)}, u32[]{:S(2)}, u32[]{:S(2)}) collective-permute-start(bf16[512,256]{1,0:T(8,128)(2,1)} %get-tuple-element.90), channel_id=1, source_target_pairs={{0,2},{1,3},{2,0},{3,1},{4,6},{5,7},{6,4},{7,5},{8,10},{9,11},{10,... | collective-permute-start | bytes 786440 | tf_op jit(solution)/shard_map/ppermute | solution.py:342
  55.7 11.5 %collective-permute-start.12 = (bf16[512,256]{1,0:T(8,128)(2,1)}, bf16[512,256]{1,0:T(8,128)(2,1)S(1)}, u32[]{:S(2)}, u32[]{:S(2)}) collective-permute-start(bf16[512,256]{1,0:T(8,128)(2,1)} %shard_map.128), channel_id=1, source_target_pairs={{254,0},{255,1},{252,2},{253,3},{2,4},{3,5},{0,6},{1,7},{6,8},{7,9... | collective-permute-start | bytes 786440 | tf_op jit(solution)/shard_map/ppermute | solution.py:347
  61.0 15.5 %all-to-all-start = ((bf16[32,8,256]{2,1,0:T(8,128)(2,1)}), bf16[32,8,256]{2,1,0:T(8,128)(2,1)S(1)}, u32[]{:S(2)}, u32[]{:S(2)}) async-start(bf16[32,8,256]{2,1,0:T(8,128)(2,1)} %bitcast.2), calls=%async_computation | async-start | bytes 262144 | tf_op jit(solution)/shard_map/all_to_all | solution.py:338
  77.3 14.6 %all-to-all-start.1 = ((f32[32,8,256]{2,1,0:T(8,128)}), f32[32,8,256]{2,1,0:T(8,128)S(1)}, u32[]{:S(2)}, u32[]{:S(2)}) async-start(f32[32,8,256]{2,1,0:T(8,128)} %shard_map.131), calls=%async_computation.1 | async-start | bytes 524288 | tf_op jit(solution)/shard_map/all_to_all | solution.py:338
  81.3 15.0 %collective-permute-start.13 = (bf16[528,256]{1,0:T(8,128)(2,1)S(1)}, bf16[528,256]{1,0:T(8,128)(2,1)S(1)}, u32[]{:S(2)}, u32[]{:S(2)}) collective-permute-start(bf16[528,256]{1,0:T(8,128)(2,1)S(1)} %shard_map.129.refs_0_), channel_id=1, source_target_pairs={{0,2},{1,3},{2,0},{3,1},{4,6},{5,7},{6,4},{7,5},{8,10},{9,11},{10,... | collective-permute-start | bytes 811016 | tf_op jit(solution)/shard_map/ppermute | solution.py:342
  81.4 20.3 %collective-permute-start.14 = (bf16[528,256]{1,0:T(8,128)(2,1)S(1)}, bf16[528,256]{1,0:T(8,128)(2,1)S(1)}, u32[]{:S(2)}, u32[]{:S(2)}) collective-permute-start(bf16[528,256]{1,0:T(8,128)(2,1)S(1)} %shard_map.129.refs_0_), channel_id=1, source_target_pairs={{0,1},{1,0},{2,3},{3,2},{4,5},{5,4},{6,7},{7,6},{8,9},{9,8},{10,11... | collective-permute-start | bytes 811016 | tf_op jit(solution)/shard_map/ppermute | solution.py:342
  92.0 9.8 %collective-permute-start.18 = (bf16[272,256]{1,0:T(8,128)(2,1)S(1)}, bf16[272,256]{1,0:T(8,128)(2,1)S(1)}, u32[]{:S(2)}, u32[]{:S(2)}) collective-permute-start(bf16[272,256]{1,0:T(8,128)(2,1)S(1)} %shard_map.132.refs_0_), channel_id=1, source_target_pairs={{0,6},{1,7},{2,4},{3,5},{4,2},{5,3},{6,0},{7,1},{8,14},{9,15},{10,... | collective-permute-start | bytes 417800 | tf_op jit(solution)/shard_map/ppermute | solution.py:342
  95.6 9.3 %collective-permute-start.17 = (bf16[272,256]{1,0:T(8,128)(2,1)S(1)}, bf16[272,256]{1,0:T(8,128)(2,1)S(1)}, u32[]{:S(2)}, u32[]{:S(2)}) collective-permute-start(bf16[272,256]{1,0:T(8,128)(2,1)S(1)} %shard_map.132.refs_0_), channel_id=1, source_target_pairs={{0,4},{1,5},{2,6},{3,7},{4,0},{5,1},{6,2},{7,3},{8,12},{9,13},{10,... | collective-permute-start | bytes 417800 | tf_op jit(solution)/shard_map/ppermute | solution.py:342
  95.6 11.7 %collective-permute-start.16 = (bf16[272,256]{1,0:T(8,128)(2,1)S(1)}, bf16[272,256]{1,0:T(8,128)(2,1)}, u32[]{:S(2)}, u32[]{:S(2)}) collective-permute-start(bf16[272,256]{1,0:T(8,128)(2,1)S(1)} %shard_map.132.refs_0_), channel_id=1, source_target_pairs={{0,2},{1,3},{2,0},{3,1},{4,6},{5,7},{6,4},{7,5},{8,10},{9,11},{10,... | collective-permute-start | bytes 417800 | tf_op jit(solution)/shard_map/ppermute | solution.py:342
  96.3 11.1 %collective-permute-start.15 = (bf16[528,256]{1,0:T(8,128)(2,1)S(1)}, bf16[528,256]{1,0:T(8,128)(2,1)}, u32[]{:S(2)}, u32[]{:S(2)}) collective-permute-start(bf16[528,256]{1,0:T(8,128)(2,1)S(1)} %collective-permute-done.13.refs_1_), channel_id=1, source_target_pairs={{0,1},{1,0},{2,3},{3,2},{4,5},{5,4},{6,7},{7,6},{8,9},{9,8},{10,11... | collective-permute-start | bytes 811016 | tf_op jit(solution)/shard_map/ppermute | solution.py:342
  101.7 8.9 %collective-permute-start.19 = (bf16[272,256]{1,0:T(8,128)(2,1)S(1)}, bf16[272,256]{1,0:T(8,128)(2,1)}, u32[]{:S(2)}, u32[]{:S(2)}) collective-permute-start(bf16[272,256]{1,0:T(8,128)(2,1)S(1)} %shard_map.132.refs_0_), channel_id=1, source_target_pairs={{0,1},{1,0},{2,3},{3,2},{4,5},{5,4},{6,7},{7,6},{8,9},{9,8},{10,11... | collective-permute-start | bytes 417800 | tf_op jit(solution)/shard_map/ppermute | solution.py:342
  101.8 8.8 %collective-permute-start.22 = (bf16[272,256]{1,0:T(8,128)(2,1)S(1)}, bf16[272,256]{1,0:T(8,128)(2,1)}, u32[]{:S(2)}, u32[]{:S(2)}) collective-permute-start(bf16[272,256]{1,0:T(8,128)(2,1)S(1)} %collective-permute-done.18.refs_3_), channel_id=1, source_target_pairs={{0,1},{1,0},{2,3},{3,2},{4,5},{5,4},{6,7},{7,6},{8,9},{9,8},{10,11... | collective-permute-start | bytes 417800 | tf_op jit(solution)/shard_map/ppermute | solution.py:342
  104.9 5.7 %collective-permute-start.21 = (bf16[272,256]{1,0:T(8,128)(2,1)S(1)}, bf16[272,256]{1,0:T(8,128)(2,1)}, u32[]{:S(2)}, u32[]{:S(2)}) collective-permute-start(bf16[272,256]{1,0:T(8,128)(2,1)S(1)} %collective-permute-done.17.refs_2_), channel_id=1, source_target_pairs={{0,1},{1,0},{2,3},{3,2},{4,5},{5,4},{6,7},{7,6},{8,9},{9,8},{10,11... | collective-permute-start | bytes 417800 | tf_op jit(solution)/shard_map/ppermute | solution.py:342
  107.3 3.3 %collective-permute-start.20 = (bf16[272,256]{1,0:T(8,128)(2,1)}, bf16[272,256]{1,0:T(8,128)(2,1)}, u32[]{:S(2)}, u32[]{:S(2)}) collective-permute-start(bf16[272,256]{1,0:T(8,128)(2,1)} %collective-permute-done.16.refs_1_), channel_id=1, source_target_pairs={{0,1},{1,0},{2,3},{3,2},{4,5},{5,4},{6,7},{7,6},{8,9},{9,8},{10,11... | collective-permute-start | bytes 417800 | tf_op jit(solution)/shard_map/ppermute | solution.py:342
  (14 other events, 247.6 us)

commit v8 on v7

--- a/solution.py
+++ b/solution.py
@@ -18,7 +18,8 @@
 NREL = 2048
 RATE = 0.1
 AXES = ("blk", "rep")
-VMEM_LIMIT = 48 * 1024 * 1024
+VMEM_LIMIT = 32 * 1024 * 1024
+SMALL_VMEM_LIMIT = 16 * 1024 * 1024
 CHUNK = 256
 UNROLL = 4
 
@@ -276,22 +277,28 @@
 
 
 def update_kernel(n, place_ref, rows_ref, acc_ref, *refs):
-    pieces, (new_ref, new_acc_ref, buf_ref, sem_ref) = refs[:n], refs[n:]
-    size = rows_ref.shape[0] // n
-    copies = []
-    for k, piece in enumerate(pieces):
-        i = lax.bitwise_xor(k, place_ref[0])
+    pieces, (new_ref, new_acc_ref, in_ref, buf_ref, in_sem, out_sem) = refs[:n], refs[n:]
+    size = in_ref.shape[0] // n
+    starts = [lax.bitwise_xor(k, place_ref[0]) * size for k in range(n)]
+    fetches, copies = [], []
+    for k, start in enumerate(starts):
+        rows = pl.ds(pl.multiple_of(start, size), size)
+        fetch = pltpu.make_async_copy(rows_ref.at[rows, :], in_ref.at[rows, :], in_sem.at[k])
+        fetch.start()
+        fetches.append(fetch)
+    for k, (start, piece) in enumerate(zip(starts, pieces)):
+        fetches[k].wait()
         for r in range(0, size, H):
             g = piece[r : r + H, :].astype(F32)
-            at = pl.ds(i * (size // H) + r // H, 1)
+            at = pl.ds(start // H + r // H, 1)
             acc = acc_ref[at, :] + means_of(piece, size, r // H)
             new_acc_ref[at, :] = acc
             scale = jnp.transpose(jnp.broadcast_to(RATE / jnp.sqrt(acc), (H, H)))
-            rows = pl.ds(pl.multiple_of(i * size + r, H), H)
-            buf_ref[rows, :H] = rows_ref[rows, :H] - g[:, :H] * scale
-            buf_ref[rows, H:] = rows_ref[rows, H:] - g[:, H:] * scale
-        rows = pl.ds(pl.multiple_of(i * size, size), size)
-        copy = pltpu.make_async_copy(buf_ref.at[rows, :], new_ref.at[rows, :], sem_ref.at[k])
+            rows = pl.ds(pl.multiple_of(start + r, H), H)
+            buf_ref[rows, :H] = in_ref[rows, :H] - g[:, :H] * scale
+            buf_ref[rows, H:] = in_ref[rows, H:] - g[:, H:] * scale
+        rows = pl.ds(pl.multiple_of(start, size), size)
+        copy = pltpu.make_async_copy(buf_ref.at[rows, :], new_ref.at[rows, :], out_sem.at[k])
         copy.start()
         copies.append(copy)
     for copy in copies:
@@ -300,17 +307,23 @@
 
 def update(rows, acc, pieces, place):
     n = rows.shape[0]
+    k = len(pieces)
     new, new_acc = pl.pallas_call(
-        functools.partial(update_kernel, len(pieces)),
+        functools.partial(update_kernel, k),
         out_shape=[
             jax.ShapeDtypeStruct((n, D), F32),
             jax.ShapeDtypeStruct((n // H, H), F32),
         ],
-        in_specs=[smem()] + [vmem()] * (2 + len(pieces)),
+        in_specs=[smem(), pl.BlockSpec(memory_space=pl.ANY)] + [vmem()] * (1 + k),
         out_specs=[pl.BlockSpec(memory_space=pl.ANY), vmem()],
-        scratch_shapes=[pltpu.VMEM((n, D), F32), pltpu.SemaphoreType.DMA((len(pieces),))],
+        scratch_shapes=[
+            pltpu.VMEM((n, D), F32),
+            pltpu.VMEM((n, D), F32),
+            pltpu.SemaphoreType.DMA((k,)),
+            pltpu.SemaphoreType.DMA((k,)),
+        ],
         cost_estimate=pl.CostEstimate(flops=8 * n * D, bytes_accessed=10 * n * D, transcendentals=n),
-        compiler_params=pltpu.CompilerParams(vmem_limit_bytes=VMEM_LIMIT),
+        compiler_params=pltpu.CompilerParams(vmem_limit_bytes=SMALL_VMEM_LIMIT),
     )(place, rows, acc.reshape(n // H, H), *pieces)
     return new, new_acc.reshape(n)
 
@@ -436,23 +449,20 @@
     src_own, src_away = add_split([src_keep, src_recv], 2, own=F32)
     dst_away, dst_own = add_split([dst_keep, dst_recv], 2)
     parts = add_split([rel_keep, rel_recv], 4, own=F32)
-    parts, src_away, dst_own, dst_away = lax.optimization_barrier(
-        (parts, src_away, dst_own, dst_away)
-    )
     recv = [swap(part, mask) for part, mask in zip(parts[1:], X_MASKS)]
+    recv, dst_away, src_away = lax.optimization_barrier((recv, dst_away, src_away))
     dst_other = swap(dst_away, XL)
     src_other = swap(src_away, XL)
-    recv, dst_other = lax.optimization_barrier((recv, dst_other))
     (mine,) = add_split([parts[0], *recv], 1)
 
     landed = spread(mine.reshape(32, 8, D))
     (dst_sum,) = add_split([dst_own, dst_other], 1)
     dst_total = shift(dst_sum, 1, XL)
     ent_own = sum_with_means([src_own, src_other, dst_total])
-    landed, ent_own = lax.optimization_barrier((landed, ent_own))
+    landed, _, src_other = lax.optimization_barrier((landed, dst_sum, src_other))
     summed = sum_rows(landed)
-    total = spread(summed)
     ent_xl = swap(ent_own, XL)
+    total, ent_xl = lax.optimization_barrier((spread(summed), ent_xl))
     ent_core = [swap(ent_own, CORE), swap(ent_xl, CORE)]
     place = (core * 2 + xl).reshape(1)
     new_entities, new_entity_acc = update(

time: 114 us -> 107 us (0.939)
  starting transfers between devices: 51.7 us -> 48.2 us
  local copies, waits for them, and re-layouts: 5.35 us -> 2.03 us
  waiting for transfers between devices: 26.6 us -> 25.2 us
    ppermute x2, starting transfers between devices: 15.6 us -> 11.1 us  [shift(): return lax.ppermute(x, AXES, route)]
    unnamed x26 -> x18, local copies, waits for them, and re-layouts: 3.36 us -> 0.04 us
    pallas_call x1, Pallas kernels: 8.45 us -> 5.9 us  [shards(): call(score_kernel, [kept, sent, kept, sent, slots_low], 1, 10, [pltpu.VME...]
    all_to_all x2, waiting for transfers between devices: 16.1 us -> 13.6 us  [spread(): lax.all_to_all(parts, 'blk', 0, 0, axis_index_groups=groups, tiled=True)]
    all_to_all x2, starting transfers between devices: 10.1 us -> 12.3 us  [spread(): lax.all_to_all(parts, 'blk', 0, 0, axis_index_groups=groups, tiled=True)]
    pallas_call x5, Pallas kernels: 2.43 us -> 4.06 us  [add_split(): call(functools.partial(add_split_kernel, len(parts), n_out), shapes, 0, l...]
    ppermute x21, waiting for transfers between devices: 10.4 us -> 11.6 us  [swap(): return lax.ppermute(x, AXES, [(i, i ^ mask) for i in range(256)])]
    ppermute x21, starting transfers between devices: 26 us -> 24.7 us  [swap(): return lax.ppermute(x, AXES, [(i, i ^ mask) for i in range(256)])]
  transfers between devices with their start and end apart: 25 -> 25, of which waited for: 9 -> 8; matrix products, arithmetic and copies ran while one was open for 2% -> 2% of each run, Pallas kernels for 13% -> 16%
where the time goes in v8:
time: 107 us
  starting transfers between devices  48.2 us (45%)
  Pallas kernels  27.7 us (26%)
  waiting for transfers between devices  25.2 us (24%)
  local copies, waits for them, and re-layouts  2.03 us (2%)
  between operations  1.8 us (2%)
  other arithmetic  1.75 us (2%)
    ppermute x21, starting transfers between devices, swap(): return lax.ppermute(x, AXES, [(i, i ^ mask) for i in range(256)])  24.7 us
    all_to_all x2, waiting for transfers between devices, spread(): lax.all_to_all(parts, 'blk', 0, 0, axis_index_groups=groups, tiled=True)  13.6 us
    all_to_all x2, starting transfers between devices, spread(): lax.all_to_all(parts, 'blk', 0, 0, axis_index_groups=groups, tiled=True)  12.3 us
    ppermute x21, waiting for transfers between devices, swap(): return lax.ppermute(x, AXES, [(i, i ^ mask) for i in range(256)])  11.6 us
    ppermute x2, starting transfers between devices, shift(): return lax.ppermute(x, AXES, route)  11.1 us
    pallas_call x2, Pallas kernels, update(): pl.pallas_call(functools.partial(update_kernel, k), out_shape=[jax.ShapeD...  7.28 us
    pallas_call x1, Pallas kernels, shards(): call(score_kernel, [kept, sent, kept, sent, slots_low], 1, 10, [pltpu.VME...  5.9 us
    pallas_call x1, Pallas kernels, shards(): call(gather_kernel, [jax.ShapeDtypeStruct((EDGES, D), BF16), jax.ShapeDty...  4.91 us
  transfers between devices with their start and end apart: 25, of which 8 were waited for; matrix products, arithmetic and copies ran while one was open for 2% of the time, Pallas kernels for 16%

profile of v8, /device:TPU:1, one launch (start us, length us, event | category | flops | bytes accessed | tf_op | source)
XLA Modules:
  0.0 106.7 jit_solution(7921246961829792696)
XLA Ops:
  0.7 1.9 %dynamic-slice_convert_fusion = bf16[512,256]{1,0:T(8,128)(2,1)} fusion(f32[2048,256]{1,0:T(8,128)} %rows_ref.2, s32[]{:T(128)S(6)} %select_n.21), kind=kLoop, calls=%fused_computation | loop fusion | bytes 524292 | tf_op jit(solution)/shard_map/convert_element_type | solution.py:376
  2.6 11.1 %collective-permute-start = (bf16[512,256]{1,0:T(8,128)(2,1)}, bf16[512,256]{1,0:T(8,128)(2,1)S(1)}, u32[]{:S(2)}, u32[]{:S(2)}) collective-permute-start(bf16[512,256]{1,0:T(8,128)(2,1)} %dynamic-slice_convert_fusion), channel_id=1, source_target_pairs={{6,0},{7,1},{4,2},{5,3},{10,4},{11,5},{8,6},{9,7},{14,8},{15,9},{1... | collective-permute-start | bytes 786440 | tf_op jit(solution)/shard_map/ppermute | solution.py:360
  13.7 1.7 %convert_element_type.7.low_ref = bf16[2048,256]{1,0:T(8,128)(2,1)S(1)} convert(f32[2048,256]{1,0:T(8,128)} %rows_ref.2) | non-fusion elementwise | flops 524288 | bytes 3145728 | tf_op jit(solution)/shard_map/convert_element_type | solution.py:374
  15.6 4.9 %shard_map.120 = (bf16[1024,256]{1,0:T(8,128)(2,1)S(1)}, f32[1024,256]{1,0:T(8,128)S(1)}, f32[1024,256]{1,0:T(8,128)S(1)}, f32[4,16,128]{2,1,0:T(8,128)S(1)}) custom-call(s32[8,1024]{1,0:T(8,128)S(1)} %concatenate.3.ids_ref, s32[4,1024]{1,0:T(4,128)S(1)} %reshape.37.negs_ref, bf16[2048,256]{1,0:T(8,128)(2,1)S(1)} %convert_element_type.7.low_ref, ...), custom_call_target="tpu_custom_call" | custom-call | flops 4294967296 | bytes 4194304 | tf_op jit(solution)/shard_map/pallas_call | solution.py:390
  21.6 1.2 %collective-permute-done.2.far_ref = bf16[512,256]{1,0:T(8,128)(2,1)S(1)} collective-permute-done((bf16[512,256]{1,0:T(8,128)(2,1)S(1)}, bf16[512,256]{1,0:T(8,128)(2,1)S(1)}, u32[]{:S(2)}, u32[]{:S(2)}) %collective-permute-start.2) | collective-permute-done | bytes 262176 | tf_op jit(solution)/shard_map/ppermute | solution.py:355
  22.7 2.2 %shard_map.121 = (bf16[1024,1024]{1,0:T(8,128)(2,1)S(1)}, f32[1024,256]{1,0:T(8,128)S(1)}, f32[1024,256]{1,0:T(8,128)S(1)}) custom-call(s32[8,1024]{1,0:T(8,128)S(1)} %concatenate.3.ids_ref, bf16[512,256]{1,0:T(8,128)(2,1)S(1)} %collective-permute-done.near_ref, bf16[512,256]{1,0:T(8,128)(2,1)S(1)} %collective-permute-done.2.far_ref, ...), custom_call_target="tpu_custom_call" | custom-call | flops 1610612736 | bytes 4194304 | tf_op jit(solution)/shard_map/pallas_call | solution.py:413
  25.0 4.5 %collective-permute-done.1.near_ref = bf16[512,256]{1,0:T(8,128)(2,1)S(1)} collective-permute-done((bf16[512,256]{1,0:T(8,128)(2,1)S(1)}, bf16[512,256]{1,0:T(8,128)(2,1)S(1)}, u32[]{:S(2)}, u32[]{:S(2)}) %collective-permute-start.1) | collective-permute-done | bytes 262176 | tf_op jit(solution)/shard_map/ppermute | solution.py:355
  31.5 5.9 %shard_map.122 = (f32[1024,256]{1,0:T(8,128)S(1)}, bf16[1024,256]{1,0:T(8,128)(2,1)S(1)}, f32[1024,256]{1,0:T(8,128)S(1)}, bf16[1024,256]{1,0:T(8,128)(2,1)S(1)}, bf16[1024,256]{1,0:T(8,128)(2,1)S(1)}) custom-call(s32[1,1]{1,0:T(1,128)S(6)} %copy.13.count_ref, s32[8,1024]{1,0:T(8,128)S(1)} %concatenate.3.ids_ref, ...), custom_call_target="tpu_custom_call" | custom-call | flops 4831838208 | bytes 8388608 | tf_op jit(solution)/shard_map/pallas_call | solution.py:423
  37.4 1.2 %shard_map.124 = (f32[1024,256]{1,0:T(8,128)S(1)}, bf16[1024,256]{1,0:T(8,128)(2,1)S(1)}) custom-call(s32[8,1024]{1,0:T(8,128)S(1)} %concatenate.3.ids_ref, bf16[1024,256]{1,0:T(8,128)(2,1)S(1)} %get-tuple-element.65.gr_ref), custom_call_target="tpu_custom_call" | custom-call | flops 1073741824 | bytes 2097152 | tf_op jit(solution)/shard_map/pallas_call | solution.py:439
  40.9 3.7 %collective-permute-start.8 = (bf16[256,256]{1,0:T(8,128)(2,1)S(1)}, bf16[256,256]{1,0:T(8,128)(2,1)S(1)}, u32[]{:S(2)}, u32[]{:S(2)}) collective-permute-start(bf16[256,256]{1,0:T(8,128)(2,1)S(1)} %get-tuple-element.70), channel_id=1, source_target_pairs={{0,6},{1,7},{2,4},{3,5},{4,2},{5,3},{6,0},{7,1},{8,14},{9,15},{10,... | collective-permute-start | bytes 393224 | tf_op jit(solution)/shard_map/ppermute | solution.py:355
  46.9 3.7 %collective-permute-done.8.refs_3_ = bf16[256,256]{1,0:T(8,128)(2,1)S(1)} collective-permute-done((bf16[256,256]{1,0:T(8,128)(2,1)S(1)}, bf16[256,256]{1,0:T(8,128)(2,1)S(1)}, u32[]{:S(2)}, u32[]{:S(2)}) %collective-permute-start.8) | collective-permute-done | bytes 131104 | tf_op jit(solution)/shard_map/ppermute | solution.py:355
  50.6 1.5 %collective-permute-start.10 = (bf16[512,256]{1,0:T(8,128)(2,1)}, bf16[512,256]{1,0:T(8,128)(2,1)S(1)}, u32[]{:S(2)}, u32[]{:S(2)}) collective-permute-start(bf16[512,256]{1,0:T(8,128)(2,1)} %get-tuple-element.75), channel_id=1, source_target_pairs={{0,2},{1,3},{2,0},{3,1},{4,6},{5,7},{6,4},{7,5},{8,10},{9,11},{10,... | collective-permute-start | bytes 786440 | tf_op jit(solution)/shard_map/ppermute | solution.py:355
  52.8 8.5 %all-to-all-start = ((bf16[32,8,256]{2,1,0:T(8,128)(2,1)}), bf16[32,8,256]{2,1,0:T(8,128)(2,1)S(1)}, u32[]{:S(2)}, u32[]{:S(2)}) async-start(bf16[32,8,256]{2,1,0:T(8,128)(2,1)} %bitcast.2), calls=%async_computation | async-start | bytes 262144 | tf_op jit(solution)/shard_map/all_to_all | solution.py:351
  61.3 1.7 %shard_map.127 = bf16[512,256]{1,0:T(8,128)(2,1)} custom-call(bf16[512,256]{1,0:T(8,128)(2,1)S(1)} %get-tuple-element.76.refs_0_, bf16[512,256]{1,0:T(8,128)(2,1)} %collective-permute-done.11.refs_1_), custom_call_target="tpu_custom_call" | custom-call | flops 262144 | bytes 786432 | tf_op jit(solution)/shard_map/pallas_call | solution.py:228
  63.1 7.6 %all-to-all-done.parts_ref = bf16[32,8,256]{2,1,0:T(8,128)(2,1)S(1)} async-done(((bf16[32,8,256]{2,1,0:T(8,128)(2,1)}), bf16[32,8,256]{2,1,0:T(8,128)(2,1)S(1)}, u32[]{:S(2)}, u32[]{:S(2)}) %all-to-all-start) | async-done | bytes 131104 | tf_op jit(solution)/shard_map/all_to_all | solution.py:351
  71.4 3.9 %all-to-all-start.1 = ((f32[32,8,256]{2,1,0:T(8,128)}), f32[32,8,256]{2,1,0:T(8,128)S(1)}, u32[]{:S(2)}, u32[]{:S(2)}) async-start(f32[32,8,256]{2,1,0:T(8,128)} %shard_map.130), calls=%async_computation.1 | async-start | bytes 524288 | tf_op jit(solution)/shard_map/all_to_all | solution.py:351
  75.3 1.2 %shard_map.128.refs_0_ = bf16[528,256]{1,0:T(8,128)(2,1)S(1)} custom-call(f32[512,256]{1,0:T(8,128)S(1)} %get-tuple-element.64.refs_0_, bf16[512,256]{1,0:T(8,128)(2,1)S(1)} %collective-permute-done.10.refs_1_, bf16[512,256]{1,0:T(8,128)(2,1)} %collective-permute-done.12.refs_2_), custom_call_target="tpu_custom_call" | custom-call | flops 393216 | bytes 1179648 | tf_op jit(solution)/shard_map/pallas_call | solution.py:264
  76.8 3.1 %collective-permute-start.14 = (bf16[528,256]{1,0:T(8,128)(2,1)S(1)}, bf16[528,256]{1,0:T(8,128)(2,1)S(1)}, u32[]{:S(2)}, u32[]{:S(2)}) collective-permute-start(bf16[528,256]{1,0:T(8,128)(2,1)S(1)} %shard_map.128.refs_0_), channel_id=1, source_target_pairs={{0,1},{1,0},{2,3},{3,2},{4,5},{5,4},{6,7},{7,6},{8,9},{9,8},{10,11... | collective-permute-start | bytes 811016 | tf_op jit(solution)/shard_map/ppermute | solution.py:355
  79.9 6.0 %all-to-all-done.1 = f32[32,8,256]{2,1,0:T(8,128)S(1)} async-done(((f32[32,8,256]{2,1,0:T(8,128)}), f32[32,8,256]{2,1,0:T(8,128)S(1)}, u32[]{:S(2)}, u32[]{:S(2)}) %all-to-all-start.1) | async-done | bytes 262176 | tf_op jit(solution)/shard_map/all_to_all | solution.py:351
  88.1 1.3 %collective-permute-start.16 = (bf16[272,256]{1,0:T(8,128)(2,1)S(1)}, bf16[272,256]{1,0:T(8,128)(2,1)}, u32[]{:S(2)}, u32[]{:S(2)}) collective-permute-start(bf16[272,256]{1,0:T(8,128)(2,1)S(1)} %shard_map.132.refs_0_), channel_id=1, source_target_pairs={{0,2},{1,3},{2,0},{3,1},{4,6},{5,7},{6,4},{7,5},{8,10},{9,11},{10,... | collective-permute-start | bytes 417800 | tf_op jit(solution)/shard_map/ppermute | solution.py:355
  89.3 5.2 %collective-permute-start.15 = (bf16[528,256]{1,0:T(8,128)(2,1)S(1)}, bf16[528,256]{1,0:T(8,128)(2,1)}, u32[]{:S(2)}, u32[]{:S(2)}) collective-permute-start(bf16[528,256]{1,0:T(8,128)(2,1)S(1)} %collective-permute-done.13.refs_1_), channel_id=1, source_target_pairs={{0,1},{1,0},{2,3},{3,2},{4,5},{5,4},{6,7},{7,6},{8,9},{9,8},{10,11... | collective-permute-start | bytes 811016 | tf_op jit(solution)/shard_map/ppermute | solution.py:355
  94.5 3.7 %collective-permute-start.22 = (bf16[272,256]{1,0:T(8,128)(2,1)S(1)}, bf16[272,256]{1,0:T(8,128)(2,1)}, u32[]{:S(2)}, u32[]{:S(2)}) collective-permute-start(bf16[272,256]{1,0:T(8,128)(2,1)S(1)} %collective-permute-done.18.refs_3_), channel_id=1, source_target_pairs={{0,1},{1,0},{2,3},{3,2},{4,5},{5,4},{6,7},{7,6},{8,9},{9,8},{10,11... | collective-permute-start | bytes 417800 | tf_op jit(solution)/shard_map/ppermute | solution.py:355
  99.1 3.4 %shard_map.131 = (f32[2048,256]{1,0:T(8,128)}, f32[16,128]{1,0:T(8,128)}) custom-call(s32[1]{0:T(128)} %bitcast.place_ref, f32[2048,256]{1,0:T(8,128)S(1)} %copy-done, f32[16,128]{1,0:T(8,128)S(1)} %bitcast.9, bf16[528,256]{1,0:T(8,128)(2,1)S(1)} %shard_map.128.refs_0_, bf16[528,256]{1,0:T(8,128)(2,1)S(1)} %collective-permute-done.13.refs_1_, ...), custom_call_target="tpu_custom_call" | custom-call | flops 4194304 | bytes 5242880 | tf_op jit(solution)/shard_map/pallas_call | solution.py:311
  102.6 3.9 %shard_map.133 = (f32[2048,256]{1,0:T(8,128)}, f32[16,128]{1,0:T(8,128)}) custom-call(s32[1]{0:T(128)} %bitcast.5.place_ref, f32[2048,256]{1,0:T(8,128)S(1)} %copy-done.2, f32[16,128]{1,0:T(8,128)S(1)} %bitcast.10, bf16[272,256]{1,0:T(8,128)(2,1)S(1)} %shard_map.132.refs_0_, bf16[272,256]{1,0:T(8,128)(2,1)} %collective-permute-done.16.refs_1_, ...), custom_call_target="tpu_custom_call" | custom-call | flops 4194304 | bytes 5242880 | tf_op jit(solution)/shard_map/pallas_call | solution.py:311
  (66 shorter events, 12.1 us)
Async XLA Ops:
  2.6 17.9 %collective-permute-start = (bf16[512,256]{1,0:T(8,128)(2,1)}, bf16[512,256]{1,0:T(8,128)(2,1)S(1)}, u32[]{:S(2)}, u32[]{:S(2)}) collective-permute-start(bf16[512,256]{1,0:T(8,128)(2,1)} %dynamic-slice_convert_fusion), channel_id=1, source_target_pairs={{6,0},{7,1},{4,2},{5,3},{10,4},{11,5},{8,6},{9,7},{14,8},{15,9},{1... | collective-permute-start | bytes 786440 | tf_op jit(solution)/shard_map/ppermute | solution.py:360
  20.5 2.2 %collective-permute-start.2 = (bf16[512,256]{1,0:T(8,128)(2,1)S(1)}, bf16[512,256]{1,0:T(8,128)(2,1)S(1)}, u32[]{:S(2)}, u32[]{:S(2)}) collective-permute-start(bf16[512,256]{1,0:T(8,128)(2,1)S(1)} %collective-permute-done.near_ref), channel_id=1, source_target_pairs={{0,1},{1,0},{2,3},{3,2},{4,5},{5,4},{6,7},{7,6},{8,9},{9,8},{10,11... | collective-permute-start | bytes 786440 | tf_op jit(solution)/shard_map/ppermute | solution.py:355
  21.6 7.9 %collective-permute-start.1 = (bf16[512,256]{1,0:T(8,128)(2,1)S(1)}, bf16[512,256]{1,0:T(8,128)(2,1)S(1)}, u32[]{:S(2)}, u32[]{:S(2)}) collective-permute-start(bf16[512,256]{1,0:T(8,128)(2,1)S(1)} %collective-permute-done.near_ref), channel_id=1, source_target_pairs={{0,2},{1,3},{2,0},{3,1},{4,6},{5,7},{6,4},{7,5},{8,10},{9,11},{10,... | collective-permute-start | bytes 786440 | tf_op jit(solution)/shard_map/ppermute | solution.py:355
  29.4 2.0 %collective-permute-start.3 = (bf16[512,256]{1,0:T(8,128)(2,1)S(1)}, bf16[512,256]{1,0:T(8,128)(2,1)S(1)}, u32[]{:S(2)}, u32[]{:S(2)}) collective-permute-start(bf16[512,256]{1,0:T(8,128)(2,1)S(1)} %collective-permute-done.1.near_ref), channel_id=1, source_target_pairs={{0,1},{1,0},{2,3},{3,2},{4,5},{5,4},{6,7},{7,6},{8,9},{9,8},{10,11... | collective-permute-start | bytes 786440 | tf_op jit(solution)/shard_map/ppermute | solution.py:355
  39.1 5.6 %collective-permute-start.4 = (bf16[1024,256]{1,0:T(8,128)(2,1)S(1)}, bf16[1024,256]{1,0:T(8,128)(2,1)S(1)}, u32[]{:S(2)}, u32[]{:S(2)}) collective-permute-start(bf16[1024,256]{1,0:T(8,128)(2,1)S(1)} %get-tuple-element.63), channel_id=1, source_target_pairs={{0,1},{1,0},{2,3},{3,2},{4,5},{5,4},{6,7},{7,6},{8,9},{9,8},{10,11... | collective-permute-start | bytes 1572872 | tf_op jit(solution)/shard_map/ppermute | solution.py:355
  39.2 6.2 %collective-permute-start.9 = (bf16[1024,256]{1,0:T(8,128)(2,1)S(1)}, bf16[1024,256]{1,0:T(8,128)(2,1)S(1)}, u32[]{:S(2)}, u32[]{:S(2)}) collective-permute-start(bf16[1024,256]{1,0:T(8,128)(2,1)S(1)} %get-tuple-element.72), channel_id=1, source_target_pairs={{0,1},{1,0},{2,3},{3,2},{4,5},{5,4},{6,7},{7,6},{8,9},{9,8},{10,11... | collective-permute-start | bytes 1572872 | tf_op jit(solution)/shard_map/ppermute | solution.py:355
  40.7 5.5 %collective-permute-start.6 = (bf16[256,256]{1,0:T(8,128)(2,1)S(1)}, bf16[256,256]{1,0:T(8,128)(2,1)S(1)}, u32[]{:S(2)}, u32[]{:S(2)}) collective-permute-start(bf16[256,256]{1,0:T(8,128)(2,1)S(1)} %get-tuple-element.68), channel_id=1, source_target_pairs={{0,2},{1,3},{2,0},{3,1},{4,6},{5,7},{6,4},{7,5},{8,10},{9,11},{10,... | collective-permute-start | bytes 393224 | tf_op jit(solution)/shard_map/ppermute | solution.py:355
  40.8 6.1 %collective-permute-start.7 = (bf16[256,256]{1,0:T(8,128)(2,1)S(1)}, bf16[256,256]{1,0:T(8,128)(2,1)S(1)}, u32[]{:S(2)}, u32[]{:S(2)}) collective-permute-start(bf16[256,256]{1,0:T(8,128)(2,1)S(1)} %get-tuple-element.69), channel_id=1, source_target_pairs={{0,4},{1,5},{2,6},{3,7},{4,0},{5,1},{6,2},{7,3},{8,12},{9,13},{10,... | collective-permute-start | bytes 393224 | tf_op jit(solution)/shard_map/ppermute | solution.py:355
  40.9 9.7 %collective-permute-start.8 = (bf16[256,256]{1,0:T(8,128)(2,1)S(1)}, bf16[256,256]{1,0:T(8,128)(2,1)S(1)}, u32[]{:S(2)}, u32[]{:S(2)}) collective-permute-start(bf16[256,256]{1,0:T(8,128)(2,1)S(1)} %get-tuple-element.70), channel_id=1, source_target_pairs={{0,6},{1,7},{2,4},{3,5},{4,2},{5,3},{6,0},{7,1},{8,14},{9,15},{10,... | collective-permute-start | bytes 393224 | tf_op jit(solution)/shard_map/ppermute | solution.py:355
  50.6 10.7 %collective-permute-start.11 = (bf16[512,256]{1,0:T(8,128)(2,1)}, bf16[512,256]{1,0:T(8,128)(2,1)}, u32[]{:S(2)}, u32[]{:S(2)}) collective-permute-start(bf16[512,256]{1,0:T(8,128)(2,1)} %get-tuple-element.77), channel_id=1, source_target_pairs={{0,2},{1,3},{2,0},{3,1},{4,6},{5,7},{6,4},{7,5},{8,10},{9,11},{10,... | collective-permute-start | bytes 786440 | tf_op jit(solution)/shard_map/ppermute | solution.py:355
  50.6 20.0 %collective-permute-start.10 = (bf16[512,256]{1,0:T(8,128)(2,1)}, bf16[512,256]{1,0:T(8,128)(2,1)S(1)}, u32[]{:S(2)}, u32[]{:S(2)}) collective-permute-start(bf16[512,256]{1,0:T(8,128)(2,1)} %get-tuple-element.75), channel_id=1, source_target_pairs={{0,2},{1,3},{2,0},{3,1},{4,6},{5,7},{6,4},{7,5},{8,10},{9,11},{10,... | collective-permute-start | bytes 786440 | tf_op jit(solution)/shard_map/ppermute | solution.py:355
  52.8 17.8 %all-to-all-start = ((bf16[32,8,256]{2,1,0:T(8,128)(2,1)}), bf16[32,8,256]{2,1,0:T(8,128)(2,1)S(1)}, u32[]{:S(2)}, u32[]{:S(2)}) async-start(bf16[32,8,256]{2,1,0:T(8,128)(2,1)} %bitcast.2), calls=%async_computation | async-start | bytes 262144 | tf_op jit(solution)/shard_map/all_to_all | solution.py:351
  63.0 12.3 %collective-permute-start.12 = (bf16[512,256]{1,0:T(8,128)(2,1)}, bf16[512,256]{1,0:T(8,128)(2,1)}, u32[]{:S(2)}, u32[]{:S(2)}) collective-permute-start(bf16[512,256]{1,0:T(8,128)(2,1)} %shard_map.127), channel_id=1, source_target_pairs={{254,0},{255,1},{252,2},{253,3},{2,4},{3,5},{0,6},{1,7},{6,8},{7,9... | collective-permute-start | bytes 786440 | tf_op jit(solution)/shard_map/ppermute | solution.py:360
  71.4 14.5 %all-to-all-start.1 = ((f32[32,8,256]{2,1,0:T(8,128)}), f32[32,8,256]{2,1,0:T(8,128)S(1)}, u32[]{:S(2)}, u32[]{:S(2)}) async-start(f32[32,8,256]{2,1,0:T(8,128)} %shard_map.130), calls=%async_computation.1 | async-start | bytes 524288 | tf_op jit(solution)/shard_map/all_to_all | solution.py:351
  76.5 9.4 %collective-permute-start.13 = (bf16[528,256]{1,0:T(8,128)(2,1)S(1)}, bf16[528,256]{1,0:T(8,128)(2,1)S(1)}, u32[]{:S(2)}, u32[]{:S(2)}) collective-permute-start(bf16[528,256]{1,0:T(8,128)(2,1)S(1)} %shard_map.128.refs_0_), channel_id=1, source_target_pairs={{0,2},{1,3},{2,0},{3,1},{4,6},{5,7},{6,4},{7,5},{8,10},{9,11},{10,... | collective-permute-start | bytes 811016 | tf_op jit(solution)/shard_map/ppermute | solution.py:355
  76.8 17.7 %collective-permute-start.14 = (bf16[528,256]{1,0:T(8,128)(2,1)S(1)}, bf16[528,256]{1,0:T(8,128)(2,1)S(1)}, u32[]{:S(2)}, u32[]{:S(2)}) collective-permute-start(bf16[528,256]{1,0:T(8,128)(2,1)S(1)} %shard_map.128.refs_0_), channel_id=1, source_target_pairs={{0,1},{1,0},{2,3},{3,2},{4,5},{5,4},{6,7},{7,6},{8,9},{9,8},{10,11... | collective-permute-start | bytes 811016 | tf_op jit(solution)/shard_map/ppermute | solution.py:355
  86.0 8.5 %collective-permute-start.18 = (bf16[272,256]{1,0:T(8,128)(2,1)S(1)}, bf16[272,256]{1,0:T(8,128)(2,1)S(1)}, u32[]{:S(2)}, u32[]{:S(2)}) collective-permute-start(bf16[272,256]{1,0:T(8,128)(2,1)S(1)} %shard_map.132.refs_0_), channel_id=1, source_target_pairs={{0,6},{1,7},{2,4},{3,5},{4,2},{5,3},{6,0},{7,1},{8,14},{9,15},{10,... | collective-permute-start | bytes 417800 | tf_op jit(solution)/shard_map/ppermute | solution.py:355
  87.0 11.2 %collective-permute-start.17 = (bf16[272,256]{1,0:T(8,128)(2,1)S(1)}, bf16[272,256]{1,0:T(8,128)(2,1)S(1)}, u32[]{:S(2)}, u32[]{:S(2)}) collective-permute-start(bf16[272,256]{1,0:T(8,128)(2,1)S(1)} %shard_map.132.refs_0_), channel_id=1, source_target_pairs={{0,4},{1,5},{2,6},{3,7},{4,0},{5,1},{6,2},{7,3},{8,12},{9,13},{10,... | collective-permute-start | bytes 417800 | tf_op jit(solution)/shard_map/ppermute | solution.py:355
  88.1 10.1 %collective-permute-start.16 = (bf16[272,256]{1,0:T(8,128)(2,1)S(1)}, bf16[272,256]{1,0:T(8,128)(2,1)}, u32[]{:S(2)}, u32[]{:S(2)}) collective-permute-start(bf16[272,256]{1,0:T(8,128)(2,1)S(1)} %shard_map.132.refs_0_), channel_id=1, source_target_pairs={{0,2},{1,3},{2,0},{3,1},{4,6},{5,7},{6,4},{7,5},{8,10},{9,11},{10,... | collective-permute-start | bytes 417800 | tf_op jit(solution)/shard_map/ppermute | solution.py:355
  89.3 9.8 %collective-permute-start.15 = (bf16[528,256]{1,0:T(8,128)(2,1)S(1)}, bf16[528,256]{1,0:T(8,128)(2,1)}, u32[]{:S(2)}, u32[]{:S(2)}) collective-permute-start(bf16[528,256]{1,0:T(8,128)(2,1)S(1)} %collective-permute-done.13.refs_1_), channel_id=1, source_target_pairs={{0,1},{1,0},{2,3},{3,2},{4,5},{5,4},{6,7},{7,6},{8,9},{9,8},{10,11... | collective-permute-start | bytes 811016 | tf_op jit(solution)/shard_map/ppermute | solution.py:355
  94.5 8.1 %collective-permute-start.19 = (bf16[272,256]{1,0:T(8,128)(2,1)S(1)}, bf16[272,256]{1,0:T(8,128)(2,1)}, u32[]{:S(2)}, u32[]{:S(2)}) collective-permute-start(bf16[272,256]{1,0:T(8,128)(2,1)S(1)} %shard_map.132.refs_0_), channel_id=1, source_target_pairs={{0,1},{1,0},{2,3},{3,2},{4,5},{5,4},{6,7},{7,6},{8,9},{9,8},{10,11... | collective-permute-start | bytes 417800 | tf_op jit(solution)/shard_map/ppermute | solution.py:355
  94.5 8.1 %collective-permute-start.22 = (bf16[272,256]{1,0:T(8,128)(2,1)S(1)}, bf16[272,256]{1,0:T(8,128)(2,1)}, u32[]{:S(2)}, u32[]{:S(2)}) collective-permute-start(bf16[272,256]{1,0:T(8,128)(2,1)S(1)} %collective-permute-done.18.refs_3_), channel_id=1, source_target_pairs={{0,1},{1,0},{2,3},{3,2},{4,5},{5,4},{6,7},{7,6},{8,9},{9,8},{10,11... | collective-permute-start | bytes 417800 | tf_op jit(solution)/shard_map/ppermute | solution.py:355
  98.2 4.4 %collective-permute-start.21 = (bf16[272,256]{1,0:T(8,128)(2,1)S(1)}, bf16[272,256]{1,0:T(8,128)(2,1)}, u32[]{:S(2)}, u32[]{:S(2)}) collective-permute-start(bf16[272,256]{1,0:T(8,128)(2,1)S(1)} %collective-permute-done.17.refs_2_), channel_id=1, source_target_pairs={{0,1},{1,0},{2,3},{3,2},{4,5},{5,4},{6,7},{7,6},{8,9},{9,8},{10,11... | collective-permute-start | bytes 417800 | tf_op jit(solution)/shard_map/ppermute | solution.py:355
  98.2 4.4 %collective-permute-start.20 = (bf16[272,256]{1,0:T(8,128)(2,1)}, bf16[272,256]{1,0:T(8,128)(2,1)}, u32[]{:S(2)}, u32[]{:S(2)}) collective-permute-start(bf16[272,256]{1,0:T(8,128)(2,1)} %collective-permute-done.16.refs_1_), channel_id=1, source_target_pairs={{0,1},{1,0},{2,3},{3,2},{4,5},{5,4},{6,7},{7,6},{8,9},{9,8},{10,11... | collective-permute-start | bytes 417800 | tf_op jit(solution)/shard_map/ppermute | solution.py:355
  (10 other events, 199.9 us)

commit v9 on v7

--- a/solution.py
+++ b/solution.py
@@ -18,7 +18,8 @@
 NREL = 2048
 RATE = 0.1
 AXES = ("blk", "rep")
-VMEM_LIMIT = 48 * 1024 * 1024
+VMEM_LIMIT = 32 * 1024 * 1024
+SMALL_VMEM_LIMIT = 16 * 1024 * 1024
 CHUNK = 256
 UNROLL = 4
 
@@ -310,7 +311,7 @@
         out_specs=[pl.BlockSpec(memory_space=pl.ANY), vmem()],
         scratch_shapes=[pltpu.VMEM((n, D), F32), pltpu.SemaphoreType.DMA((len(pieces),))],
         cost_estimate=pl.CostEstimate(flops=8 * n * D, bytes_accessed=10 * n * D, transcendentals=n),
-        compiler_params=pltpu.CompilerParams(vmem_limit_bytes=VMEM_LIMIT),
+        compiler_params=pltpu.CompilerParams(vmem_limit_bytes=SMALL_VMEM_LIMIT),
     )(place, rows, acc.reshape(n // H, H), *pieces)
     return new, new_acc.reshape(n)
 
@@ -436,23 +437,20 @@
     src_own, src_away = add_split([src_keep, src_recv], 2, own=F32)
     dst_away, dst_own = add_split([dst_keep, dst_recv], 2)
     parts = add_split([rel_keep, rel_recv], 4, own=F32)
-    parts, src_away, dst_own, dst_away = lax.optimization_barrier(
-        (parts, src_away, dst_own, dst_away)
-    )
     recv = [swap(part, mask) for part, mask in zip(parts[1:], X_MASKS)]
+    recv, dst_away, src_away = lax.optimization_barrier((recv, dst_away, src_away))
     dst_other = swap(dst_away, XL)
     src_other = swap(src_away, XL)
-    recv, dst_other = lax.optimization_barrier((recv, dst_other))
     (mine,) = add_split([parts[0], *recv], 1)
 
     landed = spread(mine.reshape(32, 8, D))
     (dst_sum,) = add_split([dst_own, dst_other], 1)
     dst_total = shift(dst_sum, 1, XL)
     ent_own = sum_with_means([src_own, src_other, dst_total])
-    landed, ent_own = lax.optimization_barrier((landed, ent_own))
+    landed, _, src_other = lax.optimization_barrier((landed, dst_sum, src_other))
     summed = sum_rows(landed)
-    total = spread(summed)
     ent_xl = swap(ent_own, XL)
+    total, ent_xl = lax.optimization_barrier((spread(summed), ent_xl))
     ent_core = [swap(ent_own, CORE), swap(ent_xl, CORE)]
     place = (core * 2 + xl).reshape(1)
     new_entities, new_entity_acc = update(
@@ -460,7 +458,7 @@
     )
     quarter = sum_with_means([total.reshape(256, D)])
     recv = [swap(quarter, mask) for mask in X_MASKS]
-
+    recv, new_entity_acc = lax.optimization_barrier((recv, new_entity_acc))
     pieces = [quarter, *recv]
     pieces = pieces + [swap(piece, CORE) for piece in pieces]
     pieces, new_entity_acc = lax.optimization_barrier((pieces, new_entity_acc))

time: 114 us -> 108 us (0.947)
  starting transfers between devices: 51.7 us -> 45.2 us
  waiting for transfers between devices: 26.6 us -> 28.9 us
  local copies, waits for them, and re-layouts: 5.35 us -> 3.62 us
    ppermute x21, waiting for transfers between devices: 10.4 us -> 15.4 us  [swap(): return lax.ppermute(x, AXES, [(i, i ^ mask) for i in range(256)])]
    ppermute x2, starting transfers between devices: 15.6 us -> 11.1 us  [shift(): return lax.ppermute(x, AXES, route)]
    ppermute x21, starting transfers between devices: 26 us -> 21.7 us  [swap(): return lax.ppermute(x, AXES, [(i, i ^ mask) for i in range(256)])]
    pallas_call x1, Pallas kernels: 8.45 us -> 5.9 us  [shards(): call(score_kernel, [kept, sent, kept, sent, slots_low], 1, 10, [pltpu.VME...]
    all_to_all x2, waiting for transfers between devices: 16.1 us -> 13.6 us  [spread(): lax.all_to_all(parts, 'blk', 0, 0, axis_index_groups=groups, tiled=True)]
    all_to_all x2, starting transfers between devices: 10.1 us -> 12.3 us  [spread(): lax.all_to_all(parts, 'blk', 0, 0, axis_index_groups=groups, tiled=True)]
    unnamed x26 -> x18, local copies, waits for them, and re-layouts: 3.36 us -> 1.63 us
    pallas_call x5, Pallas kernels: 2.43 us -> 4.06 us  [add_split(): call(functools.partial(add_split_kernel, len(parts), n_out), shapes, 0, l...]
  transfers between devices with their start and end apart: 25 -> 25, of which waited for: 9 -> 12; matrix products, arithmetic and copies ran while one was open for 2% -> 2% of each run, Pallas kernels for 13% -> 15%
where the time goes in v9:
time: 108 us
  starting transfers between devices  45.2 us (42%)
  waiting for transfers between devices  28.9 us (27%)
  Pallas kernels  26.6 us (25%)
  local copies, waits for them, and re-layouts  3.62 us (3%)
  other arithmetic  1.75 us (2%)
  between operations  1.75 us (2%)
    ppermute x21, starting transfers between devices, swap(): return lax.ppermute(x, AXES, [(i, i ^ mask) for i in range(256)])  21.7 us
    ppermute x21, waiting for transfers between devices, swap(): return lax.ppermute(x, AXES, [(i, i ^ mask) for i in range(256)])  15.4 us
    all_to_all x2, waiting for transfers between devices, spread(): lax.all_to_all(parts, 'blk', 0, 0, axis_index_groups=groups, tiled=True)  13.6 us
    all_to_all x2, starting transfers between devices, spread(): lax.all_to_all(parts, 'blk', 0, 0, axis_index_groups=groups, tiled=True)  12.3 us
    ppermute x2, starting transfers between devices, shift(): return lax.ppermute(x, AXES, route)  11.1 us
    pallas_call x2, Pallas kernels, update(): pl.pallas_call(functools.partial(update_kernel, len(pieces)), out_shape=[...  6.15 us
    pallas_call x1, Pallas kernels, shards(): call(score_kernel, [kept, sent, kept, sent, slots_low], 1, 10, [pltpu.VME...  5.9 us
    pallas_call x1, Pallas kernels, shards(): call(gather_kernel, [jax.ShapeDtypeStruct((EDGES, D), BF16), jax.ShapeDty...  4.91 us
  transfers between devices with their start and end apart: 25, of which 12 were waited for; matrix products, arithmetic and copies ran while one was open for 2% of the time, Pallas kernels for 15%

profile of v9, /device:TPU:1, one launch (start us, length us, event | category | flops | bytes accessed | tf_op | source)
XLA Modules:
  0.0 107.8 jit_solution(5437431282467007273)
XLA Ops:
  0.7 1.9 %dynamic-slice_convert_fusion = bf16[512,256]{1,0:T(8,128)(2,1)} fusion(f32[2048,256]{1,0:T(8,128)} %rows_ref.2, s32[]{:T(128)S(6)} %select_n.21), kind=kLoop, calls=%fused_computation | loop fusion | bytes 524292 | tf_op jit(solution)/shard_map/convert_element_type | solution.py:364
  2.6 11.1 %collective-permute-start = (bf16[512,256]{1,0:T(8,128)(2,1)}, bf16[512,256]{1,0:T(8,128)(2,1)S(1)}, u32[]{:S(2)}, u32[]{:S(2)}) collective-permute-start(bf16[512,256]{1,0:T(8,128)(2,1)} %dynamic-slice_convert_fusion), channel_id=1, source_target_pairs={{6,0},{7,1},{4,2},{5,3},{10,4},{11,5},{8,6},{9,7},{14,8},{15,9},{1... | collective-permute-start | bytes 786440 | tf_op jit(solution)/shard_map/ppermute | solution.py:348
  13.7 1.7 %convert_element_type.7.low_ref = bf16[2048,256]{1,0:T(8,128)(2,1)S(1)} convert(f32[2048,256]{1,0:T(8,128)} %rows_ref.2) | non-fusion elementwise | flops 524288 | bytes 3145728 | tf_op jit(solution)/shard_map/convert_element_type | solution.py:362
  15.6 4.9 %shard_map.120 = (bf16[1024,256]{1,0:T(8,128)(2,1)S(1)}, f32[1024,256]{1,0:T(8,128)S(1)}, f32[1024,256]{1,0:T(8,128)S(1)}, f32[4,16,128]{2,1,0:T(8,128)S(1)}) custom-call(s32[8,1024]{1,0:T(8,128)S(1)} %concatenate.3.ids_ref, s32[4,1024]{1,0:T(4,128)S(1)} %reshape.37.negs_ref, bf16[2048,256]{1,0:T(8,128)(2,1)S(1)} %convert_element_type.7.low_ref, ...), custom_call_target="tpu_custom_call" | custom-call | flops 4294967296 | bytes 4194304 | tf_op jit(solution)/shard_map/pallas_call | solution.py:378
  22.7 2.2 %shard_map.121 = (bf16[1024,1024]{1,0:T(8,128)(2,1)S(1)}, f32[1024,256]{1,0:T(8,128)S(1)}, f32[1024,256]{1,0:T(8,128)S(1)}) custom-call(s32[8,1024]{1,0:T(8,128)S(1)} %concatenate.3.ids_ref, bf16[512,256]{1,0:T(8,128)(2,1)S(1)} %collective-permute-done.near_ref, bf16[512,256]{1,0:T(8,128)(2,1)S(1)} %collective-permute-done.2.far_ref, ...), custom_call_target="tpu_custom_call" | custom-call | flops 1610612736 | bytes 4194304 | tf_op jit(solution)/shard_map/pallas_call | solution.py:401
  25.0 4.5 %collective-permute-done.1.near_ref = bf16[512,256]{1,0:T(8,128)(2,1)S(1)} collective-permute-done((bf16[512,256]{1,0:T(8,128)(2,1)S(1)}, bf16[512,256]{1,0:T(8,128)(2,1)S(1)}, u32[]{:S(2)}, u32[]{:S(2)}) %collective-permute-start.1) | collective-permute-done | bytes 262176 | tf_op jit(solution)/shard_map/ppermute | solution.py:343
  31.5 5.9 %shard_map.122 = (f32[1024,256]{1,0:T(8,128)S(1)}, bf16[1024,256]{1,0:T(8,128)(2,1)S(1)}, f32[1024,256]{1,0:T(8,128)S(1)}, bf16[1024,256]{1,0:T(8,128)(2,1)S(1)}, bf16[1024,256]{1,0:T(8,128)(2,1)S(1)}) custom-call(s32[1,1]{1,0:T(1,128)S(6)} %copy.13.count_ref, s32[8,1024]{1,0:T(8,128)S(1)} %concatenate.3.ids_ref, ...), custom_call_target="tpu_custom_call" | custom-call | flops 4831838208 | bytes 8388608 | tf_op jit(solution)/shard_map/pallas_call | solution.py:411
  37.4 1.2 %shard_map.124 = (f32[1024,256]{1,0:T(8,128)S(1)}, bf16[1024,256]{1,0:T(8,128)(2,1)S(1)}) custom-call(s32[8,1024]{1,0:T(8,128)S(1)} %concatenate.3.ids_ref, bf16[1024,256]{1,0:T(8,128)(2,1)S(1)} %get-tuple-element.69.gr_ref), custom_call_target="tpu_custom_call" | custom-call | flops 1073741824 | bytes 2097152 | tf_op jit(solution)/shard_map/pallas_call | solution.py:427
  40.9 3.7 %collective-permute-start.8 = (bf16[256,256]{1,0:T(8,128)(2,1)S(1)}, bf16[256,256]{1,0:T(8,128)(2,1)S(1)}, u32[]{:S(2)}, u32[]{:S(2)}) collective-permute-start(bf16[256,256]{1,0:T(8,128)(2,1)S(1)} %get-tuple-element.74), channel_id=1, source_target_pairs={{0,6},{1,7},{2,4},{3,5},{4,2},{5,3},{6,0},{7,1},{8,14},{9,15},{10,... | collective-permute-start | bytes 393224 | tf_op jit(solution)/shard_map/ppermute | solution.py:343
  46.9 3.7 %collective-permute-done.8.refs_3_ = bf16[256,256]{1,0:T(8,128)(2,1)S(1)} collective-permute-done((bf16[256,256]{1,0:T(8,128)(2,1)S(1)}, bf16[256,256]{1,0:T(8,128)(2,1)S(1)}, u32[]{:S(2)}, u32[]{:S(2)}) %collective-permute-start.8) | collective-permute-done | bytes 131104 | tf_op jit(solution)/shard_map/ppermute | solution.py:343
  50.6 1.5 %collective-permute-start.10 = (bf16[512,256]{1,0:T(8,128)(2,1)}, bf16[512,256]{1,0:T(8,128)(2,1)S(1)}, u32[]{:S(2)}, u32[]{:S(2)}) collective-permute-start(bf16[512,256]{1,0:T(8,128)(2,1)} %get-tuple-element.79), channel_id=1, source_target_pairs={{0,2},{1,3},{2,0},{3,1},{4,6},{5,7},{6,4},{7,5},{8,10},{9,11},{10,... | collective-permute-start | bytes 786440 | tf_op jit(solution)/shard_map/ppermute | solution.py:343
  52.8 8.5 %all-to-all-start = ((bf16[32,8,256]{2,1,0:T(8,128)(2,1)}), bf16[32,8,256]{2,1,0:T(8,128)(2,1)S(1)}, u32[]{:S(2)}, u32[]{:S(2)}) async-start(bf16[32,8,256]{2,1,0:T(8,128)(2,1)} %bitcast.2), calls=%async_computation | async-start | bytes 262144 | tf_op jit(solution)/shard_map/all_to_all | solution.py:339
  61.3 1.7 %shard_map.127 = bf16[512,256]{1,0:T(8,128)(2,1)} custom-call(bf16[512,256]{1,0:T(8,128)(2,1)S(1)} %get-tuple-element.80.refs_0_, bf16[512,256]{1,0:T(8,128)(2,1)} %collective-permute-done.11.refs_1_), custom_call_target="tpu_custom_call" | custom-call | flops 262144 | bytes 786432 | tf_op jit(solution)/shard_map/pallas_call | solution.py:228
  63.1 7.6 %all-to-all-done.parts_ref = bf16[32,8,256]{2,1,0:T(8,128)(2,1)S(1)} async-done(((bf16[32,8,256]{2,1,0:T(8,128)(2,1)}), bf16[32,8,256]{2,1,0:T(8,128)(2,1)S(1)}, u32[]{:S(2)}, u32[]{:S(2)}) %all-to-all-start) | async-done | bytes 131104 | tf_op jit(solution)/shard_map/all_to_all | solution.py:339
  71.4 3.9 %all-to-all-start.1 = ((f32[32,8,256]{2,1,0:T(8,128)}), f32[32,8,256]{2,1,0:T(8,128)S(1)}, u32[]{:S(2)}, u32[]{:S(2)}) async-start(f32[32,8,256]{2,1,0:T(8,128)} %shard_map.130), calls=%async_computation.1 | async-start | bytes 524288 | tf_op jit(solution)/shard_map/all_to_all | solution.py:339
  75.3 1.2 %shard_map.128.refs_0_ = bf16[528,256]{1,0:T(8,128)(2,1)S(1)} custom-call(f32[512,256]{1,0:T(8,128)S(1)} %get-tuple-element.68.refs_0_, bf16[512,256]{1,0:T(8,128)(2,1)S(1)} %collective-permute-done.10.refs_1_, bf16[512,256]{1,0:T(8,128)(2,1)} %collective-permute-done.12.refs_2_), custom_call_target="tpu_custom_call" | custom-call | flops 393216 | bytes 1179648 | tf_op jit(solution)/shard_map/pallas_call | solution.py:264
  76.8 3.1 %collective-permute-start.14 = (bf16[528,256]{1,0:T(8,128)(2,1)S(1)}, bf16[528,256]{1,0:T(8,128)(2,1)S(1)}, u32[]{:S(2)}, u32[]{:S(2)}) collective-permute-start(bf16[528,256]{1,0:T(8,128)(2,1)S(1)} %shard_map.128.refs_0_), channel_id=1, source_target_pairs={{0,1},{1,0},{2,3},{3,2},{4,5},{5,4},{6,7},{7,6},{8,9},{9,8},{10,11... | collective-permute-start | bytes 811016 | tf_op jit(solution)/shard_map/ppermute | solution.py:343
  79.9 6.0 %all-to-all-done.1 = f32[32,8,256]{2,1,0:T(8,128)S(1)} async-done(((f32[32,8,256]{2,1,0:T(8,128)}), f32[32,8,256]{2,1,0:T(8,128)S(1)}, u32[]{:S(2)}, u32[]{:S(2)}) %all-to-all-start.1) | async-done | bytes 262176 | tf_op jit(solution)/shard_map/all_to_all | solution.py:339
  85.9 4.3 %collective-permute-start.15 = (bf16[528,256]{1,0:T(8,128)(2,1)S(1)}, bf16[528,256]{1,0:T(8,128)(2,1)}, u32[]{:S(2)}, u32[]{:S(2)}) collective-permute-start(bf16[528,256]{1,0:T(8,128)(2,1)S(1)} %collective-permute-done.13.refs_1_), channel_id=1, source_target_pairs={{0,1},{1,0},{2,3},{3,2},{4,5},{5,4},{6,7},{7,6},{8,9},{9,8},{10,11... | collective-permute-start | bytes 811016 | tf_op jit(solution)/shard_map/ppermute | solution.py:343
  92.0 1.7 %collective-permute-start.16 = (bf16[272,256]{1,0:T(8,128)(2,1)S(1)}, bf16[272,256]{1,0:T(8,128)(2,1)}, u32[]{:S(2)}, u32[]{:S(2)}) collective-permute-start(bf16[272,256]{1,0:T(8,128)(2,1)S(1)} %shard_map.132.refs_0_), channel_id=1, source_target_pairs={{0,2},{1,3},{2,0},{3,1},{4,6},{5,7},{6,4},{7,5},{8,10},{9,11},{10,... | collective-permute-start | bytes 417800 | tf_op jit(solution)/shard_map/ppermute | solution.py:343
  94.5 3.1 %shard_map.131 = (f32[2048,256]{1,0:T(8,128)}, f32[16,128]{1,0:T(8,128)}) custom-call(s32[1]{0:T(128)} %bitcast.place_ref, f32[2048,256]{1,0:T(8,128)S(1)} %copy-done, f32[16,128]{1,0:T(8,128)S(1)} %bitcast.9, bf16[528,256]{1,0:T(8,128)(2,1)S(1)} %shard_map.128.refs_0_, bf16[528,256]{1,0:T(8,128)(2,1)S(1)} %collective-permute-done.13.refs_1_, ...), custom_call_target="tpu_custom_call" | custom-call | flops 4194304 | bytes 5242880 | tf_op jit(solution)/shard_map/pallas_call | solution.py:304
  97.6 2.3 %collective-permute-done.18.refs_3_ = bf16[272,256]{1,0:T(8,128)(2,1)S(1)} collective-permute-done((bf16[272,256]{1,0:T(8,128)(2,1)S(1)}, bf16[272,256]{1,0:T(8,128)(2,1)S(1)}, u32[]{:S(2)}, u32[]{:S(2)}) %collective-permute-start.18) | collective-permute-done | bytes 139296 | tf_op jit(solution)/shard_map/ppermute | solution.py:343
  103.0 1.6 %copy-done.2 = f32[2048,256]{1,0:T(8,128)S(1)} copy-done((f32[2048,256]{1,0:T(8,128)S(1)}, f32[2048,256]{1,0:T(8,128)}, u32[]{:S(2)}) %copy-start.2) | copy-done | bytes 2097176
  104.6 3.1 %shard_map.133 = (f32[2048,256]{1,0:T(8,128)}, f32[16,128]{1,0:T(8,128)}) custom-call(s32[1]{0:T(128)} %bitcast.5.place_ref, f32[2048,256]{1,0:T(8,128)S(1)} %copy-done.2, f32[16,128]{1,0:T(8,128)S(1)} %bitcast.10, bf16[272,256]{1,0:T(8,128)(2,1)S(1)} %shard_map.132.refs_0_, bf16[272,256]{1,0:T(8,128)(2,1)} %collective-permute-done.16.refs_1_, ...), custom_call_target="tpu_custom_call" | custom-call | flops 4194304 | bytes 5242880 | tf_op jit(solution)/shard_map/pallas_call | solution.py:304
  (66 shorter events, 15.8 us)
Async XLA Ops:
  2.6 17.9 %collective-permute-start = (bf16[512,256]{1,0:T(8,128)(2,1)}, bf16[512,256]{1,0:T(8,128)(2,1)S(1)}, u32[]{:S(2)}, u32[]{:S(2)}) collective-permute-start(bf16[512,256]{1,0:T(8,128)(2,1)} %dynamic-slice_convert_fusion), channel_id=1, source_target_pairs={{6,0},{7,1},{4,2},{5,3},{10,4},{11,5},{8,6},{9,7},{14,8},{15,9},{1... | collective-permute-start | bytes 786440 | tf_op jit(solution)/shard_map/ppermute | solution.py:348
  20.5 2.2 %collective-permute-start.2 = (bf16[512,256]{1,0:T(8,128)(2,1)S(1)}, bf16[512,256]{1,0:T(8,128)(2,1)S(1)}, u32[]{:S(2)}, u32[]{:S(2)}) collective-permute-start(bf16[512,256]{1,0:T(8,128)(2,1)S(1)} %collective-permute-done.near_ref), channel_id=1, source_target_pairs={{0,1},{1,0},{2,3},{3,2},{4,5},{5,4},{6,7},{7,6},{8,9},{9,8},{10,11... | collective-permute-start | bytes 786440 | tf_op jit(solution)/shard_map/ppermute | solution.py:343
  21.6 7.9 %collective-permute-start.1 = (bf16[512,256]{1,0:T(8,128)(2,1)S(1)}, bf16[512,256]{1,0:T(8,128)(2,1)S(1)}, u32[]{:S(2)}, u32[]{:S(2)}) collective-permute-start(bf16[512,256]{1,0:T(8,128)(2,1)S(1)} %collective-permute-done.near_ref), channel_id=1, source_target_pairs={{0,2},{1,3},{2,0},{3,1},{4,6},{5,7},{6,4},{7,5},{8,10},{9,11},{10,... | collective-permute-start | bytes 786440 | tf_op jit(solution)/shard_map/ppermute | solution.py:343
  29.4 2.0 %collective-permute-start.3 = (bf16[512,256]{1,0:T(8,128)(2,1)S(1)}, bf16[512,256]{1,0:T(8,128)(2,1)S(1)}, u32[]{:S(2)}, u32[]{:S(2)}) collective-permute-start(bf16[512,256]{1,0:T(8,128)(2,1)S(1)} %collective-permute-done.1.near_ref), channel_id=1, source_target_pairs={{0,1},{1,0},{2,3},{3,2},{4,5},{5,4},{6,7},{7,6},{8,9},{9,8},{10,11... | collective-permute-start | bytes 786440 | tf_op jit(solution)/shard_map/ppermute | solution.py:343
  38.6 2.0 %collective-permute-start.5 = (bf16[1024,256]{1,0:T(8,128)(2,1)S(1)}, bf16[1024,256]{1,0:T(8,128)(2,1)S(1)}, u32[]{:S(2)}, u32[]{:S(2)}) collective-permute-start(bf16[1024,256]{1,0:T(8,128)(2,1)S(1)} %get-tuple-element.71), channel_id=1, source_target_pairs={{0,1},{1,0},{2,3},{3,2},{4,5},{5,4},{6,7},{7,6},{8,9},{9,8},{10,11... | collective-permute-start | bytes 1572872 | tf_op jit(solution)/shard_map/ppermute | solution.py:343
  39.1 5.6 %collective-permute-start.4 = (bf16[1024,256]{1,0:T(8,128)(2,1)S(1)}, bf16[1024,256]{1,0:T(8,128)(2,1)S(1)}, u32[]{:S(2)}, u32[]{:S(2)}) collective-permute-start(bf16[1024,256]{1,0:T(8,128)(2,1)S(1)} %get-tuple-element.67), channel_id=1, source_target_pairs={{0,1},{1,0},{2,3},{3,2},{4,5},{5,4},{6,7},{7,6},{8,9},{9,8},{10,11... | collective-permute-start | bytes 1572872 | tf_op jit(solution)/shard_map/ppermute | solution.py:343
  39.2 6.2 %collective-permute-start.9 = (bf16[1024,256]{1,0:T(8,128)(2,1)S(1)}, bf16[1024,256]{1,0:T(8,128)(2,1)S(1)}, u32[]{:S(2)}, u32[]{:S(2)}) collective-permute-start(bf16[1024,256]{1,0:T(8,128)(2,1)S(1)} %get-tuple-element.76), channel_id=1, source_target_pairs={{0,1},{1,0},{2,3},{3,2},{4,5},{5,4},{6,7},{7,6},{8,9},{9,8},{10,11... | collective-permute-start | bytes 1572872 | tf_op jit(solution)/shard_map/ppermute | solution.py:343
  40.7 5.5 %collective-permute-start.6 = (bf16[256,256]{1,0:T(8,128)(2,1)S(1)}, bf16[256,256]{1,0:T(8,128)(2,1)S(1)}, u32[]{:S(2)}, u32[]{:S(2)}) collective-permute-start(bf16[256,256]{1,0:T(8,128)(2,1)S(1)} %get-tuple-element.72), channel_id=1, source_target_pairs={{0,2},{1,3},{2,0},{3,1},{4,6},{5,7},{6,4},{7,5},{8,10},{9,11},{10,... | collective-permute-start | bytes 393224 | tf_op jit(solution)/shard_map/ppermute | solution.py:343
  40.8 6.1 %collective-permute-start.7 = (bf16[256,256]{1,0:T(8,128)(2,1)S(1)}, bf16[256,256]{1,0:T(8,128)(2,1)S(1)}, u32[]{:S(2)}, u32[]{:S(2)}) collective-permute-start(bf16[256,256]{1,0:T(8,128)(2,1)S(1)} %get-tuple-element.73), channel_id=1, source_target_pairs={{0,4},{1,5},{2,6},{3,7},{4,0},{5,1},{6,2},{7,3},{8,12},{9,13},{10,... | collective-permute-start | bytes 393224 | tf_op jit(solution)/shard_map/ppermute | solution.py:343
  40.9 9.7 %collective-permute-start.8 = (bf16[256,256]{1,0:T(8,128)(2,1)S(1)}, bf16[256,256]{1,0:T(8,128)(2,1)S(1)}, u32[]{:S(2)}, u32[]{:S(2)}) collective-permute-start(bf16[256,256]{1,0:T(8,128)(2,1)S(1)} %get-tuple-element.74), channel_id=1, source_target_pairs={{0,6},{1,7},{2,4},{3,5},{4,2},{5,3},{6,0},{7,1},{8,14},{9,15},{10,... | collective-permute-start | bytes 393224 | tf_op jit(solution)/shard_map/ppermute | solution.py:343
  50.6 10.7 %collective-permute-start.11 = (bf16[512,256]{1,0:T(8,128)(2,1)}, bf16[512,256]{1,0:T(8,128)(2,1)}, u32[]{:S(2)}, u32[]{:S(2)}) collective-permute-start(bf16[512,256]{1,0:T(8,128)(2,1)} %get-tuple-element.81), channel_id=1, source_target_pairs={{0,2},{1,3},{2,0},{3,1},{4,6},{5,7},{6,4},{7,5},{8,10},{9,11},{10,... | collective-permute-start | bytes 786440 | tf_op jit(solution)/shard_map/ppermute | solution.py:343
  50.6 20.0 %collective-permute-start.10 = (bf16[512,256]{1,0:T(8,128)(2,1)}, bf16[512,256]{1,0:T(8,128)(2,1)S(1)}, u32[]{:S(2)}, u32[]{:S(2)}) collective-permute-start(bf16[512,256]{1,0:T(8,128)(2,1)} %get-tuple-element.79), channel_id=1, source_target_pairs={{0,2},{1,3},{2,0},{3,1},{4,6},{5,7},{6,4},{7,5},{8,10},{9,11},{10,... | collective-permute-start | bytes 786440 | tf_op jit(solution)/shard_map/ppermute | solution.py:343
  52.8 17.8 %all-to-all-start = ((bf16[32,8,256]{2,1,0:T(8,128)(2,1)}), bf16[32,8,256]{2,1,0:T(8,128)(2,1)S(1)}, u32[]{:S(2)}, u32[]{:S(2)}) async-start(bf16[32,8,256]{2,1,0:T(8,128)(2,1)} %bitcast.2), calls=%async_computation | async-start | bytes 262144 | tf_op jit(solution)/shard_map/all_to_all | solution.py:339
  63.0 12.3 %collective-permute-start.12 = (bf16[512,256]{1,0:T(8,128)(2,1)}, bf16[512,256]{1,0:T(8,128)(2,1)}, u32[]{:S(2)}, u32[]{:S(2)}) collective-permute-start(bf16[512,256]{1,0:T(8,128)(2,1)} %shard_map.127), channel_id=1, source_target_pairs={{254,0},{255,1},{252,2},{253,3},{2,4},{3,5},{0,6},{1,7},{6,8},{7,9... | collective-permute-start | bytes 786440 | tf_op jit(solution)/shard_map/ppermute | solution.py:348
  71.4 14.5 %all-to-all-start.1 = ((f32[32,8,256]{2,1,0:T(8,128)}), f32[32,8,256]{2,1,0:T(8,128)S(1)}, u32[]{:S(2)}, u32[]{:S(2)}) async-start(f32[32,8,256]{2,1,0:T(8,128)} %shard_map.130), calls=%async_computation.1 | async-start | bytes 524288 | tf_op jit(solution)/shard_map/all_to_all | solution.py:339
  76.5 9.4 %collective-permute-start.13 = (bf16[528,256]{1,0:T(8,128)(2,1)S(1)}, bf16[528,256]{1,0:T(8,128)(2,1)S(1)}, u32[]{:S(2)}, u32[]{:S(2)}) collective-permute-start(bf16[528,256]{1,0:T(8,128)(2,1)S(1)} %shard_map.128.refs_0_), channel_id=1, source_target_pairs={{0,2},{1,3},{2,0},{3,1},{4,6},{5,7},{6,4},{7,5},{8,10},{9,11},{10,... | collective-permute-start | bytes 811016 | tf_op jit(solution)/shard_map/ppermute | solution.py:343
  76.8 16.9 %collective-permute-start.14 = (bf16[528,256]{1,0:T(8,128)(2,1)S(1)}, bf16[528,256]{1,0:T(8,128)(2,1)S(1)}, u32[]{:S(2)}, u32[]{:S(2)}) collective-permute-start(bf16[528,256]{1,0:T(8,128)(2,1)S(1)} %shard_map.128.refs_0_), channel_id=1, source_target_pairs={{0,1},{1,0},{2,3},{3,2},{4,5},{5,4},{6,7},{7,6},{8,9},{9,8},{10,11... | collective-permute-start | bytes 811016 | tf_op jit(solution)/shard_map/ppermute | solution.py:343
  85.9 8.7 %collective-permute-start.15 = (bf16[528,256]{1,0:T(8,128)(2,1)S(1)}, bf16[528,256]{1,0:T(8,128)(2,1)}, u32[]{:S(2)}, u32[]{:S(2)}) collective-permute-start(bf16[528,256]{1,0:T(8,128)(2,1)S(1)} %collective-permute-done.13.refs_1_), channel_id=1, source_target_pairs={{0,1},{1,0},{2,3},{3,2},{4,5},{5,4},{6,7},{7,6},{8,9},{9,8},{10,11... | collective-permute-start | bytes 811016 | tf_op jit(solution)/shard_map/ppermute | solution.py:343
  90.3 9.6 %collective-permute-start.18 = (bf16[272,256]{1,0:T(8,128)(2,1)S(1)}, bf16[272,256]{1,0:T(8,128)(2,1)S(1)}, u32[]{:S(2)}, u32[]{:S(2)}) collective-permute-start(bf16[272,256]{1,0:T(8,128)(2,1)S(1)} %shard_map.132.refs_0_), channel_id=1, source_target_pairs={{0,6},{1,7},{2,4},{3,5},{4,2},{5,3},{6,0},{7,1},{8,14},{9,15},{10,... | collective-permute-start | bytes 417800 | tf_op jit(solution)/shard_map/ppermute | solution.py:343
  90.9 9.0 %collective-permute-start.17 = (bf16[272,256]{1,0:T(8,128)(2,1)S(1)}, bf16[272,256]{1,0:T(8,128)(2,1)S(1)}, u32[]{:S(2)}, u32[]{:S(2)}) collective-permute-start(bf16[272,256]{1,0:T(8,128)(2,1)S(1)} %shard_map.132.refs_0_), channel_id=1, source_target_pairs={{0,4},{1,5},{2,6},{3,7},{4,0},{5,1},{6,2},{7,3},{8,12},{9,13},{10,... | collective-permute-start | bytes 417800 | tf_op jit(solution)/shard_map/ppermute | solution.py:343
  92.0 8.3 %collective-permute-start.16 = (bf16[272,256]{1,0:T(8,128)(2,1)S(1)}, bf16[272,256]{1,0:T(8,128)(2,1)}, u32[]{:S(2)}, u32[]{:S(2)}) collective-permute-start(bf16[272,256]{1,0:T(8,128)(2,1)S(1)} %shard_map.132.refs_0_), channel_id=1, source_target_pairs={{0,2},{1,3},{2,0},{3,1},{4,6},{5,7},{6,4},{7,5},{8,10},{9,11},{10,... | collective-permute-start | bytes 417800 | tf_op jit(solution)/shard_map/ppermute | solution.py:343
  93.7 8.3 %collective-permute-start.19 = (bf16[272,256]{1,0:T(8,128)(2,1)S(1)}, bf16[272,256]{1,0:T(8,128)(2,1)}, u32[]{:S(2)}, u32[]{:S(2)}) collective-permute-start(bf16[272,256]{1,0:T(8,128)(2,1)S(1)} %shard_map.132.refs_0_), channel_id=1, source_target_pairs={{0,1},{1,0},{2,3},{3,2},{4,5},{5,4},{6,7},{7,6},{8,9},{9,8},{10,11... | collective-permute-start | bytes 417800 | tf_op jit(solution)/shard_map/ppermute | solution.py:343
  100.3 2.5 %collective-permute-start.20 = (bf16[272,256]{1,0:T(8,128)(2,1)}, bf16[272,256]{1,0:T(8,128)(2,1)S(1)}, u32[]{:S(2)}, u32[]{:S(2)}) collective-permute-start(bf16[272,256]{1,0:T(8,128)(2,1)} %collective-permute-done.16.refs_1_), channel_id=1, source_target_pairs={{0,1},{1,0},{2,3},{3,2},{4,5},{5,4},{6,7},{7,6},{8,9},{9,8},{10,11... | collective-permute-start | bytes 417800 | tf_op jit(solution)/shard_map/ppermute | solution.py:343
  101.4 1.6 %collective-permute-start.22 = (bf16[272,256]{1,0:T(8,128)(2,1)S(1)}, bf16[272,256]{1,0:T(8,128)(2,1)S(1)}, u32[]{:S(2)}, u32[]{:S(2)}) collective-permute-start(bf16[272,256]{1,0:T(8,128)(2,1)S(1)} %collective-permute-done.18.refs_3_), channel_id=1, source_target_pairs={{0,1},{1,0},{2,3},{3,2},{4,5},{5,4},{6,7},{7,6},{8,9},{9,8},{10,11... | collective-permute-start | bytes 417800 | tf_op jit(solution)/shard_map/ppermute | solution.py:343
  (10 other events, 188.5 us)

commit v10 on v8

--- a/solution.py
+++ b/solution.py
@@ -19,7 +19,8 @@
 RATE = 0.1
 AXES = ("blk", "rep")
 VMEM_LIMIT = 32 * 1024 * 1024
-SMALL_VMEM_LIMIT = 16 * 1024 * 1024
+UPDATE_VMEM_LIMIT = 52 * 1024 * 1024
+LARGE_VMEM_LIMIT = 62 * 1024 * 1024
 CHUNK = 256
 UNROLL = 4
 
@@ -276,16 +277,24 @@
     return tile[row : row + 1, :H] + tile[row : row + 1, H:] + tile[8 + row : 9 + row, :H]
 
 
-def update_kernel(n, place_ref, rows_ref, acc_ref, *refs):
+def update_kernel(n, total, first, place_ref, rows_ref, acc_ref, *refs):
+    if first:
+        _, old_acc_ref, *refs = refs
     pieces, (new_ref, new_acc_ref, in_ref, buf_ref, in_sem, out_sem) = refs[:n], refs[n:]
     size = in_ref.shape[0] // n
-    starts = [lax.bitwise_xor(k, place_ref[0]) * size for k in range(n)]
-    fetches, copies = [], []
-    for k, start in enumerate(starts):
-        rows = pl.ds(pl.multiple_of(start, size), size)
-        fetch = pltpu.make_async_copy(rows_ref.at[rows, :], in_ref.at[rows, :], in_sem.at[k])
+    starts = [lax.bitwise_xor(first + k, place_ref[0]) * size for k in range(n)]
+    spans = [pl.ds(pl.multiple_of(start, size), size) for start in starts]
+    fetches = [
+        pltpu.make_async_copy(
+            rows_ref.at[span, :], in_ref.at[pl.ds(k * size, size), :], in_sem.at[k]
+        )
+        for k, span in enumerate(spans)
+    ]
+    for fetch in fetches:
         fetch.start()
-        fetches.append(fetch)
+    if first:
+        new_acc_ref[...] = old_acc_ref[...]
+    copies = []
     for k, (start, piece) in enumerate(zip(starts, pieces)):
         fetches[k].wait()
         for r in range(0, size, H):
@@ -294,38 +303,75 @@
             acc = acc_ref[at, :] + means_of(piece, size, r // H)
             new_acc_ref[at, :] = acc
             scale = jnp.transpose(jnp.broadcast_to(RATE / jnp.sqrt(acc), (H, H)))
-            rows = pl.ds(pl.multiple_of(start + r, H), H)
+            rows = slice(k * size + r, k * size + r + H)
             buf_ref[rows, :H] = in_ref[rows, :H] - g[:, :H] * scale
             buf_ref[rows, H:] = in_ref[rows, H:] - g[:, H:] * scale
-        rows = pl.ds(pl.multiple_of(start, size), size)
-        copy = pltpu.make_async_copy(buf_ref.at[rows, :], new_ref.at[rows, :], out_sem.at[k])
+        copy = pltpu.make_async_copy(
+            buf_ref.at[pl.ds(k * size, size), :], new_ref.at[spans[k], :], out_sem.at[k]
+        )
         copy.start()
         copies.append(copy)
     for copy in copies:
         copy.wait()
 
 
-def update(rows, acc, pieces, place):
+def update(rows, acc, pieces, place, total=None, old=()):
     n = rows.shape[0]
     k = len(pieces)
-    new, new_acc = pl.pallas_call(
-        functools.partial(update_kernel, k),
+    total = total or k
+    first = total - k if old else 0
+    size = n // total
+    any_space = pl.BlockSpec(memory_space=pl.ANY)
+    return pl.pallas_call(
+        functools.partial(update_kernel, k, total, first),
         out_shape=[
             jax.ShapeDtypeStruct((n, D), F32),
             jax.ShapeDtypeStruct((n // H, H), F32),
         ],
-        in_specs=[smem(), pl.BlockSpec(memory_space=pl.ANY)] + [vmem()] * (1 + k),
-        out_specs=[pl.BlockSpec(memory_space=pl.ANY), vmem()],
+        in_specs=[smem(), pl.BlockSpec(memory_space=pltpu.HBM), vmem()]
+        + ([any_space, vmem()] if old else [])
+        + [vmem()] * k,
+        out_specs=[any_space, vmem()],
         scratch_shapes=[
-            pltpu.VMEM((n, D), F32),
-            pltpu.VMEM((n, D), F32),
+            pltpu.VMEM((k * size, D), F32),
+            pltpu.VMEM((k * size, D), F32),
             pltpu.SemaphoreType.DMA((k,)),
             pltpu.SemaphoreType.DMA((k,)),
         ],
+        input_output_aliases={3: 0} if old else {},
         cost_estimate=pl.CostEstimate(flops=8 * n * D, bytes_accessed=10 * n * D, transcendentals=n),
-        compiler_params=pltpu.CompilerParams(vmem_limit_bytes=SMALL_VMEM_LIMIT),
-    )(place, rows, acc.reshape(n // H, H), *pieces)
-    return new, new_acc.reshape(n)
+        compiler_params=pltpu.CompilerParams(vmem_limit_bytes=UPDATE_VMEM_LIMIT),
+    )(place, rows, acc.reshape(n // H, H), *old, *pieces)
+
+
+def low_quarter_kernel(place_ref, rows_ref, out_ref, in_ref, sem_ref):
+    size = out_ref.shape[0]
+    step = size // 4
+    fetches = []
+    for k in range(4):
+        start = pl.multiple_of(place_ref[0] * size + k * step, step)
+        fetch = pltpu.make_async_copy(
+            rows_ref.at[pl.ds(start, step), :],
+            in_ref.at[pl.ds(k * step, step), :],
+            sem_ref.at[k],
+        )
+        fetch.start()
+        fetches.append(fetch)
+    for k, fetch in enumerate(fetches):
+        fetch.wait()
+        out_ref[k * step : (k + 1) * step, :] = in_ref[k * step : (k + 1) * step, :].astype(BF16)
+
+
+def low_quarter(rows, place):
+    size = rows.shape[0] // 4
+    return pl.pallas_call(
+        low_quarter_kernel,
+        out_shape=jax.ShapeDtypeStruct((size, D), BF16),
+        in_specs=[smem(), pl.BlockSpec(memory_space=pl.ANY)],
+        out_specs=vmem(),
+        scratch_shapes=[pltpu.VMEM((size, D), F32), pltpu.SemaphoreType.DMA((4,))],
+        compiler_params=pltpu.CompilerParams(vmem_limit_bytes=LARGE_VMEM_LIMIT),
+    )(place, rows)
 
 
 def sum_rows_kernel(parts_ref, out_ref):
@@ -372,8 +418,8 @@
     x = (blk % 2) * 2 + xl
 
     low = entities.astype(BF16)
-    quarter = lax.dynamic_slice_in_dim(entities, core * 1024 + (1 - xl) * 512, 512, 0)
-    near_first = shift(quarter.astype(BF16), -1, XL)
+    quarter = low_quarter(entities, (core * 2 + 1 - xl).reshape(1))
+    near_first = shift(quarter, -1, XL)
 
     ids = jnp.concatenate(
         [
@@ -470,13 +516,20 @@
     )
     quarter = sum_with_means([total.reshape(256, D)])
     recv = [swap(quarter, mask) for mask in X_MASKS]
-
-    pieces = [quarter, *recv]
-    pieces = pieces + [swap(piece, CORE) for piece in pieces]
-    pieces, new_entity_acc = lax.optimization_barrier((pieces, new_entity_acc))
+    recv, new_entity_acc = lax.optimization_barrier((recv, new_entity_acc))
+    near_pieces = [quarter, *recv]
+    far_pieces = [swap(piece, CORE) for piece in near_pieces]
     place = (core * 4 + x).reshape(1)
-    new_relations, new_relation_acc = update(relations, relation_acc, pieces, place)
-    return (new_entities, new_entity_acc, new_relations, new_relation_acc)
+    half = update(relations, relation_acc, near_pieces, place, total=8)
+    new_relations, new_relation_acc = update(
+        relations, relation_acc, far_pieces, place, total=8, old=half
+    )
+    return (
+        new_entities,
+        new_entity_acc.reshape(ENT),
+        new_relations,
+        new_relation_acc.reshape(NREL),
+    )
 
 
 def solution(mesh):

time: 107 us -> 108 us (level)
  waiting for transfers between devices: 25.2 us -> 28 us
  local copies, waits for them, and re-layouts: 2.03 us -> 0.11 us
  Pallas kernels: 27.7 us -> 26.5 us
  starting transfers between devices: 48.2 us -> 49.3 us
    ppermute x21, waiting for transfers between devices: 11.6 us -> 15 us  [swap(): return lax.ppermute(x, AXES, [(i, i ^ mask) for i in range(256)])]
    pallas_call x5, Pallas kernels: 4.06 us -> 1.04 us  [add_split(): call(functools.partial(add_split_kernel, len(parts), n_out), shapes, 0, l...]
    pallas_call x2 -> x4, Pallas kernels: 7.28 us -> 10.1 us  [the longest x3 8.23 us: update(): pl.pallas_call(functools.partial(update_kernel, k, total, first), out_sha...]
    convert_element_type x1 -> x0, local copies, waits for them, and re-layouts: 1.92 us -> none  [shards(): near_first = shift(quarter.astype(BF16), -1, XL)]
  transfers between devices with their start and end apart: 25 -> 25, of which waited for: 8 -> 11; matrix products, arithmetic and copies ran while one was open for 2% -> 2% of each run, Pallas kernels for 16% -> 14%
where the time goes in v10:
time: 108 us
  starting transfers between devices  49.3 us (46%)
  waiting for transfers between devices  28 us (26%)
  Pallas kernels  26.5 us (25%)
  between operations  1.82 us (2%)
  other arithmetic  1.75 us (2%)
    ppermute x21, starting transfers between devices, swap(): return lax.ppermute(x, AXES, [(i, i ^ mask) for i in range(256)])  25.5 us
    ppermute x21, waiting for transfers between devices, swap(): return lax.ppermute(x, AXES, [(i, i ^ mask) for i in range(256)])  15 us
    all_to_all x2, waiting for transfers between devices, spread(): lax.all_to_all(parts, 'blk', 0, 0, axis_index_groups=groups, tiled=True)  13 us
    all_to_all x2, starting transfers between devices, spread(): lax.all_to_all(parts, 'blk', 0, 0, axis_index_groups=groups, tiled=True)  12.3 us
    ppermute x2, starting transfers between devices, shift(): return lax.ppermute(x, AXES, route)  11.5 us
    pallas_call x3, Pallas kernels, update(): pl.pallas_call(functools.partial(update_kernel, k, total, first), out_sha...  8.23 us
    pallas_call x1, Pallas kernels, shards(): call(score_kernel, [kept, sent, kept, sent, slots_low], 1, 10, [pltpu.VME...  5.89 us
    pallas_call x1, Pallas kernels, shards(): call(gather_kernel, [jax.ShapeDtypeStruct((EDGES, D), BF16), jax.ShapeDty...  4.9 us
  transfers between devices with their start and end apart: 25, of which 11 were waited for; matrix products, arithmetic and copies ran while one was open for 2% of the time, Pallas kernels for 14%

profile of v10, /device:TPU:1, one launch (start us, length us, event | category | flops | bytes accessed | tf_op | source)
XLA Modules:
  0.0 107.5 jit_solution(1976122941755294028)
XLA Ops:
  0.7 1.8 %shard_map.120 = bf16[512,256]{1,0:T(8,128)(2,1)} custom-call(s32[1]{0:T(128)} %bitcast.2.place_ref, f32[2048,256]{1,0:T(8,128)} %rows_ref.5), custom_call_target="tpu_custom_call" | custom-call | tf_op jit(solution)/shard_map/pallas_call | solution.py:367
  2.6 11.1 %collective-permute-start = (bf16[512,256]{1,0:T(8,128)(2,1)}, bf16[512,256]{1,0:T(8,128)(2,1)S(1)}, u32[]{:S(2)}, u32[]{:S(2)}) collective-permute-start(bf16[512,256]{1,0:T(8,128)(2,1)} %shard_map.120), channel_id=1, source_target_pairs={{6,0},{7,1},{4,2},{5,3},{10,4},{11,5},{8,6},{9,7},{14,8},{15,9},{1... | collective-permute-start | bytes 786440 | tf_op jit(solution)/shard_map/ppermute | solution.py:406
  13.7 1.7 %convert_element_type.3.low_ref = bf16[2048,256]{1,0:T(8,128)(2,1)S(1)} convert(f32[2048,256]{1,0:T(8,128)} %rows_ref.5) | non-fusion elementwise | flops 524288 | bytes 3145728 | tf_op jit(solution)/shard_map/convert_element_type | solution.py:420
  15.6 4.9 %shard_map.121 = (bf16[1024,256]{1,0:T(8,128)(2,1)S(1)}, f32[1024,256]{1,0:T(8,128)S(1)}, f32[1024,256]{1,0:T(8,128)S(1)}, f32[4,16,128]{2,1,0:T(8,128)S(1)}) custom-call(s32[8,1024]{1,0:T(8,128)S(1)} %concatenate.3.ids_ref, s32[4,1024]{1,0:T(4,128)S(1)} %reshape.42.negs_ref, bf16[2048,256]{1,0:T(8,128)(2,1)S(1)} %convert_element_type.3.low_ref, ...), custom_call_target="tpu_custom_call" | custom-call | flops 4294967296 | bytes 4194304 | tf_op jit(solution)/shard_map/pallas_call | solution.py:436
  21.6 1.2 %collective-permute-done.2.far_ref = bf16[512,256]{1,0:T(8,128)(2,1)S(1)} collective-permute-done((bf16[512,256]{1,0:T(8,128)(2,1)S(1)}, bf16[512,256]{1,0:T(8,128)(2,1)S(1)}, u32[]{:S(2)}, u32[]{:S(2)}) %collective-permute-start.2) | collective-permute-done | bytes 262176 | tf_op jit(solution)/shard_map/ppermute | solution.py:401
  22.7 2.2 %shard_map.122 = (bf16[1024,1024]{1,0:T(8,128)(2,1)S(1)}, f32[1024,256]{1,0:T(8,128)S(1)}, f32[1024,256]{1,0:T(8,128)S(1)}) custom-call(s32[8,1024]{1,0:T(8,128)S(1)} %concatenate.3.ids_ref, bf16[512,256]{1,0:T(8,128)(2,1)S(1)} %collective-permute-done.near_ref, bf16[512,256]{1,0:T(8,128)(2,1)S(1)} %collective-permute-done.2.far_ref, ...), custom_call_target="tpu_custom_call" | custom-call | flops 1610612736 | bytes 4194304 | tf_op jit(solution)/shard_map/pallas_call | solution.py:459
  25.0 4.5 %collective-permute-done.1.near_ref = bf16[512,256]{1,0:T(8,128)(2,1)S(1)} collective-permute-done((bf16[512,256]{1,0:T(8,128)(2,1)S(1)}, bf16[512,256]{1,0:T(8,128)(2,1)S(1)}, u32[]{:S(2)}, u32[]{:S(2)}) %collective-permute-start.1) | collective-permute-done | bytes 262176 | tf_op jit(solution)/shard_map/ppermute | solution.py:401
  31.5 5.9 %shard_map.123 = (f32[1024,256]{1,0:T(8,128)S(1)}, bf16[1024,256]{1,0:T(8,128)(2,1)S(1)}, f32[1024,256]{1,0:T(8,128)S(1)}, bf16[1024,256]{1,0:T(8,128)(2,1)S(1)}, bf16[1024,256]{1,0:T(8,128)(2,1)S(1)}) custom-call(s32[1,1]{1,0:T(1,128)S(6)} %copy.15.count_ref, s32[8,1024]{1,0:T(8,128)S(1)} %concatenate.3.ids_ref, ...), custom_call_target="tpu_custom_call" | custom-call | flops 4831838208 | bytes 8388608 | tf_op jit(solution)/shard_map/pallas_call | solution.py:469
  37.4 1.2 %shard_map.125 = (f32[1024,256]{1,0:T(8,128)S(1)}, bf16[1024,256]{1,0:T(8,128)(2,1)S(1)}) custom-call(s32[8,1024]{1,0:T(8,128)S(1)} %concatenate.3.ids_ref, bf16[1024,256]{1,0:T(8,128)(2,1)S(1)} %get-tuple-element.62.gr_ref), custom_call_target="tpu_custom_call" | custom-call | flops 1073741824 | bytes 2097152 | tf_op jit(solution)/shard_map/pallas_call | solution.py:485
  40.9 3.7 %collective-permute-start.8 = (bf16[256,256]{1,0:T(8,128)(2,1)S(1)}, bf16[256,256]{1,0:T(8,128)(2,1)S(1)}, u32[]{:S(2)}, u32[]{:S(2)}) collective-permute-start(bf16[256,256]{1,0:T(8,128)(2,1)S(1)} %get-tuple-element.67), channel_id=1, source_target_pairs={{0,6},{1,7},{2,4},{3,5},{4,2},{5,3},{6,0},{7,1},{8,14},{9,15},{10,... | collective-permute-start | bytes 393224 | tf_op jit(solution)/shard_map/ppermute | solution.py:401
  45.5 1.4 %collective-permute-done.7.refs_2_ = bf16[256,256]{1,0:T(8,128)(2,1)S(1)} collective-permute-done((bf16[256,256]{1,0:T(8,128)(2,1)S(1)}, bf16[256,256]{1,0:T(8,128)(2,1)S(1)}, u32[]{:S(2)}, u32[]{:S(2)}) %collective-permute-start.7) | collective-permute-done | bytes 131104 | tf_op jit(solution)/shard_map/ppermute | solution.py:401
  46.9 3.7 %collective-permute-done.8.refs_3_ = bf16[256,256]{1,0:T(8,128)(2,1)S(1)} collective-permute-done((bf16[256,256]{1,0:T(8,128)(2,1)S(1)}, bf16[256,256]{1,0:T(8,128)(2,1)S(1)}, u32[]{:S(2)}, u32[]{:S(2)}) %collective-permute-start.8) | collective-permute-done | bytes 131104 | tf_op jit(solution)/shard_map/ppermute | solution.py:401
  50.7 1.5 %collective-permute-start.10 = (bf16[512,256]{1,0:T(8,128)(2,1)S(1)}, bf16[512,256]{1,0:T(8,128)(2,1)S(1)}, u32[]{:S(2)}, u32[]{:S(2)}) collective-permute-start(bf16[512,256]{1,0:T(8,128)(2,1)S(1)} %get-tuple-element.72), channel_id=1, source_target_pairs={{0,2},{1,3},{2,0},{3,1},{4,6},{5,7},{6,4},{7,5},{8,10},{9,11},{10,... | collective-permute-start | bytes 786440 | tf_op jit(solution)/shard_map/ppermute | solution.py:401
  52.8 8.5 %all-to-all-start = ((bf16[32,8,256]{2,1,0:T(8,128)(2,1)}), bf16[32,8,256]{2,1,0:T(8,128)(2,1)S(1)}, u32[]{:S(2)}, u32[]{:S(2)}) async-start(bf16[32,8,256]{2,1,0:T(8,128)(2,1)} %bitcast.3), calls=%async_computation | async-start | bytes 262144 | tf_op jit(solution)/shard_map/all_to_all | solution.py:397
  61.7 9.0 %all-to-all-done.parts_ref = bf16[32,8,256]{2,1,0:T(8,128)(2,1)S(1)} async-done(((bf16[32,8,256]{2,1,0:T(8,128)(2,1)}), bf16[32,8,256]{2,1,0:T(8,128)(2,1)S(1)}, u32[]{:S(2)}, u32[]{:S(2)}) %all-to-all-start) | async-done | bytes 131104 | tf_op jit(solution)/shard_map/all_to_all | solution.py:397
  71.5 3.9 %all-to-all-start.1 = ((f32[32,8,256]{2,1,0:T(8,128)}), f32[32,8,256]{2,1,0:T(8,128)S(1)}, u32[]{:S(2)}, u32[]{:S(2)}) async-start(f32[32,8,256]{2,1,0:T(8,128)} %shard_map.131), calls=%async_computation.1 | async-start | bytes 524288 | tf_op jit(solution)/shard_map/all_to_all | solution.py:397
  75.8 6.1 %collective-permute-start.14 = (bf16[528,256]{1,0:T(8,128)(2,1)S(1)}, bf16[528,256]{1,0:T(8,128)(2,1)S(1)}, u32[]{:S(2)}, u32[]{:S(2)}) collective-permute-start(bf16[528,256]{1,0:T(8,128)(2,1)S(1)} %shard_map.129.refs_0_), channel_id=1, source_target_pairs={{0,1},{1,0},{2,3},{3,2},{4,5},{5,4},{6,7},{7,6},{8,9},{9,8},{10,11... | collective-permute-start | bytes 811016 | tf_op jit(solution)/shard_map/ppermute | solution.py:401
  81.9 4.1 %all-to-all-done.1 = f32[32,8,256]{2,1,0:T(8,128)S(1)} async-done(((f32[32,8,256]{2,1,0:T(8,128)}), f32[32,8,256]{2,1,0:T(8,128)S(1)}, u32[]{:S(2)}, u32[]{:S(2)}) %all-to-all-start.1) | async-done | bytes 262176 | tf_op jit(solution)/shard_map/all_to_all | solution.py:397
  86.0 4.3 %collective-permute-start.15 = (bf16[528,256]{1,0:T(8,128)(2,1)S(1)}, bf16[528,256]{1,0:T(8,128)(2,1)S(1)}, u32[]{:S(2)}, u32[]{:S(2)}) collective-permute-start(bf16[528,256]{1,0:T(8,128)(2,1)S(1)} %collective-permute-done.13.refs_1_), channel_id=1, source_target_pairs={{0,1},{1,0},{2,3},{3,2},{4,5},{5,4},{6,7},{7,6},{8,9},{9,8},{10,11... | collective-permute-start | bytes 811016 | tf_op jit(solution)/shard_map/ppermute | solution.py:401
  90.5 4.3 %collective-permute-start.17 = (bf16[272,256]{1,0:T(8,128)(2,1)S(1)}, bf16[272,256]{1,0:T(8,128)(2,1)S(1)}, u32[]{:S(2)}, u32[]{:S(2)}) collective-permute-start(bf16[272,256]{1,0:T(8,128)(2,1)S(1)} %shard_map.133.refs_0_), channel_id=1, source_target_pairs={{0,4},{1,5},{2,6},{3,7},{4,0},{5,1},{6,2},{7,3},{8,12},{9,13},{10,... | collective-permute-start | bytes 417800 | tf_op jit(solution)/shard_map/ppermute | solution.py:401
  95.4 3.2 %shard_map.132 = (f32[2048,256]{1,0:T(8,128)}, f32[16,128]{1,0:T(8,128)}) custom-call(s32[1]{0:T(128)} %bitcast.place_ref, f32[2048,256]{1,0:T(8,128)} %rows_ref.5, f32[16,128]{1,0:T(8,128)S(1)} %bitcast.12, bf16[528,256]{1,0:T(8,128)(2,1)S(1)} %shard_map.129.refs_0_, bf16[528,256]{1,0:T(8,128)(2,1)S(1)} %collective-permute-done.13.refs_1_, ...), custom_call_target="tpu_custom_call" | custom-call | flops 4194304 | bytes 5242880 | tf_op jit(solution)/shard_map/pallas_call | solution.py:325
  98.6 1.4 %collective-permute-done.18.refs_3_ = bf16[272,256]{1,0:T(8,128)(2,1)S(1)} collective-permute-done((bf16[272,256]{1,0:T(8,128)(2,1)S(1)}, bf16[272,256]{1,0:T(8,128)(2,1)S(1)}, u32[]{:S(2)}, u32[]{:S(2)}) %collective-permute-start.18) | collective-permute-done | bytes 139296 | tf_op jit(solution)/shard_map/ppermute | solution.py:401
  102.2 2.2 %shard_map.134 = (f32[2048,256]{1,0:T(8,128)}, f32[16,128]{1,0:T(8,128)S(1)}) custom-call(s32[1]{0:T(128)} %bitcast.6.place_ref, f32[2048,256]{1,0:T(8,128)} %rows_ref.7, f32[16,128]{1,0:T(8,128)S(1)} %bitcast.10, bf16[272,256]{1,0:T(8,128)(2,1)S(1)} %shard_map.133.refs_0_, bf16[272,256]{1,0:T(8,128)(2,1)S(1)} %collective-permute-done.16.refs_1_, ...), custom_call_target="tpu_custom_call" | custom-call | flops 4194304 | bytes 5242880 | tf_op jit(solution)/shard_map/pallas_call | solution.py:325
  104.5 2.8 %shard_map.135 = (f32[2048,256]{1,0:T(8,128)}, f32[16,128]{1,0:T(8,128)}) custom-call(s32[1]{0:T(128)} %bitcast.6.place_ref, f32[2048,256]{1,0:T(8,128)} %rows_ref.7, f32[16,128]{1,0:T(8,128)S(1)} %bitcast.11, f32[2048,256]{1,0:T(8,128)} %get-tuple-element.88.refs_0_, f32[16,128]{1,0:T(8,128)S(1)} %get-tuple-element.89.refs_1_, ...), custom_call_target="tpu_custom_call", output_to_operand_aliasing={{0}: (3, {})} | custom-call | flops 4194304 | bytes 5242880 | tf_op jit(solution)/shard_map/pallas_call | solution.py:325
  (63 shorter events, 11.1 us)
Async XLA Ops:
  2.6 18.0 %collective-permute-start = (bf16[512,256]{1,0:T(8,128)(2,1)}, bf16[512,256]{1,0:T(8,128)(2,1)S(1)}, u32[]{:S(2)}, u32[]{:S(2)}) collective-permute-start(bf16[512,256]{1,0:T(8,128)(2,1)} %shard_map.120), channel_id=1, source_target_pairs={{6,0},{7,1},{4,2},{5,3},{10,4},{11,5},{8,6},{9,7},{14,8},{15,9},{1... | collective-permute-start | bytes 786440 | tf_op jit(solution)/shard_map/ppermute | solution.py:406
  20.5 2.2 %collective-permute-start.2 = (bf16[512,256]{1,0:T(8,128)(2,1)S(1)}, bf16[512,256]{1,0:T(8,128)(2,1)S(1)}, u32[]{:S(2)}, u32[]{:S(2)}) collective-permute-start(bf16[512,256]{1,0:T(8,128)(2,1)S(1)} %collective-permute-done.near_ref), channel_id=1, source_target_pairs={{0,1},{1,0},{2,3},{3,2},{4,5},{5,4},{6,7},{7,6},{8,9},{9,8},{10,11... | collective-permute-start | bytes 786440 | tf_op jit(solution)/shard_map/ppermute | solution.py:401
  21.6 7.9 %collective-permute-start.1 = (bf16[512,256]{1,0:T(8,128)(2,1)S(1)}, bf16[512,256]{1,0:T(8,128)(2,1)S(1)}, u32[]{:S(2)}, u32[]{:S(2)}) collective-permute-start(bf16[512,256]{1,0:T(8,128)(2,1)S(1)} %collective-permute-done.near_ref), channel_id=1, source_target_pairs={{0,2},{1,3},{2,0},{3,1},{4,6},{5,7},{6,4},{7,5},{8,10},{9,11},{10,... | collective-permute-start | bytes 786440 | tf_op jit(solution)/shard_map/ppermute | solution.py:401
  29.4 2.0 %collective-permute-start.3 = (bf16[512,256]{1,0:T(8,128)(2,1)S(1)}, bf16[512,256]{1,0:T(8,128)(2,1)S(1)}, u32[]{:S(2)}, u32[]{:S(2)}) collective-permute-start(bf16[512,256]{1,0:T(8,128)(2,1)S(1)} %collective-permute-done.1.near_ref), channel_id=1, source_target_pairs={{0,1},{1,0},{2,3},{3,2},{4,5},{5,4},{6,7},{7,6},{8,9},{9,8},{10,11... | collective-permute-start | bytes 786440 | tf_op jit(solution)/shard_map/ppermute | solution.py:401
  39.1 5.6 %collective-permute-start.4 = (bf16[1024,256]{1,0:T(8,128)(2,1)S(1)}, bf16[1024,256]{1,0:T(8,128)(2,1)S(1)}, u32[]{:S(2)}, u32[]{:S(2)}) collective-permute-start(bf16[1024,256]{1,0:T(8,128)(2,1)S(1)} %get-tuple-element.60), channel_id=1, source_target_pairs={{0,1},{1,0},{2,3},{3,2},{4,5},{5,4},{6,7},{7,6},{8,9},{9,8},{10,11... | collective-permute-start | bytes 1572872 | tf_op jit(solution)/shard_map/ppermute | solution.py:401
  39.2 5.5 %collective-permute-start.9 = (bf16[1024,256]{1,0:T(8,128)(2,1)S(1)}, bf16[1024,256]{1,0:T(8,128)(2,1)S(1)}, u32[]{:S(2)}, u32[]{:S(2)}) collective-permute-start(bf16[1024,256]{1,0:T(8,128)(2,1)S(1)} %get-tuple-element.69), channel_id=1, source_target_pairs={{0,1},{1,0},{2,3},{3,2},{4,5},{5,4},{6,7},{7,6},{8,9},{9,8},{10,11... | collective-permute-start | bytes 1572872 | tf_op jit(solution)/shard_map/ppermute | solution.py:401
  40.7 4.8 %collective-permute-start.6 = (bf16[256,256]{1,0:T(8,128)(2,1)S(1)}, bf16[256,256]{1,0:T(8,128)(2,1)S(1)}, u32[]{:S(2)}, u32[]{:S(2)}) collective-permute-start(bf16[256,256]{1,0:T(8,128)(2,1)S(1)} %get-tuple-element.65), channel_id=1, source_target_pairs={{0,2},{1,3},{2,0},{3,1},{4,6},{5,7},{6,4},{7,5},{8,10},{9,11},{10,... | collective-permute-start | bytes 393224 | tf_op jit(solution)/shard_map/ppermute | solution.py:401
  40.8 6.1 %collective-permute-start.7 = (bf16[256,256]{1,0:T(8,128)(2,1)S(1)}, bf16[256,256]{1,0:T(8,128)(2,1)S(1)}, u32[]{:S(2)}, u32[]{:S(2)}) collective-permute-start(bf16[256,256]{1,0:T(8,128)(2,1)S(1)} %get-tuple-element.66), channel_id=1, source_target_pairs={{0,4},{1,5},{2,6},{3,7},{4,0},{5,1},{6,2},{7,3},{8,12},{9,13},{10,... | collective-permute-start | bytes 393224 | tf_op jit(solution)/shard_map/ppermute | solution.py:401
  40.9 9.7 %collective-permute-start.8 = (bf16[256,256]{1,0:T(8,128)(2,1)S(1)}, bf16[256,256]{1,0:T(8,128)(2,1)S(1)}, u32[]{:S(2)}, u32[]{:S(2)}) collective-permute-start(bf16[256,256]{1,0:T(8,128)(2,1)S(1)} %get-tuple-element.67), channel_id=1, source_target_pairs={{0,6},{1,7},{2,4},{3,5},{4,2},{5,3},{6,0},{7,1},{8,14},{9,15},{10,... | collective-permute-start | bytes 393224 | tf_op jit(solution)/shard_map/ppermute | solution.py:401
  50.7 10.7 %collective-permute-start.11 = (bf16[512,256]{1,0:T(8,128)(2,1)S(1)}, bf16[512,256]{1,0:T(8,128)(2,1)S(1)}, u32[]{:S(2)}, u32[]{:S(2)}) collective-permute-start(bf16[512,256]{1,0:T(8,128)(2,1)S(1)} %get-tuple-element.74), channel_id=1, source_target_pairs={{0,2},{1,3},{2,0},{3,1},{4,6},{5,7},{6,4},{7,5},{8,10},{9,11},{10,... | collective-permute-start | bytes 786440 | tf_op jit(solution)/shard_map/ppermute | solution.py:401
  50.7 20.1 %collective-permute-start.10 = (bf16[512,256]{1,0:T(8,128)(2,1)S(1)}, bf16[512,256]{1,0:T(8,128)(2,1)S(1)}, u32[]{:S(2)}, u32[]{:S(2)}) collective-permute-start(bf16[512,256]{1,0:T(8,128)(2,1)S(1)} %get-tuple-element.72), channel_id=1, source_target_pairs={{0,2},{1,3},{2,0},{3,1},{4,6},{5,7},{6,4},{7,5},{8,10},{9,11},{10,... | collective-permute-start | bytes 786440 | tf_op jit(solution)/shard_map/ppermute | solution.py:401
  52.8 17.9 %all-to-all-start = ((bf16[32,8,256]{2,1,0:T(8,128)(2,1)}), bf16[32,8,256]{2,1,0:T(8,128)(2,1)S(1)}, u32[]{:S(2)}, u32[]{:S(2)}) async-start(bf16[32,8,256]{2,1,0:T(8,128)(2,1)} %bitcast.3), calls=%async_computation | async-start | bytes 262144 | tf_op jit(solution)/shard_map/all_to_all | solution.py:397
  61.4 14.0 %collective-permute-start.12 = (bf16[512,256]{1,0:T(8,128)(2,1)S(1)}, bf16[512,256]{1,0:T(8,128)(2,1)S(1)}, u32[]{:S(2)}, u32[]{:S(2)}) collective-permute-start(bf16[512,256]{1,0:T(8,128)(2,1)S(1)} %shard_map.128), channel_id=1, source_target_pairs={{254,0},{255,1},{252,2},{253,3},{2,4},{3,5},{0,6},{1,7},{6,8},{7,9... | collective-permute-start | bytes 786440 | tf_op jit(solution)/shard_map/ppermute | solution.py:406
  71.5 14.5 %all-to-all-start.1 = ((f32[32,8,256]{2,1,0:T(8,128)}), f32[32,8,256]{2,1,0:T(8,128)S(1)}, u32[]{:S(2)}, u32[]{:S(2)}) async-start(f32[32,8,256]{2,1,0:T(8,128)} %shard_map.131), calls=%async_computation.1 | async-start | bytes 524288 | tf_op jit(solution)/shard_map/all_to_all | solution.py:397
  75.6 10.3 %collective-permute-start.13 = (bf16[528,256]{1,0:T(8,128)(2,1)S(1)}, bf16[528,256]{1,0:T(8,128)(2,1)S(1)}, u32[]{:S(2)}, u32[]{:S(2)}) collective-permute-start(bf16[528,256]{1,0:T(8,128)(2,1)S(1)} %shard_map.129.refs_0_), channel_id=1, source_target_pairs={{0,2},{1,3},{2,0},{3,1},{4,6},{5,7},{6,4},{7,5},{8,10},{9,11},{10,... | collective-permute-start | bytes 811016 | tf_op jit(solution)/shard_map/ppermute | solution.py:401
  75.8 19.1 %collective-permute-start.14 = (bf16[528,256]{1,0:T(8,128)(2,1)S(1)}, bf16[528,256]{1,0:T(8,128)(2,1)S(1)}, u32[]{:S(2)}, u32[]{:S(2)}) collective-permute-start(bf16[528,256]{1,0:T(8,128)(2,1)S(1)} %shard_map.129.refs_0_), channel_id=1, source_target_pairs={{0,1},{1,0},{2,3},{3,2},{4,5},{5,4},{6,7},{7,6},{8,9},{9,8},{10,11... | collective-permute-start | bytes 811016 | tf_op jit(solution)/shard_map/ppermute | solution.py:401
  86.0 9.5 %collective-permute-start.15 = (bf16[528,256]{1,0:T(8,128)(2,1)S(1)}, bf16[528,256]{1,0:T(8,128)(2,1)S(1)}, u32[]{:S(2)}, u32[]{:S(2)}) collective-permute-start(bf16[528,256]{1,0:T(8,128)(2,1)S(1)} %collective-permute-done.13.refs_1_), channel_id=1, source_target_pairs={{0,1},{1,0},{2,3},{3,2},{4,5},{5,4},{6,7},{7,6},{8,9},{9,8},{10,11... | collective-permute-start | bytes 811016 | tf_op jit(solution)/shard_map/ppermute | solution.py:401
  90.4 9.6 %collective-permute-start.18 = (bf16[272,256]{1,0:T(8,128)(2,1)S(1)}, bf16[272,256]{1,0:T(8,128)(2,1)S(1)}, u32[]{:S(2)}, u32[]{:S(2)}) collective-permute-start(bf16[272,256]{1,0:T(8,128)(2,1)S(1)} %shard_map.133.refs_0_), channel_id=1, source_target_pairs={{0,6},{1,7},{2,4},{3,5},{4,2},{5,3},{6,0},{7,1},{8,14},{9,15},{10,... | collective-permute-start | bytes 417800 | tf_op jit(solution)/shard_map/ppermute | solution.py:401
  90.5 9.5 %collective-permute-start.17 = (bf16[272,256]{1,0:T(8,128)(2,1)S(1)}, bf16[272,256]{1,0:T(8,128)(2,1)S(1)}, u32[]{:S(2)}, u32[]{:S(2)}) collective-permute-start(bf16[272,256]{1,0:T(8,128)(2,1)S(1)} %shard_map.133.refs_0_), channel_id=1, source_target_pairs={{0,4},{1,5},{2,6},{3,7},{4,0},{5,1},{6,2},{7,3},{8,12},{9,13},{10,... | collective-permute-start | bytes 417800 | tf_op jit(solution)/shard_map/ppermute | solution.py:401
  94.8 5.8 %collective-permute-start.16 = (bf16[272,256]{1,0:T(8,128)(2,1)S(1)}, bf16[272,256]{1,0:T(8,128)(2,1)S(1)}, u32[]{:S(2)}, u32[]{:S(2)}) collective-permute-start(bf16[272,256]{1,0:T(8,128)(2,1)S(1)} %shard_map.133.refs_0_), channel_id=1, source_target_pairs={{0,2},{1,3},{2,0},{3,1},{4,6},{5,7},{6,4},{7,5},{8,10},{9,11},{10,... | collective-permute-start | bytes 417800 | tf_op jit(solution)/shard_map/ppermute | solution.py:401
  94.9 9.6 %collective-permute-start.19 = (bf16[272,256]{1,0:T(8,128)(2,1)S(1)}, bf16[272,256]{1,0:T(8,128)(2,1)S(1)}, u32[]{:S(2)}, u32[]{:S(2)}) collective-permute-start(bf16[272,256]{1,0:T(8,128)(2,1)S(1)} %shard_map.133.refs_0_), channel_id=1, source_target_pairs={{0,1},{1,0},{2,3},{3,2},{4,5},{5,4},{6,7},{7,6},{8,9},{9,8},{10,11... | collective-permute-start | bytes 417800 | tf_op jit(solution)/shard_map/ppermute | solution.py:401
  100.6 3.9 %collective-permute-start.20 = (bf16[272,256]{1,0:T(8,128)(2,1)S(1)}, bf16[272,256]{1,0:T(8,128)(2,1)S(1)}, u32[]{:S(2)}, u32[]{:S(2)}) collective-permute-start(bf16[272,256]{1,0:T(8,128)(2,1)S(1)} %collective-permute-done.16.refs_1_), channel_id=1, source_target_pairs={{0,1},{1,0},{2,3},{3,2},{4,5},{5,4},{6,7},{7,6},{8,9},{9,8},{10,11... | collective-permute-start | bytes 417800 | tf_op jit(solution)/shard_map/ppermute | solution.py:401
  101.7 2.8 %collective-permute-start.21 = (bf16[272,256]{1,0:T(8,128)(2,1)S(1)}, bf16[272,256]{1,0:T(8,128)(2,1)S(1)}, u32[]{:S(2)}, u32[]{:S(2)}) collective-permute-start(bf16[272,256]{1,0:T(8,128)(2,1)S(1)} %collective-permute-done.17.refs_2_), channel_id=1, source_target_pairs={{0,1},{1,0},{2,3},{3,2},{4,5},{5,4},{6,7},{7,6},{8,9},{9,8},{10,11... | collective-permute-start | bytes 417800 | tf_op jit(solution)/shard_map/ppermute | solution.py:401
  101.7 2.8 %collective-permute-start.22 = (bf16[272,256]{1,0:T(8,128)(2,1)S(1)}, bf16[272,256]{1,0:T(8,128)(2,1)S(1)}, u32[]{:S(2)}, u32[]{:S(2)}) collective-permute-start(bf16[272,256]{1,0:T(8,128)(2,1)S(1)} %collective-permute-done.18.refs_3_), channel_id=1, source_target_pairs={{0,1},{1,0},{2,3},{3,2},{4,5},{5,4},{6,7},{7,6},{8,9},{9,8},{10,11... | collective-permute-start | bytes 417800 | tf_op jit(solution)/shard_map/ppermute | solution.py:401
  (8 other events, 136.8 us)

commit v11 on v9

--- a/solution.py
+++ b/solution.py
@@ -458,7 +458,6 @@
     )
     quarter = sum_with_means([total.reshape(256, D)])
     recv = [swap(quarter, mask) for mask in X_MASKS]
-    recv, new_entity_acc = lax.optimization_barrier((recv, new_entity_acc))
     pieces = [quarter, *recv]
     pieces = pieces + [swap(piece, CORE) for piece in pieces]
     pieces, new_entity_acc = lax.optimization_barrier((pieces, new_entity_acc))

time: 108 us -> 106 us (0.981)
  waiting for transfers between devices: 28.9 us -> 25.2 us
  starting transfers between devices: 45.2 us -> 48.2 us
  local copies, waits for them, and re-layouts: 3.62 us -> 2.03 us
    ppermute x21, waiting for transfers between devices: 15.4 us -> 11.6 us  [swap(): return lax.ppermute(x, AXES, [(i, i ^ mask) for i in range(256)])]
    ppermute x21, starting transfers between devices: 21.7 us -> 24.7 us  [swap(): return lax.ppermute(x, AXES, [(i, i ^ mask) for i in range(256)])]
    unnamed x18, local copies, waits for them, and re-layouts: 1.63 us -> 0.04 us
  transfers between devices with their start and end apart: 25 -> 25, of which waited for: 12 -> 8; matrix products, arithmetic and copies ran while one was open for 2% -> 2% of each run, Pallas kernels for 15% -> 16%
where the time goes in v11:
time: 106 us
  starting transfers between devices  48.2 us (45%)
  Pallas kernels  27 us (25%)
  waiting for transfers between devices  25.2 us (24%)
  local copies, waits for them, and re-layouts  2.03 us (2%)
  between operations  1.8 us (2%)
  other arithmetic  1.75 us (2%)
    ppermute x21, starting transfers between devices, swap(): return lax.ppermute(x, AXES, [(i, i ^ mask) for i in range(256)])  24.7 us
    all_to_all x2, waiting for transfers between devices, spread(): lax.all_to_all(parts, 'blk', 0, 0, axis_index_groups=groups, tiled=True)  13.6 us
    all_to_all x2, starting transfers between devices, spread(): lax.all_to_all(parts, 'blk', 0, 0, axis_index_groups=groups, tiled=True)  12.3 us
    ppermute x21, waiting for transfers between devices, swap(): return lax.ppermute(x, AXES, [(i, i ^ mask) for i in range(256)])  11.6 us
    ppermute x2, starting transfers between devices, shift(): return lax.ppermute(x, AXES, route)  11.1 us
    pallas_call x2, Pallas kernels, update(): pl.pallas_call(functools.partial(update_kernel, len(pieces)), out_shape=[...  6.51 us
    pallas_call x1, Pallas kernels, shards(): call(score_kernel, [kept, sent, kept, sent, slots_low], 1, 10, [pltpu.VME...  5.9 us
    pallas_call x1, Pallas kernels, shards(): call(gather_kernel, [jax.ShapeDtypeStruct((EDGES, D), BF16), jax.ShapeDty...  4.91 us
  transfers between devices with their start and end apart: 25, of which 8 were waited for; matrix products, arithmetic and copies ran while one was open for 2% of the time, Pallas kernels for 16%

profile of v11, /device:TPU:1, one launch (start us, length us, event | category | flops | bytes accessed | tf_op | source)
XLA Modules:
  0.0 105.9 jit_solution(14903737126458976514)
XLA Ops:
  0.7 1.9 %dynamic-slice_convert_fusion = bf16[512,256]{1,0:T(8,128)(2,1)} fusion(f32[2048,256]{1,0:T(8,128)} %rows_ref.2, s32[]{:T(128)S(6)} %select_n.21), kind=kLoop, calls=%fused_computation | loop fusion | bytes 524292 | tf_op jit(solution)/shard_map/convert_element_type | solution.py:364
  2.6 11.1 %collective-permute-start = (bf16[512,256]{1,0:T(8,128)(2,1)}, bf16[512,256]{1,0:T(8,128)(2,1)S(1)}, u32[]{:S(2)}, u32[]{:S(2)}) collective-permute-start(bf16[512,256]{1,0:T(8,128)(2,1)} %dynamic-slice_convert_fusion), channel_id=1, source_target_pairs={{6,0},{7,1},{4,2},{5,3},{10,4},{11,5},{8,6},{9,7},{14,8},{15,9},{1... | collective-permute-start | bytes 786440 | tf_op jit(solution)/shard_map/ppermute | solution.py:348
  13.7 1.7 %convert_element_type.7.low_ref = bf16[2048,256]{1,0:T(8,128)(2,1)S(1)} convert(f32[2048,256]{1,0:T(8,128)} %rows_ref.2) | non-fusion elementwise | flops 524288 | bytes 3145728 | tf_op jit(solution)/shard_map/convert_element_type | solution.py:362
  15.6 4.9 %shard_map.120 = (bf16[1024,256]{1,0:T(8,128)(2,1)S(1)}, f32[1024,256]{1,0:T(8,128)S(1)}, f32[1024,256]{1,0:T(8,128)S(1)}, f32[4,16,128]{2,1,0:T(8,128)S(1)}) custom-call(s32[8,1024]{1,0:T(8,128)S(1)} %concatenate.3.ids_ref, s32[4,1024]{1,0:T(4,128)S(1)} %reshape.37.negs_ref, bf16[2048,256]{1,0:T(8,128)(2,1)S(1)} %convert_element_type.7.low_ref, ...), custom_call_target="tpu_custom_call" | custom-call | flops 4294967296 | bytes 4194304 | tf_op jit(solution)/shard_map/pallas_call | solution.py:378
  21.6 1.2 %collective-permute-done.2.far_ref = bf16[512,256]{1,0:T(8,128)(2,1)S(1)} collective-permute-done((bf16[512,256]{1,0:T(8,128)(2,1)S(1)}, bf16[512,256]{1,0:T(8,128)(2,1)S(1)}, u32[]{:S(2)}, u32[]{:S(2)}) %collective-permute-start.2) | collective-permute-done | bytes 262176 | tf_op jit(solution)/shard_map/ppermute | solution.py:343
  22.7 2.2 %shard_map.121 = (bf16[1024,1024]{1,0:T(8,128)(2,1)S(1)}, f32[1024,256]{1,0:T(8,128)S(1)}, f32[1024,256]{1,0:T(8,128)S(1)}) custom-call(s32[8,1024]{1,0:T(8,128)S(1)} %concatenate.3.ids_ref, bf16[512,256]{1,0:T(8,128)(2,1)S(1)} %collective-permute-done.near_ref, bf16[512,256]{1,0:T(8,128)(2,1)S(1)} %collective-permute-done.2.far_ref, ...), custom_call_target="tpu_custom_call" | custom-call | flops 1610612736 | bytes 4194304 | tf_op jit(solution)/shard_map/pallas_call | solution.py:401
  25.0 4.5 %collective-permute-done.1.near_ref = bf16[512,256]{1,0:T(8,128)(2,1)S(1)} collective-permute-done((bf16[512,256]{1,0:T(8,128)(2,1)S(1)}, bf16[512,256]{1,0:T(8,128)(2,1)S(1)}, u32[]{:S(2)}, u32[]{:S(2)}) %collective-permute-start.1) | collective-permute-done | bytes 262176 | tf_op jit(solution)/shard_map/ppermute | solution.py:343
  31.5 5.9 %shard_map.122 = (f32[1024,256]{1,0:T(8,128)S(1)}, bf16[1024,256]{1,0:T(8,128)(2,1)S(1)}, f32[1024,256]{1,0:T(8,128)S(1)}, bf16[1024,256]{1,0:T(8,128)(2,1)S(1)}, bf16[1024,256]{1,0:T(8,128)(2,1)S(1)}) custom-call(s32[1,1]{1,0:T(1,128)S(6)} %copy.13.count_ref, s32[8,1024]{1,0:T(8,128)S(1)} %concatenate.3.ids_ref, ...), custom_call_target="tpu_custom_call" | custom-call | flops 4831838208 | bytes 8388608 | tf_op jit(solution)/shard_map/pallas_call | solution.py:411
  37.4 1.2 %shard_map.124 = (f32[1024,256]{1,0:T(8,128)S(1)}, bf16[1024,256]{1,0:T(8,128)(2,1)S(1)}) custom-call(s32[8,1024]{1,0:T(8,128)S(1)} %concatenate.3.ids_ref, bf16[1024,256]{1,0:T(8,128)(2,1)S(1)} %get-tuple-element.65.gr_ref), custom_call_target="tpu_custom_call" | custom-call | flops 1073741824 | bytes 2097152 | tf_op jit(solution)/shard_map/pallas_call | solution.py:427
  40.9 3.7 %collective-permute-start.8 = (bf16[256,256]{1,0:T(8,128)(2,1)S(1)}, bf16[256,256]{1,0:T(8,128)(2,1)S(1)}, u32[]{:S(2)}, u32[]{:S(2)}) collective-permute-start(bf16[256,256]{1,0:T(8,128)(2,1)S(1)} %get-tuple-element.70), channel_id=1, source_target_pairs={{0,6},{1,7},{2,4},{3,5},{4,2},{5,3},{6,0},{7,1},{8,14},{9,15},{10,... | collective-permute-start | bytes 393224 | tf_op jit(solution)/shard_map/ppermute | solution.py:343
  46.9 3.7 %collective-permute-done.8.refs_3_ = bf16[256,256]{1,0:T(8,128)(2,1)S(1)} collective-permute-done((bf16[256,256]{1,0:T(8,128)(2,1)S(1)}, bf16[256,256]{1,0:T(8,128)(2,1)S(1)}, u32[]{:S(2)}, u32[]{:S(2)}) %collective-permute-start.8) | collective-permute-done | bytes 131104 | tf_op jit(solution)/shard_map/ppermute | solution.py:343
  50.6 1.5 %collective-permute-start.10 = (bf16[512,256]{1,0:T(8,128)(2,1)}, bf16[512,256]{1,0:T(8,128)(2,1)S(1)}, u32[]{:S(2)}, u32[]{:S(2)}) collective-permute-start(bf16[512,256]{1,0:T(8,128)(2,1)} %get-tuple-element.75), channel_id=1, source_target_pairs={{0,2},{1,3},{2,0},{3,1},{4,6},{5,7},{6,4},{7,5},{8,10},{9,11},{10,... | collective-permute-start | bytes 786440 | tf_op jit(solution)/shard_map/ppermute | solution.py:343
  52.8 8.5 %all-to-all-start = ((bf16[32,8,256]{2,1,0:T(8,128)(2,1)}), bf16[32,8,256]{2,1,0:T(8,128)(2,1)S(1)}, u32[]{:S(2)}, u32[]{:S(2)}) async-start(bf16[32,8,256]{2,1,0:T(8,128)(2,1)} %bitcast.2), calls=%async_computation | async-start | bytes 262144 | tf_op jit(solution)/shard_map/all_to_all | solution.py:339
  61.3 1.7 %shard_map.127 = bf16[512,256]{1,0:T(8,128)(2,1)} custom-call(bf16[512,256]{1,0:T(8,128)(2,1)S(1)} %get-tuple-element.76.refs_0_, bf16[512,256]{1,0:T(8,128)(2,1)} %collective-permute-done.11.refs_1_), custom_call_target="tpu_custom_call" | custom-call | flops 262144 | bytes 786432 | tf_op jit(solution)/shard_map/pallas_call | solution.py:228
  63.1 7.6 %all-to-all-done.parts_ref = bf16[32,8,256]{2,1,0:T(8,128)(2,1)S(1)} async-done(((bf16[32,8,256]{2,1,0:T(8,128)(2,1)}), bf16[32,8,256]{2,1,0:T(8,128)(2,1)S(1)}, u32[]{:S(2)}, u32[]{:S(2)}) %all-to-all-start) | async-done | bytes 131104 | tf_op jit(solution)/shard_map/all_to_all | solution.py:339
  71.4 3.9 %all-to-all-start.1 = ((f32[32,8,256]{2,1,0:T(8,128)}), f32[32,8,256]{2,1,0:T(8,128)S(1)}, u32[]{:S(2)}, u32[]{:S(2)}) async-start(f32[32,8,256]{2,1,0:T(8,128)} %shard_map.130), calls=%async_computation.1 | async-start | bytes 524288 | tf_op jit(solution)/shard_map/all_to_all | solution.py:339
  75.3 1.2 %shard_map.128.refs_0_ = bf16[528,256]{1,0:T(8,128)(2,1)S(1)} custom-call(f32[512,256]{1,0:T(8,128)S(1)} %get-tuple-element.64.refs_0_, bf16[512,256]{1,0:T(8,128)(2,1)S(1)} %collective-permute-done.10.refs_1_, bf16[512,256]{1,0:T(8,128)(2,1)} %collective-permute-done.12.refs_2_), custom_call_target="tpu_custom_call" | custom-call | flops 393216 | bytes 1179648 | tf_op jit(solution)/shard_map/pallas_call | solution.py:264
  76.8 3.1 %collective-permute-start.14 = (bf16[528,256]{1,0:T(8,128)(2,1)S(1)}, bf16[528,256]{1,0:T(8,128)(2,1)S(1)}, u32[]{:S(2)}, u32[]{:S(2)}) collective-permute-start(bf16[528,256]{1,0:T(8,128)(2,1)S(1)} %shard_map.128.refs_0_), channel_id=1, source_target_pairs={{0,1},{1,0},{2,3},{3,2},{4,5},{5,4},{6,7},{7,6},{8,9},{9,8},{10,11... | collective-permute-start | bytes 811016 | tf_op jit(solution)/shard_map/ppermute | solution.py:343
  79.9 6.0 %all-to-all-done.1 = f32[32,8,256]{2,1,0:T(8,128)S(1)} async-done(((f32[32,8,256]{2,1,0:T(8,128)}), f32[32,8,256]{2,1,0:T(8,128)S(1)}, u32[]{:S(2)}, u32[]{:S(2)}) %all-to-all-start.1) | async-done | bytes 262176 | tf_op jit(solution)/shard_map/all_to_all | solution.py:339
  88.1 1.3 %collective-permute-start.16 = (bf16[272,256]{1,0:T(8,128)(2,1)S(1)}, bf16[272,256]{1,0:T(8,128)(2,1)}, u32[]{:S(2)}, u32[]{:S(2)}) collective-permute-start(bf16[272,256]{1,0:T(8,128)(2,1)S(1)} %shard_map.132.refs_0_), channel_id=1, source_target_pairs={{0,2},{1,3},{2,0},{3,1},{4,6},{5,7},{6,4},{7,5},{8,10},{9,11},{10,... | collective-permute-start | bytes 417800 | tf_op jit(solution)/shard_map/ppermute | solution.py:343
  89.3 5.2 %collective-permute-start.15 = (bf16[528,256]{1,0:T(8,128)(2,1)S(1)}, bf16[528,256]{1,0:T(8,128)(2,1)}, u32[]{:S(2)}, u32[]{:S(2)}) collective-permute-start(bf16[528,256]{1,0:T(8,128)(2,1)S(1)} %collective-permute-done.13.refs_1_), channel_id=1, source_target_pairs={{0,1},{1,0},{2,3},{3,2},{4,5},{5,4},{6,7},{7,6},{8,9},{9,8},{10,11... | collective-permute-start | bytes 811016 | tf_op jit(solution)/shard_map/ppermute | solution.py:343
  94.5 3.7 %collective-permute-start.22 = (bf16[272,256]{1,0:T(8,128)(2,1)S(1)}, bf16[272,256]{1,0:T(8,128)(2,1)}, u32[]{:S(2)}, u32[]{:S(2)}) collective-permute-start(bf16[272,256]{1,0:T(8,128)(2,1)S(1)} %collective-permute-done.18.refs_3_), channel_id=1, source_target_pairs={{0,1},{1,0},{2,3},{3,2},{4,5},{5,4},{6,7},{7,6},{8,9},{9,8},{10,11... | collective-permute-start | bytes 417800 | tf_op jit(solution)/shard_map/ppermute | solution.py:343
  99.1 3.2 %shard_map.131 = (f32[2048,256]{1,0:T(8,128)}, f32[16,128]{1,0:T(8,128)}) custom-call(s32[1]{0:T(128)} %bitcast.place_ref, f32[2048,256]{1,0:T(8,128)S(1)} %copy-done, f32[16,128]{1,0:T(8,128)S(1)} %bitcast.9, bf16[528,256]{1,0:T(8,128)(2,1)S(1)} %shard_map.128.refs_0_, bf16[528,256]{1,0:T(8,128)(2,1)S(1)} %collective-permute-done.13.refs_1_, ...), custom_call_target="tpu_custom_call" | custom-call | flops 4194304 | bytes 5242880 | tf_op jit(solution)/shard_map/pallas_call | solution.py:304
  102.4 3.3 %shard_map.133 = (f32[2048,256]{1,0:T(8,128)}, f32[16,128]{1,0:T(8,128)}) custom-call(s32[1]{0:T(128)} %bitcast.5.place_ref, f32[2048,256]{1,0:T(8,128)S(1)} %copy-done.2, f32[16,128]{1,0:T(8,128)S(1)} %bitcast.10, bf16[272,256]{1,0:T(8,128)(2,1)S(1)} %shard_map.132.refs_0_, bf16[272,256]{1,0:T(8,128)(2,1)} %collective-permute-done.16.refs_1_, ...), custom_call_target="tpu_custom_call" | custom-call | flops 4194304 | bytes 5242880 | tf_op jit(solution)/shard_map/pallas_call | solution.py:304
  (66 shorter events, 12.1 us)
Async XLA Ops:
  2.6 17.9 %collective-permute-start = (bf16[512,256]{1,0:T(8,128)(2,1)}, bf16[512,256]{1,0:T(8,128)(2,1)S(1)}, u32[]{:S(2)}, u32[]{:S(2)}) collective-permute-start(bf16[512,256]{1,0:T(8,128)(2,1)} %dynamic-slice_convert_fusion), channel_id=1, source_target_pairs={{6,0},{7,1},{4,2},{5,3},{10,4},{11,5},{8,6},{9,7},{14,8},{15,9},{1... | collective-permute-start | bytes 786440 | tf_op jit(solution)/shard_map/ppermute | solution.py:348
  20.5 2.2 %collective-permute-start.2 = (bf16[512,256]{1,0:T(8,128)(2,1)S(1)}, bf16[512,256]{1,0:T(8,128)(2,1)S(1)}, u32[]{:S(2)}, u32[]{:S(2)}) collective-permute-start(bf16[512,256]{1,0:T(8,128)(2,1)S(1)} %collective-permute-done.near_ref), channel_id=1, source_target_pairs={{0,1},{1,0},{2,3},{3,2},{4,5},{5,4},{6,7},{7,6},{8,9},{9,8},{10,11... | collective-permute-start | bytes 786440 | tf_op jit(solution)/shard_map/ppermute | solution.py:343
  21.6 7.9 %collective-permute-start.1 = (bf16[512,256]{1,0:T(8,128)(2,1)S(1)}, bf16[512,256]{1,0:T(8,128)(2,1)S(1)}, u32[]{:S(2)}, u32[]{:S(2)}) collective-permute-start(bf16[512,256]{1,0:T(8,128)(2,1)S(1)} %collective-permute-done.near_ref), channel_id=1, source_target_pairs={{0,2},{1,3},{2,0},{3,1},{4,6},{5,7},{6,4},{7,5},{8,10},{9,11},{10,... | collective-permute-start | bytes 786440 | tf_op jit(solution)/shard_map/ppermute | solution.py:343
  29.4 2.0 %collective-permute-start.3 = (bf16[512,256]{1,0:T(8,128)(2,1)S(1)}, bf16[512,256]{1,0:T(8,128)(2,1)S(1)}, u32[]{:S(2)}, u32[]{:S(2)}) collective-permute-start(bf16[512,256]{1,0:T(8,128)(2,1)S(1)} %collective-permute-done.1.near_ref), channel_id=1, source_target_pairs={{0,1},{1,0},{2,3},{3,2},{4,5},{5,4},{6,7},{7,6},{8,9},{9,8},{10,11... | collective-permute-start | bytes 786440 | tf_op jit(solution)/shard_map/ppermute | solution.py:343
  39.1 5.6 %collective-permute-start.4 = (bf16[1024,256]{1,0:T(8,128)(2,1)S(1)}, bf16[1024,256]{1,0:T(8,128)(2,1)S(1)}, u32[]{:S(2)}, u32[]{:S(2)}) collective-permute-start(bf16[1024,256]{1,0:T(8,128)(2,1)S(1)} %get-tuple-element.63), channel_id=1, source_target_pairs={{0,1},{1,0},{2,3},{3,2},{4,5},{5,4},{6,7},{7,6},{8,9},{9,8},{10,11... | collective-permute-start | bytes 1572872 | tf_op jit(solution)/shard_map/ppermute | solution.py:343
  39.2 6.2 %collective-permute-start.9 = (bf16[1024,256]{1,0:T(8,128)(2,1)S(1)}, bf16[1024,256]{1,0:T(8,128)(2,1)S(1)}, u32[]{:S(2)}, u32[]{:S(2)}) collective-permute-start(bf16[1024,256]{1,0:T(8,128)(2,1)S(1)} %get-tuple-element.72), channel_id=1, source_target_pairs={{0,1},{1,0},{2,3},{3,2},{4,5},{5,4},{6,7},{7,6},{8,9},{9,8},{10,11... | collective-permute-start | bytes 1572872 | tf_op jit(solution)/shard_map/ppermute | solution.py:343
  40.7 5.5 %collective-permute-start.6 = (bf16[256,256]{1,0:T(8,128)(2,1)S(1)}, bf16[256,256]{1,0:T(8,128)(2,1)S(1)}, u32[]{:S(2)}, u32[]{:S(2)}) collective-permute-start(bf16[256,256]{1,0:T(8,128)(2,1)S(1)} %get-tuple-element.68), channel_id=1, source_target_pairs={{0,2},{1,3},{2,0},{3,1},{4,6},{5,7},{6,4},{7,5},{8,10},{9,11},{10,... | collective-permute-start | bytes 393224 | tf_op jit(solution)/shard_map/ppermute | solution.py:343
  40.8 6.1 %collective-permute-start.7 = (bf16[256,256]{1,0:T(8,128)(2,1)S(1)}, bf16[256,256]{1,0:T(8,128)(2,1)S(1)}, u32[]{:S(2)}, u32[]{:S(2)}) collective-permute-start(bf16[256,256]{1,0:T(8,128)(2,1)S(1)} %get-tuple-element.69), channel_id=1, source_target_pairs={{0,4},{1,5},{2,6},{3,7},{4,0},{5,1},{6,2},{7,3},{8,12},{9,13},{10,... | collective-permute-start | bytes 393224 | tf_op jit(solution)/shard_map/ppermute | solution.py:343
  40.9 9.7 %collective-permute-start.8 = (bf16[256,256]{1,0:T(8,128)(2,1)S(1)}, bf16[256,256]{1,0:T(8,128)(2,1)S(1)}, u32[]{:S(2)}, u32[]{:S(2)}) collective-permute-start(bf16[256,256]{1,0:T(8,128)(2,1)S(1)} %get-tuple-element.70), channel_id=1, source_target_pairs={{0,6},{1,7},{2,4},{3,5},{4,2},{5,3},{6,0},{7,1},{8,14},{9,15},{10,... | collective-permute-start | bytes 393224 | tf_op jit(solution)/shard_map/ppermute | solution.py:343
  50.6 10.7 %collective-permute-start.11 = (bf16[512,256]{1,0:T(8,128)(2,1)}, bf16[512,256]{1,0:T(8,128)(2,1)}, u32[]{:S(2)}, u32[]{:S(2)}) collective-permute-start(bf16[512,256]{1,0:T(8,128)(2,1)} %get-tuple-element.77), channel_id=1, source_target_pairs={{0,2},{1,3},{2,0},{3,1},{4,6},{5,7},{6,4},{7,5},{8,10},{9,11},{10,... | collective-permute-start | bytes 786440 | tf_op jit(solution)/shard_map/ppermute | solution.py:343
  50.6 20.0 %collective-permute-start.10 = (bf16[512,256]{1,0:T(8,128)(2,1)}, bf16[512,256]{1,0:T(8,128)(2,1)S(1)}, u32[]{:S(2)}, u32[]{:S(2)}) collective-permute-start(bf16[512,256]{1,0:T(8,128)(2,1)} %get-tuple-element.75), channel_id=1, source_target_pairs={{0,2},{1,3},{2,0},{3,1},{4,6},{5,7},{6,4},{7,5},{8,10},{9,11},{10,... | collective-permute-start | bytes 786440 | tf_op jit(solution)/shard_map/ppermute | solution.py:343
  52.8 17.8 %all-to-all-start = ((bf16[32,8,256]{2,1,0:T(8,128)(2,1)}), bf16[32,8,256]{2,1,0:T(8,128)(2,1)S(1)}, u32[]{:S(2)}, u32[]{:S(2)}) async-start(bf16[32,8,256]{2,1,0:T(8,128)(2,1)} %bitcast.2), calls=%async_computation | async-start | bytes 262144 | tf_op jit(solution)/shard_map/all_to_all | solution.py:339
  63.0 12.3 %collective-permute-start.12 = (bf16[512,256]{1,0:T(8,128)(2,1)}, bf16[512,256]{1,0:T(8,128)(2,1)}, u32[]{:S(2)}, u32[]{:S(2)}) collective-permute-start(bf16[512,256]{1,0:T(8,128)(2,1)} %shard_map.127), channel_id=1, source_target_pairs={{254,0},{255,1},{252,2},{253,3},{2,4},{3,5},{0,6},{1,7},{6,8},{7,9... | collective-permute-start | bytes 786440 | tf_op jit(solution)/shard_map/ppermute | solution.py:348
  71.4 14.5 %all-to-all-start.1 = ((f32[32,8,256]{2,1,0:T(8,128)}), f32[32,8,256]{2,1,0:T(8,128)S(1)}, u32[]{:S(2)}, u32[]{:S(2)}) async-start(f32[32,8,256]{2,1,0:T(8,128)} %shard_map.130), calls=%async_computation.1 | async-start | bytes 524288 | tf_op jit(solution)/shard_map/all_to_all | solution.py:339
  76.5 9.4 %collective-permute-start.13 = (bf16[528,256]{1,0:T(8,128)(2,1)S(1)}, bf16[528,256]{1,0:T(8,128)(2,1)S(1)}, u32[]{:S(2)}, u32[]{:S(2)}) collective-permute-start(bf16[528,256]{1,0:T(8,128)(2,1)S(1)} %shard_map.128.refs_0_), channel_id=1, source_target_pairs={{0,2},{1,3},{2,0},{3,1},{4,6},{5,7},{6,4},{7,5},{8,10},{9,11},{10,... | collective-permute-start | bytes 811016 | tf_op jit(solution)/shard_map/ppermute | solution.py:343
  76.8 17.7 %collective-permute-start.14 = (bf16[528,256]{1,0:T(8,128)(2,1)S(1)}, bf16[528,256]{1,0:T(8,128)(2,1)S(1)}, u32[]{:S(2)}, u32[]{:S(2)}) collective-permute-start(bf16[528,256]{1,0:T(8,128)(2,1)S(1)} %shard_map.128.refs_0_), channel_id=1, source_target_pairs={{0,1},{1,0},{2,3},{3,2},{4,5},{5,4},{6,7},{7,6},{8,9},{9,8},{10,11... | collective-permute-start | bytes 811016 | tf_op jit(solution)/shard_map/ppermute | solution.py:343
  86.0 8.5 %collective-permute-start.18 = (bf16[272,256]{1,0:T(8,128)(2,1)S(1)}, bf16[272,256]{1,0:T(8,128)(2,1)S(1)}, u32[]{:S(2)}, u32[]{:S(2)}) collective-permute-start(bf16[272,256]{1,0:T(8,128)(2,1)S(1)} %shard_map.132.refs_0_), channel_id=1, source_target_pairs={{0,6},{1,7},{2,4},{3,5},{4,2},{5,3},{6,0},{7,1},{8,14},{9,15},{10,... | collective-permute-start | bytes 417800 | tf_op jit(solution)/shard_map/ppermute | solution.py:343
  87.0 11.2 %collective-permute-start.17 = (bf16[272,256]{1,0:T(8,128)(2,1)S(1)}, bf16[272,256]{1,0:T(8,128)(2,1)S(1)}, u32[]{:S(2)}, u32[]{:S(2)}) collective-permute-start(bf16[272,256]{1,0:T(8,128)(2,1)S(1)} %shard_map.132.refs_0_), channel_id=1, source_target_pairs={{0,4},{1,5},{2,6},{3,7},{4,0},{5,1},{6,2},{7,3},{8,12},{9,13},{10,... | collective-permute-start | bytes 417800 | tf_op jit(solution)/shard_map/ppermute | solution.py:343
  88.1 10.1 %collective-permute-start.16 = (bf16[272,256]{1,0:T(8,128)(2,1)S(1)}, bf16[272,256]{1,0:T(8,128)(2,1)}, u32[]{:S(2)}, u32[]{:S(2)}) collective-permute-start(bf16[272,256]{1,0:T(8,128)(2,1)S(1)} %shard_map.132.refs_0_), channel_id=1, source_target_pairs={{0,2},{1,3},{2,0},{3,1},{4,6},{5,7},{6,4},{7,5},{8,10},{9,11},{10,... | collective-permute-start | bytes 417800 | tf_op jit(solution)/shard_map/ppermute | solution.py:343
  89.3 9.8 %collective-permute-start.15 = (bf16[528,256]{1,0:T(8,128)(2,1)S(1)}, bf16[528,256]{1,0:T(8,128)(2,1)}, u32[]{:S(2)}, u32[]{:S(2)}) collective-permute-start(bf16[528,256]{1,0:T(8,128)(2,1)S(1)} %collective-permute-done.13.refs_1_), channel_id=1, source_target_pairs={{0,1},{1,0},{2,3},{3,2},{4,5},{5,4},{6,7},{7,6},{8,9},{9,8},{10,11... | collective-permute-start | bytes 811016 | tf_op jit(solution)/shard_map/ppermute | solution.py:343
  94.5 7.9 %collective-permute-start.19 = (bf16[272,256]{1,0:T(8,128)(2,1)S(1)}, bf16[272,256]{1,0:T(8,128)(2,1)}, u32[]{:S(2)}, u32[]{:S(2)}) collective-permute-start(bf16[272,256]{1,0:T(8,128)(2,1)S(1)} %shard_map.132.refs_0_), channel_id=1, source_target_pairs={{0,1},{1,0},{2,3},{3,2},{4,5},{5,4},{6,7},{7,6},{8,9},{9,8},{10,11... | collective-permute-start | bytes 417800 | tf_op jit(solution)/shard_map/ppermute | solution.py:343
  94.5 7.9 %collective-permute-start.22 = (bf16[272,256]{1,0:T(8,128)(2,1)S(1)}, bf16[272,256]{1,0:T(8,128)(2,1)}, u32[]{:S(2)}, u32[]{:S(2)}) collective-permute-start(bf16[272,256]{1,0:T(8,128)(2,1)S(1)} %collective-permute-done.18.refs_3_), channel_id=1, source_target_pairs={{0,1},{1,0},{2,3},{3,2},{4,5},{5,4},{6,7},{7,6},{8,9},{9,8},{10,11... | collective-permute-start | bytes 417800 | tf_op jit(solution)/shard_map/ppermute | solution.py:343
  98.2 4.2 %collective-permute-start.21 = (bf16[272,256]{1,0:T(8,128)(2,1)S(1)}, bf16[272,256]{1,0:T(8,128)(2,1)}, u32[]{:S(2)}, u32[]{:S(2)}) collective-permute-start(bf16[272,256]{1,0:T(8,128)(2,1)S(1)} %collective-permute-done.17.refs_2_), channel_id=1, source_target_pairs={{0,1},{1,0},{2,3},{3,2},{4,5},{5,4},{6,7},{7,6},{8,9},{9,8},{10,11... | collective-permute-start | bytes 417800 | tf_op jit(solution)/shard_map/ppermute | solution.py:343
  98.2 4.2 %collective-permute-start.20 = (bf16[272,256]{1,0:T(8,128)(2,1)}, bf16[272,256]{1,0:T(8,128)(2,1)}, u32[]{:S(2)}, u32[]{:S(2)}) collective-permute-start(bf16[272,256]{1,0:T(8,128)(2,1)} %collective-permute-done.16.refs_1_), channel_id=1, source_target_pairs={{0,1},{1,0},{2,3},{3,2},{4,5},{5,4},{6,7},{7,6},{8,9},{9,8},{10,11... | collective-permute-start | bytes 417800 | tf_op jit(solution)/shard_map/ppermute | solution.py:343
  (10 other events, 199.5 us)

commit v12 on v11

--- a/solution.py
+++ b/solution.py
@@ -19,7 +19,7 @@
 RATE = 0.1
 AXES = ("blk", "rep")
 VMEM_LIMIT = 32 * 1024 * 1024
-SMALL_VMEM_LIMIT = 16 * 1024 * 1024
+UPDATE_VMEM_LIMIT = 51 * 1024 * 1024
 CHUNK = 256
 UNROLL = 4
 
@@ -276,44 +276,76 @@
     return tile[row : row + 1, :H] + tile[row : row + 1, H:] + tile[8 + row : 9 + row, :H]
 
 
-def update_kernel(n, place_ref, rows_ref, acc_ref, *refs):
-    pieces, (new_ref, new_acc_ref, buf_ref, sem_ref) = refs[:n], refs[n:]
-    size = rows_ref.shape[0] // n
+def update_kernel(counts, place_ref, *refs):
+    tables = len(counts)
+    n_in = 2 * tables + sum(counts)
+    ins, outs = refs[:n_in], refs[n_in : n_in + 2 * tables]
+    in_sem, out_sem, *bufs = refs[n_in + 2 * tables :]
+    held, bufs = bufs[:tables], bufs[tables:]
+    fetches = []
+    for t, n in enumerate(counts):
+        rows_ref = ins[2 * t + sum(counts[:t])]
+        size = rows_ref.shape[0] // n
+        for k in range(n):
+            i = lax.bitwise_xor(k, place_ref[t])
+            rows = pl.ds(pl.multiple_of(i * size, size), size)
+            fetch = pltpu.make_async_copy(
+                rows_ref.at[rows, :], held[t].at[rows, :], in_sem.at[len(fetches)]
+            )
+            fetch.start()
+            fetches.append(fetch)
     copies = []
-    for k, piece in enumerate(pieces):
-        i = lax.bitwise_xor(k, place_ref[0])
-        for r in range(0, size, H):
-            g = piece[r : r + H, :].astype(F32)
-            at = pl.ds(i * (size // H) + r // H, 1)
-            acc = acc_ref[at, :] + means_of(piece, size, r // H)
-            new_acc_ref[at, :] = acc
-            scale = jnp.transpose(jnp.broadcast_to(RATE / jnp.sqrt(acc), (H, H)))
-            rows = pl.ds(pl.multiple_of(i * size + r, H), H)
-            buf_ref[rows, :H] = rows_ref[rows, :H] - g[:, :H] * scale
-            buf_ref[rows, H:] = rows_ref[rows, H:] - g[:, H:] * scale
-        rows = pl.ds(pl.multiple_of(i * size, size), size)
-        copy = pltpu.make_async_copy(buf_ref.at[rows, :], new_ref.at[rows, :], sem_ref.at[k])
-        copy.start()
-        copies.append(copy)
+    for t, n in enumerate(counts):
+        rows_ref, acc_ref, *rest = ins
+        pieces, ins = rest[:n], rest[n:]
+        new_ref, new_acc_ref = outs[2 * t : 2 * t + 2]
+        size = rows_ref.shape[0] // n
+        for k, piece in enumerate(pieces):
+            i = lax.bitwise_xor(k, place_ref[t])
+            fetches[len(copies)].wait()
+            for r in range(0, size, H):
+                g = piece[r : r + H, :].astype(F32)
+                at = pl.ds(i * (size // H) + r // H, 1)
+                acc = acc_ref[at, :] + means_of(piece, size, r // H)
+                new_acc_ref[at, :] = acc
+                scale = jnp.transpose(jnp.broadcast_to(RATE / jnp.sqrt(acc), (H, H)))
+                rows = pl.ds(pl.multiple_of(i * size + r, H), H)
+                bufs[t][rows, :H] = held[t][rows, :H] - g[:, :H] * scale
+                bufs[t][rows, H:] = held[t][rows, H:] - g[:, H:] * scale
+            rows = pl.ds(pl.multiple_of(i * size, size), size)
+            copy = pltpu.make_async_copy(
+                bufs[t].at[rows, :], new_ref.at[rows, :], out_sem.at[len(copies)]
+            )
+            copy.start()
+            copies.append(copy)
     for copy in copies:
         copy.wait()
 
 
-def update(rows, acc, pieces, place):
-    n = rows.shape[0]
-    new, new_acc = pl.pallas_call(
-        functools.partial(update_kernel, len(pieces)),
-        out_shape=[
+def update(place, *tables):
+    counts = tuple(len(pieces) for _, _, pieces in tables)
+    operands, shapes, bufs, specs = [], [], [], []
+    for rows, acc, pieces in tables:
+        n = rows.shape[0]
+        operands += [rows, acc.reshape(n // H, H), *pieces]
+        specs += [pl.BlockSpec(memory_space=pl.ANY)] + [vmem()] * (1 + len(pieces))
+        shapes += [
             jax.ShapeDtypeStruct((n, D), F32),
             jax.ShapeDtypeStruct((n // H, H), F32),
-        ],
-        in_specs=[smem()] + [vmem()] * (2 + len(pieces)),
-        out_specs=[pl.BlockSpec(memory_space=pl.ANY), vmem()],
-        scratch_shapes=[pltpu.VMEM((n, D), F32), pltpu.SemaphoreType.DMA((len(pieces),))],
-        cost_estimate=pl.CostEstimate(flops=8 * n * D, bytes_accessed=10 * n * D, transcendentals=n),
-        compiler_params=pltpu.CompilerParams(vmem_limit_bytes=SMALL_VMEM_LIMIT),
-    )(place, rows, acc.reshape(n // H, H), *pieces)
-    return new, new_acc.reshape(n)
+        ]
+        bufs.append(pltpu.VMEM((n, D), F32))
+    outs = pl.pallas_call(
+        functools.partial(update_kernel, counts),
+        out_shape=shapes,
+        in_specs=[smem()] + specs,
+        out_specs=[pl.BlockSpec(memory_space=pl.ANY), vmem()] * len(tables),
+        scratch_shapes=[pltpu.SemaphoreType.DMA((sum(counts),))] * 2 + bufs * 2,
+        cost_estimate=pl.CostEstimate(
+            flops=16 * ENT * D, bytes_accessed=20 * ENT * D, transcendentals=2 * ENT
+        ),
+        compiler_params=pltpu.CompilerParams(vmem_limit_bytes=UPDATE_VMEM_LIMIT),
+    )(place, *operands)
+    return [out.reshape(-1) if out.shape[1] == H else out for out in outs]
 
 
 def sum_rows_kernel(parts_ref, out_ref):
@@ -452,18 +484,18 @@
     ent_xl = swap(ent_own, XL)
     total, ent_xl = lax.optimization_barrier((spread(summed), ent_xl))
     ent_core = [swap(ent_own, CORE), swap(ent_xl, CORE)]
-    place = (core * 2 + xl).reshape(1)
-    new_entities, new_entity_acc = update(
-        entities, entity_acc, [ent_own, ent_xl, *ent_core], place
-    )
     quarter = sum_with_means([total.reshape(256, D)])
     recv = [swap(quarter, mask) for mask in X_MASKS]
     pieces = [quarter, *recv]
     pieces = pieces + [swap(piece, CORE) for piece in pieces]
-    pieces, new_entity_acc = lax.optimization_barrier((pieces, new_entity_acc))
-    place = (core * 4 + x).reshape(1)
-    new_relations, new_relation_acc = update(relations, relation_acc, pieces, place)
-    return (new_entities, new_entity_acc, new_relations, new_relation_acc)
+    place = jnp.stack([core * 2 + xl, core * 4 + x])
+    return tuple(
+        update(
+            place,
+            (entities, entity_acc, [ent_own, ent_xl, *ent_core]),
+            (relations, relation_acc, pieces),
+        )
+    )
 
 
 def solution(mesh):

time: 106 us -> 107 us (level)
  Pallas kernels: 27 us -> 21.4 us
  starting transfers between devices: 48.2 us -> 52.6 us
  waiting for transfers between devices: 25.2 us -> 26.9 us
    ppermute x21, starting transfers between devices: 24.7 us -> 28.9 us  [swap(): return lax.ppermute(x, AXES, [(i, i ^ mask) for i in range(256)])]
    pallas_call x5, Pallas kernels: 4.06 us -> 1.08 us  [add_split(): call(functools.partial(add_split_kernel, len(parts), n_out), shapes, 0, l...]
    ppermute x21, waiting for transfers between devices: 11.6 us -> 13.9 us  [swap(): return lax.ppermute(x, AXES, [(i, i ^ mask) for i in range(256)])]
    pallas_call x2 -> x1, Pallas kernels: 6.51 us -> 4.89 us  [update(): pl.pallas_call(functools.partial(update_kernel, counts), out_shape=shapes...]
  transfers between devices with their start and end apart: 25 -> 25, of which waited for: 8 -> 10; matrix products, arithmetic and copies ran while one was open for 2% -> 2% of each run, Pallas kernels for 16% -> 9%
where the time goes in v12:
time: 107 us
  starting transfers between devices  52.6 us (49%)
  waiting for transfers between devices  26.9 us (25%)
  Pallas kernels  21.4 us (20%)
  local copies, waits for them, and re-layouts  2.02 us (2%)
  other arithmetic  1.83 us (2%)
  between operations  1.78 us (2%)
    ppermute x21, starting transfers between devices, swap(): return lax.ppermute(x, AXES, [(i, i ^ mask) for i in range(256)])  28.9 us
    ppermute x21, waiting for transfers between devices, swap(): return lax.ppermute(x, AXES, [(i, i ^ mask) for i in range(256)])  13.9 us
    all_to_all x2, waiting for transfers between devices, spread(): lax.all_to_all(parts, 'blk', 0, 0, axis_index_groups=groups, tiled=True)  13.1 us
    all_to_all x2, starting transfers between devices, spread(): lax.all_to_all(parts, 'blk', 0, 0, axis_index_groups=groups, tiled=True)  12.3 us
    ppermute x2, starting transfers between devices, shift(): return lax.ppermute(x, AXES, route)  11.4 us
    pallas_call x1, Pallas kernels, shards(): call(score_kernel, [kept, sent, kept, sent, slots_low], 1, 10, [pltpu.VME...  5.9 us
    pallas_call x1, Pallas kernels, shards(): call(gather_kernel, [jax.ShapeDtypeStruct((EDGES, D), BF16), jax.ShapeDty...  4.91 us
    pallas_call x1, Pallas kernels, update(): pl.pallas_call(functools.partial(update_kernel, counts), out_shape=shapes...  4.89 us
  transfers between devices with their start and end apart: 25, of which 10 were waited for; matrix products, arithmetic and copies ran while one was open for 2% of the time, Pallas kernels for 9%

profile of v12, /device:TPU:1, one launch (start us, length us, event | category | flops | bytes accessed | tf_op | source)
XLA Modules:
  0.0 106.6 jit_solution(11888317146065618615)
XLA Ops:
  0.7 1.9 %dynamic-slice_convert_fusion = bf16[512,256]{1,0:T(8,128)(2,1)} fusion(f32[2048,256]{1,0:T(8,128)} %refs_0_.1, s32[]{:T(128)S(6)} %select_n.21), kind=kLoop, calls=%fused_computation | loop fusion | bytes 524292 | tf_op jit(solution)/shard_map/convert_element_type | solution.py:396
  2.6 11.1 %collective-permute-start = (bf16[512,256]{1,0:T(8,128)(2,1)}, bf16[512,256]{1,0:T(8,128)(2,1)S(1)}, u32[]{:S(2)}, u32[]{:S(2)}) collective-permute-start(bf16[512,256]{1,0:T(8,128)(2,1)} %dynamic-slice_convert_fusion), channel_id=1, source_target_pairs={{6,0},{7,1},{4,2},{5,3},{10,4},{11,5},{8,6},{9,7},{14,8},{15,9},{1... | collective-permute-start | bytes 786440 | tf_op jit(solution)/shard_map/ppermute | solution.py:380
  13.7 1.7 %convert_element_type.7.low_ref = bf16[2048,256]{1,0:T(8,128)(2,1)S(1)} convert(f32[2048,256]{1,0:T(8,128)} %refs_0_.1) | non-fusion elementwise | flops 524288 | bytes 3145728 | tf_op jit(solution)/shard_map/convert_element_type | solution.py:394
  15.6 4.9 %shard_map.120 = (bf16[1024,256]{1,0:T(8,128)(2,1)S(1)}, f32[1024,256]{1,0:T(8,128)S(1)}, f32[1024,256]{1,0:T(8,128)S(1)}, f32[4,16,128]{2,1,0:T(8,128)S(1)}) custom-call(s32[8,1024]{1,0:T(8,128)S(1)} %concatenate.3.ids_ref, s32[4,1024]{1,0:T(4,128)S(1)} %reshape.30.negs_ref, bf16[2048,256]{1,0:T(8,128)(2,1)S(1)} %convert_element_type.7.low_ref, ...), custom_call_target="tpu_custom_call" | custom-call | flops 4294967296 | bytes 4194304 | tf_op jit(solution)/shard_map/pallas_call | solution.py:410
  22.7 2.2 %shard_map.121 = (bf16[1024,1024]{1,0:T(8,128)(2,1)S(1)}, f32[1024,256]{1,0:T(8,128)S(1)}, f32[1024,256]{1,0:T(8,128)S(1)}) custom-call(s32[8,1024]{1,0:T(8,128)S(1)} %concatenate.3.ids_ref, bf16[512,256]{1,0:T(8,128)(2,1)S(1)} %collective-permute-done.near_ref, bf16[512,256]{1,0:T(8,128)(2,1)S(1)} %collective-permute-done.2.far_ref, ...), custom_call_target="tpu_custom_call" | custom-call | flops 1610612736 | bytes 4194304 | tf_op jit(solution)/shard_map/pallas_call | solution.py:433
  25.0 4.5 %collective-permute-done.1.near_ref = bf16[512,256]{1,0:T(8,128)(2,1)S(1)} collective-permute-done((bf16[512,256]{1,0:T(8,128)(2,1)S(1)}, bf16[512,256]{1,0:T(8,128)(2,1)S(1)}, u32[]{:S(2)}, u32[]{:S(2)}) %collective-permute-start.1) | collective-permute-done | bytes 262176 | tf_op jit(solution)/shard_map/ppermute | solution.py:375
  31.5 5.9 %shard_map.122 = (f32[1024,256]{1,0:T(8,128)S(1)}, bf16[1024,256]{1,0:T(8,128)(2,1)S(1)}, f32[1024,256]{1,0:T(8,128)S(1)}, bf16[1024,256]{1,0:T(8,128)(2,1)S(1)}, bf16[1024,256]{1,0:T(8,128)(2,1)S(1)}) custom-call(s32[1,1]{1,0:T(1,128)S(6)} %copy.13.count_ref, s32[8,1024]{1,0:T(8,128)S(1)} %concatenate.3.ids_ref, ...), custom_call_target="tpu_custom_call" | custom-call | flops 4831838208 | bytes 8388608 | tf_op jit(solution)/shard_map/pallas_call | solution.py:443
  37.4 1.2 %shard_map.124 = (f32[1024,256]{1,0:T(8,128)S(1)}, bf16[1024,256]{1,0:T(8,128)(2,1)S(1)}) custom-call(s32[8,1024]{1,0:T(8,128)S(1)} %concatenate.3.ids_ref, bf16[1024,256]{1,0:T(8,128)(2,1)S(1)} %get-tuple-element.56.gr_ref), custom_call_target="tpu_custom_call" | custom-call | flops 1073741824 | bytes 2097152 | tf_op jit(solution)/shard_map/pallas_call | solution.py:459
  41.0 3.7 %collective-permute-start.8 = (bf16[256,256]{1,0:T(8,128)(2,1)S(1)}, bf16[256,256]{1,0:T(8,128)(2,1)S(1)}, u32[]{:S(2)}, u32[]{:S(2)}) collective-permute-start(bf16[256,256]{1,0:T(8,128)(2,1)S(1)} %get-tuple-element.61), channel_id=1, source_target_pairs={{0,6},{1,7},{2,4},{3,5},{4,2},{5,3},{6,0},{7,1},{8,14},{9,15},{10,... | collective-permute-start | bytes 393224 | tf_op jit(solution)/shard_map/ppermute | solution.py:375
  45.6 1.4 %collective-permute-done.7.refs_2_ = bf16[256,256]{1,0:T(8,128)(2,1)S(1)} collective-permute-done((bf16[256,256]{1,0:T(8,128)(2,1)S(1)}, bf16[256,256]{1,0:T(8,128)(2,1)S(1)}, u32[]{:S(2)}, u32[]{:S(2)}) %collective-permute-start.7) | collective-permute-done | bytes 131104 | tf_op jit(solution)/shard_map/ppermute | solution.py:375
  47.0 3.7 %collective-permute-done.8.refs_3_ = bf16[256,256]{1,0:T(8,128)(2,1)S(1)} collective-permute-done((bf16[256,256]{1,0:T(8,128)(2,1)S(1)}, bf16[256,256]{1,0:T(8,128)(2,1)S(1)}, u32[]{:S(2)}, u32[]{:S(2)}) %collective-permute-start.8) | collective-permute-done | bytes 131104 | tf_op jit(solution)/shard_map/ppermute | solution.py:375
  50.7 1.5 %collective-permute-start.10 = (bf16[512,256]{1,0:T(8,128)(2,1)S(1)}, bf16[512,256]{1,0:T(8,128)(2,1)S(1)}, u32[]{:S(2)}, u32[]{:S(2)}) collective-permute-start(bf16[512,256]{1,0:T(8,128)(2,1)S(1)} %get-tuple-element.66), channel_id=1, source_target_pairs={{0,2},{1,3},{2,0},{3,1},{4,6},{5,7},{6,4},{7,5},{8,10},{9,11},{10,... | collective-permute-start | bytes 786440 | tf_op jit(solution)/shard_map/ppermute | solution.py:375
  52.9 8.5 %all-to-all-start = ((bf16[32,8,256]{2,1,0:T(8,128)(2,1)}), bf16[32,8,256]{2,1,0:T(8,128)(2,1)S(1)}, u32[]{:S(2)}, u32[]{:S(2)}) async-start(bf16[32,8,256]{2,1,0:T(8,128)(2,1)} %bitcast.3), calls=%async_computation | async-start | bytes 262144 | tf_op jit(solution)/shard_map/all_to_all | solution.py:371
  61.8 9.0 %all-to-all-done.parts_ref = bf16[32,8,256]{2,1,0:T(8,128)(2,1)S(1)} async-done(((bf16[32,8,256]{2,1,0:T(8,128)(2,1)}), bf16[32,8,256]{2,1,0:T(8,128)(2,1)S(1)}, u32[]{:S(2)}, u32[]{:S(2)}) %all-to-all-start) | async-done | bytes 131104 | tf_op jit(solution)/shard_map/all_to_all | solution.py:371
  71.5 3.9 %all-to-all-start.1 = ((f32[32,8,256]{2,1,0:T(8,128)}), f32[32,8,256]{2,1,0:T(8,128)S(1)}, u32[]{:S(2)}, u32[]{:S(2)}) async-start(f32[32,8,256]{2,1,0:T(8,128)} %shard_map.130), calls=%async_computation.1 | async-start | bytes 524288 | tf_op jit(solution)/shard_map/all_to_all | solution.py:371
  75.8 6.1 %collective-permute-start.14 = (bf16[528,256]{1,0:T(8,128)(2,1)S(1)}, bf16[528,256]{1,0:T(8,128)(2,1)S(1)}, u32[]{:S(2)}, u32[]{:S(2)}) collective-permute-start(bf16[528,256]{1,0:T(8,128)(2,1)S(1)} %shard_map.128.refs_2_), channel_id=1, source_target_pairs={{0,1},{1,0},{2,3},{3,2},{4,5},{5,4},{6,7},{7,6},{8,9},{9,8},{10,11... | collective-permute-start | bytes 811016 | tf_op jit(solution)/shard_map/ppermute | solution.py:375
  81.9 4.1 %all-to-all-done.1 = f32[32,8,256]{2,1,0:T(8,128)S(1)} async-done(((f32[32,8,256]{2,1,0:T(8,128)}), f32[32,8,256]{2,1,0:T(8,128)S(1)}, u32[]{:S(2)}, u32[]{:S(2)}) %all-to-all-start.1) | async-done | bytes 262176 | tf_op jit(solution)/shard_map/all_to_all | solution.py:371
  86.2 1.8 %collective-permute-start.17 = (bf16[272,256]{1,0:T(8,128)(2,1)S(1)}, bf16[272,256]{1,0:T(8,128)(2,1)S(1)}, u32[]{:S(2)}, u32[]{:S(2)}) collective-permute-start(bf16[272,256]{1,0:T(8,128)(2,1)S(1)} %shard_map.131.refs_8_), channel_id=1, source_target_pairs={{0,4},{1,5},{2,6},{3,7},{4,0},{5,1},{6,2},{7,3},{8,12},{9,13},{10,... | collective-permute-start | bytes 417800 | tf_op jit(solution)/shard_map/ppermute | solution.py:375
  88.1 1.4 %collective-permute-start.16 = (bf16[272,256]{1,0:T(8,128)(2,1)S(1)}, bf16[272,256]{1,0:T(8,128)(2,1)S(1)}, u32[]{:S(2)}, u32[]{:S(2)}) collective-permute-start(bf16[272,256]{1,0:T(8,128)(2,1)S(1)} %shard_map.131.refs_8_), channel_id=1, source_target_pairs={{0,2},{1,3},{2,0},{3,1},{4,6},{5,7},{6,4},{7,5},{8,10},{9,11},{10,... | collective-permute-start | bytes 417800 | tf_op jit(solution)/shard_map/ppermute | solution.py:375
  89.5 6.0 %collective-permute-start.15 = (bf16[528,256]{1,0:T(8,128)(2,1)S(1)}, bf16[528,256]{1,0:T(8,128)(2,1)S(1)}, u32[]{:S(2)}, u32[]{:S(2)}) collective-permute-start(bf16[528,256]{1,0:T(8,128)(2,1)S(1)} %collective-permute-done.13.refs_3_), channel_id=1, source_target_pairs={{0,1},{1,0},{2,3},{3,2},{4,5},{5,4},{6,7},{7,6},{8,9},{9,8},{10,11... | collective-permute-start | bytes 811016 | tf_op jit(solution)/shard_map/ppermute | solution.py:375
  95.5 1.3 %collective-permute-start.22 = (bf16[272,256]{1,0:T(8,128)(2,1)S(1)}, bf16[272,256]{1,0:T(8,128)(2,1)S(1)}, u32[]{:S(2)}, u32[]{:S(2)}) collective-permute-start(bf16[272,256]{1,0:T(8,128)(2,1)S(1)} %collective-permute-done.18.refs_11_), channel_id=1, source_target_pairs={{0,1},{1,0},{2,3},{3,2},{4,5},{5,4},{6,7},{7,6},{8,9},{9,8},{10,11... | collective-permute-start | bytes 417800 | tf_op jit(solution)/shard_map/ppermute | solution.py:375
  96.8 1.7 %collective-permute-start.21 = (bf16[272,256]{1,0:T(8,128)(2,1)S(1)}, bf16[272,256]{1,0:T(8,128)(2,1)S(1)}, u32[]{:S(2)}, u32[]{:S(2)}) collective-permute-start(bf16[272,256]{1,0:T(8,128)(2,1)S(1)} %collective-permute-done.17.refs_10_), channel_id=1, source_target_pairs={{0,1},{1,0},{2,3},{3,2},{4,5},{5,4},{6,7},{7,6},{8,9},{9,8},{10,11... | collective-permute-start | bytes 417800 | tf_op jit(solution)/shard_map/ppermute | solution.py:375
  98.5 2.0 %collective-permute-start.20 = (bf16[272,256]{1,0:T(8,128)(2,1)S(1)}, bf16[272,256]{1,0:T(8,128)(2,1)S(1)}, u32[]{:S(2)}, u32[]{:S(2)}) collective-permute-start(bf16[272,256]{1,0:T(8,128)(2,1)S(1)} %collective-permute-done.16.refs_9_), channel_id=1, source_target_pairs={{0,1},{1,0},{2,3},{3,2},{4,5},{5,4},{6,7},{7,6},{8,9},{9,8},{10,11... | collective-permute-start | bytes 417800 | tf_op jit(solution)/shard_map/ppermute | solution.py:375
  101.5 4.9 %shard_map.132 = (f32[2048,256]{1,0:T(8,128)}, f32[16,128]{1,0:T(8,128)}, f32[2048,256]{1,0:T(8,128)}, f32[16,128]{1,0:T(8,128)}) custom-call(s32[2]{0:T(128)S(1)} %pad_add_fusion.place_ref, f32[2048,256]{1,0:T(8,128)} %refs_0_.1, f32[16,128]{1,0:T(8,128)S(1)} %bitcast.9, bf16[528,256]{1,0:T(8,128)(2,1)S(1)} %shard_map.128.refs_2_, ...), custom_call_target="tpu_custom_call" | custom-call | flops 8388608 | bytes 10485760 | tf_op jit(solution)/shard_map/pallas_call | solution.py:337
  (62 shorter events, 10.5 us)
Async XLA Ops:
  2.6 17.9 %collective-permute-start = (bf16[512,256]{1,0:T(8,128)(2,1)}, bf16[512,256]{1,0:T(8,128)(2,1)S(1)}, u32[]{:S(2)}, u32[]{:S(2)}) collective-permute-start(bf16[512,256]{1,0:T(8,128)(2,1)} %dynamic-slice_convert_fusion), channel_id=1, source_target_pairs={{6,0},{7,1},{4,2},{5,3},{10,4},{11,5},{8,6},{9,7},{14,8},{15,9},{1... | collective-permute-start | bytes 786440 | tf_op jit(solution)/shard_map/ppermute | solution.py:380
  20.5 2.2 %collective-permute-start.2 = (bf16[512,256]{1,0:T(8,128)(2,1)S(1)}, bf16[512,256]{1,0:T(8,128)(2,1)S(1)}, u32[]{:S(2)}, u32[]{:S(2)}) collective-permute-start(bf16[512,256]{1,0:T(8,128)(2,1)S(1)} %collective-permute-done.near_ref), channel_id=1, source_target_pairs={{0,1},{1,0},{2,3},{3,2},{4,5},{5,4},{6,7},{7,6},{8,9},{9,8},{10,11... | collective-permute-start | bytes 786440 | tf_op jit(solution)/shard_map/ppermute | solution.py:375
  21.6 7.9 %collective-permute-start.1 = (bf16[512,256]{1,0:T(8,128)(2,1)S(1)}, bf16[512,256]{1,0:T(8,128)(2,1)S(1)}, u32[]{:S(2)}, u32[]{:S(2)}) collective-permute-start(bf16[512,256]{1,0:T(8,128)(2,1)S(1)} %collective-permute-done.near_ref), channel_id=1, source_target_pairs={{0,2},{1,3},{2,0},{3,1},{4,6},{5,7},{6,4},{7,5},{8,10},{9,11},{10,... | collective-permute-start | bytes 786440 | tf_op jit(solution)/shard_map/ppermute | solution.py:375
  29.4 2.0 %collective-permute-start.3 = (bf16[512,256]{1,0:T(8,128)(2,1)S(1)}, bf16[512,256]{1,0:T(8,128)(2,1)S(1)}, u32[]{:S(2)}, u32[]{:S(2)}) collective-permute-start(bf16[512,256]{1,0:T(8,128)(2,1)S(1)} %collective-permute-done.1.near_ref), channel_id=1, source_target_pairs={{0,1},{1,0},{2,3},{3,2},{4,5},{5,4},{6,7},{7,6},{8,9},{9,8},{10,11... | collective-permute-start | bytes 786440 | tf_op jit(solution)/shard_map/ppermute | solution.py:375
  39.1 5.6 %collective-permute-start.4 = (bf16[1024,256]{1,0:T(8,128)(2,1)S(1)}, bf16[1024,256]{1,0:T(8,128)(2,1)S(1)}, u32[]{:S(2)}, u32[]{:S(2)}) collective-permute-start(bf16[1024,256]{1,0:T(8,128)(2,1)S(1)} %get-tuple-element.54), channel_id=1, source_target_pairs={{0,1},{1,0},{2,3},{3,2},{4,5},{5,4},{6,7},{7,6},{8,9},{9,8},{10,11... | collective-permute-start | bytes 1572872 | tf_op jit(solution)/shard_map/ppermute | solution.py:375
  39.2 5.6 %collective-permute-start.9 = (bf16[1024,256]{1,0:T(8,128)(2,1)S(1)}, bf16[1024,256]{1,0:T(8,128)(2,1)S(1)}, u32[]{:S(2)}, u32[]{:S(2)}) collective-permute-start(bf16[1024,256]{1,0:T(8,128)(2,1)S(1)} %get-tuple-element.63), channel_id=1, source_target_pairs={{0,1},{1,0},{2,3},{3,2},{4,5},{5,4},{6,7},{7,6},{8,9},{9,8},{10,11... | collective-permute-start | bytes 1572872 | tf_op jit(solution)/shard_map/ppermute | solution.py:375
  40.8 4.8 %collective-permute-start.6 = (bf16[256,256]{1,0:T(8,128)(2,1)S(1)}, bf16[256,256]{1,0:T(8,128)(2,1)S(1)}, u32[]{:S(2)}, u32[]{:S(2)}) collective-permute-start(bf16[256,256]{1,0:T(8,128)(2,1)S(1)} %get-tuple-element.59), channel_id=1, source_target_pairs={{0,2},{1,3},{2,0},{3,1},{4,6},{5,7},{6,4},{7,5},{8,10},{9,11},{10,... | collective-permute-start | bytes 393224 | tf_op jit(solution)/shard_map/ppermute | solution.py:375
  40.9 6.1 %collective-permute-start.7 = (bf16[256,256]{1,0:T(8,128)(2,1)S(1)}, bf16[256,256]{1,0:T(8,128)(2,1)S(1)}, u32[]{:S(2)}, u32[]{:S(2)}) collective-permute-start(bf16[256,256]{1,0:T(8,128)(2,1)S(1)} %get-tuple-element.60), channel_id=1, source_target_pairs={{0,4},{1,5},{2,6},{3,7},{4,0},{5,1},{6,2},{7,3},{8,12},{9,13},{10,... | collective-permute-start | bytes 393224 | tf_op jit(solution)/shard_map/ppermute | solution.py:375
  41.0 9.7 %collective-permute-start.8 = (bf16[256,256]{1,0:T(8,128)(2,1)S(1)}, bf16[256,256]{1,0:T(8,128)(2,1)S(1)}, u32[]{:S(2)}, u32[]{:S(2)}) collective-permute-start(bf16[256,256]{1,0:T(8,128)(2,1)S(1)} %get-tuple-element.61), channel_id=1, source_target_pairs={{0,6},{1,7},{2,4},{3,5},{4,2},{5,3},{6,0},{7,1},{8,14},{9,15},{10,... | collective-permute-start | bytes 393224 | tf_op jit(solution)/shard_map/ppermute | solution.py:375
  50.7 10.7 %collective-permute-start.11 = (bf16[512,256]{1,0:T(8,128)(2,1)S(1)}, bf16[512,256]{1,0:T(8,128)(2,1)S(1)}, u32[]{:S(2)}, u32[]{:S(2)}) collective-permute-start(bf16[512,256]{1,0:T(8,128)(2,1)S(1)} %get-tuple-element.68), channel_id=1, source_target_pairs={{0,2},{1,3},{2,0},{3,1},{4,6},{5,7},{6,4},{7,5},{8,10},{9,11},{10,... | collective-permute-start | bytes 786440 | tf_op jit(solution)/shard_map/ppermute | solution.py:375
  50.7 20.1 %collective-permute-start.10 = (bf16[512,256]{1,0:T(8,128)(2,1)S(1)}, bf16[512,256]{1,0:T(8,128)(2,1)S(1)}, u32[]{:S(2)}, u32[]{:S(2)}) collective-permute-start(bf16[512,256]{1,0:T(8,128)(2,1)S(1)} %get-tuple-element.66), channel_id=1, source_target_pairs={{0,2},{1,3},{2,0},{3,1},{4,6},{5,7},{6,4},{7,5},{8,10},{9,11},{10,... | collective-permute-start | bytes 786440 | tf_op jit(solution)/shard_map/ppermute | solution.py:375
  52.9 17.9 %all-to-all-start = ((bf16[32,8,256]{2,1,0:T(8,128)(2,1)}), bf16[32,8,256]{2,1,0:T(8,128)(2,1)S(1)}, u32[]{:S(2)}, u32[]{:S(2)}) async-start(bf16[32,8,256]{2,1,0:T(8,128)(2,1)} %bitcast.3), calls=%async_computation | async-start | bytes 262144 | tf_op jit(solution)/shard_map/all_to_all | solution.py:371
  61.4 14.0 %collective-permute-start.12 = (bf16[512,256]{1,0:T(8,128)(2,1)S(1)}, bf16[512,256]{1,0:T(8,128)(2,1)S(1)}, u32[]{:S(2)}, u32[]{:S(2)}) collective-permute-start(bf16[512,256]{1,0:T(8,128)(2,1)S(1)} %shard_map.127), channel_id=1, source_target_pairs={{254,0},{255,1},{252,2},{253,3},{2,4},{3,5},{0,6},{1,7},{6,8},{7,9... | collective-permute-start | bytes 786440 | tf_op jit(solution)/shard_map/ppermute | solution.py:380
  71.5 14.5 %all-to-all-start.1 = ((f32[32,8,256]{2,1,0:T(8,128)}), f32[32,8,256]{2,1,0:T(8,128)S(1)}, u32[]{:S(2)}, u32[]{:S(2)}) async-start(f32[32,8,256]{2,1,0:T(8,128)} %shard_map.130), calls=%async_computation.1 | async-start | bytes 524288 | tf_op jit(solution)/shard_map/all_to_all | solution.py:371
  75.7 10.3 %collective-permute-start.13 = (bf16[528,256]{1,0:T(8,128)(2,1)S(1)}, bf16[528,256]{1,0:T(8,128)(2,1)S(1)}, u32[]{:S(2)}, u32[]{:S(2)}) collective-permute-start(bf16[528,256]{1,0:T(8,128)(2,1)S(1)} %shard_map.128.refs_2_), channel_id=1, source_target_pairs={{0,2},{1,3},{2,0},{3,1},{4,6},{5,7},{6,4},{7,5},{8,10},{9,11},{10,... | collective-permute-start | bytes 811016 | tf_op jit(solution)/shard_map/ppermute | solution.py:375
  75.8 19.7 %collective-permute-start.14 = (bf16[528,256]{1,0:T(8,128)(2,1)S(1)}, bf16[528,256]{1,0:T(8,128)(2,1)S(1)}, u32[]{:S(2)}, u32[]{:S(2)}) collective-permute-start(bf16[528,256]{1,0:T(8,128)(2,1)S(1)} %shard_map.128.refs_2_), channel_id=1, source_target_pairs={{0,1},{1,0},{2,3},{3,2},{4,5},{5,4},{6,7},{7,6},{8,9},{9,8},{10,11... | collective-permute-start | bytes 811016 | tf_op jit(solution)/shard_map/ppermute | solution.py:375
  86.1 9.4 %collective-permute-start.18 = (bf16[272,256]{1,0:T(8,128)(2,1)S(1)}, bf16[272,256]{1,0:T(8,128)(2,1)S(1)}, u32[]{:S(2)}, u32[]{:S(2)}) collective-permute-start(bf16[272,256]{1,0:T(8,128)(2,1)S(1)} %shard_map.131.refs_8_), channel_id=1, source_target_pairs={{0,6},{1,7},{2,4},{3,5},{4,2},{5,3},{6,0},{7,1},{8,14},{9,15},{10,... | collective-permute-start | bytes 417800 | tf_op jit(solution)/shard_map/ppermute | solution.py:375
  86.2 10.6 %collective-permute-start.17 = (bf16[272,256]{1,0:T(8,128)(2,1)S(1)}, bf16[272,256]{1,0:T(8,128)(2,1)S(1)}, u32[]{:S(2)}, u32[]{:S(2)}) collective-permute-start(bf16[272,256]{1,0:T(8,128)(2,1)S(1)} %shard_map.131.refs_8_), channel_id=1, source_target_pairs={{0,4},{1,5},{2,6},{3,7},{4,0},{5,1},{6,2},{7,3},{8,12},{9,13},{10,... | collective-permute-start | bytes 417800 | tf_op jit(solution)/shard_map/ppermute | solution.py:375
  88.1 10.4 %collective-permute-start.16 = (bf16[272,256]{1,0:T(8,128)(2,1)S(1)}, bf16[272,256]{1,0:T(8,128)(2,1)S(1)}, u32[]{:S(2)}, u32[]{:S(2)}) collective-permute-start(bf16[272,256]{1,0:T(8,128)(2,1)S(1)} %shard_map.131.refs_8_), channel_id=1, source_target_pairs={{0,2},{1,3},{2,0},{3,1},{4,6},{5,7},{6,4},{7,5},{8,10},{9,11},{10,... | collective-permute-start | bytes 417800 | tf_op jit(solution)/shard_map/ppermute | solution.py:375
  89.5 11.1 %collective-permute-start.15 = (bf16[528,256]{1,0:T(8,128)(2,1)S(1)}, bf16[528,256]{1,0:T(8,128)(2,1)S(1)}, u32[]{:S(2)}, u32[]{:S(2)}) collective-permute-start(bf16[528,256]{1,0:T(8,128)(2,1)S(1)} %collective-permute-done.13.refs_3_), channel_id=1, source_target_pairs={{0,1},{1,0},{2,3},{3,2},{4,5},{5,4},{6,7},{7,6},{8,9},{9,8},{10,11... | collective-permute-start | bytes 811016 | tf_op jit(solution)/shard_map/ppermute | solution.py:375
  95.4 5.1 %collective-permute-start.19 = (bf16[272,256]{1,0:T(8,128)(2,1)S(1)}, bf16[272,256]{1,0:T(8,128)(2,1)S(1)}, u32[]{:S(2)}, u32[]{:S(2)}) collective-permute-start(bf16[272,256]{1,0:T(8,128)(2,1)S(1)} %shard_map.131.refs_8_), channel_id=1, source_target_pairs={{0,1},{1,0},{2,3},{3,2},{4,5},{5,4},{6,7},{7,6},{8,9},{9,8},{10,11... | collective-permute-start | bytes 417800 | tf_op jit(solution)/shard_map/ppermute | solution.py:375
  95.5 5.0 %collective-permute-start.22 = (bf16[272,256]{1,0:T(8,128)(2,1)S(1)}, bf16[272,256]{1,0:T(8,128)(2,1)S(1)}, u32[]{:S(2)}, u32[]{:S(2)}) collective-permute-start(bf16[272,256]{1,0:T(8,128)(2,1)S(1)} %collective-permute-done.18.refs_11_), channel_id=1, source_target_pairs={{0,1},{1,0},{2,3},{3,2},{4,5},{5,4},{6,7},{7,6},{8,9},{9,8},{10,11... | collective-permute-start | bytes 417800 | tf_op jit(solution)/shard_map/ppermute | solution.py:375
  96.8 3.8 %collective-permute-start.21 = (bf16[272,256]{1,0:T(8,128)(2,1)S(1)}, bf16[272,256]{1,0:T(8,128)(2,1)S(1)}, u32[]{:S(2)}, u32[]{:S(2)}) collective-permute-start(bf16[272,256]{1,0:T(8,128)(2,1)S(1)} %collective-permute-done.17.refs_10_), channel_id=1, source_target_pairs={{0,1},{1,0},{2,3},{3,2},{4,5},{5,4},{6,7},{7,6},{8,9},{9,8},{10,11... | collective-permute-start | bytes 417800 | tf_op jit(solution)/shard_map/ppermute | solution.py:375
  98.5 3.0 %collective-permute-start.20 = (bf16[272,256]{1,0:T(8,128)(2,1)S(1)}, bf16[272,256]{1,0:T(8,128)(2,1)S(1)}, u32[]{:S(2)}, u32[]{:S(2)}) collective-permute-start(bf16[272,256]{1,0:T(8,128)(2,1)S(1)} %collective-permute-done.16.refs_9_), channel_id=1, source_target_pairs={{0,1},{1,0},{2,3},{3,2},{4,5},{5,4},{6,7},{7,6},{8,9},{9,8},{10,11... | collective-permute-start | bytes 417800 | tf_op jit(solution)/shard_map/ppermute | solution.py:375
  (8 other events, 174.9 us)

commit v13 on v12

--- a/solution.py
+++ b/solution.py
@@ -476,6 +476,7 @@
     (mine,) = add_split([parts[0], *recv], 1)
 
     landed = spread(mine.reshape(32, 8, D))
+    dst_other, src_other = lax.optimization_barrier((dst_other, src_other))
     (dst_sum,) = add_split([dst_own, dst_other], 1)
     dst_total = shift(dst_sum, 1, XL)
     ent_own = sum_with_means([src_own, src_other, dst_total])

time: 107 us -> 105 us (0.981)
  starting transfers between devices: 52.6 us -> 49.4 us
  waiting for transfers between devices: 26.9 us -> 28.7 us
    ppermute x21, starting transfers between devices: 28.9 us -> 23.7 us  [swap(): return lax.ppermute(x, AXES, [(i, i ^ mask) for i in range(256)])]
    ppermute x21, waiting for transfers between devices: 13.9 us -> 16.2 us  [swap(): return lax.ppermute(x, AXES, [(i, i ^ mask) for i in range(256)])]
    ppermute x2, starting transfers between devices: 11.4 us -> 13.4 us  [shift(): return lax.ppermute(x, AXES, route)]
    all_to_all x2, waiting for transfers between devices: 13.1 us -> 11.6 us  [spread(): lax.all_to_all(parts, 'blk', 0, 0, axis_index_groups=groups, tiled=True)]
  transfers between devices with their start and end apart: 25 -> 25, of which waited for: 10 -> 14; matrix products, arithmetic and copies ran while one was open for 2% -> 2% of each run, Pallas kernels for 9% -> 9%
where the time goes in v13:
time: 105 us
  starting transfers between devices  49.4 us (47%)
  waiting for transfers between devices  28.7 us (27%)
  Pallas kernels  21.4 us (20%)
  local copies, waits for them, and re-layouts  2.02 us (2%)
  other arithmetic  1.83 us (2%)
  between operations  1.76 us (2%)
    ppermute x21, starting transfers between devices, swap(): return lax.ppermute(x, AXES, [(i, i ^ mask) for i in range(256)])  23.7 us
    ppermute x21, waiting for transfers between devices, swap(): return lax.ppermute(x, AXES, [(i, i ^ mask) for i in range(256)])  16.2 us
    ppermute x2, starting transfers between devices, shift(): return lax.ppermute(x, AXES, route)  13.4 us
    all_to_all x2, starting transfers between devices, spread(): lax.all_to_all(parts, 'blk', 0, 0, axis_index_groups=groups, tiled=True)  12.3 us
    all_to_all x2, waiting for transfers between devices, spread(): lax.all_to_all(parts, 'blk', 0, 0, axis_index_groups=groups, tiled=True)  11.6 us
    pallas_call x1, Pallas kernels, shards(): call(score_kernel, [kept, sent, kept, sent, slots_low], 1, 10, [pltpu.VME...  5.9 us
    pallas_call x1, Pallas kernels, shards(): call(gather_kernel, [jax.ShapeDtypeStruct((EDGES, D), BF16), jax.ShapeDty...  4.91 us
    pallas_call x1, Pallas kernels, update(): pl.pallas_call(functools.partial(update_kernel, counts), out_shape=shapes...  4.89 us
  transfers between devices with their start and end apart: 25, of which 14 were waited for; matrix products, arithmetic and copies ran while one was open for 2% of the time, Pallas kernels for 9%

profile of v13, /device:TPU:1, one launch (start us, length us, event | category | flops | bytes accessed | tf_op | source)
XLA Modules:
  0.0 105.1 jit_solution(3572772458266602998)
XLA Ops:
  0.7 1.9 %dynamic-slice_convert_fusion = bf16[512,256]{1,0:T(8,128)(2,1)} fusion(f32[2048,256]{1,0:T(8,128)} %refs_0_.1, s32[]{:T(128)S(6)} %select_n.21), kind=kLoop, calls=%fused_computation | loop fusion | bytes 524292 | tf_op jit(solution)/shard_map/convert_element_type | solution.py:396
  2.6 11.1 %collective-permute-start = (bf16[512,256]{1,0:T(8,128)(2,1)}, bf16[512,256]{1,0:T(8,128)(2,1)S(1)}, u32[]{:S(2)}, u32[]{:S(2)}) collective-permute-start(bf16[512,256]{1,0:T(8,128)(2,1)} %dynamic-slice_convert_fusion), channel_id=1, source_target_pairs={{6,0},{7,1},{4,2},{5,3},{10,4},{11,5},{8,6},{9,7},{14,8},{15,9},{1... | collective-permute-start | bytes 786440 | tf_op jit(solution)/shard_map/ppermute | solution.py:380
  13.7 1.7 %convert_element_type.7.low_ref = bf16[2048,256]{1,0:T(8,128)(2,1)S(1)} convert(f32[2048,256]{1,0:T(8,128)} %refs_0_.1) | non-fusion elementwise | flops 524288 | bytes 3145728 | tf_op jit(solution)/shard_map/convert_element_type | solution.py:394
  15.6 4.9 %shard_map.120 = (bf16[1024,256]{1,0:T(8,128)(2,1)S(1)}, f32[1024,256]{1,0:T(8,128)S(1)}, f32[1024,256]{1,0:T(8,128)S(1)}, f32[4,16,128]{2,1,0:T(8,128)S(1)}) custom-call(s32[8,1024]{1,0:T(8,128)S(1)} %concatenate.3.ids_ref, s32[4,1024]{1,0:T(4,128)S(1)} %reshape.30.negs_ref, bf16[2048,256]{1,0:T(8,128)(2,1)S(1)} %convert_element_type.7.low_ref, ...), custom_call_target="tpu_custom_call" | custom-call | flops 4294967296 | bytes 4194304 | tf_op jit(solution)/shard_map/pallas_call | solution.py:410
  21.6 1.2 %collective-permute-done.2.far_ref = bf16[512,256]{1,0:T(8,128)(2,1)S(1)} collective-permute-done((bf16[512,256]{1,0:T(8,128)(2,1)S(1)}, bf16[512,256]{1,0:T(8,128)(2,1)S(1)}, u32[]{:S(2)}, u32[]{:S(2)}) %collective-permute-start.2) | collective-permute-done | bytes 262176 | tf_op jit(solution)/shard_map/ppermute | solution.py:375
  22.7 2.2 %shard_map.121 = (bf16[1024,1024]{1,0:T(8,128)(2,1)S(1)}, f32[1024,256]{1,0:T(8,128)S(1)}, f32[1024,256]{1,0:T(8,128)S(1)}) custom-call(s32[8,1024]{1,0:T(8,128)S(1)} %concatenate.3.ids_ref, bf16[512,256]{1,0:T(8,128)(2,1)S(1)} %collective-permute-done.near_ref, bf16[512,256]{1,0:T(8,128)(2,1)S(1)} %collective-permute-done.2.far_ref, ...), custom_call_target="tpu_custom_call" | custom-call | flops 1610612736 | bytes 4194304 | tf_op jit(solution)/shard_map/pallas_call | solution.py:433
  25.0 4.5 %collective-permute-done.1.near_ref = bf16[512,256]{1,0:T(8,128)(2,1)S(1)} collective-permute-done((bf16[512,256]{1,0:T(8,128)(2,1)S(1)}, bf16[512,256]{1,0:T(8,128)(2,1)S(1)}, u32[]{:S(2)}, u32[]{:S(2)}) %collective-permute-start.1) | collective-permute-done | bytes 262176 | tf_op jit(solution)/shard_map/ppermute | solution.py:375
  31.5 5.9 %shard_map.122 = (f32[1024,256]{1,0:T(8,128)S(1)}, bf16[1024,256]{1,0:T(8,128)(2,1)S(1)}, f32[1024,256]{1,0:T(8,128)S(1)}, bf16[1024,256]{1,0:T(8,128)(2,1)S(1)}, bf16[1024,256]{1,0:T(8,128)(2,1)S(1)}) custom-call(s32[1,1]{1,0:T(1,128)S(6)} %copy.13.count_ref, s32[8,1024]{1,0:T(8,128)S(1)} %concatenate.3.ids_ref, ...), custom_call_target="tpu_custom_call" | custom-call | flops 4831838208 | bytes 8388608 | tf_op jit(solution)/shard_map/pallas_call | solution.py:443
  37.4 1.2 %shard_map.124 = (f32[1024,256]{1,0:T(8,128)S(1)}, bf16[1024,256]{1,0:T(8,128)(2,1)S(1)}) custom-call(s32[8,1024]{1,0:T(8,128)S(1)} %concatenate.3.ids_ref, bf16[1024,256]{1,0:T(8,128)(2,1)S(1)} %get-tuple-element.58.gr_ref), custom_call_target="tpu_custom_call" | custom-call | flops 1073741824 | bytes 2097152 | tf_op jit(solution)/shard_map/pallas_call | solution.py:459
  41.0 3.7 %collective-permute-start.8 = (bf16[256,256]{1,0:T(8,128)(2,1)S(1)}, bf16[256,256]{1,0:T(8,128)(2,1)S(1)}, u32[]{:S(2)}, u32[]{:S(2)}) collective-permute-start(bf16[256,256]{1,0:T(8,128)(2,1)S(1)} %get-tuple-element.63), channel_id=1, source_target_pairs={{0,6},{1,7},{2,4},{3,5},{4,2},{5,3},{6,0},{7,1},{8,14},{9,15},{10,... | collective-permute-start | bytes 393224 | tf_op jit(solution)/shard_map/ppermute | solution.py:375
  45.6 1.4 %collective-permute-done.7.refs_2_ = bf16[256,256]{1,0:T(8,128)(2,1)S(1)} collective-permute-done((bf16[256,256]{1,0:T(8,128)(2,1)S(1)}, bf16[256,256]{1,0:T(8,128)(2,1)S(1)}, u32[]{:S(2)}, u32[]{:S(2)}) %collective-permute-start.7) | collective-permute-done | bytes 131104 | tf_op jit(solution)/shard_map/ppermute | solution.py:375
  47.0 3.7 %collective-permute-done.8.refs_3_ = bf16[256,256]{1,0:T(8,128)(2,1)S(1)} collective-permute-done((bf16[256,256]{1,0:T(8,128)(2,1)S(1)}, bf16[256,256]{1,0:T(8,128)(2,1)S(1)}, u32[]{:S(2)}, u32[]{:S(2)}) %collective-permute-start.8) | collective-permute-done | bytes 131104 | tf_op jit(solution)/shard_map/ppermute | solution.py:375
  50.7 1.5 %collective-permute-start.11 = (bf16[512,256]{1,0:T(8,128)(2,1)S(1)}, bf16[512,256]{1,0:T(8,128)(2,1)S(1)}, u32[]{:S(2)}, u32[]{:S(2)}) collective-permute-start(bf16[512,256]{1,0:T(8,128)(2,1)S(1)} %get-tuple-element.69), channel_id=1, source_target_pairs={{0,2},{1,3},{2,0},{3,1},{4,6},{5,7},{6,4},{7,5},{8,10},{9,11},{10,... | collective-permute-start | bytes 786440 | tf_op jit(solution)/shard_map/ppermute | solution.py:375
  52.9 8.5 %all-to-all-start = ((bf16[32,8,256]{2,1,0:T(8,128)(2,1)}), bf16[32,8,256]{2,1,0:T(8,128)(2,1)S(1)}, u32[]{:S(2)}, u32[]{:S(2)}) async-start(bf16[32,8,256]{2,1,0:T(8,128)(2,1)} %bitcast.3), calls=%async_computation | async-start | bytes 262144 | tf_op jit(solution)/shard_map/all_to_all | solution.py:371
  61.3 2.3 %collective-permute-done.11.refs_1_ = bf16[512,256]{1,0:T(8,128)(2,1)S(1)} collective-permute-done((bf16[512,256]{1,0:T(8,128)(2,1)S(1)}, bf16[512,256]{1,0:T(8,128)(2,1)S(1)}, u32[]{:S(2)}, u32[]{:S(2)}) %collective-permute-start.11) | collective-permute-done | bytes 262176 | tf_op jit(solution)/shard_map/ppermute | solution.py:375
  63.7 2.3 %collective-permute-start.12 = (bf16[512,256]{1,0:T(8,128)(2,1)S(1)}, bf16[512,256]{1,0:T(8,128)(2,1)S(1)}, u32[]{:S(2)}, u32[]{:S(2)}) collective-permute-start(bf16[512,256]{1,0:T(8,128)(2,1)S(1)} %shard_map.127), channel_id=1, source_target_pairs={{254,0},{255,1},{252,2},{253,3},{2,4},{3,5},{0,6},{1,7},{6,8},{7,9... | collective-permute-start | bytes 786440 | tf_op jit(solution)/shard_map/ppermute | solution.py:380
  66.1 4.6 %all-to-all-done.parts_ref = bf16[32,8,256]{2,1,0:T(8,128)(2,1)S(1)} async-done(((bf16[32,8,256]{2,1,0:T(8,128)(2,1)}), bf16[32,8,256]{2,1,0:T(8,128)(2,1)S(1)}, u32[]{:S(2)}, u32[]{:S(2)}) %all-to-all-start) | async-done | bytes 131104 | tf_op jit(solution)/shard_map/all_to_all | solution.py:371
  71.4 3.9 %all-to-all-start.1 = ((f32[32,8,256]{2,1,0:T(8,128)}), f32[32,8,256]{2,1,0:T(8,128)S(1)}, u32[]{:S(2)}, u32[]{:S(2)}) async-start(f32[32,8,256]{2,1,0:T(8,128)} %shard_map.130), calls=%async_computation.1 | async-start | bytes 524288 | tf_op jit(solution)/shard_map/all_to_all | solution.py:371
  76.5 2.4 %collective-permute-start.14 = (bf16[528,256]{1,0:T(8,128)(2,1)S(1)}, bf16[528,256]{1,0:T(8,128)(2,1)S(1)}, u32[]{:S(2)}, u32[]{:S(2)}) collective-permute-start(bf16[528,256]{1,0:T(8,128)(2,1)S(1)} %shard_map.128.refs_2_), channel_id=1, source_target_pairs={{0,1},{1,0},{2,3},{3,2},{4,5},{5,4},{6,7},{7,6},{8,9},{9,8},{10,11... | collective-permute-start | bytes 811016 | tf_op jit(solution)/shard_map/ppermute | solution.py:375
  78.9 7.0 %all-to-all-done.1 = f32[32,8,256]{2,1,0:T(8,128)S(1)} async-done(((f32[32,8,256]{2,1,0:T(8,128)}), f32[32,8,256]{2,1,0:T(8,128)S(1)}, u32[]{:S(2)}, u32[]{:S(2)}) %all-to-all-start.1) | async-done | bytes 262176 | tf_op jit(solution)/shard_map/all_to_all | solution.py:371
  88.0 1.4 %collective-permute-start.16 = (bf16[272,256]{1,0:T(8,128)(2,1)S(1)}, bf16[272,256]{1,0:T(8,128)(2,1)S(1)}, u32[]{:S(2)}, u32[]{:S(2)}) collective-permute-start(bf16[272,256]{1,0:T(8,128)(2,1)S(1)} %shard_map.131.refs_8_), channel_id=1, source_target_pairs={{0,2},{1,3},{2,0},{3,1},{4,6},{5,7},{6,4},{7,5},{8,10},{9,11},{10,... | collective-permute-start | bytes 417800 | tf_op jit(solution)/shard_map/ppermute | solution.py:375
  89.4 5.2 %collective-permute-start.15 = (bf16[528,256]{1,0:T(8,128)(2,1)S(1)}, bf16[528,256]{1,0:T(8,128)(2,1)S(1)}, u32[]{:S(2)}, u32[]{:S(2)}) collective-permute-start(bf16[528,256]{1,0:T(8,128)(2,1)S(1)} %collective-permute-done.13.refs_3_), channel_id=1, source_target_pairs={{0,1},{1,0},{2,3},{3,2},{4,5},{5,4},{6,7},{7,6},{8,9},{9,8},{10,11... | collective-permute-start | bytes 811016 | tf_op jit(solution)/shard_map/ppermute | solution.py:375
  94.6 3.7 %collective-permute-start.22 = (bf16[272,256]{1,0:T(8,128)(2,1)S(1)}, bf16[272,256]{1,0:T(8,128)(2,1)S(1)}, u32[]{:S(2)}, u32[]{:S(2)}) collective-permute-start(bf16[272,256]{1,0:T(8,128)(2,1)S(1)} %collective-permute-done.18.refs_11_), channel_id=1, source_target_pairs={{0,1},{1,0},{2,3},{3,2},{4,5},{5,4},{6,7},{7,6},{8,9},{9,8},{10,11... | collective-permute-start | bytes 417800 | tf_op jit(solution)/shard_map/ppermute | solution.py:375
  100.1 4.9 %shard_map.132 = (f32[2048,256]{1,0:T(8,128)}, f32[16,128]{1,0:T(8,128)}, f32[2048,256]{1,0:T(8,128)}, f32[16,128]{1,0:T(8,128)}) custom-call(s32[2]{0:T(128)S(1)} %pad_add_fusion.place_ref, f32[2048,256]{1,0:T(8,128)} %refs_0_.1, f32[16,128]{1,0:T(8,128)S(1)} %bitcast.9, bf16[528,256]{1,0:T(8,128)(2,1)S(1)} %shard_map.128.refs_2_, ...), custom_call_target="tpu_custom_call" | custom-call | flops 8388608 | bytes 10485760 | tf_op jit(solution)/shard_map/pallas_call | solution.py:337
  (62 shorter events, 12.4 us)
Async XLA Ops:
  2.6 17.9 %collective-permute-start = (bf16[512,256]{1,0:T(8,128)(2,1)}, bf16[512,256]{1,0:T(8,128)(2,1)S(1)}, u32[]{:S(2)}, u32[]{:S(2)}) collective-permute-start(bf16[512,256]{1,0:T(8,128)(2,1)} %dynamic-slice_convert_fusion), channel_id=1, source_target_pairs={{6,0},{7,1},{4,2},{5,3},{10,4},{11,5},{8,6},{9,7},{14,8},{15,9},{1... | collective-permute-start | bytes 786440 | tf_op jit(solution)/shard_map/ppermute | solution.py:380
  20.5 2.2 %collective-permute-start.2 = (bf16[512,256]{1,0:T(8,128)(2,1)S(1)}, bf16[512,256]{1,0:T(8,128)(2,1)S(1)}, u32[]{:S(2)}, u32[]{:S(2)}) collective-permute-start(bf16[512,256]{1,0:T(8,128)(2,1)S(1)} %collective-permute-done.near_ref), channel_id=1, source_target_pairs={{0,1},{1,0},{2,3},{3,2},{4,5},{5,4},{6,7},{7,6},{8,9},{9,8},{10,11... | collective-permute-start | bytes 786440 | tf_op jit(solution)/shard_map/ppermute | solution.py:375
  21.6 7.9 %collective-permute-start.1 = (bf16[512,256]{1,0:T(8,128)(2,1)S(1)}, bf16[512,256]{1,0:T(8,128)(2,1)S(1)}, u32[]{:S(2)}, u32[]{:S(2)}) collective-permute-start(bf16[512,256]{1,0:T(8,128)(2,1)S(1)} %collective-permute-done.near_ref), channel_id=1, source_target_pairs={{0,2},{1,3},{2,0},{3,1},{4,6},{5,7},{6,4},{7,5},{8,10},{9,11},{10,... | collective-permute-start | bytes 786440 | tf_op jit(solution)/shard_map/ppermute | solution.py:375
  29.4 2.0 %collective-permute-start.3 = (bf16[512,256]{1,0:T(8,128)(2,1)S(1)}, bf16[512,256]{1,0:T(8,128)(2,1)S(1)}, u32[]{:S(2)}, u32[]{:S(2)}) collective-permute-start(bf16[512,256]{1,0:T(8,128)(2,1)S(1)} %collective-permute-done.1.near_ref), channel_id=1, source_target_pairs={{0,1},{1,0},{2,3},{3,2},{4,5},{5,4},{6,7},{7,6},{8,9},{9,8},{10,11... | collective-permute-start | bytes 786440 | tf_op jit(solution)/shard_map/ppermute | solution.py:375
  38.6 2.0 %collective-permute-start.5 = (bf16[1024,256]{1,0:T(8,128)(2,1)S(1)}, bf16[1024,256]{1,0:T(8,128)(2,1)S(1)}, u32[]{:S(2)}, u32[]{:S(2)}) collective-permute-start(bf16[1024,256]{1,0:T(8,128)(2,1)S(1)} %get-tuple-element.60), channel_id=1, source_target_pairs={{0,1},{1,0},{2,3},{3,2},{4,5},{5,4},{6,7},{7,6},{8,9},{9,8},{10,11... | collective-permute-start | bytes 1572872 | tf_op jit(solution)/shard_map/ppermute | solution.py:375
  39.1 5.6 %collective-permute-start.4 = (bf16[1024,256]{1,0:T(8,128)(2,1)S(1)}, bf16[1024,256]{1,0:T(8,128)(2,1)S(1)}, u32[]{:S(2)}, u32[]{:S(2)}) collective-permute-start(bf16[1024,256]{1,0:T(8,128)(2,1)S(1)} %get-tuple-element.56), channel_id=1, source_target_pairs={{0,1},{1,0},{2,3},{3,2},{4,5},{5,4},{6,7},{7,6},{8,9},{9,8},{10,11... | collective-permute-start | bytes 1572872 | tf_op jit(solution)/shard_map/ppermute | solution.py:375
  39.2 5.6 %collective-permute-start.9 = (bf16[1024,256]{1,0:T(8,128)(2,1)S(1)}, bf16[1024,256]{1,0:T(8,128)(2,1)S(1)}, u32[]{:S(2)}, u32[]{:S(2)}) collective-permute-start(bf16[1024,256]{1,0:T(8,128)(2,1)S(1)} %get-tuple-element.65), channel_id=1, source_target_pairs={{0,1},{1,0},{2,3},{3,2},{4,5},{5,4},{6,7},{7,6},{8,9},{9,8},{10,11... | collective-permute-start | bytes 1572872 | tf_op jit(solution)/shard_map/ppermute | solution.py:375
  40.8 4.8 %collective-permute-start.6 = (bf16[256,256]{1,0:T(8,128)(2,1)S(1)}, bf16[256,256]{1,0:T(8,128)(2,1)S(1)}, u32[]{:S(2)}, u32[]{:S(2)}) collective-permute-start(bf16[256,256]{1,0:T(8,128)(2,1)S(1)} %get-tuple-element.61), channel_id=1, source_target_pairs={{0,2},{1,3},{2,0},{3,1},{4,6},{5,7},{6,4},{7,5},{8,10},{9,11},{10,... | collective-permute-start | bytes 393224 | tf_op jit(solution)/shard_map/ppermute | solution.py:375
  40.9 6.1 %collective-permute-start.7 = (bf16[256,256]{1,0:T(8,128)(2,1)S(1)}, bf16[256,256]{1,0:T(8,128)(2,1)S(1)}, u32[]{:S(2)}, u32[]{:S(2)}) collective-permute-start(bf16[256,256]{1,0:T(8,128)(2,1)S(1)} %get-tuple-element.62), channel_id=1, source_target_pairs={{0,4},{1,5},{2,6},{3,7},{4,0},{5,1},{6,2},{7,3},{8,12},{9,13},{10,... | collective-permute-start | bytes 393224 | tf_op jit(solution)/shard_map/ppermute | solution.py:375
  41.0 9.7 %collective-permute-start.8 = (bf16[256,256]{1,0:T(8,128)(2,1)S(1)}, bf16[256,256]{1,0:T(8,128)(2,1)S(1)}, u32[]{:S(2)}, u32[]{:S(2)}) collective-permute-start(bf16[256,256]{1,0:T(8,128)(2,1)S(1)} %get-tuple-element.63), channel_id=1, source_target_pairs={{0,6},{1,7},{2,4},{3,5},{4,2},{5,3},{6,0},{7,1},{8,14},{9,15},{10,... | collective-permute-start | bytes 393224 | tf_op jit(solution)/shard_map/ppermute | solution.py:375
  50.7 10.7 %collective-permute-start.10 = (bf16[512,256]{1,0:T(8,128)(2,1)S(1)}, bf16[512,256]{1,0:T(8,128)(2,1)S(1)}, u32[]{:S(2)}, u32[]{:S(2)}) collective-permute-start(bf16[512,256]{1,0:T(8,128)(2,1)S(1)} %get-tuple-element.68), channel_id=1, source_target_pairs={{0,2},{1,3},{2,0},{3,1},{4,6},{5,7},{6,4},{7,5},{8,10},{9,11},{10,... | collective-permute-start | bytes 786440 | tf_op jit(solution)/shard_map/ppermute | solution.py:375
  50.7 13.0 %collective-permute-start.11 = (bf16[512,256]{1,0:T(8,128)(2,1)S(1)}, bf16[512,256]{1,0:T(8,128)(2,1)S(1)}, u32[]{:S(2)}, u32[]{:S(2)}) collective-permute-start(bf16[512,256]{1,0:T(8,128)(2,1)S(1)} %get-tuple-element.69), channel_id=1, source_target_pairs={{0,2},{1,3},{2,0},{3,1},{4,6},{5,7},{6,4},{7,5},{8,10},{9,11},{10,... | collective-permute-start | bytes 786440 | tf_op jit(solution)/shard_map/ppermute | solution.py:375
  52.9 17.8 %all-to-all-start = ((bf16[32,8,256]{2,1,0:T(8,128)(2,1)}), bf16[32,8,256]{2,1,0:T(8,128)(2,1)S(1)}, u32[]{:S(2)}, u32[]{:S(2)}) async-start(bf16[32,8,256]{2,1,0:T(8,128)(2,1)} %bitcast.3), calls=%async_computation | async-start | bytes 262144 | tf_op jit(solution)/shard_map/all_to_all | solution.py:371
  63.7 12.5 %collective-permute-start.12 = (bf16[512,256]{1,0:T(8,128)(2,1)S(1)}, bf16[512,256]{1,0:T(8,128)(2,1)S(1)}, u32[]{:S(2)}, u32[]{:S(2)}) collective-permute-start(bf16[512,256]{1,0:T(8,128)(2,1)S(1)} %shard_map.127), channel_id=1, source_target_pairs={{254,0},{255,1},{252,2},{253,3},{2,4},{3,5},{0,6},{1,7},{6,8},{7,9... | collective-permute-start | bytes 786440 | tf_op jit(solution)/shard_map/ppermute | solution.py:380
  71.4 14.5 %all-to-all-start.1 = ((f32[32,8,256]{2,1,0:T(8,128)}), f32[32,8,256]{2,1,0:T(8,128)S(1)}, u32[]{:S(2)}, u32[]{:S(2)}) async-start(f32[32,8,256]{2,1,0:T(8,128)} %shard_map.130), calls=%async_computation.1 | async-start | bytes 524288 | tf_op jit(solution)/shard_map/all_to_all | solution.py:371
  76.4 9.5 %collective-permute-start.13 = (bf16[528,256]{1,0:T(8,128)(2,1)S(1)}, bf16[528,256]{1,0:T(8,128)(2,1)S(1)}, u32[]{:S(2)}, u32[]{:S(2)}) collective-permute-start(bf16[528,256]{1,0:T(8,128)(2,1)S(1)} %shard_map.128.refs_2_), channel_id=1, source_target_pairs={{0,2},{1,3},{2,0},{3,1},{4,6},{5,7},{6,4},{7,5},{8,10},{9,11},{10,... | collective-permute-start | bytes 811016 | tf_op jit(solution)/shard_map/ppermute | solution.py:375
  76.5 18.0 %collective-permute-start.14 = (bf16[528,256]{1,0:T(8,128)(2,1)S(1)}, bf16[528,256]{1,0:T(8,128)(2,1)S(1)}, u32[]{:S(2)}, u32[]{:S(2)}) collective-permute-start(bf16[528,256]{1,0:T(8,128)(2,1)S(1)} %shard_map.128.refs_2_), channel_id=1, source_target_pairs={{0,1},{1,0},{2,3},{3,2},{4,5},{5,4},{6,7},{7,6},{8,9},{9,8},{10,11... | collective-permute-start | bytes 811016 | tf_op jit(solution)/shard_map/ppermute | solution.py:375
  86.1 8.5 %collective-permute-start.18 = (bf16[272,256]{1,0:T(8,128)(2,1)S(1)}, bf16[272,256]{1,0:T(8,128)(2,1)S(1)}, u32[]{:S(2)}, u32[]{:S(2)}) collective-permute-start(bf16[272,256]{1,0:T(8,128)(2,1)S(1)} %shard_map.131.refs_8_), channel_id=1, source_target_pairs={{0,6},{1,7},{2,4},{3,5},{4,2},{5,3},{6,0},{7,1},{8,14},{9,15},{10,... | collective-permute-start | bytes 417800 | tf_op jit(solution)/shard_map/ppermute | solution.py:375
  86.9 11.3 %collective-permute-start.17 = (bf16[272,256]{1,0:T(8,128)(2,1)S(1)}, bf16[272,256]{1,0:T(8,128)(2,1)S(1)}, u32[]{:S(2)}, u32[]{:S(2)}) collective-permute-start(bf16[272,256]{1,0:T(8,128)(2,1)S(1)} %shard_map.131.refs_8_), channel_id=1, source_target_pairs={{0,4},{1,5},{2,6},{3,7},{4,0},{5,1},{6,2},{7,3},{8,12},{9,13},{10,... | collective-permute-start | bytes 417800 | tf_op jit(solution)/shard_map/ppermute | solution.py:375
  88.0 10.2 %collective-permute-start.16 = (bf16[272,256]{1,0:T(8,128)(2,1)S(1)}, bf16[272,256]{1,0:T(8,128)(2,1)S(1)}, u32[]{:S(2)}, u32[]{:S(2)}) collective-permute-start(bf16[272,256]{1,0:T(8,128)(2,1)S(1)} %shard_map.131.refs_8_), channel_id=1, source_target_pairs={{0,2},{1,3},{2,0},{3,1},{4,6},{5,7},{6,4},{7,5},{8,10},{9,11},{10,... | collective-permute-start | bytes 417800 | tf_op jit(solution)/shard_map/ppermute | solution.py:375
  89.4 9.8 %collective-permute-start.15 = (bf16[528,256]{1,0:T(8,128)(2,1)S(1)}, bf16[528,256]{1,0:T(8,128)(2,1)S(1)}, u32[]{:S(2)}, u32[]{:S(2)}) collective-permute-start(bf16[528,256]{1,0:T(8,128)(2,1)S(1)} %collective-permute-done.13.refs_3_), channel_id=1, source_target_pairs={{0,1},{1,0},{2,3},{3,2},{4,5},{5,4},{6,7},{7,6},{8,9},{9,8},{10,11... | collective-permute-start | bytes 811016 | tf_op jit(solution)/shard_map/ppermute | solution.py:375
  94.5 4.6 %collective-permute-start.19 = (bf16[272,256]{1,0:T(8,128)(2,1)S(1)}, bf16[272,256]{1,0:T(8,128)(2,1)S(1)}, u32[]{:S(2)}, u32[]{:S(2)}) collective-permute-start(bf16[272,256]{1,0:T(8,128)(2,1)S(1)} %shard_map.131.refs_8_), channel_id=1, source_target_pairs={{0,1},{1,0},{2,3},{3,2},{4,5},{5,4},{6,7},{7,6},{8,9},{9,8},{10,11... | collective-permute-start | bytes 417800 | tf_op jit(solution)/shard_map/ppermute | solution.py:375
  94.6 4.6 %collective-permute-start.22 = (bf16[272,256]{1,0:T(8,128)(2,1)S(1)}, bf16[272,256]{1,0:T(8,128)(2,1)S(1)}, u32[]{:S(2)}, u32[]{:S(2)}) collective-permute-start(bf16[272,256]{1,0:T(8,128)(2,1)S(1)} %collective-permute-done.18.refs_11_), channel_id=1, source_target_pairs={{0,1},{1,0},{2,3},{3,2},{4,5},{5,4},{6,7},{7,6},{8,9},{9,8},{10,11... | collective-permute-start | bytes 417800 | tf_op jit(solution)/shard_map/ppermute | solution.py:375
  98.2 1.8 %collective-permute-start.20 = (bf16[272,256]{1,0:T(8,128)(2,1)S(1)}, bf16[272,256]{1,0:T(8,128)(2,1)S(1)}, u32[]{:S(2)}, u32[]{:S(2)}) collective-permute-start(bf16[272,256]{1,0:T(8,128)(2,1)S(1)} %collective-permute-done.16.refs_9_), channel_id=1, source_target_pairs={{0,1},{1,0},{2,3},{3,2},{4,5},{5,4},{6,7},{7,6},{8,9},{9,8},{10,11... | collective-permute-start | bytes 417800 | tf_op jit(solution)/shard_map/ppermute | solution.py:375
  (8 other events, 171.4 us)

commit v14 on v13

--- a/solution.py
+++ b/solution.py
@@ -469,7 +469,7 @@
     src_own, src_away = add_split([src_keep, src_recv], 2, own=F32)
     dst_away, dst_own = add_split([dst_keep, dst_recv], 2)
     parts = add_split([rel_keep, rel_recv], 4, own=F32)
-    recv = [swap(part, mask) for part, mask in zip(parts[1:], X_MASKS)]
+    recv = [swap(parts[k], X_MASKS[k - 1]) for k in (2, 1, 3)]
     recv, dst_away, src_away = lax.optimization_barrier((recv, dst_away, src_away))
     dst_other = swap(dst_away, XL)
     src_other = swap(src_away, XL)

time: 105 us -> 104 us (level)
  starting transfers between devices: 49.4 us -> 46.7 us
  waiting for transfers between devices: 28.7 us -> 30.4 us
    all_to_all x2, waiting for transfers between devices: 11.6 us -> 7.81 us  [spread(): lax.all_to_all(parts, 'blk', 0, 0, axis_index_groups=groups, tiled=True)]
    ppermute x21, waiting for transfers between devices: 16.2 us -> 19.7 us  [swap(): return lax.ppermute(x, AXES, [(i, i ^ mask) for i in range(256)])]
    ppermute x2, starting transfers between devices: 13.4 us -> 11.4 us  [shift(): return lax.ppermute(x, AXES, route)]
    all_to_all x2, starting transfers between devices: 12.3 us -> 10.3 us  [spread(): lax.all_to_all(parts, 'blk', 0, 0, axis_index_groups=groups, tiled=True)]
    ppermute x2, waiting for transfers between devices: 0.87 us -> 2.86 us  [shift(): return lax.ppermute(x, AXES, route)]
    ppermute x21, starting transfers between devices: 23.7 us -> 25.1 us  [swap(): return lax.ppermute(x, AXES, [(i, i ^ mask) for i in range(256)])]
  transfers between devices with their start and end apart: 25 -> 25, of which waited for: 14 -> 12; matrix products, arithmetic and copies ran while one was open for 2% -> 2% of each run, Pallas kernels for 9% -> 9%
where the time goes in v14:
time: 104 us
  starting transfers between devices  46.7 us (45%)
  waiting for transfers between devices  30.4 us (29%)
  Pallas kernels  21.4 us (21%)
  local copies, waits for them, and re-layouts  2.02 us (2%)
  other arithmetic  1.83 us (2%)
  between operations  1.78 us (2%)
    ppermute x21, starting transfers between devices, swap(): return lax.ppermute(x, AXES, [(i, i ^ mask) for i in range(256)])  25.1 us
    ppermute x21, waiting for transfers between devices, swap(): return lax.ppermute(x, AXES, [(i, i ^ mask) for i in range(256)])  19.7 us
    ppermute x2, starting transfers between devices, shift(): return lax.ppermute(x, AXES, route)  11.4 us
    all_to_all x2, starting transfers between devices, spread(): lax.all_to_all(parts, 'blk', 0, 0, axis_index_groups=groups, tiled=True)  10.3 us
    all_to_all x2, waiting for transfers between devices, spread(): lax.all_to_all(parts, 'blk', 0, 0, axis_index_groups=groups, tiled=True)  7.81 us
    pallas_call x1, Pallas kernels, shards(): call(score_kernel, [kept, sent, kept, sent, slots_low], 1, 10, [pltpu.VME...  5.9 us
    pallas_call x1, Pallas kernels, shards(): call(gather_kernel, [jax.ShapeDtypeStruct((EDGES, D), BF16), jax.ShapeDty...  4.91 us
    pallas_call x1, Pallas kernels, update(): pl.pallas_call(functools.partial(update_kernel, counts), out_shape=shapes...  4.89 us
  transfers between devices with their start and end apart: 25, of which 12 were waited for; matrix products, arithmetic and copies ran while one was open for 2% of the time, Pallas kernels for 9%

profile of v14, /device:TPU:1, one launch (start us, length us, event | category | flops | bytes accessed | tf_op | source)
XLA Modules:
  0.0 104.1 jit_solution(4143779921591666558)
XLA Ops:
  0.7 1.9 %dynamic-slice_convert_fusion = bf16[512,256]{1,0:T(8,128)(2,1)} fusion(f32[2048,256]{1,0:T(8,128)} %refs_0_.1, s32[]{:T(128)S(6)} %select_n.21), kind=kLoop, calls=%fused_computation | loop fusion | bytes 524292 | tf_op jit(solution)/shard_map/convert_element_type | solution.py:396
  2.6 11.1 %collective-permute-start = (bf16[512,256]{1,0:T(8,128)(2,1)}, bf16[512,256]{1,0:T(8,128)(2,1)S(1)}, u32[]{:S(2)}, u32[]{:S(2)}) collective-permute-start(bf16[512,256]{1,0:T(8,128)(2,1)} %dynamic-slice_convert_fusion), channel_id=1, source_target_pairs={{6,0},{7,1},{4,2},{5,3},{10,4},{11,5},{8,6},{9,7},{14,8},{15,9},{1... | collective-permute-start | bytes 786440 | tf_op jit(solution)/shard_map/ppermute | solution.py:380
  13.7 1.7 %convert_element_type.7.low_ref = bf16[2048,256]{1,0:T(8,128)(2,1)S(1)} convert(f32[2048,256]{1,0:T(8,128)} %refs_0_.1) | non-fusion elementwise | flops 524288 | bytes 3145728 | tf_op jit(solution)/shard_map/convert_element_type | solution.py:394
  15.6 4.9 %shard_map.120 = (bf16[1024,256]{1,0:T(8,128)(2,1)S(1)}, f32[1024,256]{1,0:T(8,128)S(1)}, f32[1024,256]{1,0:T(8,128)S(1)}, f32[4,16,128]{2,1,0:T(8,128)S(1)}) custom-call(s32[8,1024]{1,0:T(8,128)S(1)} %concatenate.3.ids_ref, s32[4,1024]{1,0:T(4,128)S(1)} %reshape.30.negs_ref, bf16[2048,256]{1,0:T(8,128)(2,1)S(1)} %convert_element_type.7.low_ref, ...), custom_call_target="tpu_custom_call" | custom-call | flops 4294967296 | bytes 4194304 | tf_op jit(solution)/shard_map/pallas_call | solution.py:410
  22.7 2.2 %shard_map.121 = (bf16[1024,1024]{1,0:T(8,128)(2,1)S(1)}, f32[1024,256]{1,0:T(8,128)S(1)}, f32[1024,256]{1,0:T(8,128)S(1)}) custom-call(s32[8,1024]{1,0:T(8,128)S(1)} %concatenate.3.ids_ref, bf16[512,256]{1,0:T(8,128)(2,1)S(1)} %collective-permute-done.near_ref, bf16[512,256]{1,0:T(8,128)(2,1)S(1)} %collective-permute-done.2.far_ref, ...), custom_call_target="tpu_custom_call" | custom-call | flops 1610612736 | bytes 4194304 | tf_op jit(solution)/shard_map/pallas_call | solution.py:433
  25.0 4.5 %collective-permute-done.1.near_ref = bf16[512,256]{1,0:T(8,128)(2,1)S(1)} collective-permute-done((bf16[512,256]{1,0:T(8,128)(2,1)S(1)}, bf16[512,256]{1,0:T(8,128)(2,1)S(1)}, u32[]{:S(2)}, u32[]{:S(2)}) %collective-permute-start.1) | collective-permute-done | bytes 262176 | tf_op jit(solution)/shard_map/ppermute | solution.py:375
  31.5 5.9 %shard_map.122 = (f32[1024,256]{1,0:T(8,128)S(1)}, bf16[1024,256]{1,0:T(8,128)(2,1)S(1)}, f32[1024,256]{1,0:T(8,128)S(1)}, bf16[1024,256]{1,0:T(8,128)(2,1)S(1)}, bf16[1024,256]{1,0:T(8,128)(2,1)S(1)}) custom-call(s32[1,1]{1,0:T(1,128)S(6)} %copy.13.count_ref, s32[8,1024]{1,0:T(8,128)S(1)} %concatenate.3.ids_ref, ...), custom_call_target="tpu_custom_call" | custom-call | flops 4831838208 | bytes 8388608 | tf_op jit(solution)/shard_map/pallas_call | solution.py:443
  37.4 1.2 %shard_map.124 = (f32[1024,256]{1,0:T(8,128)S(1)}, bf16[1024,256]{1,0:T(8,128)(2,1)S(1)}) custom-call(s32[8,1024]{1,0:T(8,128)S(1)} %concatenate.3.ids_ref, bf16[1024,256]{1,0:T(8,128)(2,1)S(1)} %get-tuple-element.58.gr_ref), custom_call_target="tpu_custom_call" | custom-call | flops 1073741824 | bytes 2097152 | tf_op jit(solution)/shard_map/pallas_call | solution.py:459
  41.0 3.1 %collective-permute-start.8 = (bf16[256,256]{1,0:T(8,128)(2,1)S(1)}, bf16[256,256]{1,0:T(8,128)(2,1)S(1)}, u32[]{:S(2)}, u32[]{:S(2)}) collective-permute-start(bf16[256,256]{1,0:T(8,128)(2,1)S(1)} %get-tuple-element.63), channel_id=1, source_target_pairs={{0,6},{1,7},{2,4},{3,5},{4,2},{5,3},{6,0},{7,1},{8,14},{9,15},{10,... | collective-permute-start | bytes 393224 | tf_op jit(solution)/shard_map/ppermute | solution.py:375
  44.3 2.8 %collective-permute-done.6.refs_1_ = bf16[256,256]{1,0:T(8,128)(2,1)S(1)} collective-permute-done((bf16[256,256]{1,0:T(8,128)(2,1)S(1)}, bf16[256,256]{1,0:T(8,128)(2,1)S(1)}, u32[]{:S(2)}, u32[]{:S(2)}) %collective-permute-start.6) | collective-permute-done | bytes 131104 | tf_op jit(solution)/shard_map/ppermute | solution.py:375
  47.2 3.4 %collective-permute-done.8.refs_3_ = bf16[256,256]{1,0:T(8,128)(2,1)S(1)} collective-permute-done((bf16[256,256]{1,0:T(8,128)(2,1)S(1)}, bf16[256,256]{1,0:T(8,128)(2,1)S(1)}, u32[]{:S(2)}, u32[]{:S(2)}) %collective-permute-start.8) | collective-permute-done | bytes 131104 | tf_op jit(solution)/shard_map/ppermute | solution.py:375
  50.6 1.5 %collective-permute-start.11 = (bf16[512,256]{1,0:T(8,128)(2,1)S(1)}, bf16[512,256]{1,0:T(8,128)(2,1)S(1)}, u32[]{:S(2)}, u32[]{:S(2)}) collective-permute-start(bf16[512,256]{1,0:T(8,128)(2,1)S(1)} %get-tuple-element.69), channel_id=1, source_target_pairs={{0,2},{1,3},{2,0},{3,1},{4,6},{5,7},{6,4},{7,5},{8,10},{9,11},{10,... | collective-permute-start | bytes 786440 | tf_op jit(solution)/shard_map/ppermute | solution.py:375
  52.8 5.5 %all-to-all-start = ((bf16[32,8,256]{2,1,0:T(8,128)(2,1)}), bf16[32,8,256]{2,1,0:T(8,128)(2,1)S(1)}, u32[]{:S(2)}, u32[]{:S(2)}) async-start(bf16[32,8,256]{2,1,0:T(8,128)(2,1)} %bitcast.3), calls=%async_computation | async-start | bytes 262144 | tf_op jit(solution)/shard_map/all_to_all | solution.py:371
  58.2 5.3 %collective-permute-done.11.refs_1_ = bf16[512,256]{1,0:T(8,128)(2,1)S(1)} collective-permute-done((bf16[512,256]{1,0:T(8,128)(2,1)S(1)}, bf16[512,256]{1,0:T(8,128)(2,1)S(1)}, u32[]{:S(2)}, u32[]{:S(2)}) %collective-permute-start.11) | collective-permute-done | bytes 262176 | tf_op jit(solution)/shard_map/ppermute | solution.py:375
  64.0 3.7 %all-to-all-done.parts_ref = bf16[32,8,256]{2,1,0:T(8,128)(2,1)S(1)} async-done(((bf16[32,8,256]{2,1,0:T(8,128)(2,1)}), bf16[32,8,256]{2,1,0:T(8,128)(2,1)S(1)}, u32[]{:S(2)}, u32[]{:S(2)}) %all-to-all-start) | async-done | bytes 131104 | tf_op jit(solution)/shard_map/all_to_all | solution.py:371
  68.4 4.9 %all-to-all-start.1 = ((f32[32,8,256]{2,1,0:T(8,128)}), f32[32,8,256]{2,1,0:T(8,128)S(1)}, u32[]{:S(2)}, u32[]{:S(2)}) async-start(f32[32,8,256]{2,1,0:T(8,128)} %shard_map.130), calls=%async_computation.1 | async-start | bytes 524288 | tf_op jit(solution)/shard_map/all_to_all | solution.py:371
  73.2 2.9 %collective-permute-done.12.refs_2_ = bf16[512,256]{1,0:T(8,128)(2,1)S(1)} collective-permute-done((bf16[512,256]{1,0:T(8,128)(2,1)S(1)}, bf16[512,256]{1,0:T(8,128)(2,1)S(1)}, u32[]{:S(2)}, u32[]{:S(2)}) %collective-permute-start.12) | collective-permute-done | bytes 262176 | tf_op jit(solution)/shard_map/ppermute | solution.py:380
  76.4 3.1 %collective-permute-start.14 = (bf16[528,256]{1,0:T(8,128)(2,1)S(1)}, bf16[528,256]{1,0:T(8,128)(2,1)S(1)}, u32[]{:S(2)}, u32[]{:S(2)}) collective-permute-start(bf16[528,256]{1,0:T(8,128)(2,1)S(1)} %shard_map.128.refs_2_), channel_id=1, source_target_pairs={{0,1},{1,0},{2,3},{3,2},{4,5},{5,4},{6,7},{7,6},{8,9},{9,8},{10,11... | collective-permute-start | bytes 811016 | tf_op jit(solution)/shard_map/ppermute | solution.py:375
  79.5 4.2 %all-to-all-done.1 = f32[32,8,256]{2,1,0:T(8,128)S(1)} async-done(((f32[32,8,256]{2,1,0:T(8,128)}), f32[32,8,256]{2,1,0:T(8,128)S(1)}, u32[]{:S(2)}, u32[]{:S(2)}) %all-to-all-start.1) | async-done | bytes 262176 | tf_op jit(solution)/shard_map/all_to_all | solution.py:371
  83.8 2.3 %collective-permute-start.18 = (bf16[272,256]{1,0:T(8,128)(2,1)S(1)}, bf16[272,256]{1,0:T(8,128)(2,1)S(1)}, u32[]{:S(2)}, u32[]{:S(2)}) collective-permute-start(bf16[272,256]{1,0:T(8,128)(2,1)S(1)} %shard_map.131.refs_8_), channel_id=1, source_target_pairs={{0,6},{1,7},{2,4},{3,5},{4,2},{5,3},{6,0},{7,1},{8,14},{9,15},{10,... | collective-permute-start | bytes 417800 | tf_op jit(solution)/shard_map/ppermute | solution.py:375
  87.1 5.9 %collective-permute-start.15 = (bf16[528,256]{1,0:T(8,128)(2,1)S(1)}, bf16[528,256]{1,0:T(8,128)(2,1)S(1)}, u32[]{:S(2)}, u32[]{:S(2)}) collective-permute-start(bf16[528,256]{1,0:T(8,128)(2,1)S(1)} %collective-permute-done.13.refs_3_), channel_id=1, source_target_pairs={{0,1},{1,0},{2,3},{3,2},{4,5},{5,4},{6,7},{7,6},{8,9},{9,8},{10,11... | collective-permute-start | bytes 811016 | tf_op jit(solution)/shard_map/ppermute | solution.py:375
  93.1 1.3 %collective-permute-start.22 = (bf16[272,256]{1,0:T(8,128)(2,1)S(1)}, bf16[272,256]{1,0:T(8,128)(2,1)S(1)}, u32[]{:S(2)}, u32[]{:S(2)}) collective-permute-start(bf16[272,256]{1,0:T(8,128)(2,1)S(1)} %collective-permute-done.18.refs_11_), channel_id=1, source_target_pairs={{0,1},{1,0},{2,3},{3,2},{4,5},{5,4},{6,7},{7,6},{8,9},{9,8},{10,11... | collective-permute-start | bytes 417800 | tf_op jit(solution)/shard_map/ppermute | solution.py:375
  94.4 2.5 %collective-permute-start.21 = (bf16[272,256]{1,0:T(8,128)(2,1)S(1)}, bf16[272,256]{1,0:T(8,128)(2,1)S(1)}, u32[]{:S(2)}, u32[]{:S(2)}) collective-permute-start(bf16[272,256]{1,0:T(8,128)(2,1)S(1)} %collective-permute-done.17.refs_10_), channel_id=1, source_target_pairs={{0,1},{1,0},{2,3},{3,2},{4,5},{5,4},{6,7},{7,6},{8,9},{9,8},{10,11... | collective-permute-start | bytes 417800 | tf_op jit(solution)/shard_map/ppermute | solution.py:375
  99.1 4.9 %shard_map.132 = (f32[2048,256]{1,0:T(8,128)}, f32[16,128]{1,0:T(8,128)}, f32[2048,256]{1,0:T(8,128)}, f32[16,128]{1,0:T(8,128)}) custom-call(s32[2]{0:T(128)S(1)} %pad_add_fusion.place_ref, f32[2048,256]{1,0:T(8,128)} %refs_0_.1, f32[16,128]{1,0:T(8,128)S(1)} %bitcast.9, bf16[528,256]{1,0:T(8,128)(2,1)S(1)} %shard_map.128.refs_2_, ...), custom_call_target="tpu_custom_call" | custom-call | flops 8388608 | bytes 10485760 | tf_op jit(solution)/shard_map/pallas_call | solution.py:337
  (62 shorter events, 12.0 us)
Async XLA Ops:
  2.6 17.9 %collective-permute-start = (bf16[512,256]{1,0:T(8,128)(2,1)}, bf16[512,256]{1,0:T(8,128)(2,1)S(1)}, u32[]{:S(2)}, u32[]{:S(2)}) collective-permute-start(bf16[512,256]{1,0:T(8,128)(2,1)} %dynamic-slice_convert_fusion), channel_id=1, source_target_pairs={{6,0},{7,1},{4,2},{5,3},{10,4},{11,5},{8,6},{9,7},{14,8},{15,9},{1... | collective-permute-start | bytes 786440 | tf_op jit(solution)/shard_map/ppermute | solution.py:380
  20.5 2.2 %collective-permute-start.2 = (bf16[512,256]{1,0:T(8,128)(2,1)S(1)}, bf16[512,256]{1,0:T(8,128)(2,1)S(1)}, u32[]{:S(2)}, u32[]{:S(2)}) collective-permute-start(bf16[512,256]{1,0:T(8,128)(2,1)S(1)} %collective-permute-done.near_ref), channel_id=1, source_target_pairs={{0,1},{1,0},{2,3},{3,2},{4,5},{5,4},{6,7},{7,6},{8,9},{9,8},{10,11... | collective-permute-start | bytes 786440 | tf_op jit(solution)/shard_map/ppermute | solution.py:375
  21.6 7.9 %collective-permute-start.1 = (bf16[512,256]{1,0:T(8,128)(2,1)S(1)}, bf16[512,256]{1,0:T(8,128)(2,1)S(1)}, u32[]{:S(2)}, u32[]{:S(2)}) collective-permute-start(bf16[512,256]{1,0:T(8,128)(2,1)S(1)} %collective-permute-done.near_ref), channel_id=1, source_target_pairs={{0,2},{1,3},{2,0},{3,1},{4,6},{5,7},{6,4},{7,5},{8,10},{9,11},{10,... | collective-permute-start | bytes 786440 | tf_op jit(solution)/shard_map/ppermute | solution.py:375
  29.4 2.0 %collective-permute-start.3 = (bf16[512,256]{1,0:T(8,128)(2,1)S(1)}, bf16[512,256]{1,0:T(8,128)(2,1)S(1)}, u32[]{:S(2)}, u32[]{:S(2)}) collective-permute-start(bf16[512,256]{1,0:T(8,128)(2,1)S(1)} %collective-permute-done.1.near_ref), channel_id=1, source_target_pairs={{0,1},{1,0},{2,3},{3,2},{4,5},{5,4},{6,7},{7,6},{8,9},{9,8},{10,11... | collective-permute-start | bytes 786440 | tf_op jit(solution)/shard_map/ppermute | solution.py:375
  39.1 5.0 %collective-permute-start.4 = (bf16[1024,256]{1,0:T(8,128)(2,1)S(1)}, bf16[1024,256]{1,0:T(8,128)(2,1)S(1)}, u32[]{:S(2)}, u32[]{:S(2)}) collective-permute-start(bf16[1024,256]{1,0:T(8,128)(2,1)S(1)} %get-tuple-element.56), channel_id=1, source_target_pairs={{0,1},{1,0},{2,3},{3,2},{4,5},{5,4},{6,7},{7,6},{8,9},{9,8},{10,11... | collective-permute-start | bytes 1572872 | tf_op jit(solution)/shard_map/ppermute | solution.py:375
  39.2 5.0 %collective-permute-start.9 = (bf16[1024,256]{1,0:T(8,128)(2,1)S(1)}, bf16[1024,256]{1,0:T(8,128)(2,1)S(1)}, u32[]{:S(2)}, u32[]{:S(2)}) collective-permute-start(bf16[1024,256]{1,0:T(8,128)(2,1)S(1)} %get-tuple-element.65), channel_id=1, source_target_pairs={{0,1},{1,0},{2,3},{3,2},{4,5},{5,4},{6,7},{7,6},{8,9},{9,8},{10,11... | collective-permute-start | bytes 1572872 | tf_op jit(solution)/shard_map/ppermute | solution.py:375
  40.8 6.3 %collective-permute-start.6 = (bf16[256,256]{1,0:T(8,128)(2,1)S(1)}, bf16[256,256]{1,0:T(8,128)(2,1)S(1)}, u32[]{:S(2)}, u32[]{:S(2)}) collective-permute-start(bf16[256,256]{1,0:T(8,128)(2,1)S(1)} %get-tuple-element.61), channel_id=1, source_target_pairs={{0,4},{1,5},{2,6},{3,7},{4,0},{5,1},{6,2},{7,3},{8,12},{9,13},{10,... | collective-permute-start | bytes 393224 | tf_op jit(solution)/shard_map/ppermute | solution.py:375
  40.9 6.3 %collective-permute-start.7 = (bf16[256,256]{1,0:T(8,128)(2,1)S(1)}, bf16[256,256]{1,0:T(8,128)(2,1)S(1)}, u32[]{:S(2)}, u32[]{:S(2)}) collective-permute-start(bf16[256,256]{1,0:T(8,128)(2,1)S(1)} %get-tuple-element.62), channel_id=1, source_target_pairs={{0,2},{1,3},{2,0},{3,1},{4,6},{5,7},{6,4},{7,5},{8,10},{9,11},{10,... | collective-permute-start | bytes 393224 | tf_op jit(solution)/shard_map/ppermute | solution.py:375
  41.0 9.6 %collective-permute-start.8 = (bf16[256,256]{1,0:T(8,128)(2,1)S(1)}, bf16[256,256]{1,0:T(8,128)(2,1)S(1)}, u32[]{:S(2)}, u32[]{:S(2)}) collective-permute-start(bf16[256,256]{1,0:T(8,128)(2,1)S(1)} %get-tuple-element.63), channel_id=1, source_target_pairs={{0,6},{1,7},{2,4},{3,5},{4,2},{5,3},{6,0},{7,1},{8,14},{9,15},{10,... | collective-permute-start | bytes 393224 | tf_op jit(solution)/shard_map/ppermute | solution.py:375
  50.6 7.7 %collective-permute-start.10 = (bf16[512,256]{1,0:T(8,128)(2,1)S(1)}, bf16[512,256]{1,0:T(8,128)(2,1)S(1)}, u32[]{:S(2)}, u32[]{:S(2)}) collective-permute-start(bf16[512,256]{1,0:T(8,128)(2,1)S(1)} %get-tuple-element.68), channel_id=1, source_target_pairs={{0,2},{1,3},{2,0},{3,1},{4,6},{5,7},{6,4},{7,5},{8,10},{9,11},{10,... | collective-permute-start | bytes 786440 | tf_op jit(solution)/shard_map/ppermute | solution.py:375
  50.6 13.0 %collective-permute-start.11 = (bf16[512,256]{1,0:T(8,128)(2,1)S(1)}, bf16[512,256]{1,0:T(8,128)(2,1)S(1)}, u32[]{:S(2)}, u32[]{:S(2)}) collective-permute-start(bf16[512,256]{1,0:T(8,128)(2,1)S(1)} %get-tuple-element.69), channel_id=1, source_target_pairs={{0,2},{1,3},{2,0},{3,1},{4,6},{5,7},{6,4},{7,5},{8,10},{9,11},{10,... | collective-permute-start | bytes 786440 | tf_op jit(solution)/shard_map/ppermute | solution.py:375
  52.8 14.9 %all-to-all-start = ((bf16[32,8,256]{2,1,0:T(8,128)(2,1)}), bf16[32,8,256]{2,1,0:T(8,128)(2,1)S(1)}, u32[]{:S(2)}, u32[]{:S(2)}) async-start(bf16[32,8,256]{2,1,0:T(8,128)(2,1)} %bitcast.3), calls=%async_computation | async-start | bytes 262144 | tf_op jit(solution)/shard_map/all_to_all | solution.py:371
  63.6 12.5 %collective-permute-start.12 = (bf16[512,256]{1,0:T(8,128)(2,1)S(1)}, bf16[512,256]{1,0:T(8,128)(2,1)S(1)}, u32[]{:S(2)}, u32[]{:S(2)}) collective-permute-start(bf16[512,256]{1,0:T(8,128)(2,1)S(1)} %shard_map.127), channel_id=1, source_target_pairs={{254,0},{255,1},{252,2},{253,3},{2,4},{3,5},{0,6},{1,7},{6,8},{7,9... | collective-permute-start | bytes 786440 | tf_op jit(solution)/shard_map/ppermute | solution.py:380
  68.4 15.3 %all-to-all-start.1 = ((f32[32,8,256]{2,1,0:T(8,128)}), f32[32,8,256]{2,1,0:T(8,128)S(1)}, u32[]{:S(2)}, u32[]{:S(2)}) async-start(f32[32,8,256]{2,1,0:T(8,128)} %shard_map.130), calls=%async_computation.1 | async-start | bytes 524288 | tf_op jit(solution)/shard_map/all_to_all | solution.py:371
  76.3 7.3 %collective-permute-start.13 = (bf16[528,256]{1,0:T(8,128)(2,1)S(1)}, bf16[528,256]{1,0:T(8,128)(2,1)S(1)}, u32[]{:S(2)}, u32[]{:S(2)}) collective-permute-start(bf16[528,256]{1,0:T(8,128)(2,1)S(1)} %shard_map.128.refs_2_), channel_id=1, source_target_pairs={{0,2},{1,3},{2,0},{3,1},{4,6},{5,7},{6,4},{7,5},{8,10},{9,11},{10,... | collective-permute-start | bytes 811016 | tf_op jit(solution)/shard_map/ppermute | solution.py:375
  76.4 16.6 %collective-permute-start.14 = (bf16[528,256]{1,0:T(8,128)(2,1)S(1)}, bf16[528,256]{1,0:T(8,128)(2,1)S(1)}, u32[]{:S(2)}, u32[]{:S(2)}) collective-permute-start(bf16[528,256]{1,0:T(8,128)(2,1)S(1)} %shard_map.128.refs_2_), channel_id=1, source_target_pairs={{0,1},{1,0},{2,3},{3,2},{4,5},{5,4},{6,7},{7,6},{8,9},{9,8},{10,11... | collective-permute-start | bytes 811016 | tf_op jit(solution)/shard_map/ppermute | solution.py:375
  83.8 9.3 %collective-permute-start.18 = (bf16[272,256]{1,0:T(8,128)(2,1)S(1)}, bf16[272,256]{1,0:T(8,128)(2,1)S(1)}, u32[]{:S(2)}, u32[]{:S(2)}) collective-permute-start(bf16[272,256]{1,0:T(8,128)(2,1)S(1)} %shard_map.131.refs_8_), channel_id=1, source_target_pairs={{0,6},{1,7},{2,4},{3,5},{4,2},{5,3},{6,0},{7,1},{8,14},{9,15},{10,... | collective-permute-start | bytes 417800 | tf_op jit(solution)/shard_map/ppermute | solution.py:375
  86.1 8.3 %collective-permute-start.17 = (bf16[272,256]{1,0:T(8,128)(2,1)S(1)}, bf16[272,256]{1,0:T(8,128)(2,1)S(1)}, u32[]{:S(2)}, u32[]{:S(2)}) collective-permute-start(bf16[272,256]{1,0:T(8,128)(2,1)S(1)} %shard_map.131.refs_8_), channel_id=1, source_target_pairs={{0,4},{1,5},{2,6},{3,7},{4,0},{5,1},{6,2},{7,3},{8,12},{9,13},{10,... | collective-permute-start | bytes 417800 | tf_op jit(solution)/shard_map/ppermute | solution.py:375
  86.1 10.8 %collective-permute-start.16 = (bf16[272,256]{1,0:T(8,128)(2,1)S(1)}, bf16[272,256]{1,0:T(8,128)(2,1)S(1)}, u32[]{:S(2)}, u32[]{:S(2)}) collective-permute-start(bf16[272,256]{1,0:T(8,128)(2,1)S(1)} %shard_map.131.refs_8_), channel_id=1, source_target_pairs={{0,2},{1,3},{2,0},{3,1},{4,6},{5,7},{6,4},{7,5},{8,10},{9,11},{10,... | collective-permute-start | bytes 417800 | tf_op jit(solution)/shard_map/ppermute | solution.py:375
  87.1 11.0 %collective-permute-start.15 = (bf16[528,256]{1,0:T(8,128)(2,1)S(1)}, bf16[528,256]{1,0:T(8,128)(2,1)S(1)}, u32[]{:S(2)}, u32[]{:S(2)}) collective-permute-start(bf16[528,256]{1,0:T(8,128)(2,1)S(1)} %collective-permute-done.13.refs_3_), channel_id=1, source_target_pairs={{0,1},{1,0},{2,3},{3,2},{4,5},{5,4},{6,7},{7,6},{8,9},{9,8},{10,11... | collective-permute-start | bytes 811016 | tf_op jit(solution)/shard_map/ppermute | solution.py:375
  93.0 5.1 %collective-permute-start.19 = (bf16[272,256]{1,0:T(8,128)(2,1)S(1)}, bf16[272,256]{1,0:T(8,128)(2,1)S(1)}, u32[]{:S(2)}, u32[]{:S(2)}) collective-permute-start(bf16[272,256]{1,0:T(8,128)(2,1)S(1)} %shard_map.131.refs_8_), channel_id=1, source_target_pairs={{0,1},{1,0},{2,3},{3,2},{4,5},{5,4},{6,7},{7,6},{8,9},{9,8},{10,11... | collective-permute-start | bytes 417800 | tf_op jit(solution)/shard_map/ppermute | solution.py:375
  93.1 5.0 %collective-permute-start.22 = (bf16[272,256]{1,0:T(8,128)(2,1)S(1)}, bf16[272,256]{1,0:T(8,128)(2,1)S(1)}, u32[]{:S(2)}, u32[]{:S(2)}) collective-permute-start(bf16[272,256]{1,0:T(8,128)(2,1)S(1)} %collective-permute-done.18.refs_11_), channel_id=1, source_target_pairs={{0,1},{1,0},{2,3},{3,2},{4,5},{5,4},{6,7},{7,6},{8,9},{9,8},{10,11... | collective-permute-start | bytes 417800 | tf_op jit(solution)/shard_map/ppermute | solution.py:375
  94.4 3.8 %collective-permute-start.21 = (bf16[272,256]{1,0:T(8,128)(2,1)S(1)}, bf16[272,256]{1,0:T(8,128)(2,1)S(1)}, u32[]{:S(2)}, u32[]{:S(2)}) collective-permute-start(bf16[272,256]{1,0:T(8,128)(2,1)S(1)} %collective-permute-done.17.refs_10_), channel_id=1, source_target_pairs={{0,1},{1,0},{2,3},{3,2},{4,5},{5,4},{6,7},{7,6},{8,9},{9,8},{10,11... | collective-permute-start | bytes 417800 | tf_op jit(solution)/shard_map/ppermute | solution.py:375
  96.9 2.2 %collective-permute-start.20 = (bf16[272,256]{1,0:T(8,128)(2,1)S(1)}, bf16[272,256]{1,0:T(8,128)(2,1)S(1)}, u32[]{:S(2)}, u32[]{:S(2)}) collective-permute-start(bf16[272,256]{1,0:T(8,128)(2,1)S(1)} %collective-permute-done.16.refs_9_), channel_id=1, source_target_pairs={{0,1},{1,0},{2,3},{3,2},{4,5},{5,4},{6,7},{7,6},{8,9},{9,8},{10,11... | collective-permute-start | bytes 417800 | tf_op jit(solution)/shard_map/ppermute | solution.py:375
  (8 other events, 170.3 us)
